TPU v7x, 32 devices: a whole 2x2x4 slice. The times are simulated.
32 devices in a mesh: section: 2 (over x), dp: 4 (over y, core), seq: 4 (over z).
Axes of the slice: x: 2, y: 2, z: 4, core: 2. Of those that a mesh axis runs over, the one named last changes fastest.
Arguments:
- boundary: bfloat16 [2, 2, 4, 672, 384], P('section', None, 'dp', 'seq'), may hold values from -6 to 6
- lengths: int32 [2, 4, 4], P(None, 'dp'), may hold values from 1 to 168, 577 in all within a row
- w_qkv: bfloat16 [2, 384, 1152], P('section', ('dp', 'seq')), may hold values from -0.3125 to 0.3125
- w_out: bfloat16 [2, 384, 384], P('section', ('dp', 'seq')), may hold values from -3.5 to 3.5
- w_fc1: bfloat16 [2, 384, 1536], P('section', ('dp', 'seq')), may hold values from -0.3125 to 0.3125
- w_fc2: bfloat16 [2, 1536, 384], P('section', ('dp', 'seq')), may hold values from -0.15625 to 0.15625
- gains: bfloat16 [2, 768], P('section', ('dp', 'seq')), may hold values from 0.5 to 1.5
- shifts: bfloat16 [2, 2304], P('section', ('dp', 'seq')), may hold values from -2 to 2
- fc1_bias: bfloat16 [2, 1536], P('section', ('dp', 'seq')), may hold values from -2 to 2
Outputs:
- boundary_out: bfloat16 [2, 2, 4, 672, 384], P('section', None, 'dp', 'seq')
- grad_qkv: float32 [2, 384, 1152], P('section', ('dp', 'seq'))
- grad_out: float32 [2, 384, 384], P('section', ('dp', 'seq'))
- grad_fc1: float32 [2, 384, 1536], P('section', ('dp', 'seq'))
- grad_fc2: float32 [2, 1536, 384], P('section', ('dp', 'seq'))
- grad_gains: float32 [2, 768], P('section', ('dp', 'seq'))
- grad_shifts: float32 [2, 2304], P('section', ('dp', 'seq'))
- grad_fc1_bias: float32 [2, 1536], P('section', ('dp', 'seq'))
Inputs may be any that keep to these rules, and one draw needn't show every extreme that they name: `lengths`: for each micro-batch and image the 4 entries are the token counts of consecutive ranges in index order, together 577; an index holds its range in its first slots, each entry is at least 1, and in every image one entry is exactly 168.
All inputs are finite; a program needn't handle non-finite values.
Results may differ from a plain program's by a relative error of at most 0.022.
Values may be sent and summed in bfloat16 or wider, within the bound.
No kernel may reach another device: no remote copies, remote signals or barrier semaphores. Data moves between devices by JAX's collectives and lax.ppermute only.
A program may use at most 128 MiB of HBM per device.

v0:
```python
import jax
import jax.numpy as jnp
from jax import lax
from jax.sharding import PartitionSpec as P

HEADS = 6


norm_eps = 1e-06


def shifted(value, axis, steps):
    count = lax.axis_size(axis)
    first, last = (max(0, -steps), min(count, count - steps))
    return lax.ppermute(value, axis, [(source, source + steps) for source in range(first, last)])


def norm_rows(rows_in, gain, shift):
    centre = jnp.mean(rows_in, axis=-1, keepdims=True)
    centred = rows_in - centre
    spread = jnp.mean(centred * centred, axis=-1, keepdims=True)
    return centred * lax.rsqrt(spread + norm_eps) * gain + shift


def exact_gelu(values_in):
    return jax.nn.gelu(values_in, approximate=False)


def unpack(gathered):
    w_qkv, w_out, w_fc1, w_fc2, gains, shifts, fc1_bias = [member[0] for member in gathered]
    model_width = w_out.shape[0]
    gains = gains.astype(jnp.float32).reshape(2, model_width)
    shifts = shifts.astype(jnp.float32).reshape(6, model_width)
    return (w_qkv, w_out, w_fc1, w_fc2, gains, shifts, fc1_bias.astype(jnp.float32))


def slot_masks(lengths_now, slot_count, seq_index):
    range_count = lengths_now.shape[1]
    positions = jnp.arange(range_count * slot_count, dtype=jnp.int32)
    owners = positions // slot_count
    places = positions % slot_count
    ranks = jnp.arange(range_count, dtype=jnp.int32)
    picker = (owners[:, None] == ranks[None, :]).astype(jnp.int32)
    reached = jnp.sum(lengths_now[:, None, :] * picker[None, :, :], axis=-1)
    key_valid = places[None, :] < reached
    own_count = jnp.sum(lengths_now * (ranks == seq_index).astype(jnp.int32)[None, :], axis=-1)
    row_valid = (jnp.arange(slot_count, dtype=jnp.int32)[None, :] < own_count[:, None]).astype(
        jnp.float32
    )
    return (key_valid, row_valid)


def forward_layer(block_in, weights, key_valid, row_valid):
    w_qkv, w_out, w_fc1, w_fc2, gains, shifts, fc1_bias = weights
    images, slot_count, model_width = block_in.shape
    head_dim = model_width // HEADS
    score_scale = head_dim ** (-0.5)
    block_in = block_in * row_valid[..., None]
    normed = norm_rows(block_in, gains[0], shifts[0]).astype(jnp.bfloat16)
    projected = jnp.dot(normed.reshape(-1, model_width), w_qkv, preferred_element_type=jnp.float32)
    projected = projected.reshape(images, slot_count, 3 * model_width)
    queries = (projected[..., :model_width] + shifts[2]).astype(jnp.bfloat16)
    own_keys = projected[..., model_width : 2 * model_width].astype(jnp.bfloat16)
    own_values = (projected[..., 2 * model_width :] + shifts[3]).astype(jnp.bfloat16)
    all_keys, all_values = (
        lax.all_gather(own_keys, "seq", axis=1, tiled=True),
        lax.all_gather(own_values, "seq", axis=1, tiled=True),
    )
    key_total = all_keys.shape[1]
    query_heads = queries.reshape(images, slot_count, HEADS, head_dim)
    key_heads = all_keys.reshape(images, key_total, HEADS, head_dim)
    value_heads = all_values.reshape(images, key_total, HEADS, head_dim)
    scores = (
        jnp.einsum("ichd,ishd->ihcs", query_heads, key_heads, preferred_element_type=jnp.float32)
        * score_scale
    )
    scores = jnp.where(key_valid[:, None, None, :], scores, -1e30)
    row_max = jnp.max(scores, axis=-1, keepdims=True)
    exponent = jnp.exp(scores - row_max)
    summed = jnp.sum(exponent, axis=-1, keepdims=True)
    attn_probs = (exponent / summed).astype(jnp.bfloat16)
    logsum = row_max + jnp.log(summed)
    attended = jnp.einsum(
        "ihcs,ishd->ichd", attn_probs, value_heads, preferred_element_type=jnp.float32
    )
    attended = attended.reshape(images, slot_count, model_width).astype(jnp.bfloat16)
    branch = jnp.dot(attended.reshape(-1, model_width), w_out, preferred_element_type=jnp.float32)
    middle = block_in + branch.reshape(block_in.shape) + shifts[4]
    normed_two = norm_rows(middle, gains[1], shifts[1]).astype(jnp.bfloat16)
    hidden = (
        jnp.dot(normed_two.reshape(-1, model_width), w_fc1, preferred_element_type=jnp.float32)
        + fc1_bias
    )
    active = exact_gelu(hidden).astype(jnp.bfloat16)
    second = (
        jnp.dot(active, w_fc2, preferred_element_type=jnp.float32).reshape(block_in.shape)
        + shifts[5]
    )
    block_out = (middle + second) * row_valid[..., None]
    stored = (
        block_in,
        normed,
        queries,
        all_keys,
        all_values,
        logsum,
        attended,
        middle,
        normed_two,
        hidden,
        active,
        key_valid,
        row_valid,
    )
    return (block_out, stored)


def backward_layer(grad_out, weights, stored):
    w_qkv, w_out, w_fc1, w_fc2, gains, shifts, fc1_bias = weights
    (
        block_in,
        normed,
        queries,
        all_keys,
        all_values,
        logsum,
        attended,
        middle,
        normed_two,
        hidden,
        active,
        key_valid,
        row_valid,
    ) = stored
    images, slot_count, model_width = block_in.shape
    key_total = all_keys.shape[1]
    head_dim = model_width // HEADS
    score_scale = head_dim ** (-0.5)
    grad_y = grad_out * row_valid[..., None]
    grad_second = grad_y.reshape(-1, model_width).astype(jnp.bfloat16)
    grad_active = jnp.einsum("rd,fd->rf", grad_second, w_fc2, preferred_element_type=jnp.float32)
    unused_gelu, gelu_back = jax.vjp(exact_gelu, hidden)
    grad_hidden = gelu_back(grad_active)[0].astype(jnp.bfloat16)
    grad_normed_two = jnp.einsum(
        "rf,df->rd", grad_hidden, w_fc1, preferred_element_type=jnp.float32
    ).reshape(block_in.shape)
    unused_two, norm_two_back = jax.vjp(norm_rows, middle, gains[1], shifts[1])
    grad_mid_part, grad_gain_two, grad_shift_two = norm_two_back(grad_normed_two)
    grad_middle = grad_y + grad_mid_part
    grad_branch = grad_middle.reshape(-1, model_width).astype(jnp.bfloat16)
    grad_attended = jnp.einsum(
        "rd,ed->re", grad_branch, w_out, preferred_element_type=jnp.float32
    ).astype(jnp.bfloat16)
    grad_att_heads = grad_attended.reshape(images, slot_count, HEADS, head_dim)
    query_heads = queries.reshape(images, slot_count, HEADS, head_dim)
    key_heads = all_keys.reshape(images, key_total, HEADS, head_dim)
    value_heads = all_values.reshape(images, key_total, HEADS, head_dim)
    scores = (
        jnp.einsum("ichd,ishd->ihcs", query_heads, key_heads, preferred_element_type=jnp.float32)
        * score_scale
    )
    scores = jnp.where(key_valid[:, None, None, :], scores, -1e30)
    probs_full = jnp.exp(scores - logsum)
    attn_probs = probs_full.astype(jnp.bfloat16)
    grad_probs = jnp.einsum(
        "ichd,ishd->ihcs", grad_att_heads, value_heads, preferred_element_type=jnp.float32
    )
    row_dot = jnp.sum(probs_full * grad_probs, axis=-1, keepdims=True)
    grad_scores = (probs_full * (grad_probs - row_dot)).astype(jnp.bfloat16)
    grad_queries = (
        jnp.einsum("ihcs,ishd->ichd", grad_scores, key_heads, preferred_element_type=jnp.float32)
        * score_scale
    )
    grad_queries = grad_queries.reshape(images, slot_count, model_width).astype(jnp.bfloat16)
    grad_keys_all = (
        jnp.einsum("ihcs,ichd->ishd", grad_scores, query_heads, preferred_element_type=jnp.float32)
        * score_scale
    )
    grad_values_all = jnp.einsum(
        "ihcs,ichd->ishd", attn_probs, grad_att_heads, preferred_element_type=jnp.float32
    )
    grad_keys, grad_values = (
        lax.psum_scatter(
            grad_keys_all.reshape(images, key_total, model_width).astype(jnp.bfloat16),
            "seq",
            scatter_dimension=1,
            tiled=True,
        ).astype(jnp.float32),
        lax.psum_scatter(
            grad_values_all.reshape(images, key_total, model_width).astype(jnp.bfloat16),
            "seq",
            scatter_dimension=1,
            tiled=True,
        ).astype(jnp.float32),
    )
    grad_projected = jnp.concatenate(
        [grad_queries, grad_keys.astype(jnp.bfloat16), grad_values.astype(jnp.bfloat16)], axis=-1
    )
    grad_proj_rows = grad_projected.reshape(-1, 3 * model_width)
    grad_normed = jnp.einsum(
        "rk,dk->rd", grad_proj_rows, w_qkv, preferred_element_type=jnp.float32
    ).reshape(block_in.shape)
    unused_one, norm_one_back = jax.vjp(norm_rows, block_in, gains[0], shifts[0])
    grad_in_part, grad_gain_one, grad_shift_one = norm_one_back(grad_normed)
    grad_in = (grad_middle + grad_in_part) * row_valid[..., None]
    gain_terms = jnp.concatenate([grad_gain_one, grad_gain_two])
    shift_terms = jnp.concatenate(
        [
            grad_shift_one,
            grad_shift_two,
            jnp.sum(grad_queries.astype(jnp.float32).reshape(-1, model_width), axis=0),
            jnp.sum(
                grad_values.astype(jnp.bfloat16).astype(jnp.float32).reshape(-1, model_width),
                axis=0,
            ),
            jnp.sum(grad_branch.astype(jnp.float32), axis=0),
            jnp.sum(grad_second.astype(jnp.float32), axis=0),
        ]
    )
    bias_terms = jnp.sum(grad_hidden.astype(jnp.float32), axis=0)
    row_pairs = (
        normed.reshape(-1, model_width),
        grad_proj_rows,
        attended.reshape(-1, model_width),
        grad_branch,
        normed_two.reshape(-1, model_width),
        grad_hidden,
        active,
        grad_second,
    )
    return (grad_in, row_pairs, (gain_terms, shift_terms, bias_terms))


def on_device(boundary, lengths, w_qkv, w_out, w_fc1, w_fc2, gains, shifts, fc1_bias):
    section_index = lax.axis_index("section")
    seq_index = lax.axis_index("seq")
    micro_count = boundary.shape[1]
    slot_count = boundary.shape[3]
    weights = unpack(
        (
            lax.all_gather(w_qkv, ("dp", "seq"), axis=1, tiled=True),
            lax.all_gather(w_out, ("dp", "seq"), axis=1, tiled=True),
            lax.all_gather(w_fc1, ("dp", "seq"), axis=1, tiled=True),
            lax.all_gather(w_fc2, ("dp", "seq"), axis=1, tiled=True),
            lax.all_gather(gains, ("dp", "seq"), axis=1, tiled=True),
            lax.all_gather(shifts, ("dp", "seq"), axis=1, tiled=True),
            lax.all_gather(fc1_bias, ("dp", "seq"), axis=1, tiled=True),
        )
    )
    inputs = boundary[0].astype(jnp.float32)
    arriving = jnp.zeros(inputs.shape[1:], jnp.float32)
    stored_ticks = []
    output_ticks = []
    for tick_index in range(micro_count + 1):
        micro_now = jnp.clip(tick_index - section_index, 0, micro_count - 1)
        lengths_now = lax.dynamic_index_in_dim(lengths, micro_now, 0, keepdims=False)
        key_valid, row_valid = slot_masks(lengths_now, slot_count, seq_index)
        first_input = inputs[min(tick_index, micro_count - 1)]
        block_in = jnp.where(section_index == 0, first_input, arriving)
        block_out, stored = forward_layer(block_in, weights, key_valid, row_valid)
        block_out = block_out.astype(jnp.bfloat16)
        stored_ticks.append(stored)
        output_ticks.append(block_out)
        if tick_index < micro_count:
            arriving = shifted(block_out, "section", 1).astype(jnp.float32)
    weights = unpack(
        (
            lax.all_gather(w_qkv, ("dp", "seq"), axis=1, tiled=True),
            lax.all_gather(w_out, ("dp", "seq"), axis=1, tiled=True),
            lax.all_gather(w_fc1, ("dp", "seq"), axis=1, tiled=True),
            lax.all_gather(w_fc2, ("dp", "seq"), axis=1, tiled=True),
            lax.all_gather(gains, ("dp", "seq"), axis=1, tiled=True),
            lax.all_gather(shifts, ("dp", "seq"), axis=1, tiled=True),
            lax.all_gather(fc1_bias, ("dp", "seq"), axis=1, tiled=True),
        )
    )
    returning = jnp.zeros(inputs.shape[1:], jnp.float32)
    back_ticks = []
    pair_ticks = []
    small_ticks = []
    for turn_index in range(micro_count + 1):
        stored = stored_ticks[micro_count - turn_index]
        if turn_index < micro_count:
            supplied = inputs[micro_count - 1 - turn_index]
        else:
            supplied = jnp.zeros(inputs.shape[1:], jnp.float32)
        grad_out = jnp.where(section_index == 1, supplied, returning)
        grad_in, row_pairs, small_terms = backward_layer(grad_out, weights, stored)
        grad_in = grad_in.astype(jnp.bfloat16)
        back_ticks.append(grad_in)
        pair_ticks.append(row_pairs)
        small_ticks.append(small_terms)
        if turn_index < micro_count:
            returning = shifted(grad_in, "section", -1).astype(jnp.float32)
    first_valid = 1 - section_index

    def valid_rows(member_index):
        stacked = jnp.stack([pairs[member_index] for pairs in pair_ticks])
        chosen = lax.dynamic_slice_in_dim(stacked, first_valid, micro_count, 0)
        return chosen.reshape(-1, stacked.shape[-1])

    def weight_term(left_index):
        return jnp.einsum(
            "rd,rk->dk",
            valid_rows(left_index),
            valid_rows(left_index + 1),
            preferred_element_type=jnp.float32,
        )

    def small_sum(member_index):
        stacked = jnp.stack([terms[member_index] for terms in small_ticks])
        return jnp.sum(lax.dynamic_slice_in_dim(stacked, first_valid, micro_count, 0), axis=0)

    summed = (
        lax.psum_scatter(weight_term(0)[None], ("dp", "seq"), scatter_dimension=1, tiled=True),
        lax.psum_scatter(weight_term(2)[None], ("dp", "seq"), scatter_dimension=1, tiled=True),
        lax.psum_scatter(weight_term(4)[None], ("dp", "seq"), scatter_dimension=1, tiled=True),
        lax.psum_scatter(weight_term(6)[None], ("dp", "seq"), scatter_dimension=1, tiled=True),
        lax.psum_scatter(small_sum(0)[None], ("dp", "seq"), scatter_dimension=1, tiled=True),
        lax.psum_scatter(small_sum(1)[None], ("dp", "seq"), scatter_dimension=1, tiled=True),
        lax.psum_scatter(small_sum(2)[None], ("dp", "seq"), scatter_dimension=1, tiled=True),
    )
    per_micro = []
    for micro_index in range(micro_count):
        per_micro.append(
            jnp.where(
                section_index == 1,
                output_ticks[micro_index + 1],
                back_ticks[micro_count - micro_index],
            )
        )
    boundary_out = jnp.stack(per_micro)[None]
    return (
        boundary_out,
        summed[0],
        summed[1],
        summed[2],
        summed[3],
        summed[4],
        summed[5],
        summed[6],
    )


def solution(mesh):
    placed = (
        P("section", None, "dp", "seq", None),
        P(None, "dp", None),
        P("section", ("dp", "seq"), None),
        P("section", ("dp", "seq"), None),
        P("section", ("dp", "seq"), None),
        P("section", ("dp", "seq"), None),
        P("section", ("dp", "seq")),
        P("section", ("dp", "seq")),
        P("section", ("dp", "seq")),
    )
    return jax.shard_map(
        on_device,
        mesh=mesh,
        in_specs=placed,
        out_specs=(
            P("section", None, "dp", "seq", None),
            P("section", ("dp", "seq"), None),
            P("section", ("dp", "seq"), None),
            P("section", ("dp", "seq"), None),
            P("section", ("dp", "seq"), None),
            P("section", ("dp", "seq")),
            P("section", ("dp", "seq")),
            P("section", ("dp", "seq")),
        ),
        check_vma=False,
    )
```

profile of v0, /device:TPU:0, one launch (start us, length us, event | category | flops | bytes accessed | tf_op | source)
XLA Modules:
  0.0 960.2 jit_solution(2470191726275286025)
XLA Ops:
  17.4 63.6 %all-reduce.11 = (bf16[768]{0:T(1024)(128)(2,1)S(1)}, bf16[2304]{0:T(1024)(128)(2,1)S(1)}, bf16[1536]{0:T(1024)(128)(2,1)S(1)}) all-reduce(bf16[768]{0:T(1024)(128)(2,1)S(1)} %dynamic-update-slice, bf16[2304]{0:T(1024)(128)(2,1)S(1)} %dynamic-update-slice.1, ...), channel_id=1, replica_groups=mesh['section'=2,'dp'=4,'seq'=4] {'dp','seq'}, use_global_device_ids=true, to_apply=%add | all-reduce | flops 4608 | bytes 18432
  83.2 37.5 %all_gather.46 = bf16[1,384,1152]{2,1,0:T(8,128)(2,1)S(1)} all-gather(bf16[1,24,1152]{2,1,0:T(8,128)(2,1)S(1)} %copy-done.104), channel_id=1, replica_groups=mesh['section'=2,'dp'=4,'seq'=4] {'dp','seq'}, dimensions={1}, use_global_device_ids=true | all-gather | bytes 940032 | tf_op jit(solution)/shard_map/all_gather | solution.py:241
  122.1 15.1 %all_gather.48 = bf16[1,672,384]{2,1,0:T(8,128)(2,1)S(1)} all-gather(bf16[1,168,384]{2,1,0:T(8,128)(2,1)S(1)} %slice.243), channel_id=1, replica_groups=mesh['section'=2,'dp'=4,'seq'=4] {'seq'}, dimensions={1}, use_global_device_ids=true | all-gather | bytes 645120 | tf_op jit(solution)/shard_map/all_gather | solution.py:66
  138.3 15.9 %all_gather.47 = bf16[1,672,384]{2,1,0:T(8,128)(2,1)S(1)} all-gather(bf16[1,168,384]{2,1,0:T(8,128)(2,1)S(1)} %get-tuple-element.109), channel_id=1, replica_groups=mesh['section'=2,'dp'=4,'seq'=4] {'seq'}, dimensions={1}, use_global_device_ids=true | all-gather | bytes 645120 | tf_op jit(solution)/shard_map/all_gather | solution.py:67
  155.3 1.8 fusion.318
  158.0 31.2 %all_gather.49 = bf16[1,384,384]{2,1,0:T(8,128)(2,1)S(1)} all-gather(bf16[1,24,384]{2,1,0:T(8,128)(2,1)S(1)} %copy-done.135), channel_id=1, replica_groups=mesh['section'=2,'dp'=4,'seq'=4] {'dp','seq'}, dimensions={1}, use_global_device_ids=true | all-gather | bytes 313344 | tf_op jit(solution)/shard_map/all_gather | solution.py:242
  192.1 5.4 multiply_convert_fusion.5
  197.6 2.0 fusion.110
  199.6 4.2 collective-permute-start
  209.2 1.7 copy.108
  210.9 16.2 %all_gather.54 = bf16[1,672,384]{2,1,0:T(8,128)(2,1)} all-gather(bf16[1,168,384]{2,1,0:T(8,128)(2,1)S(1)} %slice.242), channel_id=1, replica_groups=mesh['section'=2,'dp'=4,'seq'=4] {'seq'}, dimensions={1}, use_global_device_ids=true | all-gather | bytes 645120 | tf_op jit(solution)/shard_map/all_gather | solution.py:66
  227.1 2.1 copy.109
  229.2 16.0 %all_gather.53 = bf16[1,672,384]{2,1,0:T(8,128)(2,1)} all-gather(bf16[1,168,384]{2,1,0:T(8,128)(2,1)} %get-tuple-element.107), channel_id=1, replica_groups=mesh['section'=2,'dp'=4,'seq'=4] {'seq'}, dimensions={1}, use_global_device_ids=true | all-gather | bytes 645120 | tf_op jit(solution)/shard_map/all_gather | solution.py:67
  245.2 2.1 copy.107
  247.3 1.9 fusion.320
  253.8 3.6 multiply_convert_fusion.4
  258.2 5.0 collective-permute-start.1
  265.0 1.8 fusion.312
  269.5 1.7 copy.111
  271.2 16.6 %all_gather.56 = bf16[1,672,384]{2,1,0:T(8,128)(2,1)} all-gather(bf16[1,168,384]{2,1,0:T(8,128)(2,1)S(1)} %slice.241), channel_id=1, replica_groups=mesh['section'=2,'dp'=4,'seq'=4] {'seq'}, dimensions={1}, use_global_device_ids=true | all-gather | bytes 645120 | tf_op jit(solution)/shard_map/all_gather | solution.py:66
  287.8 2.1 copy.112
  289.9 16.0 %all_gather.55 = bf16[1,672,384]{2,1,0:T(8,128)(2,1)} all-gather(bf16[1,168,384]{2,1,0:T(8,128)(2,1)} %get-tuple-element.105), channel_id=1, replica_groups=mesh['section'=2,'dp'=4,'seq'=4] {'seq'}, dimensions={1}, use_global_device_ids=true | all-gather | bytes 645120 | tf_op jit(solution)/shard_map/all_gather | solution.py:67
  305.9 2.1 copy.110
  308.0 1.9 fusion.322
  313.9 3.3 multiply_convert_fusion.3
  322.6 3.6 fusion.21
  326.2 2.1 copy.115
  328.3 3.3 multiply_reduce_fusion.2
  334.7 2.1 copy.114
  336.9 1.7 copy.127
  338.6 1.7 copy.126
  340.3 3.5 convert_reduce_fusion.5
  344.9 6.7 reduce-scatter.56.cloned.1.call-done
  351.6 22.4 %reduce-scatter.54.cloned.1.call-done = bf16[1,168,384]{2,1,0:T(8,128)(2,1)} async-done(((bf16[1,672,384]{2,1,0:T(8,128)(2,1)}), bf16[1,168,384]{2,1,0:T(8,128)(2,1)}) %reduce-scatter.54.cloned.1.call-update) | async-done | bytes 129040
  374.1 2.7 fusion.206
  381.9 1.7 copy.125
  389.4 1.6 convert_reduce_fusion.9
  391.0 3.4 convert_reduce_fusion.1
  399.0 1.7 copy.117
  400.7 3.6 fusion.24
  404.3 2.1 copy.119
  406.5 3.3 multiply_reduce_fusion.1
  412.9 2.1 copy.118
  426.6 2.9 convert_reduce_fusion.4
  430.2 1.7 copy.120
  431.9 18.1 %reduce-scatter.58.cloned.1.call-done = bf16[1,168,384]{2,1,0:T(8,128)(2,1)} async-done(((bf16[1,672,384]{2,1,0:T(8,128)(2,1)}), bf16[1,168,384]{2,1,0:T(8,128)(2,1)}) %reduce-scatter.58.cloned.1.call-update) | async-done | bytes 129040
  450.0 3.1 fusion.204
  463.3 2.2 collective-permute-done.3
  466.2 3.1 convert_reduce_fusion
  475.3 1.6 fusion.27
  476.9 2.1 copy.123
  479.1 2.1 multiply_reduce_fusion
  487.6 10.8 %reduce-scatter.64.cloned.1.call-done = bf16[1,168,384]{2,1,0:T(8,128)(2,1)} async-done(((bf16[1,672,384]{2,1,0:T(8,128)(2,1)}), bf16[1,168,384]{2,1,0:T(8,128)(2,1)}) %reduce-scatter.64.cloned.1.call-update) | async-done | bytes 129040
  498.4 22.5 %reduce-scatter.62.cloned.1.call-done = bf16[1,168,384]{2,1,0:T(8,128)(2,1)} async-done(((bf16[1,672,384]{2,1,0:T(8,128)(2,1)}), bf16[1,168,384]{2,1,0:T(8,128)(2,1)}) %reduce-scatter.62.cloned.1.call-update) | async-done | bytes 129040
  527.1 3.6 convolution_bitcast_fusion
  532.2 2.6 convolution_bitcast_fusion.1
  536.2 2.5 convolution_bitcast_fusion.2
  541.7 37.8 %reduce-scatter.52.cloned.1.call-done = f32[96,1]{1,0:T(8,128)} async-done(((f32[1536,1]{1,0:T(8,128)}), f32[96,1]{1,0:T(8,128)}) %reduce-scatter.52.cloned.1.call-update) | async-done | bytes 400
  582.1 55.8 %reduce-scatter.48.cloned.1.call-done = f32[48,1]{1,0:T(8,128)} async-done(((f32[768,1]{1,0:T(8,128)}), f32[48,1]{1,0:T(8,128)}) %reduce-scatter.48.cloned.1.call-update) | async-done | bytes 208
  639.2 59.4 %reduce-scatter.50.cloned.1.call-done = f32[144,1]{1,0:T(8,128)} async-done(((f32[2304,1]{1,0:T(8,128)}), f32[144,1]{1,0:T(8,128)}) %reduce-scatter.50.cloned.1.call-update) | async-done | bytes 592
  700.1 56.3 %reduce-scatter.68.cloned.1.call-done = f32[1,24,384]{2,1,0:T(8,128)} async-done(((f32[1,384,384]{2,1,0:T(8,128)}), f32[1,24,384]{2,1,0:T(8,128)}) %reduce-scatter.68.cloned.1.call-update) | async-done | bytes 36880
  756.4 66.9 %reduce-scatter.46.cloned.1.call-done = f32[1,96,384]{2,1,0:T(8,128)} async-done(((f32[1,1536,384]{2,1,0:T(8,128)}), f32[1,96,384]{2,1,0:T(8,128)}) %reduce-scatter.46.cloned.1.call-update) | async-done | bytes 147472 | tf_op jit(solution)/shard_map/reduce_scatter | solution.py:318
  823.2 66.2 %reduce-scatter.44.cloned.1.call-done = f32[1,24,1536]{2,1,0:T(8,128)} async-done(((f32[1,384,1536]{2,1,0:T(8,128)}), f32[1,24,1536]{2,1,0:T(8,128)}) %reduce-scatter.44.cloned.1.call-update) | async-done | bytes 147472 | tf_op jit(solution)/shard_map/reduce_scatter | solution.py:317
  889.4 64.0 %reduce-scatter.66.cloned.1.call-done = f32[1,24,1152]{2,1,0:T(8,128)} async-done(((f32[1,384,1152]{2,1,0:T(8,128)}), f32[1,24,1152]{2,1,0:T(8,128)}) %reduce-scatter.66.cloned.1.call-update) | async-done | bytes 110608
  (598 shorter events, 116.4 us)
Async XLA Ops:
  7.2 76.0 %copy-start.104 = (bf16[1,24,1152]{2,1,0:T(8,128)(2,1)S(1)}, bf16[1,24,1152]{2,1,0:T(8,128)(2,1)}, u32[]{:S(2)}) copy-start(bf16[1,24,1152]{2,1,0:T(8,128)(2,1)} %param.11) | copy-start | bytes 165892
  7.2 184.4 %all-gather.3.cloned.1.call-start = ((), (), s32[]{:S(2)}) async-start(), calls=%async_computation.13 | async-start | bytes 1253376 | tf_op jit(solution)/shard_map/all_gather | solution.py:243
  7.9 189.6 %all-gather.5.cloned.1.call-start = ((), (), s32[]{:S(2)}) async-start(), calls=%async_computation.14 | async-start | bytes 1253376 | tf_op jit(solution)/shard_map/all_gather | solution.py:244
  8.7 343.0 %reduce-scatter.56.cloned.1.call-start = ((), (), s32[]{:S(2)}) async-start(), calls=%async_computation.21 | async-start | bytes 645120
  81.7 110.4 %copy-start.183 = (f32[1536]{0:T(1024)}, f32[1536]{0:T(1024)S(1)}, u32[]{:S(2)}) copy-start(f32[1536]{0:T(1024)S(1)} %add.449) | copy-start | bytes 18436
  82.7 39.1 %copy-start.4 = (f32[1,2,1,168,384]{4,3,2,1,0:T(8,128)}, f32[1,2,1,168,384]{4,3,2,1,0:T(8,128)S(1)}, u32[]{:S(2)}) copy-start(f32[1,2,1,168,384]{4,3,2,1,0:T(8,128)S(1)} %convert_element_type.640) | copy-start | bytes 1548292
  82.9 38.9 %copy-start.124 = (f32[168]{0:T(256)}, f32[168]{0:T(256)S(1)}, u32[]{:S(2)}) copy-start(f32[168]{0:T(256)S(1)} %broadcast_multiply_fusion.5) | copy-start | bytes 2020
  83.2 38.7 %copy-start.162 = (f32[168]{0:T(256)}, f32[168]{0:T(256)S(1)}, u32[]{:S(2)}) copy-start(f32[168]{0:T(256)S(1)} %multiply_reduce_fusion.12) | copy-start | bytes 2020
  83.2 38.7 %copy-start.136 = (f32[168]{0:T(256)}, f32[168]{0:T(256)S(1)}, u32[]{:S(2)}) copy-start(f32[168]{0:T(256)S(1)} %fusion.276) | copy-start | bytes 2020
  121.4 68.7 %copy-start.109 = (f32[384]{0:T(512)}, f32[384]{0:T(512)S(1)}, u32[]{:S(2)}) copy-start(f32[384]{0:T(512)S(1)} %get-tuple-element.57) | copy-start | bytes 4612
  121.4 70.7 %copy-start.105 = (f32[384]{0:T(512)}, f32[384]{0:T(512)S(1)}, u32[]{:S(2)}) copy-start(f32[384]{0:T(512)S(1)} %get-tuple-element.56) | copy-start | bytes 4612
  122.1 33.1 %copy-start.49 = (bf16[1,168,384]{1,2,0:T(8,128)(2,1)}, bf16[1,168,384]{1,2,0:T(8,128)(2,1)S(1)}, u32[]{:S(2)}) copy-start(bf16[1,168,384]{1,2,0:T(8,128)(2,1)S(1)} %copy.105) | copy-start | bytes 387076
  157.1 32.1 %copy-start.39 = (bf16[1,672,384]{1,2,0:T(8,128)(2,1)S(1)}, bf16[1,672,384]{1,2,0:T(8,128)(2,1)}, u32[]{:S(2)}) copy-start(bf16[1,672,384]{1,2,0:T(8,128)(2,1)} %copy.104) | copy-start | bytes 1548292
  158.0 32.1 %copy-start.118 = (f32[6,168]{1,0:T(8,128)}, f32[6,168]{1,0:T(8,128)S(1)}, u32[]{:S(2)}) copy-start(f32[6,168]{1,0:T(8,128)S(1)} %fusion) | copy-start | bytes 12100
  190.6 6.9 copy-start.139
  197.5 8.7 copy-start.6
  197.6 10.4 %copy-start.12 = (bf16[1,384,1152]{2,1,0:T(8,128)(2,1)S(1)}, bf16[1,384,1152]{2,1,0:T(8,128)(2,1)}, u32[]{:S(2)}) copy-start(bf16[1,384,1152]{2,1,0:T(8,128)(2,1)} %copy-done.11) | copy-start | bytes 2654212
  199.6 6.7 collective-permute-start
  227.1 20.3 %copy-start.189 = (pred[672]{0:T(1024)(128)(4,1)S(1)}, pred[672]{0:T(1024)(128)(4,1)}, u32[]{:S(2)}) copy-start(pred[672]{0:T(1024)(128)(4,1)} %fusion.272) | copy-start | bytes 2020
  258.2 10.1 %copy-start.66 = (bf16[1,168,384]{2,1,0:T(8,128)(2,1)}, bf16[1,168,384]{2,1,0:T(8,128)(2,1)S(1)}, u32[]{:S(2)}) copy-start(bf16[1,168,384]{2,1,0:T(8,128)(2,1)S(1)} %fusion.98) | copy-start | bytes 387076
  258.2 6.9 collective-permute-start.1
  287.8 20.2 %copy-start.188 = (pred[672]{0:T(1024)(128)(4,1)S(1)}, pred[672]{0:T(1024)(128)(4,1)}, u32[]{:S(2)}) copy-start(pred[672]{0:T(1024)(128)(4,1)} %fusion.271) | copy-start | bytes 2020
  313.0 6.9 copy-start.27
  328.3 45.8 %reduce-scatter.54.cloned.1.call-start = ((), (), s32[]{:S(2)}) async-start(), calls=%async_computation.20 | async-start | bytes 645120
  336.9 95.0 %reduce-scatter.60.cloned.1.call-start = ((), (), s32[]{:S(2)}) async-start(), calls=%async_computation.23 | async-start | bytes 645120
  343.8 33.5 %copy-start.146 = (f32[168]{0:T(256)S(1)}, f32[168]{0:T(256)}, u32[]{:S(2)}) copy-start(f32[168]{0:T(256)} %copy-done.145) | copy-start | bytes 2020
  344.9 33.4 %copy-start.85 = (bf16[1,168,384]{2,1,0:T(8,128)(2,1)}, bf16[1,168,384]{2,1,0:T(8,128)(2,1)S(1)}, u32[]{:S(2)}) copy-start(bf16[1,168,384]{2,1,0:T(8,128)(2,1)S(1)} %copy.116) | copy-start | bytes 387076
  344.9 33.4 %copy-start.151 = (f32[168]{0:T(256)S(1)}, f32[168]{0:T(256)}, u32[]{:S(2)}) copy-start(f32[168]{0:T(256)} %copy-done.149) | copy-start | bytes 2020
  379.7 9.6 %collective-permute-start.2 = (bf16[1,168,384]{2,1,0:T(8,128)(2,1)}, bf16[1,168,384]{2,1,0:T(8,128)(2,1)S(1)}, u32[]{:S(2)}, u32[]{:S(2)}) collective-permute-start(bf16[1,168,384]{2,1,0:T(8,128)(2,1)} %multiply_convert_fusion.7), channel_id=1, source_target_pairs={{16,0},{17,1},{18,2},{19,3},{20,4},{21,5},{22,6},{23,7},{24,8},{25... | collective-permute-start | bytes 387080 | tf_op jit(solution)/shard_map/ppermute | solution.py:15
  406.4 43.6 %reduce-scatter.58.cloned.1.call-start = ((), (), s32[]{:S(2)}) async-start(), calls=%async_computation.22 | async-start | bytes 645120
  415.0 83.4 %reduce-scatter.64.cloned.1.call-start = ((), (), s32[]{:S(2)}) async-start(), calls=%async_computation.25 | async-start | bytes 645120
  418.9 31.1 %copy-start.142 = (f32[168]{0:T(256)S(1)}, f32[168]{0:T(256)}, u32[]{:S(2)}) copy-start(f32[168]{0:T(256)} %copy-done.141) | copy-start | bytes 2020
  418.9 31.1 %copy-start.160 = (f32[168]{0:T(256)S(1)}, f32[168]{0:T(256)}, u32[]{:S(2)}) copy-start(f32[168]{0:T(256)} %copy-done.159) | copy-start | bytes 2020
  431.9 25.5 %copy-start.132 = (f32[168]{0:T(256)S(1)}, f32[168]{0:T(256)}, u32[]{:S(2)}) copy-start(f32[168]{0:T(256)} %copy-done.129) | copy-start | bytes 2020
  456.0 6.6 copy-start.190
  456.0 10.2 %copy-start.21 = (bf16[1,1536,384]{2,1,0:T(8,128)(2,1)S(1)}, bf16[1,1536,384]{2,1,0:T(8,128)(2,1)}, u32[]{:S(2)}) copy-start(bf16[1,1536,384]{2,1,0:T(8,128)(2,1)} %all-gather.5.cloned.1.call-done) | copy-start | bytes 3538948
  458.7 7.6 copy-start.61
  458.7 6.8 collective-permute-start.3
  479.1 41.8 %reduce-scatter.62.cloned.1.call-start = ((), (), s32[]{:S(2)}) async-start(), calls=%async_computation.24 | async-start | bytes 645120
  484.6 94.9 %reduce-scatter.52.cloned.1.call-start = ((), (), s32[]{:S(2)}) async-start(), calls=%async_computation.19 | async-start | bytes 835584
  485.9 35.0 %copy-start.10 = (f32[1,2,1,168,384]{4,3,2,1,0:T(8,128)S(1)}, f32[1,2,1,168,384]{4,3,2,1,0:T(8,128)}, u32[]{:S(2)}) copy-start(f32[1,2,1,168,384]{4,3,2,1,0:T(8,128)} %copy-done.4) | copy-start | bytes 1548292
  485.9 35.0 %copy-start.14 = (bf16[1,384,1152]{2,1,0:T(8,128)(2,1)S(1)}, bf16[1,384,1152]{2,1,0:T(8,128)(2,1)}, u32[]{:S(2)}) copy-start(bf16[1,384,1152]{2,1,0:T(8,128)(2,1)} %copy-done.11) | copy-start | bytes 2654212
  485.9 35.0 %copy-start.126 = (f32[168]{0:T(256)S(1)}, f32[168]{0:T(256)}, u32[]{:S(2)}) copy-start(f32[168]{0:T(256)} %copy-done.124) | copy-start | bytes 2020
  486.0 34.9 %copy-start.138 = (f32[168]{0:T(256)S(1)}, f32[168]{0:T(256)}, u32[]{:S(2)}) copy-start(f32[168]{0:T(256)} %copy-done.136) | copy-start | bytes 2020
  486.0 34.9 %copy-start.152 = (f32[168]{0:T(256)S(1)}, f32[168]{0:T(256)}, u32[]{:S(2)}) copy-start(f32[168]{0:T(256)} %copy-done.149) | copy-start | bytes 2020
  486.2 36.3 %copy-start.95 = (bf16[1,168,384]{2,1,0:T(8,128)(2,1)}, bf16[1,168,384]{2,1,0:T(8,128)(2,1)S(1)}, u32[]{:S(2)}) copy-start(bf16[1,168,384]{2,1,0:T(8,128)(2,1)S(1)} %copy.124) | copy-start | bytes 387076
  487.5 35.0 %copy-start.187 = (f32[384]{0:T(512)S(1)}, f32[384]{0:T(512)}, u32[]{:S(2)}) copy-start(f32[384]{0:T(512)} %get-tuple-element.50) | copy-start | bytes 4612
  487.5 35.0 %copy-start.153 = (f32[1,768]{1,0:T(1,128)S(1)}, f32[1,768]{1,0:T(1,128)}, u32[]{:S(2)}) copy-start(f32[1,768]{1,0:T(1,128)} %stack.110) | copy-start | bytes 9220
  487.5 36.0 %copy-start.154 = (f32[2304]{0:T(1024)S(1)}, f32[2304]{0:T(1024)}, u32[]{:S(2)}) copy-start(f32[2304]{0:T(1024)} %custom-call) | copy-start | bytes 27652
  487.5 36.0 %copy-start.186 = (f32[384]{0:T(512)S(1)}, f32[384]{0:T(512)}, u32[]{:S(2)}) copy-start(f32[384]{0:T(512)} %get-tuple-element.54) | copy-start | bytes 4612
  487.5 36.1 %copy-start.177 = (f32[384]{0:T(512)S(1)}, f32[384]{0:T(512)}, u32[]{:S(2)}) copy-start(f32[384]{0:T(512)} %get-tuple-element.80) | copy-start | bytes 4612
  487.5 36.1 %copy-start.176 = (f32[384]{0:T(512)S(1)}, f32[384]{0:T(512)}, u32[]{:S(2)}) copy-start(f32[384]{0:T(512)} %get-tuple-element.78) | copy-start | bytes 4612
  487.6 36.1 %copy-start.156 = (f32[2304]{0:T(1024)S(1)}, f32[2304]{0:T(1024)}, u32[]{:S(2)}) copy-start(f32[2304]{0:T(1024)} %constant_dynamic-update-slice_fusion.3) | copy-start | bytes 27652
  487.6 150.3 %reduce-scatter.48.cloned.1.call-start = ((), (), s32[]{:S(2)}) async-start(), calls=%async_computation.17 | async-start | bytes 417792
  498.4 25.2 %copy-start.101 = (bf16[1,168,384]{2,1,0:T(8,128)(2,1)S(1)}, bf16[1,168,384]{2,1,0:T(8,128)(2,1)}, u32[]{:S(2)}) copy-start(bf16[1,168,384]{2,1,0:T(8,128)(2,1)} %reduce-scatter.64.cloned.1.call-done) | copy-start | bytes 387076
  523.8 174.8 %reduce-scatter.50.cloned.1.call-start = ((), (), s32[]{:S(2)}) async-start(), calls=%async_computation.18 | async-start | bytes 1253376
  525.5 230.9 %reduce-scatter.68.cloned.1.call-start = ((), (), s32[]{:S(2)}) async-start(), calls=%async_computation.27 | async-start | bytes 626688
  527.0 296.3 %reduce-scatter.46.cloned.1.call-start = ((), (), s32[]{:S(2)}) async-start(), calls=%async_computation.16 | async-start | bytes 2506752 | tf_op jit(solution)/shard_map/reduce_scatter | solution.py:318
  530.8 358.7 %reduce-scatter.44.cloned.1.call-start = ((), (), s32[]{:S(2)}) async-start(), calls=%async_computation.15 | async-start | bytes 2506752 | tf_op jit(solution)/shard_map/reduce_scatter | solution.py:317
  534.8 418.5 %reduce-scatter.66.cloned.1.call-start = ((), (), s32[]{:S(2)}) async-start(), calls=%async_computation.26 | async-start | bytes 1880064
  540.1 40.8 %copy-start.163 = (f32[168]{0:T(256)S(1)}, f32[168]{0:T(256)}, u32[]{:S(2)}) copy-start(f32[168]{0:T(256)} %copy-done.162) | copy-start | bytes 2020
  540.1 41.1 %copy-start.44 = (f32[168,384]{1,0:T(8,128)S(1)}, f32[168,384]{1,0:T(8,128)}, u32[]{:S(2)}) copy-start(f32[168,384]{1,0:T(8,128)} %copy-done.43) | copy-start | bytes 774148
  540.1 41.1 %copy-start.67 = (bf16[1,168,384]{2,1,0:T(8,128)(2,1)S(1)}, bf16[1,168,384]{2,1,0:T(8,128)(2,1)}, u32[]{:S(2)}) copy-start(bf16[1,168,384]{2,1,0:T(8,128)(2,1)} %copy-done.66) | copy-start | bytes 387076
  540.1 41.1 %copy-start.171 = (f32[168]{0:T(256)S(1)}, f32[168]{0:T(256)}, u32[]{:S(2)}) copy-start(f32[168]{0:T(256)} %copy-done.170) | copy-start | bytes 2020
  (149 other events, 312.8 us)
Sparse Core Ops, SparseCore 0:
  10.3 41.1 all-gather.2
  53.8 37.8 all-gather.4
  328.4 23.2 reduce-scatter.55
  353.9 20.1 reduce-scatter.53
  406.5 21.1 reduce-scatter.59
  430.0 19.9 reduce-scatter.57
  479.2 19.1 reduce-scatter.63
  500.8 20.0 reduce-scatter.61
  524.4 55.0 reduce-scatter.51
  583.2 54.5 reduce-scatter.47
  641.5 57.0 reduce-scatter.49
  702.6 53.7 reduce-scatter.67
  761.2 62.0 reduce-scatter.45
  827.4 61.9 reduce-scatter.43
  894.1 59.2 reduce-scatter.65
where the time goes:
time: 970 us; the launch traced here: 960 us
  waiting for transfers between devices  492 us (51%)
  blocking collectives  228 us (24%)
  matrix products  85.4 us (9%)
  local copies, waits for them, and re-layouts  81.7 us (8%)
  other arithmetic  41.4 us (4%)
  between operations  18.5 us (2%)
  starting transfers between devices  12.8 us (1%)
    unnamed x26, waiting for transfers between devices  355 us
    reduce_scatter x1, waiting for transfers between devices, on_device(): lax.psum_scatter(weight_term(6)[None], ('dp', 'seq'), scatter_dimension=1...  66.9 us
    reduce_scatter x1, waiting for transfers between devices, on_device(): lax.psum_scatter(weight_term(4)[None], ('dp', 'seq'), scatter_dimension=1...  66.2 us
    unnamed x1, blocking collectives  63.6 us
    all_gather x3, blocking collectives, forward_layer(): lax.all_gather(own_values, 'seq', axis=1, tiled=True)  47.9 us
    all_gather x3, blocking collectives, forward_layer(): lax.all_gather(own_keys, 'seq', axis=1, tiled=True)  47.8 us
    unnamed x416, local copies, waits for them, and re-layouts  37.7 us
    all_gather x1, blocking collectives, on_device(): lax.all_gather(w_qkv, ('dp', 'seq'), axis=1, tiled=True)  37.5 us
  transfers between devices with their start and end apart: 19, of which 15 were waited for; matrix products, arithmetic and copies ran while one was open for 11% of the time, Pallas kernels for 0%

commit v1 on v0

v1 whole, which is shorter than its diff:
```python
import functools
import math
import jax
import jax.numpy as jnp
from jax import lax
from jax.experimental import pallas as pl
from jax.experimental.pallas import tpu as pltpu
from jax.sharding import PartitionSpec as P

HEADS = 6
norm_eps = 1e-06
F32 = jnp.float32
BF16 = jnp.bfloat16


def mul(left, right, left_dim=1, right_dim=0):
    return lax.dot_general(
        left, right, (((left_dim,), (right_dim,)), ((), ())), preferred_element_type=F32
    )


def norm_parts(rows_in):
    centre = jnp.mean(rows_in, axis=-1, keepdims=True)
    centred = rows_in - centre
    spread = jnp.mean(centred * centred, axis=-1, keepdims=True)
    scale = lax.rsqrt(spread + norm_eps)
    return centred * scale, scale


def norm_grad(grad, gain, unit, scale):
    scaled = grad * gain
    inner = jnp.mean(scaled * unit, axis=-1, keepdims=True)
    return scale * (scaled - jnp.mean(scaled, axis=-1, keepdims=True) - unit * inner)


def gelu_parts(hidden):
    cdf = 0.5 + 0.5 * lax.erf(hidden * math.sqrt(0.5))
    return cdf


def layer_kernel(backward, grads, own, *refs):
    refs = list(refs)
    x_ref, mask_ref, w_ref, vec_ref = refs[:4]
    refs = refs[4:]
    if backward:
        dy_ref = refs.pop(0)
    y_ref = refs.pop(0)
    if backward:
        du_ref = refs.pop(0)
    if grads:
        gw_ref, gv_ref = refs[:2]
        refs = refs[2:]
    q_s, k_s, v_s, vt_s, ot_s, mid_s, c_s, acc_s = refs[:8]
    refs = refs[8:]
    if backward:
        kt_s, p_s, do_s, dq_s, dk_s, dv_s, h_s = refs
    total, width = x_ref.shape
    pairs = k_s.shape[0]
    slabs = (w_ref.shape[0] - 4) // 2
    head_dim = width // HEADS
    score_scale = head_dim ** (-0.5)

    def vec(index):
        return vec_ref[index : index + 1, :]

    mask = mask_ref[...]
    unit1, scale1 = norm_parts(x_ref[...].astype(F32) * mask)
    normed = (unit1 * vec(0) + vec(2)).astype(BF16)
    queries = (mul(normed[:own], w_ref[0]) + vec(4)).astype(BF16)
    queries = (queries.astype(F32) * score_scale).astype(BF16)
    keys = mul(normed, w_ref[1]).astype(BF16)
    values = (mul(normed, w_ref[2]) + vec(5)).astype(BF16)
    for j in range(pairs):
        lanes = slice(j * 128, (j + 1) * 128)
        q_s[j] = queries[:, lanes]
        k_s[j] = keys[:, lanes]
        v_s[j] = values[:, lanes]
        vt_s[j] = values[:, lanes].T
        if backward:
            kt_s[j] = keys[:, lanes].T
    lane = lax.broadcasted_iota(jnp.int32, (1, 128), 1)
    first_half = (lane < head_dim).astype(BF16)
    halves = (first_half, 1 - first_half)

    @pl.loop(0, pairs)
    def _(j):
        bias = (mask_ref[...] - 1.0) * 1e30
        for e in range(2):
            score = mul(k_s[j], q_s[j] * halves[e], 1, 1) + bias
            top = jnp.max(score, axis=0, keepdims=True)
            expo = jnp.exp(score - top)
            probs = (expo * (1.0 / jnp.sum(expo, axis=0, keepdims=True))).astype(BF16)
            rows = slice(e * head_dim, (e + 1) * head_dim)
            ot_s[j, rows, :] = mul(vt_s[j, rows, :], probs).astype(BF16)
            if backward:
                p_s[2 * j + e] = probs

    attended = jnp.concatenate([ot_s[j].T for j in range(pairs)], axis=1)
    mid_s[...] = x_ref[:own, :].astype(F32) * mask[:own] + mul(attended, w_ref[3]) + vec(6)
    unit2, scale2 = norm_parts(mid_s[...])
    c_s[...] = (unit2 * vec(1) + vec(3)).astype(BF16)
    acc_s[...] = jnp.zeros_like(acc_s)

    @pl.loop(0, slabs)
    def _(k):
        hidden = mul(c_s[...], w_ref[4 + k]) + vec_ref[pl.ds(8 + k, 1), :]
        if backward:
            h_s[k] = hidden
        active = (hidden * gelu_parts(hidden)).astype(BF16)
        acc_s[...] += mul(active, w_ref[4 + slabs + k])

    y_ref[...] = ((mid_s[...] + acc_s[...] + vec(7)) * mask[:own]).astype(BF16)
    if not backward:
        return

    grad_y = dy_ref[...].astype(F32) * mask[:own]
    grad_second = grad_y.astype(BF16)
    c_now = c_s[...]
    c_turned = c_now.T if grads else None
    acc_s[...] = jnp.zeros_like(acc_s)

    @pl.loop(0, slabs)
    def _(k):
        hidden = h_s[k]
        cdf = gelu_parts(hidden)
        slope = cdf + hidden * jnp.exp(-0.5 * hidden * hidden) * (1.0 / math.sqrt(2 * math.pi))
        grad_second = (dy_ref[...].astype(F32) * mask_ref[:own, :]).astype(BF16)
        grad_hidden = mul(grad_second, w_ref[4 + slabs + k], 1, 1) * slope
        grad_low = grad_hidden.astype(BF16)
        acc_s[...] += mul(grad_low, w_ref[4 + k], 1, 1)
        if grads:
            active = (hidden * cdf).astype(BF16)
            gw_ref[4 + k] = mul(c_s[...], grad_low, 0, 0).astype(BF16)
            gw_ref[4 + slabs + k] = mul(active, grad_second, 0, 0).astype(BF16)
            gv_ref[pl.ds(8 + k, 1), :] = jnp.sum(grad_low.astype(F32), axis=0, keepdims=True)

    def total_of(rows):
        return jnp.sum(rows, axis=0, keepdims=True)

    grad_c = acc_s[...]
    unit2, scale2 = norm_parts(mid_s[...])
    grad_mid = grad_y + norm_grad(grad_c, vec(1), unit2, scale2)
    grad_branch = grad_mid.astype(BF16)
    grad_att = mul(grad_branch, w_ref[3], 1, 1).astype(BF16)
    if grads:
        gv_ref[1:2, :] = total_of(grad_c * unit2)
        gv_ref[3:4, :] = total_of(grad_c)
        gv_ref[6:7, :] = total_of(grad_branch.astype(F32))
        gv_ref[7:8, :] = total_of(grad_second.astype(F32))
        for j in range(pairs):
            gw_ref[3, j * 128 : (j + 1) * 128, :] = mul(ot_s[j], grad_branch).astype(BF16)
    for j in range(pairs):
        do_s[j] = grad_att[:, j * 128 : (j + 1) * 128]
    mid_s[...] = grad_mid

    @pl.loop(0, pairs)
    def _(j):
        grad_k = None
        for e in range(2):
            half_do = do_s[j] * halves[e]
            half_q = q_s[j] * halves[e]
            grad_p = mul(v_s[j], half_do, 1, 1)
            probs_low = p_s[2 * j + e]
            probs = probs_low.astype(F32)
            row_dot = jnp.sum(probs * grad_p, axis=0, keepdims=True)
            grad_s = (probs * (grad_p - row_dot)).astype(BF16)
            rows = slice(e * head_dim, (e + 1) * head_dim)
            dq_s[j, rows, :] = (mul(kt_s[j, rows, :], grad_s) * score_scale).astype(BF16)
            part_k = mul(grad_s, half_q)
            part_v = mul(probs_low, half_do)
            grad_k, grad_v = (part_k, part_v) if grad_k is None else (grad_k + part_k, grad_v + part_v)
        dk_s[j] = grad_k.astype(BF16)
        dv_s[j] = grad_v.astype(BF16)

    grad_q = jnp.concatenate([dq_s[j].T for j in range(pairs)], axis=1)
    grad_k = jnp.concatenate([dk_s[j] for j in range(pairs)], axis=1)
    grad_v = jnp.concatenate([dv_s[j] for j in range(pairs)], axis=1)
    unit1, scale1 = norm_parts(x_ref[...].astype(F32) * mask)
    if grads:
        normed = (unit1 * vec(0) + vec(2)).astype(BF16)
        gw_ref[0] = mul(normed[:own], grad_q, 0, 0).astype(BF16)
        turned = normed.T
        gw_ref[1] = mul(turned, grad_k).astype(BF16)
        gw_ref[2] = mul(turned, grad_v).astype(BF16)
        gv_ref[4:5, :] = total_of(grad_q.astype(F32))
        gv_ref[5:6, :] = total_of(grad_v.astype(F32))
    grad_n = mul(grad_k, w_ref[1], 1, 1) + mul(grad_v, w_ref[2], 1, 1)
    grad_n = jnp.concatenate([grad_n[:own] + mul(grad_q, w_ref[0], 1, 1), grad_n[own:]], axis=0)
    if grads:
        gv_ref[0:1, :] = total_of(grad_n * unit1)
        gv_ref[2:3, :] = total_of(grad_n)
    grad_u = norm_grad(grad_n, vec(0), unit1, scale1)
    grad_u = jnp.concatenate([grad_u[:own] + mid_s[...], grad_u[own:]], axis=0)
    du_ref[...] = (grad_u * mask).astype(BF16)


def run_layer(x_all, mask, weights, vectors, own, grad_out=None, grads=False):
    backward = grad_out is not None
    total, width = x_all.shape
    pairs = width // 128
    slabs = (weights.shape[0] - 4) // 2
    operands = [x_all, mask, weights, vectors]
    shapes = [jax.ShapeDtypeStruct((own, width), BF16)]
    scratch = [
        pltpu.VMEM((pairs, own, 128), BF16),
        pltpu.VMEM((pairs, total, 128), BF16),
        pltpu.VMEM((pairs, total, 128), BF16),
        pltpu.VMEM((pairs, 128, total), BF16),
        pltpu.VMEM((pairs, 128, own), BF16),
        pltpu.VMEM((own, width), F32),
        pltpu.VMEM((own, width), BF16),
        pltpu.VMEM((own, width), F32),
    ]
    if backward:
        operands.append(grad_out)
        shapes.append(jax.ShapeDtypeStruct((total, width), BF16))
        scratch += [
            pltpu.VMEM((pairs, 128, total), BF16),
            pltpu.VMEM((HEADS, total, own), BF16),
            pltpu.VMEM((pairs, own, 128), BF16),
            pltpu.VMEM((pairs, 128, own), BF16),
            pltpu.VMEM((pairs, total, 128), BF16),
            pltpu.VMEM((pairs, total, 128), BF16),
            pltpu.VMEM((slabs, own, width), F32),
        ]
    if grads:
        shapes.append(jax.ShapeDtypeStruct(weights.shape, BF16))
        shapes.append(jax.ShapeDtypeStruct((16, width), F32))
    whole = pl.BlockSpec(memory_space=pltpu.VMEM)
    return pl.pallas_call(
        functools.partial(layer_kernel, backward, grads, own),
        out_shape=shapes,
        in_specs=[whole] * len(operands),
        out_specs=[whole] * len(shapes),
        scratch_shapes=scratch,
        compiler_params=pltpu.CompilerParams(vmem_limit_bytes=50 * 1024 * 1024),
        cost_estimate=pl.CostEstimate(flops=2 * 10**9, bytes_accessed=4 * 10**6, transcendentals=2 * 10**6),
    )(*operands)


def axis_sizes():
    return lax.axis_size("dp"), lax.axis_size("seq")


def core_pairs(dp_count):
    return [(index, index ^ 1) for index in range(dp_count)]


def swap_core(value):
    return lax.ppermute(value, "dp", core_pairs(lax.axis_size("dp")))


def turn_outer(value, steps):
    count = lax.axis_size("dp")
    return lax.ppermute(value, "dp", [(d, (d + 2 * steps) % count) for d in range(count)])


def joint_permute(value, moves):
    seq_count = lax.axis_size("seq")
    pairs = [(a[0] * seq_count + a[1], b[0] * seq_count + b[1]) for a, b in moves]
    return lax.ppermute(value, ("dp", "seq"), pairs)


def along_line(value, steps):
    count = lax.axis_size("seq")
    return lax.ppermute(
        value, "seq", [(z, z + steps) for z in range(count) if 0 <= z + steps < count]
    )


def in_order(relative, index, count):
    return lax.dynamic_slice_in_dim(jnp.stack(relative), count - 1 - index, count, 0)


def gather_pieces(piece):
    dp_count, seq_count = axis_sizes()
    outer_count = dp_count // 2
    d, z = lax.axis_index("dp"), lax.axis_index("seq")
    o, c = d // 2, d % 2
    ups, downs = [piece], [piece]
    for step in range(1, seq_count):
        ups.append(along_line(ups[-1], 1))
        downs.append(along_line(downs[-1], -1))
    line = in_order(ups[:0:-1] + [piece] + downs[1:], z, seq_count)
    others = [line] + [turn_outer(line, k) for k in range(1, outer_count)]
    relative = [others[(outer_count - 1 - i) % outer_count] for i in range(2 * outer_count - 1)]
    mine = in_order(relative, o, outer_count)
    theirs = swap_core(mine)
    both = jnp.stack([jnp.where(c == 0, mine, theirs), jnp.where(c == 0, theirs, mine)], axis=1)
    return both.reshape((dp_count * seq_count,) + piece.shape)


def scatter_pieces(pieces):
    dp_count, seq_count = axis_sizes()
    outer_count = dp_count // 2
    d, z = lax.axis_index("dp"), lax.axis_index("seq")
    o, c = d // 2, d % 2
    shape = pieces.shape[1:]
    pieces = pieces.reshape((outer_count, 2, seq_count) + shape)
    kept = lax.dynamic_index_in_dim(pieces, c, 1, keepdims=False)
    sent = lax.dynamic_index_in_dim(pieces, 1 - c, 1, keepdims=False)
    now = kept.astype(F32) + swap_core(sent).astype(F32)
    low = now.astype(BF16)
    total = lax.dynamic_index_in_dim(now, o, 0, keepdims=False)
    for k in range(1, outer_count):
        sent = lax.dynamic_index_in_dim(low, (o + k) % outer_count, 0, keepdims=False)
        total = total + turn_outer(sent, k).astype(F32)
    low = total.astype(BF16)
    result = lax.dynamic_index_in_dim(total, z, 0, keepdims=False)
    for k in range(1, seq_count):
        sent = lax.dynamic_index_in_dim(low, (z + k) % seq_count, 0, keepdims=False)
        moved = lax.ppermute(sent, "seq", [(i, (i + k) % seq_count) for i in range(seq_count)])
        result = result + moved.astype(F32)
    return result


def pack_rows(w_qkv, w_out, w_fc1, w_fc2, gains, shifts, fc1_bias):
    rows, width = w_out.shape
    parts = [
        w_qkv.reshape(rows, 3, width).transpose(1, 0, 2).reshape(-1, width),
        w_out,
        w_fc1.reshape(rows, -1, width).transpose(1, 0, 2).reshape(-1, width),
        w_fc2,
    ]
    vector = jnp.concatenate([gains, shifts, fc1_bias])
    used = sum(part.shape[0] for part in parts)
    padded = -(-(used + 1) // 16) * 16
    tail = jnp.pad(vector[None], ((0, padded - used - 1), (0, width - vector.shape[0])))
    return jnp.concatenate(parts + [tail], axis=0)


def unpack_gathered(gathered, rows, lengths):
    count, padded, width = gathered.shape
    slabs = 4
    wide = gathered[:, : 8 * rows].reshape(count, 8, rows, width)
    wide = wide.transpose(1, 0, 2, 3).reshape(8, count * rows, width)
    tall = gathered[:, 8 * rows : 12 * rows].reshape(slabs, width, width)
    weights = jnp.concatenate([wide, tall], axis=0)
    vector = gathered[:, 12 * rows, :].astype(F32)
    parts, start = [], 0
    for length in lengths:
        parts.append(vector[:, start : start + length].reshape(-1, width))
        start += length
    vectors = jnp.concatenate(parts + [jnp.zeros((4, width), F32)], axis=0)
    return weights, vectors


def pack_grads(grad_weights, grad_vectors, rows, lengths):
    width = grad_weights.shape[-1]
    count = width // rows
    wide = grad_weights[:8].reshape(8, count, rows, width).transpose(1, 0, 2, 3)
    wide = wide.reshape(count, 8 * rows, width)
    tall = grad_weights[8:].reshape(count, 4 * rows, width)
    parts, start = [], 0
    for length in lengths:
        used = length * count // width
        parts.append(grad_vectors[start : start + used].reshape(count, length))
        start += used
    vector = jnp.concatenate(parts, axis=1).astype(BF16)
    padded = -(-(12 * rows + 1) // 16) * 16
    tail = jnp.pad(
        vector[:, None], ((0, 0), (0, padded - 12 * rows - 1), (0, width - vector.shape[1]))
    )
    return jnp.concatenate([wide, tall, tail], axis=1)


def unpack_scattered(piece, rows, lengths):
    width = piece.shape[1]
    qkv = piece[: 3 * rows].reshape(3, rows, width).transpose(1, 0, 2).reshape(rows, 3 * width)
    out = piece[3 * rows : 4 * rows]
    fc1 = piece[4 * rows : 8 * rows].reshape(4, rows, width).transpose(1, 0, 2)
    fc1 = fc1.reshape(rows, 4 * width)
    fc2 = piece[8 * rows : 12 * rows]
    parts, start = [], 0
    for length in lengths:
        parts.append(piece[12 * rows, start : start + length])
        start += length
    return [member[None] for member in (qkv, out, fc1, fc2, *parts)]


def image_moves(step):
    dp_count, seq_count = axis_sizes()
    block = seq_count // 4
    moves = []
    for d in range(dp_count):
        for z in range(seq_count):
            micro = (step + z) % 2
            rank = z // 2
            target = (d - d % 2 + rank % 2, (2 * micro + d % 2) * block + rank // 2)
            moves.append(((d, z), target))
    return moves


def to_images(blocks):
    seq_count = lax.axis_size("seq")
    z = lax.axis_index("seq")
    micro = z // (seq_count // 4) // 2
    arrived = []
    for step in range(2):
        sent = jnp.where((step + z) % 2 == 0, blocks[0], blocks[1])
        arrived.append(joint_permute(sent, image_moves(step)))
    low = jnp.where(micro == 0, arrived[0], arrived[1])
    high = jnp.where(micro == 0, arrived[1], arrived[0])
    return jnp.concatenate([low, high], axis=0)


def from_images(rows_own):
    seq_count = lax.axis_size("seq")
    z = lax.axis_index("seq")
    micro = z // (seq_count // 4) // 2
    half = rows_own.shape[0] // 2
    low, high = rows_own[:half], rows_own[half:]
    arrived = []
    for step in range(2):
        sent = jnp.where(micro == step, low, high)
        arrived.append(joint_permute(sent, [(b, a) for a, b in image_moves(step)]))
    return jnp.stack(
        [jnp.where(z % 2 == m, arrived[0], arrived[1]) for m in range(2)]
    )


def group_members():
    block = lax.axis_size("seq") // 4
    return [(turn, flip) for turn in range(block) for flip in range(2)][1:]


def group_moves(turn, flip):
    dp_count, seq_count = axis_sizes()
    block = seq_count // 4
    moves = []
    for d in range(dp_count):
        for z in range(seq_count):
            base = z - z % block
            moves.append(((d ^ flip, base + (z % block + turn) % block), (d, z)))
    return moves


def gather_group(own_rows):
    arrived = [joint_permute(own_rows, group_moves(*member)) for member in group_members()]
    return jnp.concatenate([own_rows] + arrived, axis=0)


def scatter_group(partial, own):
    total = partial[:own].astype(F32)
    for place, member in enumerate(group_members()):
        sent = partial[(place + 1) * own : (place + 2) * own]
        back = [(b, a) for a, b in group_moves(*member)]
        total = total + joint_permute(sent, back).astype(F32)
    return total.astype(BF16)


def slot_mask(lengths, slot_count):
    seq_count = lax.axis_size("seq")
    block = seq_count // 4
    d, z = lax.axis_index("dp"), lax.axis_index("seq")
    c, group = d % 2, z // block
    theirs = swap_core(lengths[:, 0])
    counts = jnp.where(group % 2 == c, lengths[:, 0], theirs)
    counts = jnp.where(group // 2 == 0, counts[0], counts[1])
    places = jnp.arange(slot_count, dtype=jnp.int32)
    parts = []
    for turn, flip in [(0, 0)] + group_members():
        rank = (z % block + turn) % block * 2 + (c ^ flip)
        picked = lax.dynamic_slice_in_dim(counts, 2 * rank, 2, 0)
        parts.append((places[None, :] < picked[:, None]).astype(F32).reshape(-1, 1))
    return jnp.concatenate(parts, axis=0)


def to_section(value, steps):
    return lax.ppermute(value, "section", [(0, 1)] if steps == 1 else [(1, 0)])


def on_device(boundary, lengths, w_qkv, w_out, w_fc1, w_fc2, gains, shifts, fc1_bias):
    section = lax.axis_index("section")
    slot_count = boundary.shape[3]
    own = 2 * slot_count
    rows = w_out.shape[1]
    lens = (gains.shape[1], shifts.shape[1], fc1_bias.shape[1])
    own_start = to_images(boundary[0, :, 0])
    piece = pack_rows(
        w_qkv[0], w_out[0], w_fc1[0], w_fc2[0], gains[0], shifts[0], fc1_bias[0]
    )
    mask = slot_mask(lengths, slot_count)
    weights, vectors = unpack_gathered(gather_pieces(piece), rows, lens)
    all_start = gather_group(own_start)
    (middle,) = run_layer(all_start, mask, weights, vectors, own)
    arrived = gather_group(to_section(middle, 1))
    layer_in = jnp.where(section == 0, all_start, arrived)
    layer_out, partial = run_layer(layer_in, mask, weights, vectors, own, own_start)
    returned = to_section(scatter_group(partial, own), -1)
    grad_out = jnp.where(section == 0, returned, own_start)
    unused, partial, grad_weights, grad_vectors = run_layer(
        layer_in, mask, weights, vectors, own, grad_out, True
    )
    grad_in = scatter_group(partial, own)
    rows_out = from_images(jnp.where(section == 0, grad_in, layer_out))
    summed = scatter_pieces(pack_grads(grad_weights, grad_vectors, rows, lens))
    return (rows_out[None, :, None], *unpack_scattered(summed, rows, lens))


def solution(mesh):
    sharded = P("section", ("dp", "seq"), None)
    vector = P("section", ("dp", "seq"))
    images = P("section", None, "dp", "seq", None)
    grads = (sharded, sharded, sharded, sharded, vector, vector, vector)
    return jax.shard_map(
        on_device,
        mesh=mesh,
        in_specs=(images, P(None, "dp", None), *grads),
        out_specs=(images, *grads),
        check_vma=False,
    )
```

time: 970 us -> 234 us (0.24)
  waiting for transfers between devices: 492 us -> 95.5 us
  blocking collectives: 228 us -> 0 us
  matrix products: 85.4 us -> 0 us
  local copies, waits for them, and re-layouts: 81.7 us -> 24 us
  Pallas kernels: 0 us -> 57.4 us
  starting transfers between devices: 12.8 us -> 37.9 us
  other arithmetic: 41.4 us -> 17.5 us
  between operations: 18.5 us -> 1.24 us
    unnamed x26 -> x0, waiting for transfers between devices: 355 us -> none
    all_gather x8 -> x0, blocking collectives: 164 us -> none  [the longest x3 47.9 us: forward_layer(): lax.all_gather(own_values, 'seq', axis=1, tiled=True)]
    reduce_scatter x2 -> x0, waiting for transfers between devices: 133 us -> none  [the longest x1 66.9 us: on_device(): lax.psum_scatter(weight_term(6)[None], ('dp', 'seq'), scatter_dimension=1...]
    ppermute x4 -> x24, waiting for transfers between devices: 3.9 us -> 95.5 us  [the longest x2 36.5 us: turn_outer(): lax.ppermute(value, 'dp', [(d, (d + 2 * steps) % count) for d in range(co...]
    dot_general x46 -> x0, matrix products: 85.4 us -> none  [the longest x3 12.3 us: forward_layer(): jnp.dot(normed_two.reshape(-1, model_width), w_fc1, preferred_element_typ...]
    unnamed x1 -> x0, blocking collectives: 63.6 us -> none
    pallas_call x0 -> x3, Pallas kernels: none -> 57.4 us  [run_layer(): pl.pallas_call(functools.partial(layer_kernel, backward, grads, own), out...]
    unnamed x416 -> x30, local copies, waits for them, and re-layouts: 37.7 us -> 6.15 us
  transfers between devices with their start and end apart: 19 -> 24, of which waited for: 15 -> 17; matrix products, arithmetic and copies ran while one was open for 11% -> 2% of each run, Pallas kernels for 0% -> 0%
where the time goes in v1:
time: 234 us
  waiting for transfers between devices  95.5 us (41%)
  Pallas kernels  57.4 us (25%)
  starting transfers between devices  37.9 us (16%)
  local copies, waits for them, and re-layouts  24 us (10%)
  other arithmetic  17.5 us (7%)
    pallas_call x3, Pallas kernels, run_layer(): pl.pallas_call(functools.partial(layer_kernel, backward, grads, own), out...  57.4 us
    ppermute x2, waiting for transfers between devices, turn_outer(): lax.ppermute(value, 'dp', [(d, (d + 2 * steps) % count) for d in range(co...  36.5 us
    ppermute x3, waiting for transfers between devices, scatter_pieces(): lax.ppermute(sent, 'seq', [(i, (i + k) % seq_count) for i in range(seq_co...  18.4 us
    ppermute x6, starting transfers between devices, along_line(): lax.ppermute(value, 'seq', [(z, z + steps) for z in range(count) if 0 <=...  17.6 us
    ppermute x2, waiting for transfers between devices, to_section(): return lax.ppermute(value, 'section', [(0, 1)] if steps == 1 else [(1, 0)])  14.5 us
    ppermute x6, waiting for transfers between devices, along_line(): lax.ppermute(value, 'seq', [(z, z + steps) for z in range(count) if 0 <=...  12.8 us
    ppermute x8, waiting for transfers between devices, joint_permute(): return lax.ppermute(value, ('dp', 'seq'), pairs)  9.28 us
    ppermute x8, starting transfers between devices, joint_permute(): return lax.ppermute(value, ('dp', 'seq'), pairs)  7.73 us
  transfers between devices with their start and end apart: 24, of which 17 were waited for; matrix products, arithmetic and copies ran while one was open for 2% of the time, Pallas kernels for 0%

profile of v1, /device:TPU:0, one launch (start us, length us, event | category | flops | bytes accessed | tf_op | source)
XLA Modules:
  0.0 233.6 jit_solution(10040244181272023242)
XLA Ops:
  0.6 0.7 reduce
  1.3 0.7 pad_maximum_fusion.6
  2.1 0.8 reshape_squeeze.6
  2.9 0.9 reshape_squeeze.7
  3.9 0.7 constant_dynamic-update-slice_fusion.2
  4.6 0.9 bitcast_dynamic-update-slice_fusion.7
  5.6 4.9 %collective-permute-start.4 = (bf16[304,384]{1,0:T(8,128)(2,1)S(1)}, bf16[304,384]{1,0:T(8,128)(2,1)S(1)}, u32[]{:S(2)}, u32[]{:S(2)}) collective-permute-start(bf16[304,384]{1,0:T(8,128)(2,1)S(1)} %constant_dynamic-update-slice_fusion), channel_id=1, source_target_pairs={{0,1},{1,2},{2,3},{4,5},{5,6},{6,7},{8,9},{9,10},{10,11},{12,13},{... | collective-permute-start | bytes 700424 | tf_op jit(solution)/shard_map/ppermute | solution.py:266
  10.5 1.3 collective-permute-start.7
  11.8 3.6 %collective-permute-done.4 = bf16[304,384]{1,0:T(8,128)(2,1)S(1)} collective-permute-done((bf16[304,384]{1,0:T(8,128)(2,1)S(1)}, bf16[304,384]{1,0:T(8,128)(2,1)S(1)}, u32[]{:S(2)}, u32[]{:S(2)}) %collective-permute-start.4) | collective-permute-done | bytes 233504 | tf_op jit(solution)/shard_map/ppermute | solution.py:266
  15.4 4.4 %collective-permute-start.5 = (bf16[304,384]{1,0:T(8,128)(2,1)S(1)}, bf16[304,384]{1,0:T(8,128)(2,1)S(1)}, u32[]{:S(2)}, u32[]{:S(2)}) collective-permute-start(bf16[304,384]{1,0:T(8,128)(2,1)S(1)} %collective-permute-done.4), channel_id=1, source_target_pairs={{0,1},{1,2},{2,3},{4,5},{5,6},{6,7},{8,9},{9,10},{10,11},{12,13},{... | collective-permute-start | bytes 700424 | tf_op jit(solution)/shard_map/ppermute | solution.py:266
  19.8 1.3 collective-permute-start.8
  21.1 2.7 %collective-permute-done.5 = bf16[304,384]{1,0:T(8,128)(2,1)S(1)} collective-permute-done((bf16[304,384]{1,0:T(8,128)(2,1)S(1)}, bf16[304,384]{1,0:T(8,128)(2,1)S(1)}, u32[]{:S(2)}, u32[]{:S(2)}) %collective-permute-start.5) | collective-permute-done | bytes 233504 | tf_op jit(solution)/shard_map/ppermute | solution.py:266
  23.9 4.4 %collective-permute-start.6 = (bf16[304,384]{1,0:T(8,128)(2,1)S(1)}, bf16[304,384]{1,0:T(8,128)(2,1)S(1)}, u32[]{:S(2)}, u32[]{:S(2)}) collective-permute-start(bf16[304,384]{1,0:T(8,128)(2,1)S(1)} %collective-permute-done.5), channel_id=1, source_target_pairs={{0,1},{1,2},{2,3},{4,5},{5,6},{6,7},{8,9},{9,10},{10,11},{12,13},{... | collective-permute-start | bytes 700424 | tf_op jit(solution)/shard_map/ppermute | solution.py:266
  28.3 1.3 collective-permute-start.9
  29.6 2.2 collective-permute-done.6
  32.1 4.2 %collective-permute-done.9 = bf16[304,384]{1,0:T(8,128)(2,1)S(1)} collective-permute-done((bf16[304,384]{1,0:T(8,128)(2,1)S(1)}, bf16[304,384]{1,0:T(8,128)(2,1)S(1)}, u32[]{:S(2)}, u32[]{:S(2)}) %collective-permute-start.9) | collective-permute-done | bytes 233504 | tf_op jit(solution)/shard_map/ppermute | solution.py:266
  36.3 1.0 constant_dynamic-slice_fusion
  37.3 1.5 collective-permute-start.10
  38.9 17.8 %collective-permute-done.10 = bf16[4,304,384]{2,1,0:T(8,128)(2,1)S(1)} collective-permute-done((bf16[4,304,384]{2,1,0:T(8,128)(2,1)}, bf16[4,304,384]{2,1,0:T(8,128)(2,1)S(1)}, u32[]{:S(2)}, u32[]{:S(2)}) %collective-permute-start.10) | collective-permute-done | bytes 933920 | tf_op jit(solution)/shard_map/ppermute | solution.py:255
  56.8 2.4 %fusion.1 = bf16[2,4,304,384]{3,2,1,0:T(8,128)(2,1)} fusion(s32[]{:T(128)S(6)} %select_n.229, bf16[1,4,304,384]{3,2,1,0:T(8,128)(2,1)S(1)} %bitcast.108, bf16[1,4,304,384]{3,2,1,0:T(8,128)(2,1)S(1)} %fusion.9), kind=kLoop, calls=%fused_computation.8 | loop fusion | flops 1867776 | bytes 3735556 | tf_op jit(solution)/shard_map/stack | solution.py:272
  59.7 0.7 collective-permute-start
  60.4 3.9 %collective-permute-start.1 = (bf16[168,384]{1,0:T(8,128)(2,1)S(1)}, bf16[168,384]{1,0:T(8,128)(2,1)S(1)}, u32[]{:S(2)}, u32[]{:S(2)}) collective-permute-start(bf16[168,384]{1,0:T(8,128)(2,1)S(1)} %get-tuple-element.66), channel_id=1, source_target_pairs={{0,2},{1,0},{2,6},{3,4},{4,3},{5,1},{6,7},{7,5},{8,10},{9,8},{10,1... | collective-permute-start | bytes 387080 | tf_op jit(solution)/shard_map/ppermute | solution.py:261
  64.4 4.2 %collective-permute-done.1 = bf16[168,384]{1,0:T(8,128)(2,1)S(1)} collective-permute-done((bf16[168,384]{1,0:T(8,128)(2,1)S(1)}, bf16[168,384]{1,0:T(8,128)(2,1)S(1)}, u32[]{:S(2)}, u32[]{:S(2)}) %collective-permute-start.1) | collective-permute-done | bytes 129056 | tf_op jit(solution)/shard_map/ppermute | solution.py:261
  68.8 2.2 collective-permute-start.2
  71.5 0.7 collective-permute-done.2
  72.2 1.0 pad_maximum_fusion.3.refs_0_
  73.2 2.8 %select_bitcast_fusion.1 = (bf16[2,1,4,304,384]{4,3,2,1,0:T(8,128)(2,1)S(1)}, bf16[2,1,4,304,384]{4,3,2,1,0:T(8,128)(2,1)S(1)}) fusion(bf16[2,4,304,384]{3,2,1,0:T(8,128)(2,1)} %collective-permute-done.11, pred[]{:T(512)S(6)} %eq.53, s32[]{:T(128)S(6)} %select_n.229, bf16[1,4,304,384]{3,2,1,0:T(8,128)(2,1)S(1)} %bitcast.109, ...), kind=kLoop, calls=%fused_computation.13 | loop fusion | flops 3735552 | bytes 7471109 | tf_op jit(solution)/shard_map/stack | solution.py:289
  76.8 1.8 slice.119
  78.8 2.0 copy.51
  80.8 2.1 pad_maximum_fusion.2.refs_2_
  83.1 10.9 %shard_map.152 = bf16[336,384]{1,0:T(8,128)(2,1)S(1)} custom-call(bf16[672,384]{1,0:T(8,128)(2,1)S(1)} %pad_maximum_fusion.3.refs_0_, f32[672,1]{1,0:T(8,128)S(1)} %concatenate.57.refs_1_, bf16[12,384,384]{2,1,0:T(8,128)(2,1)} %pad_maximum_fusion.2.refs_2_, f32[16,384]{1,0:T(8,128)S(1)} %maximum_maximum_fusion.refs_3_), custom_call_target="tpu_custom_call" | custom-call | flops 2000000000 | bytes 4000000 | tf_op jit(solution)/shard_map/pallas_call | solution.py:230
  94.0 3.6 %collective-permute-start.12 = (bf16[336,384]{1,0:T(8,128)(2,1)S(1)}, bf16[336,384]{1,0:T(8,128)(2,1)S(1)}, u32[]{:S(2)}, u32[]{:S(2)}) collective-permute-start(bf16[336,384]{1,0:T(8,128)(2,1)S(1)} %shard_map.152), channel_id=1, source_target_pairs={{0,16},{1,17},{2,18},{3,19},{4,20},{5,21},{6,22},{7,23},{8,24},{9,... | collective-permute-start | bytes 774152 | tf_op jit(solution)/shard_map/ppermute | solution.py:470
  97.6 5.8 %collective-permute-done.12 = bf16[336,384]{1,0:T(8,128)(2,1)S(1)} collective-permute-done((bf16[336,384]{1,0:T(8,128)(2,1)S(1)}, bf16[336,384]{1,0:T(8,128)(2,1)S(1)}, u32[]{:S(2)}, u32[]{:S(2)}) %collective-permute-start.12) | collective-permute-done | bytes 258080 | tf_op jit(solution)/shard_map/ppermute | solution.py:470
  103.4 1.5 collective-permute-done.13
  104.9 1.1 maximum_select_fusion.refs_0_
  106.0 21.4 %shard_map.153 = (bf16[336,384]{1,0:T(8,128)(2,1)S(1)}, bf16[672,384]{1,0:T(8,128)(2,1)S(1)}) custom-call(bf16[672,384]{1,0:T(8,128)(2,1)S(1)} %maximum_select_fusion.refs_0_, f32[672,1]{1,0:T(8,128)S(1)} %concatenate.57.refs_1_, bf16[12,384,384]{2,1,0:T(8,128)(2,1)} %pad_maximum_fusion.2.refs_2_, f32[16,384]{1,0:T(8,128)S(1)} %maximum_maximum_fusion.refs_3_, ...), custom_call_target="tpu_custom_call" | custom-call | flops 2000000000 | bytes 4000000 | tf_op jit(solution)/shard_map/pallas_call | solution.py:230
  127.6 1.4 collective-permute-done.14
  129.1 1.5 collective-permute-start.15
  130.6 8.7 %collective-permute-done.15 = bf16[336,384]{1,0:T(8,128)(2,1)S(1)} collective-permute-done((bf16[336,384]{1,0:T(8,128)(2,1)S(1)}, bf16[336,384]{1,0:T(8,128)(2,1)S(1)}, u32[]{:S(2)}, u32[]{:S(2)}) %collective-permute-start.15) | collective-permute-done | bytes 258080 | tf_op jit(solution)/shard_map/ppermute | solution.py:470
  139.4 25.1 %shard_map.154 = (bf16[336,384]{1,0:T(8,128)(2,1)}, bf16[672,384]{1,0:T(8,128)(2,1)S(1)}, bf16[12,384,384]{2,1,0:T(8,128)(2,1)}, f32[16,384]{1,0:T(8,128)S(1)}) custom-call(bf16[672,384]{1,0:T(8,128)(2,1)S(1)} %maximum_select_fusion.refs_0_, f32[672,1]{1,0:T(8,128)S(1)} %concatenate.57.refs_1_, bf16[12,384,384]{2,1,0:T(8,128)(2,1)} %pad_maximum_fusion.2.refs_2_, ...), custom_call_target="tpu_custom_call" | custom-call | flops 2000000000 | bytes 4000000 | tf_op jit(solution)/shard_map/pallas_call | solution.py:230
  164.6 2.4 %slice.108 = bf16[4,384,384]{2,1,0:T(8,128)(2,1)} slice(bf16[12,384,384]{2,1,0:T(8,128)(2,1)} %get-tuple-element.16), slice={[8:12], [0:384], [0:384]} | slice | bytes 2359296 | tf_op jit(solution)/shard_map/slice | solution.py:353
  167.0 1.9 slice.107
  169.8 0.8 copy-done.2
  171.2 1.6 copy-done
  172.8 4.0 %collective-permute-done.19 = bf16[2,4,304,384]{3,2,1,0:T(8,128)(2,1)} collective-permute-done((bf16[2,4,304,384]{3,2,1,0:T(8,128)(2,1)S(1)}, bf16[2,4,304,384]{3,2,1,0:T(8,128)(2,1)}, u32[]{:S(2)}, u32[]{:S(2)}) %collective-permute-start.19) | collective-permute-done | bytes 1867808 | tf_op jit(solution)/shard_map/ppermute | solution.py:250
  176.8 2.4 %convert_add_fusion = f32[2,4,304,384]{3,2,1,0:T(8,128)S(1)} fusion(bf16[2,4,304,384]{3,2,1,0:T(8,128)(2,1)} %collective-permute-done.19, bf16[2,2,4,304,384]{4,3,2,1,0:T(8,128)(2,1)} %copy-done, s32[]{:T(128)S(6)} %select_n.241), kind=kLoop, calls=%fused_computation.2 | loop fusion | flops 2801664 | bytes 7471108 | tf_op jit(solution)/shard_map/add | solution.py:302
  179.3 1.8 copy-done.1
  181.2 1.6 collective-permute-start.20
  182.9 1.5 collective-permute-done.16
  184.6 0.7 collective-permute-start.17
  185.3 18.7 %collective-permute-done.20 = bf16[4,304,384]{2,1,0:T(8,128)(2,1)S(1)} collective-permute-done((bf16[4,304,384]{2,1,0:T(8,128)(2,1)S(1)}, bf16[4,304,384]{2,1,0:T(8,128)(2,1)S(1)}, u32[]{:S(2)}, u32[]{:S(2)}) %collective-permute-start.20) | collective-permute-done | bytes 933920 | tf_op jit(solution)/shard_map/ppermute | solution.py:255
  204.0 1.8 fusion.8
  205.9 3.8 %collective-permute-start.23 = (bf16[304,384]{1,0:T(8,128)(2,1)S(1)}, bf16[304,384]{1,0:T(8,128)(2,1)S(1)}, u32[]{:S(2)}, u32[]{:S(2)}) collective-permute-start(bf16[304,384]{1,0:T(8,128)(2,1)S(1)} %get-tuple-element.55), channel_id=1, source_target_pairs={{0,3},{1,0},{2,1},{3,2},{4,7},{5,4},{6,5},{7,6},{8,11},{9,8},{10,9... | collective-permute-start | bytes 700424 | tf_op jit(solution)/shard_map/ppermute | solution.py:312
  209.8 0.7 maximum_bitcast_fusion
  210.5 5.8 %collective-permute-done.21 = bf16[304,384]{1,0:T(8,128)(2,1)S(1)} collective-permute-done((bf16[304,384]{1,0:T(8,128)(2,1)S(1)}, bf16[304,384]{1,0:T(8,128)(2,1)S(1)}, u32[]{:S(2)}, u32[]{:S(2)}) %collective-permute-start.21) | collective-permute-done | bytes 233504 | tf_op jit(solution)/shard_map/ppermute | solution.py:312
  216.3 1.5 collective-permute-done.23
  217.9 11.1 %collective-permute-done.22 = bf16[304,384]{1,0:T(8,128)(2,1)S(1)} collective-permute-done((bf16[304,384]{1,0:T(8,128)(2,1)S(1)}, bf16[304,384]{1,0:T(8,128)(2,1)S(1)}, u32[]{:S(2)}, u32[]{:S(2)}) %collective-permute-start.22) | collective-permute-done | bytes 233504 | tf_op jit(solution)/shard_map/ppermute | solution.py:312
  229.1 0.5 slice.134
  229.6 0.6 slice.136
  230.2 0.6 slice.135
  230.8 0.6 slice_bitcast_fusion.1
  231.4 0.7 slice_bitcast_fusion
  232.2 0.7 broadcast_in_dim_reshape.7
  232.9 0.7 broadcast_in_dim_reshape.6
  (96 shorter events, 5.4 us)
Async XLA Ops:
  5.6 9.9 %collective-permute-start.4 = (bf16[304,384]{1,0:T(8,128)(2,1)S(1)}, bf16[304,384]{1,0:T(8,128)(2,1)S(1)}, u32[]{:S(2)}, u32[]{:S(2)}) collective-permute-start(bf16[304,384]{1,0:T(8,128)(2,1)S(1)} %constant_dynamic-update-slice_fusion), channel_id=1, source_target_pairs={{0,1},{1,2},{2,3},{4,5},{5,6},{6,7},{8,9},{9,10},{10,11},{12,13},{... | collective-permute-start | bytes 700424 | tf_op jit(solution)/shard_map/ppermute | solution.py:266
  10.5 9.3 %collective-permute-start.7 = (bf16[304,384]{1,0:T(8,128)(2,1)S(1)}, bf16[304,384]{1,0:T(8,128)(2,1)S(1)}, u32[]{:S(2)}, u32[]{:S(2)}) collective-permute-start(bf16[304,384]{1,0:T(8,128)(2,1)S(1)} %constant_dynamic-update-slice_fusion), channel_id=1, source_target_pairs={{1,0},{2,1},{3,2},{5,4},{6,5},{7,6},{9,8},{10,9},{11,10},{13,12},{... | collective-permute-start | bytes 700424 | tf_op jit(solution)/shard_map/ppermute | solution.py:266
  15.4 8.4 %collective-permute-start.5 = (bf16[304,384]{1,0:T(8,128)(2,1)S(1)}, bf16[304,384]{1,0:T(8,128)(2,1)S(1)}, u32[]{:S(2)}, u32[]{:S(2)}) collective-permute-start(bf16[304,384]{1,0:T(8,128)(2,1)S(1)} %collective-permute-done.4), channel_id=1, source_target_pairs={{0,1},{1,2},{2,3},{4,5},{5,6},{6,7},{8,9},{9,10},{10,11},{12,13},{... | collective-permute-start | bytes 700424 | tf_op jit(solution)/shard_map/ppermute | solution.py:266
  19.8 8.4 %collective-permute-start.8 = (bf16[304,384]{1,0:T(8,128)(2,1)S(1)}, bf16[304,384]{1,0:T(8,128)(2,1)S(1)}, u32[]{:S(2)}, u32[]{:S(2)}) collective-permute-start(bf16[304,384]{1,0:T(8,128)(2,1)S(1)} %collective-permute-done.7), channel_id=1, source_target_pairs={{1,0},{2,1},{3,2},{5,4},{6,5},{7,6},{9,8},{10,9},{11,10},{13,12},{... | collective-permute-start | bytes 700424 | tf_op jit(solution)/shard_map/ppermute | solution.py:266
  23.9 7.9 %collective-permute-start.6 = (bf16[304,384]{1,0:T(8,128)(2,1)S(1)}, bf16[304,384]{1,0:T(8,128)(2,1)S(1)}, u32[]{:S(2)}, u32[]{:S(2)}) collective-permute-start(bf16[304,384]{1,0:T(8,128)(2,1)S(1)} %collective-permute-done.5), channel_id=1, source_target_pairs={{0,1},{1,2},{2,3},{4,5},{5,6},{6,7},{8,9},{9,10},{10,11},{12,13},{... | collective-permute-start | bytes 700424 | tf_op jit(solution)/shard_map/ppermute | solution.py:266
  28.3 8.0 %collective-permute-start.9 = (bf16[304,384]{1,0:T(8,128)(2,1)S(1)}, bf16[304,384]{1,0:T(8,128)(2,1)S(1)}, u32[]{:S(2)}, u32[]{:S(2)}) collective-permute-start(bf16[304,384]{1,0:T(8,128)(2,1)S(1)} %collective-permute-done.8), channel_id=1, source_target_pairs={{1,0},{2,1},{3,2},{5,4},{6,5},{7,6},{9,8},{10,9},{11,10},{13,12},{... | collective-permute-start | bytes 700424 | tf_op jit(solution)/shard_map/ppermute | solution.py:266
  37.3 19.4 %collective-permute-start.10 = (bf16[4,304,384]{2,1,0:T(8,128)(2,1)}, bf16[4,304,384]{2,1,0:T(8,128)(2,1)S(1)}, u32[]{:S(2)}, u32[]{:S(2)}) collective-permute-start(bf16[4,304,384]{2,1,0:T(8,128)(2,1)} %constant_dynamic-slice_fusion), channel_id=1, source_target_pairs={{0,8},{4,12},{8,0},{12,4},{1,9},{5,13},{9,1},{13,5},{2,10},{6,14},... | collective-permute-start | bytes 2801672 | tf_op jit(solution)/shard_map/ppermute | solution.py:255
  56.8 2.4 %copy-start.8 = (s32[2,1,4]{2,1,0:T(1,128)S(1)}, s32[2,1,4]{2,1,0:T(1,128)}, u32[]{:S(2)}) copy-start(s32[2,1,4]{2,1,0:T(1,128)} %param.10) | copy-start | bytes 100
  56.8 2.9 %copy-start.7 = (bf16[1,2,1,168,384]{4,3,2,1,0:T(8,128)(2,1)S(1)}, bf16[1,2,1,168,384]{4,3,2,1,0:T(8,128)(2,1)}, u32[]{:S(2)}) copy-start(bf16[1,2,1,168,384]{4,3,2,1,0:T(8,128)(2,1)} %param.9) | copy-start | bytes 774148
  59.2 14.1 %collective-permute-start.11 = (bf16[2,4,304,384]{3,2,1,0:T(8,128)(2,1)}, bf16[2,4,304,384]{3,2,1,0:T(8,128)(2,1)}, u32[]{:S(2)}, u32[]{:S(2)}) collective-permute-start(bf16[2,4,304,384]{3,2,1,0:T(8,128)(2,1)} %fusion.1), channel_id=1, source_target_pairs={{0,4},{4,0},{8,12},{12,8},{1,5},{5,1},{9,13},{13,9},{2,6},{6,2},{1... | collective-permute-start | bytes 5603336 | tf_op jit(solution)/shard_map/ppermute | solution.py:250
  59.2 5.2 %collective-permute-start.3 = (s32[2,4]{1,0:T(2,128)S(1)}, s32[2,4]{1,0:T(2,128)S(1)}, u32[]{:S(2)}, u32[]{:S(2)}) collective-permute-start(s32[2,4]{1,0:T(2,128)S(1)} %bitcast.120), channel_id=1, source_target_pairs={{0,4},{4,0},{8,12},{12,8},{1,5},{5,1},{9,13},{13,9},{2,6},{6,2},{1... | collective-permute-start | bytes 104 | tf_op jit(solution)/shard_map/ppermute | solution.py:250
  59.7 4.7 %collective-permute-start = (bf16[168,384]{1,0:T(8,128)(2,1)S(1)}, bf16[168,384]{1,0:T(8,128)(2,1)S(1)}, u32[]{:S(2)}, u32[]{:S(2)}) collective-permute-start(bf16[168,384]{1,0:T(8,128)(2,1)S(1)} %get-tuple-element.65), channel_id=1, source_target_pairs={{0,0},{1,2},{2,4},{3,6},{4,1},{5,3},{6,5},{7,7},{8,8},{9,10},{10,1... | collective-permute-start | bytes 387080 | tf_op jit(solution)/shard_map/ppermute | solution.py:261
  60.4 8.3 %collective-permute-start.1 = (bf16[168,384]{1,0:T(8,128)(2,1)S(1)}, bf16[168,384]{1,0:T(8,128)(2,1)S(1)}, u32[]{:S(2)}, u32[]{:S(2)}) collective-permute-start(bf16[168,384]{1,0:T(8,128)(2,1)S(1)} %get-tuple-element.66), channel_id=1, source_target_pairs={{0,2},{1,0},{2,6},{3,4},{4,3},{5,1},{6,7},{7,5},{8,10},{9,8},{10,1... | collective-permute-start | bytes 387080 | tf_op jit(solution)/shard_map/ppermute | solution.py:261
  68.7 7.4 %copy-start.5 = (bf16[168,384]{1,0:T(8,128)(2,1)}, bf16[168,384]{1,0:T(8,128)(2,1)S(1)}, u32[]{:S(2)}) copy-start(bf16[168,384]{1,0:T(8,128)(2,1)S(1)} %get-tuple-element.64) | copy-start | bytes 387076
  68.7 36.2 %copy-start.3 = (bf16[168,384]{1,0:T(8,128)(2,1)}, bf16[168,384]{1,0:T(8,128)(2,1)S(1)}, u32[]{:S(2)}) copy-start(bf16[168,384]{1,0:T(8,128)(2,1)S(1)} %get-tuple-element.63) | copy-start | bytes 387076
  68.8 3.5 %collective-permute-start.2 = (bf16[336,384]{1,0:T(8,128)(2,1)S(1)}, bf16[336,384]{1,0:T(8,128)(2,1)}, u32[]{:S(2)}, u32[]{:S(2)}) collective-permute-start(bf16[336,384]{1,0:T(8,128)(2,1)S(1)} %pad_maximum_fusion.4.refs_4_), channel_id=1, source_target_pairs={{4,0},{5,1},{6,2},{7,3},{0,4},{1,5},{2,6},{3,7},{12,8},{13,9},{14,... | collective-permute-start | bytes 774152 | tf_op jit(solution)/shard_map/ppermute | solution.py:261
  83.1 21.9 %copy-start.6 = (bf16[168,384]{1,0:T(8,128)(2,1)S(1)}, bf16[168,384]{1,0:T(8,128)(2,1)}, u32[]{:S(2)}) copy-start(bf16[168,384]{1,0:T(8,128)(2,1)} %copy-done.5) | copy-start | bytes 387076
  94.0 9.4 %collective-permute-start.12 = (bf16[336,384]{1,0:T(8,128)(2,1)S(1)}, bf16[336,384]{1,0:T(8,128)(2,1)S(1)}, u32[]{:S(2)}, u32[]{:S(2)}) collective-permute-start(bf16[336,384]{1,0:T(8,128)(2,1)S(1)} %shard_map.152), channel_id=1, source_target_pairs={{0,16},{1,17},{2,18},{3,19},{4,20},{5,21},{6,22},{7,23},{8,24},{9,... | collective-permute-start | bytes 774152 | tf_op jit(solution)/shard_map/ppermute | solution.py:470
  103.4 1.5 collective-permute-start.13
  106.0 33.4 %copy-start.4 = (bf16[168,384]{1,0:T(8,128)(2,1)S(1)}, bf16[168,384]{1,0:T(8,128)(2,1)}, u32[]{:S(2)}) copy-start(bf16[168,384]{1,0:T(8,128)(2,1)} %copy-done.3) | copy-start | bytes 387076
  127.4 1.6 collective-permute-start.14
  129.1 10.3 %collective-permute-start.15 = (bf16[336,384]{1,0:T(8,128)(2,1)S(1)}, bf16[336,384]{1,0:T(8,128)(2,1)S(1)}, u32[]{:S(2)}, u32[]{:S(2)}) collective-permute-start(bf16[336,384]{1,0:T(8,128)(2,1)S(1)} %add_convert_fusion.1), channel_id=1, source_target_pairs={{16,0},{17,1},{18,2},{19,3},{20,4},{21,5},{22,6},{23,7},{24,8},{25... | collective-permute-start | bytes 774152 | tf_op jit(solution)/shard_map/ppermute | solution.py:470
  169.3 1.3 copy-start.2
  171.0 1.8 copy-start
  172.8 4.0 %collective-permute-start.19 = (bf16[2,4,304,384]{3,2,1,0:T(8,128)(2,1)S(1)}, bf16[2,4,304,384]{3,2,1,0:T(8,128)(2,1)}, u32[]{:S(2)}, u32[]{:S(2)}) collective-permute-start(bf16[2,4,304,384]{3,2,1,0:T(8,128)(2,1)S(1)} %dynamic-slice_bitcast_fusion), channel_id=1, source_target_pairs={{0,4},{4,0},{8,12},{12,8},{1,5},{5,1},{9,13},{13,9},{2,6},{6,2},{1... | collective-permute-start | bytes 5603336 | tf_op jit(solution)/shard_map/ppermute | solution.py:250
  179.2 1.8 copy-start.1
  181.2 22.8 %collective-permute-start.20 = (bf16[4,304,384]{2,1,0:T(8,128)(2,1)S(1)}, bf16[4,304,384]{2,1,0:T(8,128)(2,1)S(1)}, u32[]{:S(2)}, u32[]{:S(2)}) collective-permute-start(bf16[4,304,384]{2,1,0:T(8,128)(2,1)S(1)} %fusion.2), channel_id=1, source_target_pairs={{0,8},{4,12},{8,0},{12,4},{1,9},{5,13},{9,1},{13,5},{2,10},{6,14},... | collective-permute-start | bytes 2801672 | tf_op jit(solution)/shard_map/ppermute | solution.py:255
  182.8 1.6 collective-permute-start.16
  184.5 25.2 %collective-permute-start.18 = (bf16[168,384]{1,0:T(8,128)(2,1)S(1)}, bf16[168,384]{1,0:T(8,128)(2,1)S(1)}, u32[]{:S(2)}, u32[]{:S(2)}) collective-permute-start(bf16[168,384]{1,0:T(8,128)(2,1)S(1)} %get-tuple-element.61), channel_id=1, source_target_pairs={{2,0},{0,1},{6,2},{4,3},{3,4},{1,5},{7,6},{5,7},{10,8},{8,9},{14,1... | collective-permute-start | bytes 387080 | tf_op jit(solution)/shard_map/ppermute | solution.py:261
  184.6 25.2 %collective-permute-start.17 = (bf16[168,384]{1,0:T(8,128)(2,1)S(1)}, bf16[168,384]{1,0:T(8,128)(2,1)S(1)}, u32[]{:S(2)}, u32[]{:S(2)}) collective-permute-start(bf16[168,384]{1,0:T(8,128)(2,1)S(1)} %get-tuple-element.62), channel_id=1, source_target_pairs={{0,0},{2,1},{4,2},{6,3},{1,4},{3,5},{5,6},{7,7},{8,8},{10,9},{12,1... | collective-permute-start | bytes 387080 | tf_op jit(solution)/shard_map/ppermute | solution.py:261
  205.9 10.5 %collective-permute-start.21 = (bf16[304,384]{1,0:T(8,128)(2,1)S(1)}, bf16[304,384]{1,0:T(8,128)(2,1)S(1)}, u32[]{:S(2)}, u32[]{:S(2)}) collective-permute-start(bf16[304,384]{1,0:T(8,128)(2,1)S(1)} %get-tuple-element.54), channel_id=1, source_target_pairs={{0,1},{1,2},{2,3},{3,0},{4,5},{5,6},{6,7},{7,4},{8,9},{9,10},{10,1... | collective-permute-start | bytes 700424 | tf_op jit(solution)/shard_map/ppermute | solution.py:312
  205.9 12.0 %collective-permute-start.23 = (bf16[304,384]{1,0:T(8,128)(2,1)S(1)}, bf16[304,384]{1,0:T(8,128)(2,1)S(1)}, u32[]{:S(2)}, u32[]{:S(2)}) collective-permute-start(bf16[304,384]{1,0:T(8,128)(2,1)S(1)} %get-tuple-element.55), channel_id=1, source_target_pairs={{0,3},{1,0},{2,1},{3,2},{4,7},{5,4},{6,5},{7,6},{8,11},{9,8},{10,9... | collective-permute-start | bytes 700424 | tf_op jit(solution)/shard_map/ppermute | solution.py:312
  209.7 19.2 %collective-permute-start.22 = (bf16[304,384]{1,0:T(8,128)(2,1)S(1)}, bf16[304,384]{1,0:T(8,128)(2,1)S(1)}, u32[]{:S(2)}, u32[]{:S(2)}) collective-permute-start(bf16[304,384]{1,0:T(8,128)(2,1)S(1)} %get-tuple-element.56), channel_id=1, source_target_pairs={{0,2},{1,3},{2,0},{3,1},{4,6},{5,7},{6,4},{7,5},{8,10},{9,11},{10,... | collective-permute-start | bytes 700424 | tf_op jit(solution)/shard_map/ppermute | solution.py:312

commit v2 on v1

v2 whole, which is shorter than its diff:
```python
import functools
import math
import jax
import jax.numpy as jnp
from jax import lax
from jax.experimental import pallas as pl
from jax.experimental.pallas import tpu as pltpu
from jax.sharding import PartitionSpec as P

HEADS = 6
norm_eps = 1e-06
F32 = jnp.float32
BF16 = jnp.bfloat16


def mul(left, right, left_dim=1, right_dim=0):
    return lax.dot_general(
        left, right, (((left_dim,), (right_dim,)), ((), ())), preferred_element_type=F32
    )


def total_of(rows):
    return jnp.sum(rows, axis=0, keepdims=True)


def norm_parts(rows_in):
    centre = jnp.mean(rows_in, axis=-1, keepdims=True)
    centred = rows_in - centre
    spread = jnp.mean(centred * centred, axis=-1, keepdims=True)
    scale = lax.rsqrt(spread + norm_eps)
    return centred * scale, scale


def norm_grad(grad, gain, unit, scale):
    scaled = grad * gain
    inner = jnp.mean(scaled * unit, axis=-1, keepdims=True)
    return scale * (scaled - jnp.mean(scaled, axis=-1, keepdims=True) - unit * inner)


def gelu_cdf(hidden):
    return 0.5 + 0.5 * lax.erf(hidden * math.sqrt(0.5))


def row_of(vec_ref, index):
    return vec_ref[index : index + 1, :]


def head_halves(head_dim):
    lane = lax.broadcasted_iota(jnp.int32, (1, 128), 1)
    first_half = (lane < head_dim).astype(BF16)
    return (first_half, 1 - first_half)


def attend_forward(x_ref, mask_ref, wa_ref, vec_ref, refs, mid_ref):
    q_s, k_s, v_s, vt_s, ot_s, kt_s, p_s = refs
    own = q_s.shape[1]
    width = x_ref.shape[1]
    pairs = k_s.shape[0]
    head_dim = width // HEADS
    mask = mask_ref[...]
    masked = x_ref[...].astype(F32) * mask
    unit, _ = norm_parts(masked)
    normed = (unit * row_of(vec_ref, 0) + row_of(vec_ref, 2)).astype(BF16)
    queries = (mul(normed[:own], wa_ref[0]) + row_of(vec_ref, 4)).astype(BF16)
    queries = (queries.astype(F32) * head_dim ** (-0.5)).astype(BF16)
    keys = mul(normed, wa_ref[1]).astype(BF16)
    values = (mul(normed, wa_ref[2]) + row_of(vec_ref, 5)).astype(BF16)
    for j in range(pairs):
        lanes = slice(j * 128, (j + 1) * 128)
        q_s[j] = queries[:, lanes]
        k_s[j] = keys[:, lanes]
        v_s[j] = values[:, lanes]
        vt_s[j] = values[:, lanes].T
        if kt_s is not None:
            kt_s[j] = keys[:, lanes].T
    halves = head_halves(head_dim)

    @pl.loop(0, pairs)
    def _(j):
        bias = (mask_ref[...] - 1.0) * 1e30
        for e in range(2):
            score = mul(k_s[j], q_s[j] * halves[e], 1, 1) + bias
            top = jnp.max(score, axis=0, keepdims=True)
            expo = jnp.exp(score - top)
            probs = (expo * (1.0 / total_of(expo))).astype(BF16)
            rows = slice(e * head_dim, (e + 1) * head_dim)
            ot_s[j, rows, :] = mul(vt_s[j, rows, :], probs).astype(BF16)
            if p_s is not None:
                p_s[2 * j + e] = probs

    attended = jnp.concatenate([ot_s[j].T for j in range(pairs)], axis=1)
    mid_ref[...] = masked[:own] + mul(attended, wa_ref[3]) + row_of(vec_ref, 6)


def feed_forward(mid_ref, mask_ref, w1_ref, w2_ref, vec_ref, c_s, acc_s, h_s, y_ref):
    own, width = mid_ref.shape
    unit, _ = norm_parts(mid_ref[...])
    c_s[...] = (unit * row_of(vec_ref, 1) + row_of(vec_ref, 3)).astype(BF16)
    acc_s[...] = jnp.zeros_like(acc_s)

    @pl.loop(0, w1_ref.shape[0])
    def _(k):
        hidden = mul(c_s[...], w1_ref[k]) + vec_ref[pl.ds(8 + k, 1), :]
        if h_s is not None:
            h_s[k] = hidden
        active = (hidden * gelu_cdf(hidden)).astype(BF16)
        rows = pl.ds(pl.multiple_of(k * width, 128), width)
        acc_s[...] += mul(active, w2_ref[rows, :])

    y_ref[...] = (
        (mid_ref[...] + acc_s[...] + row_of(vec_ref, 7)) * mask_ref[:own, :]
    ).astype(BF16)


def feed_backward(
    mid_ref, mask_ref, dy_ref, w1_ref, w2_ref, vec_ref, c_s, acc_s, h_s, gmid_ref, grads
):
    own, width = mid_ref.shape
    acc_s[...] = jnp.zeros_like(acc_s)
    g1_s, g2_s, gv_ref = grads or (None, None, None)

    @pl.loop(0, w1_ref.shape[0])
    def _(k):
        if h_s is None:
            hidden = mul(c_s[...], w1_ref[k]) + vec_ref[pl.ds(8 + k, 1), :]
        else:
            hidden = h_s[k]
        cdf = gelu_cdf(hidden)
        slope = cdf + hidden * jnp.exp(-0.5 * hidden * hidden) * (1.0 / math.sqrt(2 * math.pi))
        grad_second = (dy_ref[...].astype(F32) * mask_ref[:own, :]).astype(BF16)
        rows = pl.ds(pl.multiple_of(k * width, 128), width)
        grad_hidden = (mul(grad_second, w2_ref[rows, :], 1, 1) * slope).astype(BF16)
        acc_s[...] += mul(grad_hidden, w1_ref[k], 1, 1)
        if grads is not None:
            active = (hidden * cdf).astype(BF16)
            g1_s[k] = mul(c_s[...], grad_hidden, 0, 0).astype(BF16)
            g2_s[rows, :] = mul(active, grad_second, 0, 0).astype(BF16)
            gv_ref[pl.ds(8 + k, 1), :] = total_of(grad_hidden.astype(F32))

    grad_y = dy_ref[...].astype(F32) * mask_ref[:own, :]
    grad_c = acc_s[...]
    unit, scale = norm_parts(mid_ref[...])
    grad_mid = grad_y + norm_grad(grad_c, row_of(vec_ref, 1), unit, scale)
    gmid_ref[...] = grad_mid
    if grads is not None:
        gv_ref[1:2, :] = total_of(grad_c * unit)
        gv_ref[3:4, :] = total_of(grad_c)
        gv_ref[6:7, :] = total_of(grad_mid.astype(BF16).astype(F32))
        gv_ref[7:8, :] = total_of(grad_y.astype(BF16).astype(F32))


def attend_backward(x_ref, mask_ref, wa_ref, vec_ref, kept, scratch, gmid_ref, du_ref, grads):
    q_s, k_s, v_s, ot_s, kt_s, p_s = kept
    do_s, dq_s, dk_s, dv_s = scratch
    own, width = gmid_ref.shape
    pairs = k_s.shape[0]
    head_dim = width // HEADS
    grad_branch = gmid_ref[...].astype(BF16)
    grad_att = mul(grad_branch, wa_ref[3], 1, 1).astype(BF16)
    for j in range(pairs):
        do_s[j] = grad_att[:, j * 128 : (j + 1) * 128]
    if grads is not None:
        ga_s, gv_ref = grads
        for j in range(pairs):
            ga_s[3, j * 128 : (j + 1) * 128, :] = mul(ot_s[j], grad_branch).astype(BF16)
    halves = head_halves(head_dim)

    @pl.loop(0, pairs)
    def _(j):
        grad_k = None
        for e in range(2):
            half_do = do_s[j] * halves[e]
            half_q = q_s[j] * halves[e]
            grad_p = mul(v_s[j], half_do, 1, 1)
            probs_low = p_s[2 * j + e]
            probs = probs_low.astype(F32)
            row_dot = total_of(probs * grad_p)
            grad_s = (probs * (grad_p - row_dot)).astype(BF16)
            rows = slice(e * head_dim, (e + 1) * head_dim)
            dq_s[j, rows, :] = (mul(kt_s[j, rows, :], grad_s) * head_dim ** (-0.5)).astype(BF16)
            part_k = mul(grad_s, half_q)
            part_v = mul(probs_low, half_do)
            grad_k, grad_v = (part_k, part_v) if grad_k is None else (grad_k + part_k, grad_v + part_v)
        dk_s[j] = grad_k.astype(BF16)
        dv_s[j] = grad_v.astype(BF16)

    grad_q = jnp.concatenate([dq_s[j].T for j in range(pairs)], axis=1)
    grad_k = jnp.concatenate([dk_s[j] for j in range(pairs)], axis=1)
    grad_v = jnp.concatenate([dv_s[j] for j in range(pairs)], axis=1)
    mask = mask_ref[...]
    unit, scale = norm_parts(x_ref[...].astype(F32) * mask)
    if grads is not None:
        normed = (unit * row_of(vec_ref, 0) + row_of(vec_ref, 2)).astype(BF16)
        ga_s[0] = mul(normed[:own], grad_q, 0, 0).astype(BF16)
        turned = normed.T
        ga_s[1] = mul(turned, grad_k).astype(BF16)
        ga_s[2] = mul(turned, grad_v).astype(BF16)
        gv_ref[4:5, :] = total_of(grad_q.astype(F32))
        gv_ref[5:6, :] = total_of(grad_v.astype(F32))
    grad_n = mul(grad_k, wa_ref[1], 1, 1) + mul(grad_v, wa_ref[2], 1, 1)
    grad_n = jnp.concatenate([grad_n[:own] + mul(grad_q, wa_ref[0], 1, 1), grad_n[own:]], axis=0)
    if grads is not None:
        gv_ref[0:1, :] = total_of(grad_n * unit)
        gv_ref[2:3, :] = total_of(grad_n)
    grad_u = norm_grad(grad_n, row_of(vec_ref, 0), unit, scale)
    grad_u = jnp.concatenate([grad_u[:own] + gmid_ref[...], grad_u[own:]], axis=0)
    du_ref[...] = (grad_u * mask).astype(BF16)


def piece_groups(place_ref, mine, theirs):
    outer, core, line = place_ref[0], place_ref[1], place_ref[2]
    count = mine[0].shape[0]
    for side, members in enumerate((mine, theirs)):
        for turn, ref in enumerate(members):
            index = lax.rem(outer + (len(mine) - turn), len(mine)) * 2 + (core if side == 0 else 1 - core)
            blocks = [
                ref[lax.rem(line - z + count, count)].astype(F32) for z in range(count)
            ]
            yield index, blocks


def first_kernel(loose, rows, *refs):
    refs = list(refs)
    place_ref, x_ref, mask_ref = refs[:3]
    refs = refs[3:]
    if loose:
        mine, theirs = refs[:loose], refs[loose : 2 * loose]
        refs = refs[2 * loose :]
        mid_ref, wa_ref, vec_ref, *scratch = refs
        width = x_ref.shape[1]
        vector = None
        for index, blocks in piece_groups(place_ref, mine, theirs):
            span = rows * len(blocks)
            start = pl.multiple_of(index * span, 16)
            for s in range(4):
                group = jnp.concatenate([b[s * rows : (s + 1) * rows] for b in blocks], axis=0)
                wa_ref[s, pl.ds(start, span), :] = group.astype(BF16)
            for b in blocks:
                tail = b[4 * rows : 4 * rows + 16]
                vector = tail if vector is None else vector + tail
        vec_ref[...] = vector
    else:
        wa_ref, vec_ref, mid_ref, *scratch = refs
    attend_forward(x_ref, mask_ref, wa_ref, vec_ref, (*scratch, None, None), mid_ref)


def second_kernel(loose, rows, *refs):
    refs = list(refs)
    place_ref, mid_ref, mask_ref, vec_ref = refs[:4]
    refs = refs[4:]
    if loose:
        mine, theirs = refs[:loose], refs[loose : 2 * loose]
        refs = refs[2 * loose :]
        y_ref, w1_ref, w2_ref, c_s, acc_s = refs
        for index, blocks in piece_groups(place_ref, mine, theirs):
            span = rows * len(blocks)
            start = pl.multiple_of(index * span, 16)
            for s in range(4):
                group = jnp.concatenate([b[s * rows : (s + 1) * rows] for b in blocks], axis=0)
                w1_ref[s, pl.ds(start, span), :] = group.astype(BF16)
            group = jnp.concatenate([b[4 * rows : 8 * rows] for b in blocks], axis=0)
            w2_ref[pl.ds(pl.multiple_of(4 * start, 16), 4 * span), :] = group.astype(BF16)
    else:
        w1_ref, w2_ref, y_ref, c_s, acc_s = refs
    feed_forward(mid_ref, mask_ref, w1_ref, w2_ref, vec_ref, c_s, acc_s, None, y_ref)


def middle_kernel(*refs):
    x_ref, mask_ref, dy_ref, wa_ref, w1_ref, w2_ref, vec_ref = refs[:7]
    y_ref, du_ref, mid_ref, q_s, k_s, v_s, ot_s, kt_s, p_s = refs[7:16]
    vt_s, c_s, acc_s, h_s, gmid_s, do_s, dq_s, dk_s, dv_s = refs[16:]
    attend_forward(
        x_ref, mask_ref, wa_ref, vec_ref, (q_s, k_s, v_s, vt_s, ot_s, kt_s, p_s), mid_ref
    )
    feed_forward(mid_ref, mask_ref, w1_ref, w2_ref, vec_ref, c_s, acc_s, h_s, y_ref)
    feed_backward(
        mid_ref, mask_ref, dy_ref, w1_ref, w2_ref, vec_ref, c_s, acc_s, h_s, gmid_s, None
    )
    attend_backward(
        x_ref, mask_ref, wa_ref, vec_ref, (q_s, k_s, v_s, ot_s, kt_s, p_s),
        (do_s, dq_s, dk_s, dv_s), gmid_s, du_ref, None,
    )


def share_out(core, blocks_of, outer_count, start, size, kept_ref, sent_ref):
    for o in range(outer_count):
        even, odd = blocks_of(2 * o), blocks_of(2 * o + 1)
        kept_ref[o, start : start + size, :] = jnp.where(core == 0, even, odd)
        sent_ref[o, start : start + size, :] = jnp.where(core == 0, odd, even)


def feed_grad_kernel(*refs):
    place_ref, mid_ref, mask_ref, dy_ref, w1_ref, w2_ref, vec_ref = refs[:7]
    gmid_ref, gv_ref, kept_ref, sent_ref = refs[7:11]
    c_s, acc_s, g1_s, g2_s = refs[11:]
    outer_count = kept_ref.shape[0]
    span = w1_ref.shape[1] // (2 * outer_count)
    unit, _ = norm_parts(mid_ref[...])
    c_s[...] = (unit * row_of(vec_ref, 1) + row_of(vec_ref, 3)).astype(BF16)
    gv_ref[...] = jnp.zeros_like(gv_ref)
    feed_backward(
        mid_ref, mask_ref, dy_ref, w1_ref, w2_ref, vec_ref, c_s, acc_s, None, gmid_ref,
        (g1_s, g2_s, gv_ref),
    )
    core = place_ref[1]
    for s in range(4):
        share_out(
            core, lambda d: g1_s[s, d * span : (d + 1) * span, :], outer_count,
            s * span, span, kept_ref, sent_ref,
        )
    share_out(
        core, lambda d: g2_s[4 * d * span : 4 * (d + 1) * span, :], outer_count,
        4 * span, 4 * span, kept_ref, sent_ref,
    )


def attend_grad_kernel(*refs):
    place_ref, x_ref, mask_ref, wa_ref, vec_ref = refs[:5]
    q_s, k_s, v_s, ot_s, kt_s, p_s, gmid_ref, gv_in_ref = refs[5:13]
    du_ref, kept_ref, sent_ref = refs[13:16]
    do_s, dq_s, dk_s, dv_s, ga_s, gv_s = refs[16:]
    outer_count = kept_ref.shape[0]
    span = wa_ref.shape[1] // (2 * outer_count)
    gv_s[...] = gv_in_ref[...]
    attend_backward(
        x_ref, mask_ref, wa_ref, vec_ref, (q_s, k_s, v_s, ot_s, kt_s, p_s),
        (do_s, dq_s, dk_s, dv_s), gmid_ref, du_ref, (ga_s, gv_s),
    )
    core = place_ref[1]
    for s in range(4):
        share_out(
            core, lambda d: ga_s[s, d * span : (d + 1) * span, :], outer_count,
            s * span, span, kept_ref, sent_ref,
        )
    tail = gv_s[...].astype(BF16)
    for o in range(outer_count):
        kept_ref[o, 4 * span :, :] = tail
        sent_ref[o, 4 * span :, :] = tail


def call(kernel, operands, shapes, scratch, flops, scalars=0):
    whole = pl.BlockSpec(memory_space=pltpu.VMEM)
    scalar = pl.BlockSpec(memory_space=pltpu.SMEM)
    return pl.pallas_call(
        kernel,
        out_shape=[jax.ShapeDtypeStruct(*shape) for shape in shapes],
        in_specs=[scalar] * scalars + [whole] * (len(operands) - scalars),
        out_specs=[whole] * len(shapes),
        scratch_shapes=[pltpu.VMEM(*shape) for shape in scratch],
        compiler_params=pltpu.CompilerParams(vmem_limit_bytes=VMEM_LIMIT),
        cost_estimate=pl.CostEstimate(flops=flops, bytes_accessed=4 * 10**6, transcendentals=10**6),
    )(*operands)


VMEM_LIMIT = 32 * 1024 * 1024


def axis_sizes():
    return lax.axis_size("dp"), lax.axis_size("seq")


def swap_core(value):
    return lax.ppermute(value, "dp", [(d, d ^ 1) for d in range(lax.axis_size("dp"))])


def turn_outer(value, steps):
    count = lax.axis_size("dp")
    return lax.ppermute(value, "dp", [(d, (d + 2 * steps) % count) for d in range(count)])


def turn_line(value, steps):
    count = lax.axis_size("seq")
    return lax.ppermute(value, "seq", [(z, (z + steps) % count) for z in range(count)])


def joint_permute(value, moves):
    seq_count = lax.axis_size("seq")
    pairs = [(a[0] * seq_count + a[1], b[0] * seq_count + b[1]) for a, b in moves]
    return lax.ppermute(value, ("dp", "seq"), pairs)


def gather_line(piece):
    return [piece] + [turn_line(piece, k) for k in range(1, lax.axis_size("seq"))]


def gather_rest(line):
    outer_count = lax.axis_size("dp") // 2
    stacked = jnp.stack(line)
    mine = [stacked] + [turn_outer(stacked, k) for k in range(1, outer_count)]
    return mine, [swap_core(member) for member in mine]


def assemble(mine, theirs):
    outer_count, seq_count = len(mine), lax.axis_size("seq")
    d, z = lax.axis_index("dp"), lax.axis_index("seq")
    o, c = d // 2, d % 2
    turned = jnp.stack([jnp.stack(mine), jnp.stack(theirs)])
    sides = (jnp.arange(2) + c) % 2
    outers = (o - jnp.arange(outer_count)) % outer_count
    lines = (z - jnp.arange(seq_count)) % seq_count
    ordered = turned[sides][:, outers][:, :, lines]
    return ordered.transpose(1, 0, 2, 3, 4).reshape((-1,) + mine[0].shape[1:])


def scatter_sum(kept, sent, take):
    d, z = lax.axis_index("dp"), lax.axis_index("seq")
    outer_count, seq_count = lax.axis_size("dp") // 2, lax.axis_size("seq")
    o = d // 2
    came = swap_core(sent)

    def both(index):
        return lax.dynamic_index_in_dim(kept, index, 0, keepdims=False).astype(
            F32
        ) + lax.dynamic_index_in_dim(came, index, 0, keepdims=False).astype(F32)

    total = both(o)
    for k in range(1, outer_count):
        total = total + turn_outer(both((o + k) % outer_count).astype(BF16), k).astype(F32)
    low = total.astype(BF16)
    result = take(total, z)
    for k in range(1, seq_count):
        result = result + turn_line(take(low, (z + k) % seq_count), k).astype(F32)
    return result


def image_moves(step):
    dp_count, seq_count = axis_sizes()
    block = seq_count // 4
    moves = []
    for d in range(dp_count):
        for z in range(seq_count):
            micro = (step + z) % 2
            rank = z // 2
            target = (d - d % 2 + rank % 2, (2 * micro + d % 2) * block + rank // 2)
            moves.append(((d, z), target))
    return moves


def to_images(blocks):
    z = lax.axis_index("seq")
    micro = z // (lax.axis_size("seq") // 4) // 2
    arrived = []
    for step in range(2):
        sent = jnp.where((step + z) % 2 == 0, blocks[0], blocks[1])
        arrived.append(joint_permute(sent, image_moves(step)))
    low = jnp.where(micro == 0, arrived[0], arrived[1])
    high = jnp.where(micro == 0, arrived[1], arrived[0])
    return jnp.concatenate([low, high], axis=0)


def from_images(rows_own):
    z = lax.axis_index("seq")
    micro = z // (lax.axis_size("seq") // 4) // 2
    half = rows_own.shape[0] // 2
    low, high = rows_own[:half], rows_own[half:]
    arrived = []
    for step in range(2):
        sent = jnp.where(micro == step, low, high)
        arrived.append(joint_permute(sent, [(b, a) for a, b in image_moves(step)]))
    return jnp.stack([jnp.where(z % 2 == m, arrived[0], arrived[1]) for m in range(2)])


def group_members():
    block = lax.axis_size("seq") // 4
    return [(turn, flip) for turn in range(block) for flip in range(2)][1:]


def group_moves(turn, flip):
    dp_count, seq_count = axis_sizes()
    block = seq_count // 4
    moves = []
    for d in range(dp_count):
        for z in range(seq_count):
            base = z - z % block
            moves.append(((d ^ flip, base + (z % block + turn) % block), (d, z)))
    return moves


def gather_group(own_rows):
    arrived = [joint_permute(own_rows, group_moves(*member)) for member in group_members()]
    return jnp.concatenate([own_rows] + arrived, axis=0)


def scatter_group(partial, own):
    total = partial[:own].astype(F32)
    for place, member in enumerate(group_members()):
        sent = partial[(place + 1) * own : (place + 2) * own]
        back = [(b, a) for a, b in group_moves(*member)]
        total = total + joint_permute(sent, back).astype(F32)
    return total.astype(BF16)


def slot_mask(lengths, slot_count):
    block = lax.axis_size("seq") // 4
    d, z = lax.axis_index("dp"), lax.axis_index("seq")
    c, group = d % 2, z // block
    theirs = swap_core(lengths[:, 0])
    counts = jnp.where(group % 2 == c, lengths[:, 0], theirs)
    counts = jnp.where(group // 2 == 0, counts[0], counts[1])
    places = jnp.arange(slot_count, dtype=jnp.int32)
    parts = []
    for turn, flip in [(0, 0)] + group_members():
        rank = (z % block + turn) % block * 2 + (c ^ flip)
        picked = lax.dynamic_slice_in_dim(counts, 2 * rank, 2, 0)
        parts.append((places[None, :] < picked[:, None]).astype(F32).reshape(-1, 1))
    return jnp.concatenate(parts, axis=0)


def to_section(value, steps):
    return lax.ppermute(value, "section", [(0, 1)] if steps == 1 else [(1, 0)])


def vector_slots(members, width):
    index = lax.axis_index("dp") * lax.axis_size("seq") + lax.axis_index("seq")
    count = lax.axis_size("dp") * lax.axis_size("seq")
    parts = []
    for member in members:
        length = member.shape[0]
        spread = jnp.zeros((count * length,), BF16)
        spread = lax.dynamic_update_slice_in_dim(spread, member, index * length, 0)
        parts.append(spread.reshape(-1, width))
    parts.append(jnp.zeros((4, width), BF16))
    return jnp.concatenate(parts, axis=0)


def own_slots(vectors, lengths):
    index = lax.axis_index("dp") * lax.axis_size("seq") + lax.axis_index("seq")
    count = lax.axis_size("dp") * lax.axis_size("seq")
    parts, start = [], 0
    for length in lengths:
        used = length * count // vectors.shape[1]
        flat = vectors[start : start + used].reshape(-1)
        parts.append(lax.dynamic_slice_in_dim(flat, index * length, length, 0))
        start += used
    return parts


def by_column(member, width):
    rows = member.shape[0]
    return member.reshape(rows, -1, width).transpose(1, 0, 2).reshape(-1, width)


def from_columns(block, rows):
    width = block.shape[1]
    return block.reshape(-1, rows, width).transpose(1, 0, 2).reshape(rows, -1)


def on_device(boundary, lengths, w_qkv, w_out, w_fc1, w_fc2, gains, shifts, fc1_bias):
    section = lax.axis_index("section")
    dp_count, seq_count = axis_sizes()
    outer_count = dp_count // 2
    d = lax.axis_index("dp")
    place = jnp.stack([d // 2, d % 2, lax.axis_index("seq")]).astype(jnp.int32)
    slot_count = boundary.shape[3]
    own = 2 * slot_count
    total = lengths.shape[2] * slot_count
    rows, width = w_out.shape[1:]
    hidden = rows * 4 * dp_count * seq_count
    pairs = width // 128
    span = width // dp_count
    lens = (gains.shape[1], shifts.shape[1], fc1_bias.shape[1])
    piece_a = jnp.concatenate(
        [by_column(w_qkv[0], width), w_out[0], vector_slots((gains[0], shifts[0], fc1_bias[0]), width)]
    )
    piece_b = jnp.concatenate([by_column(w_fc1[0], width), w_fc2[0]])
    line_a = gather_line(piece_a)
    own_start = to_images(boundary[0, :, 0])
    line_b = gather_line(piece_b)
    mask = slot_mask(lengths, slot_count)
    all_start = gather_group(own_start)
    mine_a, theirs_a = gather_rest(line_a)
    mine_b, theirs_b = gather_rest(line_b)
    loose = outer_count if rows % 8 == 0 else 0

    w_shape = ((4, width, width), BF16)
    tall_shape = ((hidden, width), BF16)
    vec_shape = ((16, width), F32)
    mid_shape = ((own, width), F32)
    low_shape = ((own, width), BF16)
    all_shape = ((total, width), BF16)
    q_shape = ((pairs, own, 128), BF16)
    k_shape = ((pairs, total, 128), BF16)
    qt_shape = ((pairs, 128, own), BF16)
    kt_shape = ((pairs, 128, total), BF16)
    p_shape = ((HEADS, total, own), BF16)
    h_shape = ((4, own, width), F32)
    shared_b = ((outer_count, 8 * span, width), BF16)
    shared_a = ((outer_count, 4 * span + 16, width), BF16)

    head_scratch = [q_shape, k_shape, k_shape, kt_shape, qt_shape]
    if loose:
        middle, w_a, vectors = call(
            functools.partial(first_kernel, loose, rows),
            [place, all_start, mask, *mine_a, *theirs_a],
            [mid_shape, w_shape, vec_shape], head_scratch, 10**9, 1,
        )
        first_out, w_1, w_2 = call(
            functools.partial(second_kernel, loose, rows),
            [place, middle, mask, vectors, *mine_b, *theirs_b],
            [low_shape, w_shape, tall_shape], [low_shape, mid_shape], 10**9, 1,
        )
    else:
        ordered = assemble(mine_a, theirs_a)
        w_a = ordered[:, : 4 * rows].reshape(-1, 4, rows, width).transpose(1, 0, 2, 3)
        w_a = w_a.reshape(4, width, width)
        vectors = jnp.sum(ordered[:, 4 * rows :].astype(F32), axis=0)
        ordered = assemble(mine_b, theirs_b)
        w_1 = ordered[:, : 4 * rows].reshape(-1, 4, rows, width).transpose(1, 0, 2, 3)
        w_1 = w_1.reshape(4, width, width)
        w_2 = ordered[:, 4 * rows :].reshape(hidden, width)
        (middle,) = call(
            functools.partial(first_kernel, loose, rows),
            [place, all_start, mask, w_a, vectors], [mid_shape], head_scratch, 10**9, 1,
        )
        (first_out,) = call(
            functools.partial(second_kernel, loose, rows),
            [place, middle, mask, vectors, w_1, w_2],
            [low_shape], [low_shape, mid_shape], 10**9, 1,
        )
    arrived = gather_group(to_section(first_out, 1))
    layer_in = jnp.where(section == 0, all_start, arrived)
    grad_scratch = [q_shape, qt_shape, k_shape, k_shape]
    layer_out, partial, middle, *kept = call(
        middle_kernel,
        [layer_in, mask, own_start, w_a, w_1, w_2, vectors],
        [low_shape, all_shape, mid_shape, q_shape, k_shape, k_shape, qt_shape, kt_shape, p_shape],
        [kt_shape, low_shape, mid_shape, h_shape, mid_shape, *grad_scratch], 4 * 10**9,
    )
    returned = to_section(scatter_group(partial, own), -1)
    grad_out = jnp.where(section == 0, returned, own_start)
    grad_mid, grad_vectors, kept_b, sent_b = call(
        feed_grad_kernel,
        [place, middle, mask, grad_out, w_1, w_2, vectors],
        [mid_shape, vec_shape, shared_b, shared_b],
        [low_shape, mid_shape, w_shape, tall_shape], 2 * 10**9, 1,
    )
    partial, kept_a, sent_a = call(
        attend_grad_kernel,
        [place, layer_in, mask, w_a, vectors, *kept, grad_mid, grad_vectors],
        [all_shape, shared_a, shared_a],
        [*grad_scratch, w_shape, vec_shape], 2 * 10**9, 1,
    )

    def line_block(wide, index):
        split = wide.reshape(4, seq_count, rows, width)
        return lax.dynamic_index_in_dim(split, index, 1, keepdims=False).reshape(-1, width)

    def take_b(value, index):
        tall = value[4 * span :].reshape(seq_count, 4 * rows, width)
        tall = lax.dynamic_index_in_dim(tall, index, 0, keepdims=False)
        return jnp.concatenate([line_block(value[: 4 * span], index), tall])

    def take_a(value, index):
        return jnp.concatenate([line_block(value[: 4 * span], index), value[4 * span :]])

    summed_b = scatter_sum(kept_b, sent_b, take_b)
    grad_in = scatter_group(partial, own)
    rows_out = from_images(jnp.where(section == 0, grad_in, layer_out))
    summed_a = scatter_sum(kept_a, sent_a, take_a)
    grads = (
        from_columns(summed_a[: 3 * rows], rows),
        summed_a[3 * rows : 4 * rows],
        from_columns(summed_b[: 4 * rows], rows),
        summed_b[4 * rows :],
        *own_slots(summed_a[4 * rows :], lens),
    )
    return (rows_out[None, :, None], *[member[None] for member in grads])


def solution(mesh):
    sharded = P("section", ("dp", "seq"), None)
    vector = P("section", ("dp", "seq"))
    images = P("section", None, "dp", "seq", None)
    grads = (sharded, sharded, sharded, sharded, vector, vector, vector)
    return jax.shard_map(
        on_device,
        mesh=mesh,
        in_specs=(images, P(None, "dp", None), *grads),
        out_specs=(images, *grads),
        check_vma=False,
    )
```

time: 234 us -> 191 us (0.82)
  waiting for transfers between devices: 95.5 us -> 65.2 us
  starting transfers between devices: 37.9 us -> 47.8 us
  Pallas kernels: 57.4 us -> 47.7 us
  other arithmetic: 17.5 us -> 10.1 us
  local copies, waits for them, and re-layouts: 24 us -> 18 us
    ppermute x12 -> x19, waiting for transfers between devices: 35.2 us -> 18.1 us  [the longest x12 17 us: turn_line(): lax.ppermute(value, 'seq', [(z, (z + steps) % count) for z in range(count)])]
    ppermute x2 -> x4, waiting for transfers between devices: 36.5 us -> 22.8 us  [turn_outer(): lax.ppermute(value, 'dp', [(d, (d + 2 * steps) % count) for d in range(co...]
    pallas_call x3 -> x5, Pallas kernels: 57.4 us -> 47.7 us  [call(): pl.pallas_call(kernel, out_shape=[jax.ShapeDtypeStruct(*shape) for shape...]
    slice x14 -> x10, local copies, waits for them, and re-layouts: 8.15 us -> 0.24 us  [the longest x2 0.14 us: take_b(): return jnp.concatenate([line_block(value[:4 * span], index), tall])]
    ppermute x12 -> x19, starting transfers between devices: 22 us -> 28.7 us  [the longest x12 26.7 us: turn_line(): lax.ppermute(value, 'seq', [(z, (z + steps) % count) for z in range(count)])]
    another operation x4, other arithmetic: 5.65 us -> 1.14 us  [the longest x3 1.06 us: gather_rest(): stacked = jnp.stack(line)]
    concatenate x5 -> x4, other arithmetic: 3.45 us -> 0.08 us  [the longest x3 0.05 us: take_b(): return jnp.concatenate([line_block(value[:4 * span], index), tall])]
    convert_element_type x2 -> x4, other arithmetic: 1.81 us -> 4.47 us  [the longest x2 2.41 us: scatter_sum(): low = total.astype(BF16)]
  transfers between devices with their start and end apart: 24 -> 33, of which waited for: 17 -> 18; matrix products, arithmetic and copies ran while one was open for 2% -> 6% of each run, Pallas kernels for 0% -> 4%
where the time goes in v2:
time: 191 us; the launch traced here: 190 us
  waiting for transfers between devices  65.2 us (34%)
  starting transfers between devices  47.8 us (25%)
  Pallas kernels  47.7 us (25%)
  local copies, waits for them, and re-layouts  18 us (9%)
  other arithmetic  10.1 us (5%)
    pallas_call x5, Pallas kernels, call(): pl.pallas_call(kernel, out_shape=[jax.ShapeDtypeStruct(*shape) for shape...  47.7 us
    ppermute x12, starting transfers between devices, turn_line(): lax.ppermute(value, 'seq', [(z, (z + steps) % count) for z in range(count)])  26.7 us
    ppermute x4, waiting for transfers between devices, turn_outer(): lax.ppermute(value, 'dp', [(d, (d + 2 * steps) % count) for d in range(co...  22.8 us
    ppermute x12, waiting for transfers between devices, turn_line(): lax.ppermute(value, 'seq', [(z, (z + steps) % count) for z in range(count)])  17 us
    ppermute x2, waiting for transfers between devices, to_section(): return lax.ppermute(value, 'section', [(0, 1)] if steps == 1 else [(1, 0)])  14.6 us
    ppermute x8, waiting for transfers between devices, joint_permute(): return lax.ppermute(value, ('dp', 'seq'), pairs)  9.73 us
    ppermute x8, starting transfers between devices, joint_permute(): return lax.ppermute(value, ('dp', 'seq'), pairs)  8.71 us
    unnamed x44, local copies, waits for them, and re-layouts  7.86 us
  transfers between devices with their start and end apart: 33, of which 18 were waited for; matrix products, arithmetic and copies ran while one was open for 6% of the time, Pallas kernels for 4%

profile of v2, /device:TPU:0, one launch (start us, length us, event | category | flops | bytes accessed | tf_op | source)
XLA Modules:
  0.0 190.2 jit_solution(9301162374610454115)
XLA Ops:
  0.7 0.9 reshape_squeeze.6
  1.6 0.9 dynamic_update_slice.9
  2.4 0.7 reduce
  3.4 0.9 dynamic_update_slice.11
  4.3 0.8 concatenate.49
  5.1 5.1 %collective-permute-start.6 = (bf16[112,384]{1,0:T(8,128)(2,1)S(1)}, bf16[112,384]{1,0:T(8,128)(2,1)S(1)}, u32[]{:S(2)}, u32[]{:S(2)}) collective-permute-start(bf16[112,384]{1,0:T(8,128)(2,1)S(1)} %concatenate.49), channel_id=1, source_target_pairs={{0,3},{1,0},{2,1},{3,2},{4,7},{5,4},{6,5},{7,6},{8,11},{9,8},{10,9... | collective-permute-start | bytes 258056 | tf_op jit(solution)/shard_map/ppermute | solution.py:373
  10.2 0.9 reshape_squeeze.7
  11.1 0.9 fusion.9
  12.6 2.6 %collective-permute-start.11 = (bf16[192,384]{1,0:T(8,128)(2,1)S(1)}, bf16[192,384]{1,0:T(8,128)(2,1)S(1)}, u32[]{:S(2)}, u32[]{:S(2)}) collective-permute-start(bf16[192,384]{1,0:T(8,128)(2,1)S(1)} %get-tuple-element.104), channel_id=1, source_target_pairs={{0,2},{1,3},{2,0},{3,1},{4,6},{5,7},{6,4},{7,5},{8,10},{9,11},{10,... | collective-permute-start | bytes 442376 | tf_op jit(solution)/shard_map/ppermute | solution.py:373
  15.2 1.0 collective-permute-done.3
  16.2 1.9 %collective-permute-start.10 = (bf16[192,384]{1,0:T(8,128)(2,1)S(1)}, bf16[192,384]{1,0:T(8,128)(2,1)S(1)}, u32[]{:S(2)}, u32[]{:S(2)}) collective-permute-start(bf16[192,384]{1,0:T(8,128)(2,1)S(1)} %get-tuple-element.104), channel_id=1, source_target_pairs={{0,1},{1,2},{2,3},{3,0},{4,5},{5,6},{6,7},{7,4},{8,9},{9,10},{10,1... | collective-permute-start | bytes 442376 | tf_op jit(solution)/shard_map/ppermute | solution.py:373
  18.9 9.7 %collective-permute-start.4 = (bf16[112,384]{1,0:T(8,128)(2,1)S(1)}, bf16[112,384]{1,0:T(8,128)(2,1)S(1)}, u32[]{:S(2)}, u32[]{:S(2)}) collective-permute-start(bf16[112,384]{1,0:T(8,128)(2,1)S(1)} %concatenate.49), channel_id=1, source_target_pairs={{0,1},{1,2},{2,3},{3,0},{4,5},{5,6},{6,7},{7,4},{8,9},{9,10},{10,1... | collective-permute-start | bytes 258056 | tf_op jit(solution)/shard_map/ppermute | solution.py:373
  28.6 2.1 %collective-permute-done.11 = bf16[192,384]{1,0:T(8,128)(2,1)S(1)} collective-permute-done((bf16[192,384]{1,0:T(8,128)(2,1)S(1)}, bf16[192,384]{1,0:T(8,128)(2,1)S(1)}, u32[]{:S(2)}, u32[]{:S(2)}) %collective-permute-start.11) | collective-permute-done | bytes 147488 | tf_op jit(solution)/shard_map/ppermute | solution.py:373
  30.7 0.7 collective-permute-start
  31.5 1.6 collective-permute-start.13
  33.1 3.5 %collective-permute-start.1 = (bf16[168,384]{1,0:T(8,128)(2,1)S(1)}, bf16[168,384]{1,0:T(8,128)(2,1)S(1)}, u32[]{:S(2)}, u32[]{:S(2)}) collective-permute-start(bf16[168,384]{1,0:T(8,128)(2,1)S(1)} %get-tuple-element.102), channel_id=1, source_target_pairs={{0,2},{1,0},{2,6},{3,4},{4,3},{5,1},{6,7},{7,5},{8,10},{9,8},{10,1... | collective-permute-start | bytes 387080 | tf_op jit(solution)/shard_map/ppermute | solution.py:379
  37.3 1.8 collective-permute-done.1
  39.1 1.3 collective-permute-start.14
  40.4 7.4 %collective-permute-done.13.refs_5_ = bf16[4,192,384]{2,1,0:T(8,128)(2,1)} collective-permute-done((bf16[4,192,384]{2,1,0:T(8,128)(2,1)S(1)}, bf16[4,192,384]{2,1,0:T(8,128)(2,1)}, u32[]{:S(2)}, u32[]{:S(2)}) %collective-permute-start.13) | collective-permute-done | bytes 589856 | tf_op jit(solution)/shard_map/ppermute | solution.py:368
  48.5 6.6 %collective-permute-done.7.refs_4_ = bf16[4,112,384]{2,1,0:T(8,128)(2,1)S(1)} collective-permute-done((bf16[4,112,384]{2,1,0:T(8,128)(2,1)S(1)}, bf16[4,112,384]{2,1,0:T(8,128)(2,1)S(1)}, u32[]{:S(2)}, u32[]{:S(2)}) %collective-permute-start.7) | collective-permute-done | bytes 344096 | tf_op jit(solution)/shard_map/ppermute | solution.py:368
  56.5 0.7 copy-done.9
  57.2 0.7 copy-done.11
  57.9 1.0 copy-done.2
  58.9 1.0 copy-done.8
  59.9 1.0 copy-done.10
  60.8 1.0 copy-done.12
  61.8 6.8 %shard_map.152 = (f32[336,384]{1,0:T(8,128)S(1)}, bf16[4,384,384]{2,1,0:T(8,128)(2,1)S(1)}, f32[16,384]{1,0:T(8,128)S(1)}) custom-call(s32[3]{0:T(128)S(1)} %pad_add_fusion.1.refs_0_, bf16[672,384]{1,0:T(8,128)(2,1)S(1)} %pad_maximum_fusion.1.refs_1_, f32[672,1]{1,0:T(8,128)S(1)} %concatenate.48.refs_2_.refs_1_, bf16[4,112,384]{2,1,0:T(8,128)(2,1)S(1)} %copy-done.2, ...), custom_call_target="tpu_custom_call" | custom-call | flops 1000000000 | bytes 4000000 | tf_op jit(solution)/shard_map/pallas_call | solution.py:344
  68.7 4.5 %shard_map.153 = (bf16[336,384]{1,0:T(8,128)(2,1)S(1)}, bf16[4,384,384]{2,1,0:T(8,128)(2,1)S(1)}, bf16[1536,384]{1,0:T(8,128)(2,1)S(1)}) custom-call(s32[3]{0:T(128)S(1)} %pad_add_fusion.1.refs_0_, f32[336,384]{1,0:T(8,128)S(1)} %get-tuple-element.30.refs_1_, f32[672,1]{1,0:T(8,128)S(1)} %concatenate.48.refs_2_.refs_1_, ...), custom_call_target="tpu_custom_call" | custom-call | flops 1000000000 | bytes 4000000 | tf_op jit(solution)/shard_map/pallas_call | solution.py:344
  73.1 1.0 copy-done.15
  74.2 3.7 %collective-permute-start.16 = (bf16[336,384]{1,0:T(8,128)(2,1)S(1)}, bf16[336,384]{1,0:T(8,128)(2,1)S(1)}, u32[]{:S(2)}, u32[]{:S(2)}) collective-permute-start(bf16[336,384]{1,0:T(8,128)(2,1)S(1)} %get-tuple-element.32), channel_id=1, source_target_pairs={{0,16},{1,17},{2,18},{3,19},{4,20},{5,21},{6,22},{7,23},{8,24},{9,... | collective-permute-start | bytes 774152 | tf_op jit(solution)/shard_map/ppermute | solution.py:510
  77.9 5.9 %collective-permute-done.16 = bf16[336,384]{1,0:T(8,128)(2,1)S(1)} collective-permute-done((bf16[336,384]{1,0:T(8,128)(2,1)S(1)}, bf16[336,384]{1,0:T(8,128)(2,1)S(1)}, u32[]{:S(2)}, u32[]{:S(2)}) %collective-permute-start.16) | collective-permute-done | bytes 258080 | tf_op jit(solution)/shard_map/ppermute | solution.py:510
  83.8 1.7 collective-permute-done.17
  85.5 1.3 maximum_select_fusion.refs_0_.refs_1_
  86.8 19.5 %shard_map.154 = (bf16[336,384]{1,0:T(8,128)(2,1)S(1)}, bf16[672,384]{1,0:T(8,128)(2,1)S(1)}, f32[336,384]{1,0:T(8,128)S(1)}, bf16[3,336,128]{2,1,0:T(8,128)(2,1...) custom-call(bf16[672,384]{1,0:T(8,128)(2,1)S(1)} %maximum_select_fus, ...), custom_call_target="tpu_custom_call" | custom-call | flops 4000000000 | bytes 4000000 | tf_op jit(solution)/shard_map/pallas_call | solution.py:344
  106.6 1.4 collective-permute-done.18
  108.1 1.5 collective-permute-start.19
  109.6 8.8 %collective-permute-done.19 = bf16[336,384]{1,0:T(8,128)(2,1)S(1)} collective-permute-done((bf16[336,384]{1,0:T(8,128)(2,1)S(1)}, bf16[336,384]{1,0:T(8,128)(2,1)S(1)}, u32[]{:S(2)}, u32[]{:S(2)}) %collective-permute-start.19) | collective-permute-done | bytes 258080 | tf_op jit(solution)/shard_map/ppermute | solution.py:510
  118.4 6.5 %shard_map.155 = (f32[336,384]{1,0:T(8,128)S(1)}, f32[16,384]{1,0:T(8,128)S(1)}, bf16[2,768,384]{2,1,0:T(8,128)(2,1)S(1)}, bf16[2,768,384]{2,1,0:T(8,128)(2,1)S(1)}) custom-call(s32[3]{0:T(128)S(1)} %pad_add_fusion.1.refs_0_, f32[336,384]{1,0:T(8,128)S(1)} %get-tuple-element.42.refs_1_, f32[672,1]{1,0:T(8,128)S(1)} %concatenate.48.refs_2_.refs_1_, ...), custom_call_target="tpu_custom_call" | custom-call | flops 2000000000 | bytes 4000000 | tf_op jit(solution)/shard_map/pallas_call | solution.py:344
  124.9 10.4 %shard_map.156 = (bf16[672,384]{1,0:T(8,128)(2,1)S(1)}, bf16[2,400,384]{2,1,0:T(8,128)(2,1)S(1)}, bf16[2,400,384]{2,1,0:T(8,128)(2,1)}) custom-call(s32[3]{0:T(128)S(1)} %pad_add_fusion.1.refs_0_, bf16[672,384]{1,0:T(8,128)(2,1)S(1)} %maximum_select_fusion.refs_0_.refs_1_, f32[672,1]{1,0:T(8,128)S(1)} %concatenate.48.refs_2_.refs_1_, ...), custom_call_target="tpu_custom_call" | custom-call | flops 2000000000 | bytes 4000000 | tf_op jit(solution)/shard_map/pallas_call | solution.py:344
  135.4 0.8 copy-done
  136.9 0.9 collective-permute-done.20
  137.8 1.1 fusion.4
  138.9 0.7 collective-permute-start.21
  139.6 3.1 %collective-permute-start.22 = (bf16[168,384]{1,0:T(8,128)(2,1)S(1)}, bf16[168,384]{1,0:T(8,128)(2,1)S(1)}, u32[]{:S(2)}, u32[]{:S(2)}) collective-permute-start(bf16[168,384]{1,0:T(8,128)(2,1)S(1)} %get-tuple-element.97), channel_id=1, source_target_pairs={{2,0},{0,1},{6,2},{4,3},{3,4},{1,5},{7,6},{5,7},{10,8},{8,9},{14,1... | collective-permute-start | bytes 387080 | tf_op jit(solution)/shard_map/ppermute | solution.py:379
  142.6 1.0 fusion.1
  143.7 1.6 collective-permute-start.24
  145.3 4.0 %collective-permute-done.22 = bf16[168,384]{1,0:T(8,128)(2,1)S(1)} collective-permute-done((bf16[168,384]{1,0:T(8,128)(2,1)S(1)}, bf16[168,384]{1,0:T(8,128)(2,1)S(1)}, u32[]{:S(2)}, u32[]{:S(2)}) %collective-permute-start.22) | collective-permute-done | bytes 129056 | tf_op jit(solution)/shard_map/ppermute | solution.py:379
  149.3 0.7 maximum_bitcast_fusion
  150.0 3.3 %collective-permute-done.24 = bf16[400,384]{1,0:T(8,128)(2,1)S(1)} collective-permute-done((bf16[400,384]{1,0:T(8,128)(2,1)S(1)}, bf16[400,384]{1,0:T(8,128)(2,1)S(1)}, u32[]{:S(2)}, u32[]{:S(2)}) %collective-permute-start.24) | collective-permute-done | bytes 307232 | tf_op jit(solution)/shard_map/ppermute | solution.py:368
  153.3 1.1 fusion.11
  154.7 1.9 %collective-permute-start.25 = (bf16[112,384]{1,0:T(8,128)(2,1)S(1)}, bf16[112,384]{1,0:T(8,128)(2,1)S(1)}, u32[]{:S(2)}, u32[]{:S(2)}) collective-permute-start(bf16[112,384]{1,0:T(8,128)(2,1)S(1)} %get-tuple-element.105), channel_id=1, source_target_pairs={{0,1},{1,2},{2,3},{3,0},{4,5},{5,6},{6,7},{7,4},{8,9},{9,10},{10,1... | collective-permute-start | bytes 258056 | tf_op jit(solution)/shard_map/ppermute | solution.py:373
  156.7 1.0 fusion
  157.7 1.5 collective-permute-start.29
  159.6 3.8 %collective-permute-done.26 = bf16[112,384]{1,0:T(8,128)(2,1)S(1)} collective-permute-done((bf16[112,384]{1,0:T(8,128)(2,1)S(1)}, bf16[112,384]{1,0:T(8,128)(2,1)S(1)}, u32[]{:S(2)}, u32[]{:S(2)}) %collective-permute-start.26) | collective-permute-done | bytes 86048 | tf_op jit(solution)/shard_map/ppermute | solution.py:373
  163.6 0.7 broadcast_in_dim_reshape.6
  166.8 5.5 %collective-permute-done.29 = bf16[768,384]{1,0:T(8,128)(2,1)} collective-permute-done((bf16[768,384]{1,0:T(8,128)(2,1)}, bf16[768,384]{1,0:T(8,128)(2,1)}, u32[]{:S(2)}, u32[]{:S(2)}) %collective-permute-start.29) | collective-permute-done | bytes 589856 | tf_op jit(solution)/shard_map/ppermute | solution.py:368
  172.2 1.3 fusion.10
  173.8 2.4 %collective-permute-start.32 = (bf16[192,384]{1,0:T(8,128)(2,1)S(1)}, bf16[192,384]{1,0:T(8,128)(2,1)S(1)}, u32[]{:S(2)}, u32[]{:S(2)}) collective-permute-start(bf16[192,384]{1,0:T(8,128)(2,1)S(1)} %pad_maximum_fusion.7), channel_id=1, source_target_pairs={{0,3},{1,0},{2,1},{3,2},{4,7},{5,4},{6,5},{7,6},{8,11},{9,8},{10,9... | collective-permute-start | bytes 442376 | tf_op jit(solution)/shard_map/ppermute | solution.py:373
  176.3 0.7 collective-permute-start.31
  177.0 1.7 collective-permute-start.30
  178.8 1.8 collective-permute-done.32
  180.6 8.1 %collective-permute-done.31 = bf16[192,384]{1,0:T(8,128)(2,1)S(1)} collective-permute-done((bf16[192,384]{1,0:T(8,128)(2,1)S(1)}, bf16[192,384]{1,0:T(8,128)(2,1)S(1)}, u32[]{:S(2)}, u32[]{:S(2)}) %collective-permute-start.31) | collective-permute-done | bytes 147488 | tf_op jit(solution)/shard_map/ppermute | solution.py:373
  188.8 0.7 slice_bitcast_fusion
  189.5 0.7 broadcast_in_dim_reshape.7
  (131 shorter events, 9.2 us)
Async XLA Ops:
  0.6 14.5 %copy-start.21 = (s32[2,1,4]{2,1,0:T(1,128)S(1)}, s32[2,1,4]{2,1,0:T(1,128)}, u32[]{:S(2)}) copy-start(s32[2,1,4]{2,1,0:T(1,128)} %param.10) | copy-start | bytes 100
  0.6 14.5 %copy-start.20 = (bf16[1,2,1,168,384]{4,3,2,1,0:T(8,128)(2,1)S(1)}, bf16[1,2,1,168,384]{4,3,2,1,0:T(8,128)(2,1)}, u32[]{:S(2)}) copy-start(bf16[1,2,1,168,384]{4,3,2,1,0:T(8,128)(2,1)} %param.9) | copy-start | bytes 774148
  5.1 28.0 %collective-permute-start.6 = (bf16[112,384]{1,0:T(8,128)(2,1)S(1)}, bf16[112,384]{1,0:T(8,128)(2,1)S(1)}, u32[]{:S(2)}, u32[]{:S(2)}) collective-permute-start(bf16[112,384]{1,0:T(8,128)(2,1)S(1)} %concatenate.49), channel_id=1, source_target_pairs={{0,3},{1,0},{2,1},{3,2},{4,7},{5,4},{6,5},{7,6},{8,11},{9,8},{10,9... | collective-permute-start | bytes 258056 | tf_op jit(solution)/shard_map/ppermute | solution.py:373
  10.2 26.4 %collective-permute-start.5 = (bf16[112,384]{1,0:T(8,128)(2,1)S(1)}, bf16[112,384]{1,0:T(8,128)(2,1)S(1)}, u32[]{:S(2)}, u32[]{:S(2)}) collective-permute-start(bf16[112,384]{1,0:T(8,128)(2,1)S(1)} %concatenate.49), channel_id=1, source_target_pairs={{0,2},{1,3},{2,0},{3,1},{4,6},{5,7},{6,4},{7,5},{8,10},{9,11},{10,... | collective-permute-start | bytes 258056 | tf_op jit(solution)/shard_map/ppermute | solution.py:373
  12.1 6.8 %collective-permute-start.12 = (bf16[192,384]{1,0:T(8,128)(2,1)S(1)}, bf16[192,384]{1,0:T(8,128)(2,1)S(1)}, u32[]{:S(2)}, u32[]{:S(2)}) collective-permute-start(bf16[192,384]{1,0:T(8,128)(2,1)S(1)} %get-tuple-element.104), channel_id=1, source_target_pairs={{0,3},{1,0},{2,1},{3,2},{4,7},{5,4},{6,5},{7,6},{8,11},{9,8},{10,9... | collective-permute-start | bytes 442376 | tf_op jit(solution)/shard_map/ppermute | solution.py:373
  12.6 18.2 %collective-permute-start.11 = (bf16[192,384]{1,0:T(8,128)(2,1)S(1)}, bf16[192,384]{1,0:T(8,128)(2,1)S(1)}, u32[]{:S(2)}, u32[]{:S(2)}) collective-permute-start(bf16[192,384]{1,0:T(8,128)(2,1)S(1)} %get-tuple-element.104), channel_id=1, source_target_pairs={{0,2},{1,3},{2,0},{3,1},{4,6},{5,7},{6,4},{7,5},{8,10},{9,11},{10,... | collective-permute-start | bytes 442376 | tf_op jit(solution)/shard_map/ppermute | solution.py:373
  15.1 1.1 collective-permute-start.3
  16.2 15.1 %collective-permute-start.10 = (bf16[192,384]{1,0:T(8,128)(2,1)S(1)}, bf16[192,384]{1,0:T(8,128)(2,1)S(1)}, u32[]{:S(2)}, u32[]{:S(2)}) collective-permute-start(bf16[192,384]{1,0:T(8,128)(2,1)S(1)} %get-tuple-element.104), channel_id=1, source_target_pairs={{0,1},{1,2},{2,3},{3,0},{4,5},{5,6},{6,7},{7,4},{8,9},{9,10},{10,1... | collective-permute-start | bytes 442376 | tf_op jit(solution)/shard_map/ppermute | solution.py:373
  18.9 17.8 %collective-permute-start.4 = (bf16[112,384]{1,0:T(8,128)(2,1)S(1)}, bf16[112,384]{1,0:T(8,128)(2,1)S(1)}, u32[]{:S(2)}, u32[]{:S(2)}) collective-permute-start(bf16[112,384]{1,0:T(8,128)(2,1)S(1)} %concatenate.49), channel_id=1, source_target_pairs={{0,1},{1,2},{2,3},{3,0},{4,5},{5,6},{6,7},{7,4},{8,9},{9,10},{10,1... | collective-permute-start | bytes 258056 | tf_op jit(solution)/shard_map/ppermute | solution.py:373
  30.7 6.6 %collective-permute-start = (bf16[168,384]{1,0:T(8,128)(2,1)S(1)}, bf16[168,384]{1,0:T(8,128)(2,1)S(1)}, u32[]{:S(2)}, u32[]{:S(2)}) collective-permute-start(bf16[168,384]{1,0:T(8,128)(2,1)S(1)} %get-tuple-element.101), channel_id=1, source_target_pairs={{0,0},{1,2},{2,4},{3,6},{4,1},{5,3},{6,5},{7,7},{8,8},{9,10},{10,1... | collective-permute-start | bytes 387080 | tf_op jit(solution)/shard_map/ppermute | solution.py:379
  31.5 16.4 %collective-permute-start.13 = (bf16[4,192,384]{2,1,0:T(8,128)(2,1)S(1)}, bf16[4,192,384]{2,1,0:T(8,128)(2,1)}, u32[]{:S(2)}, u32[]{:S(2)}) collective-permute-start(bf16[4,192,384]{2,1,0:T(8,128)(2,1)S(1)} %pad_maximum_fusion.refs_4_), channel_id=1, source_target_pairs={{0,8},{4,12},{8,0},{12,4},{1,9},{5,13},{9,1},{13,5},{2,10},{6,14},... | collective-permute-start | bytes 1769480 | tf_op jit(solution)/shard_map/ppermute | solution.py:368
  33.1 6.0 %collective-permute-start.1 = (bf16[168,384]{1,0:T(8,128)(2,1)S(1)}, bf16[168,384]{1,0:T(8,128)(2,1)S(1)}, u32[]{:S(2)}, u32[]{:S(2)}) collective-permute-start(bf16[168,384]{1,0:T(8,128)(2,1)S(1)} %get-tuple-element.102), channel_id=1, source_target_pairs={{0,2},{1,0},{2,6},{3,4},{4,3},{5,1},{6,7},{7,5},{8,10},{9,8},{10,1... | collective-permute-start | bytes 387080 | tf_op jit(solution)/shard_map/ppermute | solution.py:379
  36.7 19.1 %copy-start.1 = (bf16[4,112,384]{2,1,0:T(8,128)(2,1)}, bf16[4,112,384]{2,1,0:T(8,128)(2,1)S(1)}, u32[]{:S(2)}) copy-start(bf16[4,112,384]{2,1,0:T(8,128)(2,1)S(1)} %pad_maximum_fusion.2.refs_3_) | copy-start | bytes 1032196
  36.7 18.4 %collective-permute-start.7 = (bf16[4,112,384]{2,1,0:T(8,128)(2,1)S(1)}, bf16[4,112,384]{2,1,0:T(8,128)(2,1)S(1)}, u32[]{:S(2)}, u32[]{:S(2)}) collective-permute-start(bf16[4,112,384]{2,1,0:T(8,128)(2,1)S(1)} %pad_maximum_fusion.2.refs_3_), channel_id=1, source_target_pairs={{0,8},{4,12},{8,0},{12,4},{1,9},{5,13},{9,1},{13,5},{2,10},{6,14},... | collective-permute-start | bytes 1032200 | tf_op jit(solution)/shard_map/ppermute | solution.py:368
  37.3 18.5 %collective-permute-start.8 = (bf16[4,112,384]{2,1,0:T(8,128)(2,1)S(1)}, bf16[4,112,384]{2,1,0:T(8,128)(2,1)S(1)}, u32[]{:S(2)}, u32[]{:S(2)}) collective-permute-start(bf16[4,112,384]{2,1,0:T(8,128)(2,1)S(1)} %pad_maximum_fusion.2.refs_3_), channel_id=1, source_target_pairs={{0,4},{4,0},{8,12},{12,8},{1,5},{5,1},{9,13},{13,9},{2,6},{6,2},{1... | collective-permute-start | bytes 1032200 | tf_op jit(solution)/shard_map/ppermute | solution.py:363
  39.1 16.8 %copy-start.17 = (bf16[168,384]{1,0:T(8,128)(2,1)}, bf16[168,384]{1,0:T(8,128)(2,1)S(1)}, u32[]{:S(2)}) copy-start(bf16[168,384]{1,0:T(8,128)(2,1)S(1)} %get-tuple-element.100) | copy-start | bytes 387076
  39.1 29.6 %collective-permute-start.14 = (bf16[4,192,384]{2,1,0:T(8,128)(2,1)S(1)}, bf16[4,192,384]{2,1,0:T(8,128)(2,1)}, u32[]{:S(2)}, u32[]{:S(2)}) collective-permute-start(bf16[4,192,384]{2,1,0:T(8,128)(2,1)S(1)} %pad_maximum_fusion.refs_4_), channel_id=1, source_target_pairs={{0,4},{4,0},{8,12},{12,8},{1,5},{5,1},{9,13},{13,9},{2,6},{6,2},{1... | collective-permute-start | bytes 1769480 | tf_op jit(solution)/shard_map/ppermute | solution.py:363
  47.9 20.8 %collective-permute-start.15 = (bf16[4,192,384]{2,1,0:T(8,128)(2,1)}, bf16[4,192,384]{2,1,0:T(8,128)(2,1)}, u32[]{:S(2)}, u32[]{:S(2)}) collective-permute-start(bf16[4,192,384]{2,1,0:T(8,128)(2,1)} %collective-permute-done.13.refs_5_), channel_id=1, source_target_pairs={{0,4},{4,0},{8,12},{12,8},{1,5},{5,1},{9,13},{13,9},{2,6},{6,2},{1... | collective-permute-start | bytes 1769480 | tf_op jit(solution)/shard_map/ppermute | solution.py:363
  47.9 7.8 %copy-start.4 = (bf16[336,384]{1,0:T(8,128)(2,1)}, bf16[336,384]{1,0:T(8,128)(2,1)S(1)}, u32[]{:S(2)}) copy-start(bf16[336,384]{1,0:T(8,128)(2,1)S(1)} %pad_maximum_fusion.3.refs_2_) | copy-start | bytes 774148
  47.9 7.8 %collective-permute-start.2 = (bf16[336,384]{1,0:T(8,128)(2,1)S(1)}, bf16[336,384]{1,0:T(8,128)(2,1)S(1)}, u32[]{:S(2)}, u32[]{:S(2)}) collective-permute-start(bf16[336,384]{1,0:T(8,128)(2,1)S(1)} %pad_maximum_fusion.3.refs_2_), channel_id=1, source_target_pairs={{4,0},{5,1},{6,2},{7,3},{0,4},{1,5},{2,6},{3,7},{12,8},{13,9},{14,... | collective-permute-start | bytes 774152 | tf_op jit(solution)/shard_map/ppermute | solution.py:379
  55.1 0.8 copy-start.7
  55.1 2.1 %collective-permute-start.9 = (bf16[4,112,384]{2,1,0:T(8,128)(2,1)S(1)}, bf16[4,112,384]{2,1,0:T(8,128)(2,1)S(1)}, u32[]{:S(2)}, u32[]{:S(2)}) collective-permute-start(bf16[4,112,384]{2,1,0:T(8,128)(2,1)S(1)} %collective-permute-done.7.refs_4_), channel_id=1, source_target_pairs={{0,4},{4,0},{8,12},{12,8},{1,5},{5,1},{9,13},{13,9},{2,6},{6,2},{1... | collective-permute-start | bytes 1032200 | tf_op jit(solution)/shard_map/ppermute | solution.py:363
  55.8 0.7 copy-start.19
  56.5 0.7 copy-start.9
  57.2 0.7 copy-start.11
  57.9 1.0 copy-start.2
  58.9 1.0 copy-start.8
  59.9 1.0 copy-start.10
  60.8 1.0 copy-start.12
  73.1 1.1 copy-start.15
  74.2 32.1 %copy-start.13 = (bf16[4,384,384]{2,1,0:T(8,128)(2,1)}, bf16[4,384,384]{2,1,0:T(8,128)(2,1)S(1)}, u32[]{:S(2)}) copy-start(bf16[4,384,384]{2,1,0:T(8,128)(2,1)S(1)} %get-tuple-element.34.refs_4_) | copy-start | bytes 3538948
  74.2 12.6 %copy-start.5 = (bf16[336,384]{1,0:T(8,128)(2,1)S(1)}, bf16[336,384]{1,0:T(8,128)(2,1)}, u32[]{:S(2)}) copy-start(bf16[336,384]{1,0:T(8,128)(2,1)} %copy-done.4) | copy-start | bytes 774148
  74.2 9.6 %collective-permute-start.16 = (bf16[336,384]{1,0:T(8,128)(2,1)S(1)}, bf16[336,384]{1,0:T(8,128)(2,1)S(1)}, u32[]{:S(2)}, u32[]{:S(2)}) collective-permute-start(bf16[336,384]{1,0:T(8,128)(2,1)S(1)} %get-tuple-element.32), channel_id=1, source_target_pairs={{0,16},{1,17},{2,18},{3,19},{4,20},{5,21},{6,22},{7,23},{8,24},{9,... | collective-permute-start | bytes 774152 | tf_op jit(solution)/shard_map/ppermute | solution.py:510
  83.8 1.7 collective-permute-start.17
  83.8 3.0 %copy-start.16 = (bf16[1536,384]{1,0:T(8,128)(2,1)S(1)}, bf16[1536,384]{1,0:T(8,128)(2,1)}, u32[]{:S(2)}) copy-start(bf16[1536,384]{1,0:T(8,128)(2,1)} %copy-done.15) | copy-start | bytes 3538948
  106.3 12.1 %copy-start.3 = (bf16[336,384]{1,0:T(8,128)(2,1)}, bf16[336,384]{1,0:T(8,128)(2,1)S(1)}, u32[]{:S(2)}) copy-start(bf16[336,384]{1,0:T(8,128)(2,1)S(1)} %get-tuple-element.47) | copy-start | bytes 774148
  106.3 12.0 %copy-start.18 = (bf16[168,384]{1,0:T(8,128)(2,1)S(1)}, bf16[168,384]{1,0:T(8,128)(2,1)}, u32[]{:S(2)}) copy-start(bf16[168,384]{1,0:T(8,128)(2,1)} %copy-done.17) | copy-start | bytes 387076
  106.3 12.1 %copy-start.14 = (bf16[4,384,384]{2,1,0:T(8,128)(2,1)S(1)}, bf16[4,384,384]{2,1,0:T(8,128)(2,1)}, u32[]{:S(2)}) copy-start(bf16[4,384,384]{2,1,0:T(8,128)(2,1)} %copy-done.13) | copy-start | bytes 3538948
  106.4 1.6 collective-permute-start.18
  108.1 10.3 %collective-permute-start.19 = (bf16[336,384]{1,0:T(8,128)(2,1)S(1)}, bf16[336,384]{1,0:T(8,128)(2,1)S(1)}, u32[]{:S(2)}, u32[]{:S(2)}) collective-permute-start(bf16[336,384]{1,0:T(8,128)(2,1)S(1)} %add_convert_fusion.3), channel_id=1, source_target_pairs={{16,0},{17,1},{18,2},{19,3},{20,4},{21,5},{22,6},{23,7},{24,8},{25... | collective-permute-start | bytes 774152 | tf_op jit(solution)/shard_map/ppermute | solution.py:510
  124.9 10.5 %copy-start.6 = (bf16[2,768,384]{2,1,0:T(8,128)(2,1)}, bf16[2,768,384]{2,1,0:T(8,128)(2,1)S(1)}, u32[]{:S(2)}) copy-start(bf16[2,768,384]{2,1,0:T(8,128)(2,1)S(1)} %get-tuple-element.51) | copy-start | bytes 3538948
  135.4 0.8 copy-start
  136.2 1.6 collective-permute-start.20
  136.3 6.4 %collective-permute-start.23 = (bf16[2,400,384]{2,1,0:T(8,128)(2,1)}, bf16[2,400,384]{2,1,0:T(8,128)(2,1)}, u32[]{:S(2)}, u32[]{:S(2)}) collective-permute-start(bf16[2,400,384]{2,1,0:T(8,128)(2,1)} %get-tuple-element.49), channel_id=1, source_target_pairs={{0,4},{4,0},{8,12},{12,8},{1,5},{5,1},{9,13},{13,9},{2,6},{6,2},{1... | collective-permute-start | bytes 1843208 | tf_op jit(solution)/shard_map/ppermute | solution.py:363
  136.8 19.9 %collective-permute-start.28 = (bf16[2,768,384]{2,1,0:T(8,128)(2,1)}, bf16[2,768,384]{2,1,0:T(8,128)(2,1)S(1)}, u32[]{:S(2)}, u32[]{:S(2)}) collective-permute-start(bf16[2,768,384]{2,1,0:T(8,128)(2,1)} %copy-done.6), channel_id=1, source_target_pairs={{0,4},{4,0},{8,12},{12,8},{1,5},{5,1},{9,13},{13,9},{2,6},{6,2},{1... | collective-permute-start | bytes 3538952 | tf_op jit(solution)/shard_map/ppermute | solution.py:363
  138.9 6.4 %collective-permute-start.21 = (bf16[168,384]{1,0:T(8,128)(2,1)S(1)}, bf16[168,384]{1,0:T(8,128)(2,1)S(1)}, u32[]{:S(2)}, u32[]{:S(2)}) collective-permute-start(bf16[168,384]{1,0:T(8,128)(2,1)S(1)} %get-tuple-element.98), channel_id=1, source_target_pairs={{0,0},{2,1},{4,2},{6,3},{1,4},{3,5},{5,6},{7,7},{8,8},{10,9},{12,1... | collective-permute-start | bytes 387080 | tf_op jit(solution)/shard_map/ppermute | solution.py:379
  139.6 9.7 %collective-permute-start.22 = (bf16[168,384]{1,0:T(8,128)(2,1)S(1)}, bf16[168,384]{1,0:T(8,128)(2,1)S(1)}, u32[]{:S(2)}, u32[]{:S(2)}) collective-permute-start(bf16[168,384]{1,0:T(8,128)(2,1)S(1)} %get-tuple-element.97), channel_id=1, source_target_pairs={{2,0},{0,1},{6,2},{4,3},{3,4},{1,5},{7,6},{5,7},{10,8},{8,9},{14,1... | collective-permute-start | bytes 387080 | tf_op jit(solution)/shard_map/ppermute | solution.py:379
  143.7 9.6 %collective-permute-start.24 = (bf16[400,384]{1,0:T(8,128)(2,1)S(1)}, bf16[400,384]{1,0:T(8,128)(2,1)S(1)}, u32[]{:S(2)}, u32[]{:S(2)}) collective-permute-start(bf16[400,384]{1,0:T(8,128)(2,1)S(1)} %fusion.1), channel_id=1, source_target_pairs={{0,8},{4,12},{8,0},{12,4},{1,9},{5,13},{9,1},{13,5},{2,10},{6,14},... | collective-permute-start | bytes 921608 | tf_op jit(solution)/shard_map/ppermute | solution.py:368
  154.6 5.1 %collective-permute-start.27 = (bf16[112,384]{1,0:T(8,128)(2,1)S(1)}, bf16[112,384]{1,0:T(8,128)(2,1)S(1)}, u32[]{:S(2)}, u32[]{:S(2)}) collective-permute-start(bf16[112,384]{1,0:T(8,128)(2,1)S(1)} %get-tuple-element.107), channel_id=1, source_target_pairs={{0,3},{1,0},{2,1},{3,2},{4,7},{5,4},{6,5},{7,6},{8,11},{9,8},{10,9... | collective-permute-start | bytes 258056 | tf_op jit(solution)/shard_map/ppermute | solution.py:373
  154.6 8.8 %collective-permute-start.26 = (bf16[112,384]{1,0:T(8,128)(2,1)S(1)}, bf16[112,384]{1,0:T(8,128)(2,1)S(1)}, u32[]{:S(2)}, u32[]{:S(2)}) collective-permute-start(bf16[112,384]{1,0:T(8,128)(2,1)S(1)} %get-tuple-element.106), channel_id=1, source_target_pairs={{0,2},{1,3},{2,0},{3,1},{4,6},{5,7},{6,4},{7,5},{8,10},{9,11},{10,... | collective-permute-start | bytes 258056 | tf_op jit(solution)/shard_map/ppermute | solution.py:373
  154.7 8.8 %collective-permute-start.25 = (bf16[112,384]{1,0:T(8,128)(2,1)S(1)}, bf16[112,384]{1,0:T(8,128)(2,1)S(1)}, u32[]{:S(2)}, u32[]{:S(2)}) collective-permute-start(bf16[112,384]{1,0:T(8,128)(2,1)S(1)} %get-tuple-element.105), channel_id=1, source_target_pairs={{0,1},{1,2},{2,3},{3,0},{4,5},{5,6},{6,7},{7,4},{8,9},{9,10},{10,1... | collective-permute-start | bytes 258056 | tf_op jit(solution)/shard_map/ppermute | solution.py:373
  157.7 14.6 %collective-permute-start.29 = (bf16[768,384]{1,0:T(8,128)(2,1)}, bf16[768,384]{1,0:T(8,128)(2,1)}, u32[]{:S(2)}, u32[]{:S(2)}) collective-permute-start(bf16[768,384]{1,0:T(8,128)(2,1)} %fusion), channel_id=1, source_target_pairs={{0,8},{4,12},{8,0},{12,4},{1,9},{5,13},{9,1},{13,5},{2,10},{6,14},... | collective-permute-start | bytes 1769480 | tf_op jit(solution)/shard_map/ppermute | solution.py:368
  173.8 6.7 %collective-permute-start.32 = (bf16[192,384]{1,0:T(8,128)(2,1)S(1)}, bf16[192,384]{1,0:T(8,128)(2,1)S(1)}, u32[]{:S(2)}, u32[]{:S(2)}) collective-permute-start(bf16[192,384]{1,0:T(8,128)(2,1)S(1)} %pad_maximum_fusion.7), channel_id=1, source_target_pairs={{0,3},{1,0},{2,1},{3,2},{4,7},{5,4},{6,5},{7,6},{8,11},{9,8},{10,9... | collective-permute-start | bytes 442376 | tf_op jit(solution)/shard_map/ppermute | solution.py:373
  176.3 12.4 %collective-permute-start.31 = (bf16[192,384]{1,0:T(8,128)(2,1)S(1)}, bf16[192,384]{1,0:T(8,128)(2,1)S(1)}, u32[]{:S(2)}, u32[]{:S(2)}) collective-permute-start(bf16[192,384]{1,0:T(8,128)(2,1)S(1)} %pad_maximum_fusion.6), channel_id=1, source_target_pairs={{0,2},{1,3},{2,0},{3,1},{4,6},{5,7},{6,4},{7,5},{8,10},{9,11},{10,... | collective-permute-start | bytes 442376 | tf_op jit(solution)/shard_map/ppermute | solution.py:373
  177.0 11.7 %collective-permute-start.30 = (bf16[192,384]{1,0:T(8,128)(2,1)S(1)}, bf16[192,384]{1,0:T(8,128)(2,1)S(1)}, u32[]{:S(2)}, u32[]{:S(2)}) collective-permute-start(bf16[192,384]{1,0:T(8,128)(2,1)S(1)} %pad_maximum_fusion.5), channel_id=1, source_target_pairs={{0,1},{1,2},{2,3},{3,0},{4,5},{5,6},{6,7},{7,4},{8,9},{9,10},{10,1... | collective-permute-start | bytes 442376 | tf_op jit(solution)/shard_map/ppermute | solution.py:373

commit v3 on v2

--- a/solution.py
+++ b/solution.py
@@ -57,7 +57,7 @@
     width = x_ref.shape[1]
     pairs = k_s.shape[0]
     head_dim = width // HEADS
-    mask = mask_ref[...]
+    mask = mask_ref[:, :1]
     masked = x_ref[...].astype(F32) * mask
     unit, _ = norm_parts(masked)
     normed = (unit * row_of(vec_ref, 0) + row_of(vec_ref, 2)).astype(BF16)
@@ -75,9 +75,8 @@
             kt_s[j] = keys[:, lanes].T
     halves = head_halves(head_dim)
 
-    @pl.loop(0, pairs)
-    def _(j):
-        bias = (mask_ref[...] - 1.0) * 1e30
+    for j in range(pairs):
+        bias = (mask_ref[:, :1] - 1.0) * 1e30
         for e in range(2):
             score = mul(k_s[j], q_s[j] * halves[e], 1, 1) + bias
             top = jnp.max(score, axis=0, keepdims=True)
@@ -108,7 +107,7 @@
         acc_s[...] += mul(active, w2_ref[rows, :])
 
     y_ref[...] = (
-        (mid_ref[...] + acc_s[...] + row_of(vec_ref, 7)) * mask_ref[:own, :]
+        (mid_ref[...] + acc_s[...] + row_of(vec_ref, 7)) * mask_ref[:own, :1]
     ).astype(BF16)
 
 
@@ -127,7 +126,7 @@
             hidden = h_s[k]
         cdf = gelu_cdf(hidden)
         slope = cdf + hidden * jnp.exp(-0.5 * hidden * hidden) * (1.0 / math.sqrt(2 * math.pi))
-        grad_second = (dy_ref[...].astype(F32) * mask_ref[:own, :]).astype(BF16)
+        grad_second = (dy_ref[...].astype(F32) * mask_ref[:own, :1]).astype(BF16)
         rows = pl.ds(pl.multiple_of(k * width, 128), width)
         grad_hidden = (mul(grad_second, w2_ref[rows, :], 1, 1) * slope).astype(BF16)
         acc_s[...] += mul(grad_hidden, w1_ref[k], 1, 1)
@@ -137,7 +136,7 @@
             g2_s[rows, :] = mul(active, grad_second, 0, 0).astype(BF16)
             gv_ref[pl.ds(8 + k, 1), :] = total_of(grad_hidden.astype(F32))
 
-    grad_y = dy_ref[...].astype(F32) * mask_ref[:own, :]
+    grad_y = dy_ref[...].astype(F32) * mask_ref[:own, :1]
     grad_c = acc_s[...]
     unit, scale = norm_parts(mid_ref[...])
     grad_mid = grad_y + norm_grad(grad_c, row_of(vec_ref, 1), unit, scale)
@@ -153,7 +152,7 @@
     q_s, k_s, v_s, ot_s, kt_s, p_s = kept
     do_s, dq_s, dk_s, dv_s = scratch
     own, width = gmid_ref.shape
-    pairs = k_s.shape[0]
+    pairs = do_s.shape[0]
     head_dim = width // HEADS
     grad_branch = gmid_ref[...].astype(BF16)
     grad_att = mul(grad_branch, wa_ref[3], 1, 1).astype(BF16)
@@ -165,8 +164,7 @@
             ga_s[3, j * 128 : (j + 1) * 128, :] = mul(ot_s[j], grad_branch).astype(BF16)
     halves = head_halves(head_dim)
 
-    @pl.loop(0, pairs)
-    def _(j):
+    for j in range(pairs):
         grad_k = None
         for e in range(2):
             half_do = do_s[j] * halves[e]
@@ -187,7 +185,7 @@
     grad_q = jnp.concatenate([dq_s[j].T for j in range(pairs)], axis=1)
     grad_k = jnp.concatenate([dk_s[j] for j in range(pairs)], axis=1)
     grad_v = jnp.concatenate([dv_s[j] for j in range(pairs)], axis=1)
-    mask = mask_ref[...]
+    mask = mask_ref[:, :1]
     unit, scale = norm_parts(x_ref[...].astype(F32) * mask)
     if grads is not None:
         normed = (unit * row_of(vec_ref, 0) + row_of(vec_ref, 2)).astype(BF16)
@@ -207,6 +205,34 @@
     du_ref[...] = (grad_u * mask).astype(BF16)
 
 
+def pack_kernel(place_ref, qkv_ref, out_ref, fc1_ref, fc2_ref, gains_ref, shifts_ref, bias_ref, a_ref, b_ref):
+    rows, width = out_ref.shape
+    index = place_ref[3]
+
+    def columns(ref, count):
+        wide = ref[...].astype(F32)
+        return [wide[:, s * width : (s + 1) * width] for s in range(count)]
+
+    lane = lax.broadcasted_iota(jnp.int32, (1, width), 1)
+    row = lax.broadcasted_iota(jnp.int32, (16, width), 0)
+    tail, base = jnp.zeros((16, width), F32), 0
+    for ref, used in ((gains_ref, 2), (shifts_ref, 6), (bias_ref, 4)):
+        length = ref.shape[1]
+        start = index * length
+        first, offset = start // width, lax.rem(start, width)
+        spread = jnp.concatenate(
+            [ref[...].astype(F32), jnp.zeros((1, width - length), F32)], axis=1
+        )
+        spread = pltpu.roll(jnp.broadcast_to(spread, (8, width)), offset, 1)[:1]
+        target = base + first + jnp.where(lane < offset, 1, 0)
+        tail = tail + jnp.where(row == target, spread, 0.0)
+        base += used
+    blocks = columns(qkv_ref, 3) + [out_ref[...].astype(F32), tail]
+    a_ref[...] = jnp.concatenate(blocks, axis=0).astype(BF16)
+    blocks = columns(fc1_ref, 4) + [fc2_ref[...].astype(F32)]
+    b_ref[...] = jnp.concatenate(blocks, axis=0).astype(BF16)
+
+
 def piece_groups(place_ref, mine, theirs):
     outer, core, line = place_ref[0], place_ref[1], place_ref[2]
     count = mine[0].shape[0]
@@ -219,15 +245,12 @@
             yield index, blocks
 
 
-def first_kernel(loose, rows, *refs):
-    refs = list(refs)
-    place_ref, x_ref, mask_ref = refs[:3]
-    refs = refs[3:]
+def first_kernel(loose, rows, ins, outs, scratch):
+    place_ref, x_ref, mask_ref = ins[:3]
     if loose:
-        mine, theirs = refs[:loose], refs[loose : 2 * loose]
-        refs = refs[2 * loose :]
-        mid_ref, wa_ref, vec_ref, *scratch = refs
-        width = x_ref.shape[1]
+        mine, theirs = ins[3 : 3 + loose], ins[3 + loose :]
+        mid_ref, wa_out, vec_out = outs
+        wa_ref, vec_ref = wa_out, vec_out
         vector = None
         for index, blocks in piece_groups(place_ref, mine, theirs):
             span = rows * len(blocks)
@@ -240,18 +263,18 @@
                 vector = tail if vector is None else vector + tail
         vec_ref[...] = vector
     else:
-        wa_ref, vec_ref, mid_ref, *scratch = refs
+        wa_ref, vec_ref = (member for member in ins[3:])
+        (mid_ref,) = outs
     attend_forward(x_ref, mask_ref, wa_ref, vec_ref, (*scratch, None, None), mid_ref)
 
 
-def second_kernel(loose, rows, *refs):
-    refs = list(refs)
-    place_ref, mid_ref, mask_ref, vec_ref = refs[:4]
-    refs = refs[4:]
+def second_kernel(loose, rows, ins, outs, scratch):
+    place_ref, mid_ref = ins[:2]
+    c_s, acc_s = scratch
     if loose:
-        mine, theirs = refs[:loose], refs[loose : 2 * loose]
-        refs = refs[2 * loose :]
-        y_ref, w1_ref, w2_ref, c_s, acc_s = refs
+        mine, theirs = ins[4 : 4 + loose], ins[4 + loose :]
+        y_ref, w1_out, w2_out = outs
+        w1_ref, w2_ref = w1_out, w2_out
         for index, blocks in piece_groups(place_ref, mine, theirs):
             span = rows * len(blocks)
             start = pl.multiple_of(index * span, 16)
@@ -261,20 +284,26 @@
             group = jnp.concatenate([b[4 * rows : 8 * rows] for b in blocks], axis=0)
             w2_ref[pl.ds(pl.multiple_of(4 * start, 16), 4 * span), :] = group.astype(BF16)
     else:
-        w1_ref, w2_ref, y_ref, c_s, acc_s = refs
+        w1_ref, w2_ref = (member for member in ins[4:])
+        (y_ref,) = outs
+    mask_ref, vec_ref = ins[2], ins[3]
     feed_forward(mid_ref, mask_ref, w1_ref, w2_ref, vec_ref, c_s, acc_s, None, y_ref)
 
 
-def middle_kernel(*refs):
-    x_ref, mask_ref, dy_ref, wa_ref, w1_ref, w2_ref, vec_ref = refs[:7]
-    y_ref, du_ref, mid_ref, q_s, k_s, v_s, ot_s, kt_s, p_s = refs[7:16]
-    vt_s, c_s, acc_s, h_s, gmid_s, do_s, dq_s, dk_s, dv_s = refs[16:]
+def middle_kernel(ins, outs, scratch):
+    x_ref, mask_in, vec_in, wa_in, w1_in, w2_in, dy_in = ins
+    du_ref, y_out, mid_out, *kept = outs
+    vt_s, c_s, acc_s, h_s, gmid_s, do_s, dq_s, dk_s, dv_s = scratch
+    q_s, k_s, v_s, ot_s, kt_s, p_s = [member for member in kept]
+    mid_ref, y_ref = mid_out, y_out
+    mask_ref, vec_ref, wa_ref = mask_in, vec_in, wa_in
     attend_forward(
         x_ref, mask_ref, wa_ref, vec_ref, (q_s, k_s, v_s, vt_s, ot_s, kt_s, p_s), mid_ref
     )
+    w1_ref, w2_ref = w1_in, w2_in
     feed_forward(mid_ref, mask_ref, w1_ref, w2_ref, vec_ref, c_s, acc_s, h_s, y_ref)
     feed_backward(
-        mid_ref, mask_ref, dy_ref, w1_ref, w2_ref, vec_ref, c_s, acc_s, h_s, gmid_s, None
+        mid_ref, mask_ref, dy_in, w1_ref, w2_ref, vec_ref, c_s, acc_s, h_s, gmid_s, None
     )
     attend_backward(
         x_ref, mask_ref, wa_ref, vec_ref, (q_s, k_s, v_s, ot_s, kt_s, p_s),
@@ -289,15 +318,18 @@
         sent_ref[o, start : start + size, :] = jnp.where(core == 0, odd, even)
 
 
-def feed_grad_kernel(*refs):
-    place_ref, mid_ref, mask_ref, dy_ref, w1_ref, w2_ref, vec_ref = refs[:7]
-    gmid_ref, gv_ref, kept_ref, sent_ref = refs[7:11]
-    c_s, acc_s, g1_s, g2_s = refs[11:]
-    outer_count = kept_ref.shape[0]
-    span = w1_ref.shape[1] // (2 * outer_count)
+def feed_grad_kernel(ins, outs, scratch):
+    place_ref, dy_ref, mid_in, vec_in, mask_in, w1_in, w2_in = ins
+    kept_ref, sent_ref, gmid_out, gv_out = outs
+    c_s, acc_s, g1_s, g2_s = scratch
+    gmid_ref, gv_ref = gmid_out, gv_out
+    mid_ref, vec_ref = mid_in, vec_in
     unit, _ = norm_parts(mid_ref[...])
     c_s[...] = (unit * row_of(vec_ref, 1) + row_of(vec_ref, 3)).astype(BF16)
     gv_ref[...] = jnp.zeros_like(gv_ref)
+    mask_ref, w1_ref, w2_ref = mask_in, w1_in, w2_in
+    outer_count = kept_ref.shape[0]
+    span = w1_ref.shape[1] // (2 * outer_count)
     feed_backward(
         mid_ref, mask_ref, dy_ref, w1_ref, w2_ref, vec_ref, c_s, acc_s, None, gmid_ref,
         (g1_s, g2_s, gv_ref),
@@ -314,16 +346,16 @@
     )
 
 
-def attend_grad_kernel(*refs):
-    place_ref, x_ref, mask_ref, wa_ref, vec_ref = refs[:5]
-    q_s, k_s, v_s, ot_s, kt_s, p_s, gmid_ref, gv_in_ref = refs[5:13]
-    du_ref, kept_ref, sent_ref = refs[13:16]
-    do_s, dq_s, dk_s, dv_s, ga_s, gv_s = refs[16:]
+def attend_grad_kernel(ins, outs, scratch):
+    place_ref, gmid_in, wa_in, ot_in, v_in, q_in, kt_in, p_in, k_in, x_in, mask_in, vec_in, gv_in = ins
+    du_ref, kept_ref, sent_ref = outs
+    do_s, dq_s, dk_s, dv_s, ga_s, gv_s = scratch
+    gmid_ref, wa_ref, ot_s = gmid_in, wa_in, ot_in
     outer_count = kept_ref.shape[0]
     span = wa_ref.shape[1] // (2 * outer_count)
-    gv_s[...] = gv_in_ref[...]
+    gv_s[...] = gv_in[...]
     attend_backward(
-        x_ref, mask_ref, wa_ref, vec_ref, (q_s, k_s, v_s, ot_s, kt_s, p_s),
+        x_in, mask_in, wa_ref, vec_in, (q_in, k_in, v_in, ot_s, kt_in, p_in),
         (do_s, dq_s, dk_s, dv_s), gmid_ref, du_ref, (ga_s, gv_s),
     )
     core = place_ref[1]
@@ -338,25 +370,66 @@
         sent_ref[o, 4 * span :, :] = tail
 
 
-def call(kernel, operands, shapes, scratch, flops, scalars=0):
-    whole = pl.BlockSpec(memory_space=pltpu.VMEM)
-    scalar = pl.BlockSpec(memory_space=pltpu.SMEM)
+def call(kernel, operands, results, scratch, flops, after=()):
+    space = {"s": pltpu.SMEM, "v": pltpu.VMEM}
+
+    def body(*refs):
+        refs = list(refs[len(after) :])
+        given, refs = refs[: len(operands)], refs[len(operands) :]
+        kernel(given, refs[: len(results)], refs[len(results) :])
+
     return pl.pallas_call(
-        kernel,
-        out_shape=[jax.ShapeDtypeStruct(*shape) for shape in shapes],
-        in_specs=[scalar] * scalars + [whole] * (len(operands) - scalars),
-        out_specs=[whole] * len(shapes),
+        body,
+        out_shape=[jax.ShapeDtypeStruct(*result) for result in results],
+        in_specs=[pl.BlockSpec(memory_space=pl.ANY)] * len(after)
+        + [pl.BlockSpec(memory_space=space[kind]) for kind, _ in operands],
+        out_specs=[pl.BlockSpec(memory_space=pltpu.VMEM)] * len(results),
         scratch_shapes=[pltpu.VMEM(*shape) for shape in scratch],
         compiler_params=pltpu.CompilerParams(vmem_limit_bytes=VMEM_LIMIT),
         cost_estimate=pl.CostEstimate(flops=flops, bytes_accessed=4 * 10**6, transcendentals=10**6),
+    )(*after, *[array for _, array in operands])
+
+
+def call_whole(kernel, operands, shapes):
+    def block(shape):
+        return pl.BlockSpec(shape, lambda i: (0,) * len(shape))
+
+    return pl.pallas_call(
+        kernel,
+        grid=(1,),
+        out_shape=[jax.ShapeDtypeStruct(*shape) for shape in shapes],
+        in_specs=[pl.BlockSpec(memory_space=pltpu.SMEM)]
+        + [block(operand.shape) for operand in operands[1:]],
+        out_specs=[block(shape[0]) for shape in shapes],
     )(*operands)
 
 
-VMEM_LIMIT = 32 * 1024 * 1024
+VMEM_LIMIT = 24 * 1024 * 1024
 
 
 def axis_sizes():
     return lax.axis_size("dp"), lax.axis_size("seq")
+
+
+def places(lengths):
+    dp_count, seq_count = axis_sizes()
+    outer_count = dp_count // 2
+    d, z = lax.axis_index("dp"), lax.axis_index("seq")
+    o, index = d // 2, d * seq_count + z
+    block = seq_count // 4
+
+    def unsigned(value):
+        return value.astype(jnp.uint32)
+
+    return {
+        "first": lax.axis_index("section") == 0,
+        "operand": jnp.stack([o, d % 2, z, index]).astype(jnp.int32),
+        "outer": [unsigned((o + k) % outer_count) for k in range(outer_count)],
+        "line": [unsigned((z + k) % seq_count) for k in range(seq_count)],
+        "even": z % 2 == 0,
+        "micro": z // block // 2 == 0,
+        "slots": [unsigned(index * length) for length in lengths],
+    }
 
 
 def swap_core(value):
@@ -383,11 +456,8 @@
     return [piece] + [turn_line(piece, k) for k in range(1, lax.axis_size("seq"))]
 
 
-def gather_rest(line):
-    outer_count = lax.axis_size("dp") // 2
-    stacked = jnp.stack(line)
-    mine = [stacked] + [turn_outer(stacked, k) for k in range(1, outer_count)]
-    return mine, [swap_core(member) for member in mine]
+def gather_outer(stacked):
+    return [stacked] + [turn_outer(stacked, k) for k in range(1, lax.axis_size("dp") // 2)]
 
 
 def assemble(mine, theirs):
@@ -402,10 +472,7 @@
     return ordered.transpose(1, 0, 2, 3, 4).reshape((-1,) + mine[0].shape[1:])
 
 
-def scatter_sum(kept, sent, take):
-    d, z = lax.axis_index("dp"), lax.axis_index("seq")
-    outer_count, seq_count = lax.axis_size("dp") // 2, lax.axis_size("seq")
-    o = d // 2
+def scatter_core(kept, sent, at):
     came = swap_core(sent)
 
     def both(index):
@@ -413,13 +480,20 @@
             F32
         ) + lax.dynamic_index_in_dim(came, index, 0, keepdims=False).astype(F32)
 
-    total = both(o)
-    for k in range(1, outer_count):
-        total = total + turn_outer(both((o + k) % outer_count).astype(BF16), k).astype(F32)
+    return both(at["outer"][0]), [both(index).astype(BF16) for index in at["outer"][1:]]
+
+
+def scatter_outer(total, sent):
+    for k, member in enumerate(sent):
+        total = total + turn_outer(member, k + 1).astype(F32)
+    return total
+
+
+def scatter_line(total, take, at):
     low = total.astype(BF16)
-    result = take(total, z)
-    for k in range(1, seq_count):
-        result = result + turn_line(take(low, (z + k) % seq_count), k).astype(F32)
+    result = take(total, at["line"][0])
+    for k in range(1, len(at["line"])):
+        result = result + turn_line(take(low, at["line"][k]), k).astype(F32)
     return result
 
 
@@ -436,28 +510,24 @@
     return moves
 
 
-def to_images(blocks):
-    z = lax.axis_index("seq")
-    micro = z // (lax.axis_size("seq") // 4) // 2
+def to_images(blocks, at):
     arrived = []
     for step in range(2):
-        sent = jnp.where((step + z) % 2 == 0, blocks[0], blocks[1])
+        sent = jnp.where(at["even"], blocks[step], blocks[1 - step])
         arrived.append(joint_permute(sent, image_moves(step)))
-    low = jnp.where(micro == 0, arrived[0], arrived[1])
-    high = jnp.where(micro == 0, arrived[1], arrived[0])
+    low = jnp.where(at["micro"], arrived[0], arrived[1])
+    high = jnp.where(at["micro"], arrived[1], arrived[0])
     return jnp.concatenate([low, high], axis=0)
 
 
-def from_images(rows_own):
-    z = lax.axis_index("seq")
-    micro = z // (lax.axis_size("seq") // 4) // 2
+def from_images(rows_own, at):
     half = rows_own.shape[0] // 2
     low, high = rows_own[:half], rows_own[half:]
     arrived = []
     for step in range(2):
-        sent = jnp.where(micro == step, low, high)
+        sent = jnp.where(at["micro"], *((low, high) if step == 0 else (high, low)))
         arrived.append(joint_permute(sent, [(b, a) for a, b in image_moves(step)]))
-    return jnp.stack([jnp.where(z % 2 == m, arrived[0], arrived[1]) for m in range(2)])
+    return jnp.stack([jnp.where(at["even"], arrived[m], arrived[1 - m]) for m in range(2)])
 
 
 def group_members():
@@ -503,7 +573,7 @@
         rank = (z % block + turn) % block * 2 + (c ^ flip)
         picked = lax.dynamic_slice_in_dim(counts, 2 * rank, 2, 0)
         parts.append((places[None, :] < picked[:, None]).astype(F32).reshape(-1, 1))
-    return jnp.concatenate(parts, axis=0)
+    return jnp.broadcast_to(jnp.concatenate(parts, axis=0), (len(parts) * 2 * slot_count, 128))
 
 
 def to_section(value, steps):
@@ -523,14 +593,11 @@
     return jnp.concatenate(parts, axis=0)
 
 
-def own_slots(vectors, lengths):
-    index = lax.axis_index("dp") * lax.axis_size("seq") + lax.axis_index("seq")
-    count = lax.axis_size("dp") * lax.axis_size("seq")
+def own_slots(vectors, lengths, at):
     parts, start = [], 0
-    for length in lengths:
-        used = length * count // vectors.shape[1]
+    for length, used, place in zip(lengths, (2, 6, 4), at["slots"]):
         flat = vectors[start : start + used].reshape(-1)
-        parts.append(lax.dynamic_slice_in_dim(flat, index * length, length, 0))
+        parts.append(lax.dynamic_slice_in_dim(flat, place, length, 0))
         start += used
     return parts
 
@@ -546,11 +613,11 @@
 
 
 def on_device(boundary, lengths, w_qkv, w_out, w_fc1, w_fc2, gains, shifts, fc1_bias):
-    section = lax.axis_index("section")
     dp_count, seq_count = axis_sizes()
     outer_count = dp_count // 2
-    d = lax.axis_index("dp")
-    place = jnp.stack([d // 2, d % 2, lax.axis_index("seq")]).astype(jnp.int32)
+    lens = (gains.shape[1], shifts.shape[1], fc1_bias.shape[1])
+    at = places(lens)
+    place = at["operand"]
     slot_count = boundary.shape[3]
     own = 2 * slot_count
     total = lengths.shape[2] * slot_count
@@ -558,19 +625,28 @@
     hidden = rows * 4 * dp_count * seq_count
     pairs = width // 128
     span = width // dp_count
-    lens = (gains.shape[1], shifts.shape[1], fc1_bias.shape[1])
-    piece_a = jnp.concatenate(
-        [by_column(w_qkv[0], width), w_out[0], vector_slots((gains[0], shifts[0], fc1_bias[0]), width)]
-    )
-    piece_b = jnp.concatenate([by_column(w_fc1[0], width), w_fc2[0]])
-    line_a = gather_line(piece_a)
-    own_start = to_images(boundary[0, :, 0])
-    line_b = gather_line(piece_b)
+    loose = outer_count if rows % 8 == 0 else 0
+    own_start = to_images(boundary[0, :, 0], at)
+    if loose:
+        piece_a, piece_b = call_whole(
+            pack_kernel,
+            [place, w_qkv[0], w_out[0], w_fc1[0], w_fc2[0], gains, shifts, fc1_bias],
+            [((4 * rows + 16, width), BF16), ((8 * rows, width), BF16)],
+        )
+    else:
+        tail = vector_slots((gains[0], shifts[0], fc1_bias[0]), width)
+        piece_a = jnp.concatenate([by_column(w_qkv[0], width), w_out[0], tail])
+        piece_b = jnp.concatenate([by_column(w_fc1[0], width), w_fc2[0]])
+    piece_a, at = lax.optimization_barrier((piece_a, at))
+    line_a = jnp.stack(gather_line(piece_a))
+    line_a, piece_b, own_start = lax.optimization_barrier((line_a, piece_b, own_start))
+    line_b = jnp.stack(gather_line(piece_b))
+    mine_a = gather_outer(line_a)
+    line_b, *mine_a = lax.optimization_barrier((line_b, *mine_a))
+    mine_b = gather_outer(line_b)
     mask = slot_mask(lengths, slot_count)
     all_start = gather_group(own_start)
-    mine_a, theirs_a = gather_rest(line_a)
-    mine_b, theirs_b = gather_rest(line_b)
-    loose = outer_count if rows % 8 == 0 else 0
+    theirs_a = [swap_core(member) for member in mine_a]
 
     w_shape = ((4, width, width), BF16)
     tall_shape = ((hidden, width), BF16)
@@ -591,15 +667,22 @@
     if loose:
         middle, w_a, vectors = call(
             functools.partial(first_kernel, loose, rows),
-            [place, all_start, mask, *mine_a, *theirs_a],
-            [mid_shape, w_shape, vec_shape], head_scratch, 10**9, 1,
+            [("s", place), ("v", all_start), ("v", mask)]
+            + [("v", member) for member in (*mine_a, *theirs_a)],
+            [mid_shape, w_shape, vec_shape],
+            head_scratch, 10**9, [line_b],
         )
+        middle, *mine_b = lax.optimization_barrier((middle, *mine_b))
+        theirs_b = [swap_core(member) for member in mine_b]
         first_out, w_1, w_2 = call(
             functools.partial(second_kernel, loose, rows),
-            [place, middle, mask, vectors, *mine_b, *theirs_b],
-            [low_shape, w_shape, tall_shape], [low_shape, mid_shape], 10**9, 1,
+            [("s", place), ("v", middle), ("v", mask), ("v", vectors)]
+            + [("v", member) for member in (*mine_b, *theirs_b)],
+            [low_shape, w_shape, tall_shape],
+            [low_shape, mid_shape], 10**9,
         )
     else:
+        theirs_b = [swap_core(member) for member in mine_b]
         ordered = assemble(mine_a, theirs_a)
         w_a = ordered[:, : 4 * rows].reshape(-1, 4, rows, width).transpose(1, 0, 2, 3)
         w_a = w_a.reshape(4, width, width)
@@ -610,35 +693,46 @@
         w_2 = ordered[:, 4 * rows :].reshape(hidden, width)
         (middle,) = call(
             functools.partial(first_kernel, loose, rows),
-            [place, all_start, mask, w_a, vectors], [mid_shape], head_scratch, 10**9, 1,
+            [("s", place), ("v", all_start), ("v", mask), ("v", w_a), ("v", vectors)],
+            [mid_shape], head_scratch, 10**9,
         )
         (first_out,) = call(
             functools.partial(second_kernel, loose, rows),
-            [place, middle, mask, vectors, w_1, w_2],
-            [low_shape], [low_shape, mid_shape], 10**9, 1,
+            [("s", place), ("v", middle), ("v", mask), ("v", vectors), ("v", w_1), ("v", w_2)],
+            [low_shape], [low_shape, mid_shape], 10**9,
         )
     arrived = gather_group(to_section(first_out, 1))
-    layer_in = jnp.where(section == 0, all_start, arrived)
+    layer_in = jnp.where(at["first"], all_start, arrived)
     grad_scratch = [q_shape, qt_shape, k_shape, k_shape]
-    layer_out, partial, middle, *kept = call(
+    saved = [mid_shape, q_shape, k_shape, k_shape, qt_shape, kt_shape, p_shape]
+    partial, layer_out, middle, q, k, v, ot, kt, p = call(
         middle_kernel,
-        [layer_in, mask, own_start, w_a, w_1, w_2, vectors],
-        [low_shape, all_shape, mid_shape, q_shape, k_shape, k_shape, qt_shape, kt_shape, p_shape],
+        [("v", layer_in)]
+        + [("v", member) for member in (mask, vectors, w_a, w_1, w_2, own_start)],
+        [all_shape, low_shape, *saved],
         [kt_shape, low_shape, mid_shape, h_shape, mid_shape, *grad_scratch], 4 * 10**9,
     )
     returned = to_section(scatter_group(partial, own), -1)
-    grad_out = jnp.where(section == 0, returned, own_start)
-    grad_mid, grad_vectors, kept_b, sent_b = call(
+    grad_out = jnp.where(at["first"], returned, own_start)
+    kept_b, sent_b, grad_mid, grad_vectors = call(
         feed_grad_kernel,
-        [place, middle, mask, grad_out, w_1, w_2, vectors],
-        [mid_shape, vec_shape, shared_b, shared_b],
-        [low_shape, mid_shape, w_shape, tall_shape], 2 * 10**9, 1,
-    )
+        [("s", place), ("v", grad_out)]
+        + [("v", member) for member in (middle, vectors, mask, w_1, w_2)],
+        [shared_b, shared_b, mid_shape, vec_shape],
+        [low_shape, mid_shape, w_shape, tall_shape], 2 * 10**9,
+    )
+    kept_b, sent_b = scatter_core(kept_b, sent_b, at)
     partial, kept_a, sent_a = call(
         attend_grad_kernel,
-        [place, layer_in, mask, w_a, vectors, *kept, grad_mid, grad_vectors],
+        [("s", place)]
+        + [
+            ("v", member)
+            for member in (
+                grad_mid, w_a, ot, v, q, kt, p, k, layer_in, mask, vectors, grad_vectors
+            )
+        ],
         [all_shape, shared_a, shared_a],
-        [*grad_scratch, w_shape, vec_shape], 2 * 10**9, 1,
+        [*grad_scratch, w_shape, vec_shape], 10**10, sent_b,
     )
 
     def line_block(wide, index):
@@ -653,16 +747,20 @@
     def take_a(value, index):
         return jnp.concatenate([line_block(value[: 4 * span], index), value[4 * span :]])
 
-    summed_b = scatter_sum(kept_b, sent_b, take_b)
+    total_b = scatter_outer(kept_b, sent_b)
     grad_in = scatter_group(partial, own)
-    rows_out = from_images(jnp.where(section == 0, grad_in, layer_out))
-    summed_a = scatter_sum(kept_a, sent_a, take_a)
+    rows_out = from_images(jnp.where(at["first"], grad_in, layer_out), at)
+    total_b, sent_a = lax.optimization_barrier((total_b, sent_a))
+    kept_a, sent_a = scatter_core(kept_a, sent_a, at)
+    total_a = scatter_outer(kept_a, sent_a)
+    summed_b = scatter_line(total_b, take_b, at)
+    summed_a = scatter_line(total_a, take_a, at)
     grads = (
         from_columns(summed_a[: 3 * rows], rows),
         summed_a[3 * rows : 4 * rows],
         from_columns(summed_b[: 4 * rows], rows),
         summed_b[4 * rows :],
-        *own_slots(summed_a[4 * rows :], lens),
+        *own_slots(summed_a[4 * rows :], lens, at),
     )
     return (rows_out[None, :, None], *[member[None] for member in grads])
 

time: 191 us -> 161 us (0.84)
  local copies, waits for them, and re-layouts: 18 us -> 5.53 us
  starting transfers between devices: 47.8 us -> 42.6 us
  other arithmetic: 10.1 us -> 5.46 us
  Pallas kernels: 47.7 us -> 43.6 us
  waiting for transfers between devices: 65.2 us -> 62.7 us
    ppermute x4, waiting for transfers between devices: 22.8 us -> 7.12 us  [turn_outer(): lax.ppermute(value, 'dp', [(d, (d + 2 * steps) % count) for d in range(co...]
    unnamed x44 -> x5, local copies, waits for them, and re-layouts: 7.86 us -> 0.04 us
    ppermute x12, waiting for transfers between devices: 17 us -> 22.5 us  [turn_line(): lax.ppermute(value, 'seq', [(z, (z + steps) % count) for z in range(count)])]
    ppermute x12, starting transfers between devices: 26.7 us -> 21.3 us  [turn_line(): lax.ppermute(value, 'seq', [(z, (z + steps) % count) for z in range(count)])]
    ppermute x7, waiting for transfers between devices: 1.04 us -> 6.35 us  [swap_core(): lax.ppermute(value, 'dp', [(d, d ^ 1) for d in range(lax.axis_size('dp'))])]
    pallas_call x5 -> x6, Pallas kernels: 47.7 us -> 43.6 us  [the longest x5 41.9 us: call(): pl.pallas_call(body, out_shape=[jax.ShapeDtypeStruct(*result) for result...]
    convert_element_type x4, other arithmetic: 4.47 us -> 0.42 us  [the longest x2 0.22 us: scatter_core(): both(index).astype(BF16)]
    ppermute x8, waiting for transfers between devices: 9.73 us -> 12.2 us  [joint_permute(): return lax.ppermute(value, ('dp', 'seq'), pairs)]
  transfers between devices with their start and end apart: 33 -> 33, of which waited for: 18 -> 22; matrix products, arithmetic and copies ran while one was open for 6% -> 4% of each run, Pallas kernels for 4% -> 4%
where the time goes in v3:
time: 161 us
  waiting for transfers between devices  62.7 us (39%)
  Pallas kernels  43.6 us (27%)
  starting transfers between devices  42.6 us (26%)
  local copies, waits for them, and re-layouts  5.53 us (3%)
  other arithmetic  5.46 us (3%)
    pallas_call x5, Pallas kernels, call(): pl.pallas_call(body, out_shape=[jax.ShapeDtypeStruct(*result) for result...  41.9 us
    ppermute x12, waiting for transfers between devices, turn_line(): lax.ppermute(value, 'seq', [(z, (z + steps) % count) for z in range(count)])  22.5 us
    ppermute x12, starting transfers between devices, turn_line(): lax.ppermute(value, 'seq', [(z, (z + steps) % count) for z in range(count)])  21.3 us
    ppermute x2, waiting for transfers between devices, to_section(): return lax.ppermute(value, 'section', [(0, 1)] if steps == 1 else [(1, 0)])  14.5 us
    ppermute x8, waiting for transfers between devices, joint_permute(): return lax.ppermute(value, ('dp', 'seq'), pairs)  12.2 us
    ppermute x8, starting transfers between devices, joint_permute(): return lax.ppermute(value, ('dp', 'seq'), pairs)  9.08 us
    ppermute x4, waiting for transfers between devices, turn_outer(): lax.ppermute(value, 'dp', [(d, (d + 2 * steps) % count) for d in range(co...  7.12 us
    ppermute x7, waiting for transfers between devices, swap_core(): lax.ppermute(value, 'dp', [(d, d ^ 1) for d in range(lax.axis_size('dp'))])  6.35 us
  transfers between devices with their start and end apart: 33, of which 22 were waited for; matrix products, arithmetic and copies ran while one was open for 4% of the time, Pallas kernels for 4%

profile of v3, /device:TPU:0, one launch (start us, length us, event | category | flops | bytes accessed | tf_op | source)
XLA Modules:
  0.0 161.1 jit_solution(3340807083004584970)
XLA Ops:
  0.7 0.6 pad_add_fusion.place_ref.refs_1_.refs_0_
  1.3 1.7 %shard_map.152 = (bf16[112,384]{1,0:T(8,128)(2,1)}, bf16[192,384]{1,0:T(8,128)(2,1)}) custom-call(s32[4]{0:T(128)} %pad_add_fusion.place_ref.refs_1_.refs_0_, bf16[24,1152]{1,0:T(8,128)(2,1)} %bitcast.107, bf16[24,384]{1,0:T(8,128)(2,1)} %bitcast.108, bf16[24,1536]{1,0:T(8,128)(2,1)} %bitcast.105, bf16[96,384]{1,0:T(8,128)(2,1)} %bitcast.106, ...), custom_call_target="tpu_custom_call" | custom-call | tf_op jit(solution)/shard_map/pallas_call | solution.py:397
  3.1 5.0 %collective-permute-start.2 = (bf16[112,384]{1,0:T(8,128)(2,1)}, bf16[112,384]{1,0:T(8,128)(2,1)S(1)}, u32[]{:S(2)}, u32[]{:S(2)}) collective-permute-start(bf16[112,384]{1,0:T(8,128)(2,1)} %get-tuple-element.60), channel_id=1, source_target_pairs={{0,3},{1,0},{2,1},{3,2},{4,7},{5,4},{6,5},{7,6},{8,11},{9,8},{10,9... | collective-permute-start | bytes 258056 | tf_op jit(solution)/shard_map/ppermute | solution.py:446
  8.1 1.0 collective-permute-start
  9.1 1.0 select_bitcast_fusion.3
  10.1 0.7 collective-permute-start.3
  10.8 4.3 %collective-permute-start.4 = (bf16[168,384]{1,0:T(8,128)(2,1)S(1)}, bf16[168,384]{1,0:T(8,128)(2,1)S(1)}, u32[]{:S(2)}, u32[]{:S(2)}) collective-permute-start(bf16[168,384]{1,0:T(8,128)(2,1)S(1)} %get-tuple-element.144), channel_id=1, source_target_pairs={{0,2},{1,0},{2,6},{3,4},{4,3},{5,1},{6,7},{7,5},{8,10},{9,8},{10,1... | collective-permute-start | bytes 387080 | tf_op jit(solution)/shard_map/ppermute | solution.py:452
  15.2 0.7 broadcast_select_fusion.5
  15.9 0.3 collective-permute-done.1
  16.2 0.9 pad_maximum_fusion.1.refs_4_
  17.1 2.0 %collective-permute-done.4 = bf16[168,384]{1,0:T(8,128)(2,1)S(1)} collective-permute-done((bf16[168,384]{1,0:T(8,128)(2,1)S(1)}, bf16[168,384]{1,0:T(8,128)(2,1)S(1)}, u32[]{:S(2)}, u32[]{:S(2)}) %collective-permute-start.4) | collective-permute-done | bytes 129056 | tf_op jit(solution)/shard_map/ppermute | solution.py:452
  19.2 5.3 %collective-permute-start.8 = (bf16[192,384]{1,0:T(8,128)(2,1)S(1)}, bf16[192,384]{1,0:T(8,128)(2,1)S(1)}, u32[]{:S(2)}, u32[]{:S(2)}) collective-permute-start(bf16[192,384]{1,0:T(8,128)(2,1)S(1)} %copy-done.1), channel_id=1, source_target_pairs={{0,3},{1,0},{2,1},{3,2},{4,7},{5,4},{6,5},{7,6},{8,11},{9,8},{10,9... | collective-permute-start | bytes 442376 | tf_op jit(solution)/shard_map/ppermute | solution.py:446
  24.5 1.5 collective-permute-start.6
  26.0 1.5 collective-permute-start.9
  27.5 1.2 collective-permute-done.8
  28.7 8.6 %collective-permute-done.7 = bf16[192,384]{1,0:T(8,128)(2,1)S(1)} collective-permute-done((bf16[192,384]{1,0:T(8,128)(2,1)S(1)}, bf16[192,384]{1,0:T(8,128)(2,1)S(1)}, u32[]{:S(2)}, u32[]{:S(2)}) %collective-permute-start.7) | collective-permute-done | bytes 147488 | tf_op jit(solution)/shard_map/ppermute | solution.py:446
  37.4 1.6 collective-permute-start.13
  39.1 0.5 collective-permute-start.11
  40.0 0.6 collective-permute-done.5
  40.7 0.4 collective-permute-done.11.refs_6_
  41.1 0.5 collective-permute-done.12.refs_7_
  41.8 6.0 %shard_map.153 = (f32[336,384]{1,0:T(8,128)S(1)}, bf16[4,384,384]{2,1,0:T(8,128)(2,1)S(1)}, f32[16,384]{1,0:T(8,128)S(1)}) custom-call(bf16[4,192,384]{2,1,0:T(8,128)(2,1)S(1)} %pad_maximum_fusion.refs_0_.refs_4_, s32[4]{0:T(128)S(1)} %copy-done, bf16[672,384]{1,0:T(8,128)(2,1)S(1)} %constant_dynamic-update-slice_fusion.refs_2_, ...), custom_call_target="tpu_custom_call" | custom-call | flops 1000000000 | bytes 4000000 | tf_op jit(solution)/shard_map/pallas_call | solution.py:381
  47.8 4.3 %collective-permute-done.13.refs_5_ = bf16[4,192,384]{2,1,0:T(8,128)(2,1)S(1)} collective-permute-done((bf16[4,192,384]{2,1,0:T(8,128)(2,1)S(1)}, bf16[4,192,384]{2,1,0:T(8,128)(2,1)S(1)}, u32[]{:S(2)}, u32[]{:S(2)}) %collective-permute-start.13) | collective-permute-done | bytes 589856 | tf_op jit(solution)/shard_map/ppermute | solution.py:441
  52.0 0.5 collective-permute-start.15
  52.6 1.5 collective-permute-done.14.refs_6_
  54.0 0.8 collective-permute-done.15.refs_7_
  54.9 3.6 %shard_map.154 = (bf16[336,384]{1,0:T(8,128)(2,1)S(1)}, bf16[4,384,384]{2,1,0:T(8,128)(2,1)S(1)}, bf16[1536,384]{1,0:T(8,128)(2,1)S(1)}) custom-call(s32[4]{0:T(128)S(1)} %copy-done, f32[336,384]{1,0:T(8,128)S(1)} %get-tuple-element.69.refs_1_, f32[672,128]{1,0:T(8,128)S(1)} %broadcast_in_dim.34.refs_3_.refs_2_.refs_1_.refs_4_.refs_11_, ...), custom_call_target="tpu_custom_call" | custom-call | flops 1000000000 | bytes 4000000 | tf_op jit(solution)/shard_map/pallas_call | solution.py:381
  58.5 3.6 %collective-permute-start.16 = (bf16[336,384]{1,0:T(8,128)(2,1)S(1)}, bf16[336,384]{1,0:T(8,128)(2,1)S(1)}, u32[]{:S(2)}, u32[]{:S(2)}) collective-permute-start(bf16[336,384]{1,0:T(8,128)(2,1)S(1)} %get-tuple-element.73), channel_id=1, source_target_pairs={{0,16},{1,17},{2,18},{3,19},{4,20},{5,21},{6,22},{7,23},{8,24},{9,... | collective-permute-start | bytes 774152 | tf_op jit(solution)/shard_map/ppermute | solution.py:580
  62.1 5.6 %collective-permute-done.16 = bf16[336,384]{1,0:T(8,128)(2,1)S(1)} collective-permute-done((bf16[336,384]{1,0:T(8,128)(2,1)S(1)}, bf16[336,384]{1,0:T(8,128)(2,1)S(1)}, u32[]{:S(2)}, u32[]{:S(2)}) %collective-permute-start.16) | collective-permute-done | bytes 258080 | tf_op jit(solution)/shard_map/ppermute | solution.py:580
  67.6 1.5 collective-permute-done.17
  69.3 18.0 %shard_map.155 = (bf16[672,384]{1,0:T(8,128)(2,1)S(1)}, bf16[336,384]{1,0:T(8,128)(2,1)S(1)}, f32[336,384]{1,0:T(8,128)S(1)}, bf16[3,336,128]{2,1,0:T(8,128)(2,1...) custom-call(bf16[672,384]{1,0:T(8,128)(2,1)S(1)} %maximum_select_fus, ...), custom_call_target="tpu_custom_call" | custom-call | flops 4000000000 | bytes 4000000 | tf_op jit(solution)/shard_map/pallas_call | solution.py:381
  87.4 0.2 collective-permute-start.18
  87.5 1.4 collective-permute-done.18
  89.0 1.3 collective-permute-start.19
  90.3 9.0 %collective-permute-done.19 = bf16[336,384]{1,0:T(8,128)(2,1)S(1)} collective-permute-done((bf16[336,384]{1,0:T(8,128)(2,1)S(1)}, bf16[336,384]{1,0:T(8,128)(2,1)S(1)}, u32[]{:S(2)}, u32[]{:S(2)}) %collective-permute-start.19) | collective-permute-done | bytes 258080 | tf_op jit(solution)/shard_map/ppermute | solution.py:580
  99.3 6.7 %shard_map.156 = (bf16[2,768,384]{2,1,0:T(8,128)(2,1)S(1)}, bf16[2,768,384]{2,1,0:T(8,128)(2,1)S(1)}, f32[336,384]{1,0:T(8,128)S(1)}, f32[16,384]{1,0:T(8,128)S(1)}) custom-call(s32[4]{0:T(128)S(1)} %copy-done, bf16[336,384]{1,0:T(8,128)(2,1)S(1)} %broadcast_select_fusion.refs_1_, f32[336,384]{1,0:T(8,128)S(1)} %get-tuple-element.78.refs_2_, ...), custom_call_target="tpu_custom_call" | custom-call | flops 2000000000 | bytes 4000000 | tf_op jit(solution)/shard_map/pallas_call | solution.py:381
  106.1 2.8 %collective-permute-done.20 = bf16[2,768,384]{2,1,0:T(8,128)(2,1)S(1)} collective-permute-done((bf16[2,768,384]{2,1,0:T(8,128)(2,1)S(1)}, bf16[2,768,384]{2,1,0:T(8,128)(2,1)S(1)}, u32[]{:S(2)}, u32[]{:S(2)}) %collective-permute-start.20) | collective-permute-done | bytes 1179680 | tf_op jit(solution)/shard_map/ppermute | solution.py:436
  109.1 7.6 %shard_map.157 = (bf16[672,384]{1,0:T(8,128)(2,1)S(1)}, bf16[2,400,384]{2,1,0:T(8,128)(2,1)S(1)}, bf16[2,400,384]{2,1,0:T(8,128)(2,1)S(1)}) custom-call(bf16[768,384]{1,0:T(8,128)(2,1)S(1)} %fusion.refs_0_, s32[4]{0:T(128)S(1)} %copy-done, f32[336,384]{1,0:T(8,128)S(1)} %get-tuple-element.82.refs_2_, bf16[4,384,384]{2,1,0:T(8,128)(2,1)S(1)} %get-tuple-element.74.refs_3_, ...), custom_call_target="tpu_custom_call" | custom-call | flops 10000000000 | bytes 4000000 | tf_op jit(solution)/shard_map/pallas_call | solution.py:381
  116.8 0.2 collective-permute-start.21
  117.0 1.5 collective-permute-start.24
  118.7 0.7 collective-permute-start.22
  119.3 3.0 %collective-permute-start.23 = (bf16[168,384]{1,0:T(8,128)(2,1)S(1)}, bf16[168,384]{1,0:T(8,128)(2,1)S(1)}, u32[]{:S(2)}, u32[]{:S(2)}) collective-permute-start(bf16[168,384]{1,0:T(8,128)(2,1)S(1)} %get-tuple-element.140), channel_id=1, source_target_pairs={{2,0},{0,1},{6,2},{4,3},{3,4},{1,5},{7,6},{5,7},{10,8},{8,9},{14,1... | collective-permute-start | bytes 387080 | tf_op jit(solution)/shard_map/ppermute | solution.py:452
  122.3 6.6 %collective-permute-done.23 = bf16[168,384]{1,0:T(8,128)(2,1)S(1)} collective-permute-done((bf16[168,384]{1,0:T(8,128)(2,1)S(1)}, bf16[168,384]{1,0:T(8,128)(2,1)S(1)}, u32[]{:S(2)}, u32[]{:S(2)}) %collective-permute-start.23) | collective-permute-done | bytes 129056 | tf_op jit(solution)/shard_map/ppermute | solution.py:452
  129.0 0.7 maximum_bitcast_fusion
  129.7 2.8 %collective-permute-done.24 = bf16[768,384]{1,0:T(8,128)(2,1)S(1)} collective-permute-done((bf16[768,384]{1,0:T(8,128)(2,1)S(1)}, bf16[768,384]{1,0:T(8,128)(2,1)S(1)}, u32[]{:S(2)}, u32[]{:S(2)}) %collective-permute-start.24) | collective-permute-done | bytes 589856 | tf_op jit(solution)/shard_map/ppermute | solution.py:441
  132.6 0.2 bitcast_add_fusion
  133.0 1.4 collective-permute-start.31
  134.5 0.5 collective-permute-start.32
  135.0 1.6 %collective-permute-start.30 = (bf16[192,384]{1,0:T(8,128)(2,1)S(1)}, bf16[192,384]{1,0:T(8,128)(2,1)S(1)}, u32[]{:S(2)}, u32[]{:S(2)}) collective-permute-start(bf16[192,384]{1,0:T(8,128)(2,1)S(1)} %pad_maximum_fusion.3), channel_id=1, source_target_pairs={{0,1},{1,2},{2,3},{3,0},{4,5},{5,6},{6,7},{7,4},{8,9},{9,10},{10,1... | collective-permute-start | bytes 442376 | tf_op jit(solution)/shard_map/ppermute | solution.py:446
  136.8 0.2 collective-permute-done.25
  137.1 1.6 collective-permute-start.26
  138.7 6.0 %collective-permute-done.31 = bf16[192,384]{1,0:T(8,128)(2,1)S(1)} collective-permute-done((bf16[192,384]{1,0:T(8,128)(2,1)S(1)}, bf16[192,384]{1,0:T(8,128)(2,1)S(1)}, u32[]{:S(2)}, u32[]{:S(2)}) %collective-permute-start.31) | collective-permute-done | bytes 147488 | tf_op jit(solution)/shard_map/ppermute | solution.py:446
  144.7 1.2 collective-permute-done.32
  145.9 0.7 slice_bitcast_fusion
  146.7 0.7 broadcast_in_dim_reshape.7
  147.7 2.5 %collective-permute-start.27 = (bf16[112,384]{1,0:T(8,128)(2,1)S(1)}, bf16[112,384]{1,0:T(8,128)(2,1)S(1)}, u32[]{:S(2)}, u32[]{:S(2)}) collective-permute-start(bf16[112,384]{1,0:T(8,128)(2,1)S(1)} %get-tuple-element.145), channel_id=1, source_target_pairs={{0,1},{1,2},{2,3},{3,0},{4,5},{5,6},{6,7},{7,4},{8,9},{9,10},{10,1... | collective-permute-start | bytes 258056 | tf_op jit(solution)/shard_map/ppermute | solution.py:446
  150.2 2.4 %collective-permute-start.29 = (bf16[112,384]{1,0:T(8,128)(2,1)S(1)}, bf16[112,384]{1,0:T(8,128)(2,1)S(1)}, u32[]{:S(2)}, u32[]{:S(2)}) collective-permute-start(bf16[112,384]{1,0:T(8,128)(2,1)S(1)} %get-tuple-element.147), channel_id=1, source_target_pairs={{0,3},{1,0},{2,1},{3,2},{4,7},{5,4},{6,5},{7,6},{8,11},{9,8},{10,9... | collective-permute-start | bytes 258056 | tf_op jit(solution)/shard_map/ppermute | solution.py:446
  152.6 2.4 %collective-permute-done.27 = bf16[112,384]{1,0:T(8,128)(2,1)S(1)} collective-permute-done((bf16[112,384]{1,0:T(8,128)(2,1)S(1)}, bf16[112,384]{1,0:T(8,128)(2,1)S(1)}, u32[]{:S(2)}, u32[]{:S(2)}) %collective-permute-start.27) | collective-permute-done | bytes 86048 | tf_op jit(solution)/shard_map/ppermute | solution.py:446
  155.0 2.8 %collective-permute-done.28 = bf16[112,384]{1,0:T(8,128)(2,1)S(1)} collective-permute-done((bf16[112,384]{1,0:T(8,128)(2,1)S(1)}, bf16[112,384]{1,0:T(8,128)(2,1)S(1)}, u32[]{:S(2)}, u32[]{:S(2)}) %collective-permute-start.28) | collective-permute-done | bytes 86048 | tf_op jit(solution)/shard_map/ppermute | solution.py:446
  157.9 0.6 slice_bitcast_fusion.1
  158.6 0.7 broadcast_in_dim_reshape.6
  159.3 0.6 dynamic-slice_bitcast_fusion.5
  159.9 0.6 dynamic-slice_bitcast_fusion.4
  160.5 0.6 dynamic_slice.110
  (76 shorter events, 2.5 us)
Async XLA Ops:
  3.1 16.1 %copy-start.1 = (bf16[192,384]{1,0:T(8,128)(2,1)S(1)}, bf16[192,384]{1,0:T(8,128)(2,1)}, u32[]{:S(2)}) copy-start(bf16[192,384]{1,0:T(8,128)(2,1)} %get-tuple-element.63) | copy-start | bytes 442372
  3.1 12.8 %collective-permute-start.2 = (bf16[112,384]{1,0:T(8,128)(2,1)}, bf16[112,384]{1,0:T(8,128)(2,1)S(1)}, u32[]{:S(2)}, u32[]{:S(2)}) collective-permute-start(bf16[112,384]{1,0:T(8,128)(2,1)} %get-tuple-element.60), channel_id=1, source_target_pairs={{0,3},{1,0},{2,1},{3,2},{4,7},{5,4},{6,5},{7,6},{8,11},{9,8},{10,9... | collective-permute-start | bytes 258056 | tf_op jit(solution)/shard_map/ppermute | solution.py:446
  8.1 8.0 %collective-permute-start.1 = (bf16[112,384]{1,0:T(8,128)(2,1)}, bf16[112,384]{1,0:T(8,128)(2,1)S(1)}, u32[]{:S(2)}, u32[]{:S(2)}) collective-permute-start(bf16[112,384]{1,0:T(8,128)(2,1)} %get-tuple-element.60), channel_id=1, source_target_pairs={{0,2},{1,3},{2,0},{3,1},{4,6},{5,7},{6,4},{7,5},{8,10},{9,11},{10,... | collective-permute-start | bytes 258056 | tf_op jit(solution)/shard_map/ppermute | solution.py:446
  8.1 8.0 %collective-permute-start = (bf16[112,384]{1,0:T(8,128)(2,1)}, bf16[112,384]{1,0:T(8,128)(2,1)S(1)}, u32[]{:S(2)}, u32[]{:S(2)}) collective-permute-start(bf16[112,384]{1,0:T(8,128)(2,1)} %get-tuple-element.60), channel_id=1, source_target_pairs={{0,1},{1,2},{2,3},{3,0},{4,5},{5,6},{6,7},{7,4},{8,9},{9,10},{10,1... | collective-permute-start | bytes 258056 | tf_op jit(solution)/shard_map/ppermute | solution.py:446
  9.1 1.7 %collective-permute-start.10 = (s32[2,4]{1,0:T(2,128)}, s32[2,4]{1,0:T(2,128)S(1)}, u32[]{:S(2)}, u32[]{:S(2)}) collective-permute-start(s32[2,4]{1,0:T(2,128)} %bitcast.109), channel_id=1, source_target_pairs={{0,4},{4,0},{8,12},{12,8},{1,5},{5,1},{9,13},{13,9},{2,6},{6,2},{1... | collective-permute-start | bytes 104 | tf_op jit(solution)/shard_map/ppermute | solution.py:436
  10.1 7.0 %collective-permute-start.3 = (bf16[168,384]{1,0:T(8,128)(2,1)S(1)}, bf16[168,384]{1,0:T(8,128)(2,1)S(1)}, u32[]{:S(2)}, u32[]{:S(2)}) collective-permute-start(bf16[168,384]{1,0:T(8,128)(2,1)S(1)} %get-tuple-element.143), channel_id=1, source_target_pairs={{0,0},{1,2},{2,4},{3,6},{4,1},{5,3},{6,5},{7,7},{8,8},{9,10},{10,1... | collective-permute-start | bytes 387080 | tf_op jit(solution)/shard_map/ppermute | solution.py:452
  10.8 8.3 %collective-permute-start.4 = (bf16[168,384]{1,0:T(8,128)(2,1)S(1)}, bf16[168,384]{1,0:T(8,128)(2,1)S(1)}, u32[]{:S(2)}, u32[]{:S(2)}) collective-permute-start(bf16[168,384]{1,0:T(8,128)(2,1)S(1)} %get-tuple-element.144), channel_id=1, source_target_pairs={{0,2},{1,0},{2,6},{3,4},{4,3},{5,1},{6,7},{7,5},{8,10},{9,8},{10,1... | collective-permute-start | bytes 387080 | tf_op jit(solution)/shard_map/ppermute | solution.py:452
  19.2 9.5 %collective-permute-start.8 = (bf16[192,384]{1,0:T(8,128)(2,1)S(1)}, bf16[192,384]{1,0:T(8,128)(2,1)S(1)}, u32[]{:S(2)}, u32[]{:S(2)}) collective-permute-start(bf16[192,384]{1,0:T(8,128)(2,1)S(1)} %copy-done.1), channel_id=1, source_target_pairs={{0,3},{1,0},{2,1},{3,2},{4,7},{5,4},{6,5},{7,6},{8,11},{9,8},{10,9... | collective-permute-start | bytes 442376 | tf_op jit(solution)/shard_map/ppermute | solution.py:446
  24.5 12.9 %collective-permute-start.7 = (bf16[192,384]{1,0:T(8,128)(2,1)S(1)}, bf16[192,384]{1,0:T(8,128)(2,1)S(1)}, u32[]{:S(2)}, u32[]{:S(2)}) collective-permute-start(bf16[192,384]{1,0:T(8,128)(2,1)S(1)} %copy-done.1), channel_id=1, source_target_pairs={{0,2},{1,3},{2,0},{3,1},{4,6},{5,7},{6,4},{7,5},{8,10},{9,11},{10,... | collective-permute-start | bytes 442376 | tf_op jit(solution)/shard_map/ppermute | solution.py:446
  24.5 12.9 %collective-permute-start.6 = (bf16[192,384]{1,0:T(8,128)(2,1)S(1)}, bf16[192,384]{1,0:T(8,128)(2,1)S(1)}, u32[]{:S(2)}, u32[]{:S(2)}) collective-permute-start(bf16[192,384]{1,0:T(8,128)(2,1)S(1)} %copy-done.1), channel_id=1, source_target_pairs={{0,1},{1,2},{2,3},{3,0},{4,5},{5,6},{6,7},{7,4},{8,9},{9,10},{10,1... | collective-permute-start | bytes 442376 | tf_op jit(solution)/shard_map/ppermute | solution.py:446
  26.0 11.4 %collective-permute-start.9 = (bf16[4,112,384]{2,1,0:T(8,128)(2,1)S(1)}, bf16[4,112,384]{2,1,0:T(8,128)(2,1)S(1)}, u32[]{:S(2)}, u32[]{:S(2)}) collective-permute-start(bf16[4,112,384]{2,1,0:T(8,128)(2,1)S(1)} %pad_maximum_fusion.1.refs_4_), channel_id=1, source_target_pairs={{0,8},{4,12},{8,0},{12,4},{1,9},{5,13},{9,1},{13,5},{2,10},{6,14},... | collective-permute-start | bytes 1032200 | tf_op jit(solution)/shard_map/ppermute | solution.py:441
  37.3 4.4 %copy-start = (s32[4]{0:T(128)S(1)}, s32[4]{0:T(128)}, u32[]{:S(2)}) copy-start(s32[4]{0:T(128)} %pad_add_fusion.place_ref.refs_1_.refs_0_) | copy-start | bytes 52
  37.4 14.6 %collective-permute-start.13 = (bf16[4,192,384]{2,1,0:T(8,128)(2,1)S(1)}, bf16[4,192,384]{2,1,0:T(8,128)(2,1)S(1)}, u32[]{:S(2)}, u32[]{:S(2)}) collective-permute-start(bf16[4,192,384]{2,1,0:T(8,128)(2,1)S(1)} %pad_maximum_fusion.refs_0_.refs_4_), channel_id=1, source_target_pairs={{0,8},{4,12},{8,0},{12,4},{1,9},{5,13},{9,1},{13,5},{2,10},{6,14},... | collective-permute-start | bytes 1769480 | tf_op jit(solution)/shard_map/ppermute | solution.py:441
  39.1 1.5 collective-permute-start.5
  39.1 2.0 %collective-permute-start.11 = (bf16[4,112,384]{2,1,0:T(8,128)(2,1)S(1)}, bf16[4,112,384]{2,1,0:T(8,128)(2,1)S(1)}, u32[]{:S(2)}, u32[]{:S(2)}) collective-permute-start(bf16[4,112,384]{2,1,0:T(8,128)(2,1)S(1)} %pad_maximum_fusion.1.refs_4_), channel_id=1, source_target_pairs={{0,4},{4,0},{8,12},{12,8},{1,5},{5,1},{9,13},{13,9},{2,6},{6,2},{1... | collective-permute-start | bytes 1032200 | tf_op jit(solution)/shard_map/ppermute | solution.py:436
  39.6 2.0 %collective-permute-start.12 = (bf16[4,112,384]{2,1,0:T(8,128)(2,1)S(1)}, bf16[4,112,384]{2,1,0:T(8,128)(2,1)S(1)}, u32[]{:S(2)}, u32[]{:S(2)}) collective-permute-start(bf16[4,112,384]{2,1,0:T(8,128)(2,1)S(1)} %collective-permute-done.9.refs_5_), channel_id=1, source_target_pairs={{0,4},{4,0},{8,12},{12,8},{1,5},{5,1},{9,13},{13,9},{2,6},{6,2},{1... | collective-permute-start | bytes 1032200 | tf_op jit(solution)/shard_map/ppermute | solution.py:436
  52.0 2.0 %collective-permute-start.14 = (bf16[4,192,384]{2,1,0:T(8,128)(2,1)S(1)}, bf16[4,192,384]{2,1,0:T(8,128)(2,1)S(1)}, u32[]{:S(2)}, u32[]{:S(2)}) collective-permute-start(bf16[4,192,384]{2,1,0:T(8,128)(2,1)S(1)} %pad_maximum_fusion.refs_0_.refs_4_), channel_id=1, source_target_pairs={{0,4},{4,0},{8,12},{12,8},{1,5},{5,1},{9,13},{13,9},{2,6},{6,2},{1... | collective-permute-start | bytes 1769480 | tf_op jit(solution)/shard_map/ppermute | solution.py:436
  52.0 2.8 %collective-permute-start.15 = (bf16[4,192,384]{2,1,0:T(8,128)(2,1)S(1)}, bf16[4,192,384]{2,1,0:T(8,128)(2,1)S(1)}, u32[]{:S(2)}, u32[]{:S(2)}) collective-permute-start(bf16[4,192,384]{2,1,0:T(8,128)(2,1)S(1)} %collective-permute-done.13.refs_5_), channel_id=1, source_target_pairs={{0,4},{4,0},{8,12},{12,8},{1,5},{5,1},{9,13},{13,9},{2,6},{6,2},{1... | collective-permute-start | bytes 1769480 | tf_op jit(solution)/shard_map/ppermute | solution.py:436
  58.5 9.2 %collective-permute-start.16 = (bf16[336,384]{1,0:T(8,128)(2,1)S(1)}, bf16[336,384]{1,0:T(8,128)(2,1)S(1)}, u32[]{:S(2)}, u32[]{:S(2)}) collective-permute-start(bf16[336,384]{1,0:T(8,128)(2,1)S(1)} %get-tuple-element.73), channel_id=1, source_target_pairs={{0,16},{1,17},{2,18},{3,19},{4,20},{5,21},{6,22},{7,23},{8,24},{9,... | collective-permute-start | bytes 774152 | tf_op jit(solution)/shard_map/ppermute | solution.py:580
  67.6 1.5 collective-permute-start.17
  87.4 1.6 collective-permute-start.18
  89.0 10.3 %collective-permute-start.19 = (bf16[336,384]{1,0:T(8,128)(2,1)S(1)}, bf16[336,384]{1,0:T(8,128)(2,1)S(1)}, u32[]{:S(2)}, u32[]{:S(2)}) collective-permute-start(bf16[336,384]{1,0:T(8,128)(2,1)S(1)} %add_convert_fusion.3), channel_id=1, source_target_pairs={{16,0},{17,1},{18,2},{19,3},{20,4},{21,5},{22,6},{23,7},{24,8},{25... | collective-permute-start | bytes 774152 | tf_op jit(solution)/shard_map/ppermute | solution.py:580
  106.0 2.9 %collective-permute-start.20 = (bf16[2,768,384]{2,1,0:T(8,128)(2,1)S(1)}, bf16[2,768,384]{2,1,0:T(8,128)(2,1)S(1)}, u32[]{:S(2)}, u32[]{:S(2)}) collective-permute-start(bf16[2,768,384]{2,1,0:T(8,128)(2,1)S(1)} %get-tuple-element.81), channel_id=1, source_target_pairs={{0,4},{4,0},{8,12},{12,8},{1,5},{5,1},{9,13},{13,9},{2,6},{6,2},{1... | collective-permute-start | bytes 3538952 | tf_op jit(solution)/shard_map/ppermute | solution.py:436
  116.8 1.7 %collective-permute-start.21 = (bf16[336,384]{1,0:T(8,128)(2,1)S(1)}, bf16[336,384]{1,0:T(8,128)(2,1)S(1)}, u32[]{:S(2)}, u32[]{:S(2)}) collective-permute-start(bf16[336,384]{1,0:T(8,128)(2,1)S(1)} %slice.98), channel_id=1, source_target_pairs={{0,4},{1,5},{2,6},{3,7},{4,0},{5,1},{6,2},{7,3},{8,12},{9,13},{10,... | collective-permute-start | bytes 774152 | tf_op jit(solution)/shard_map/ppermute | solution.py:452
  117.0 15.6 %collective-permute-start.24 = (bf16[768,384]{1,0:T(8,128)(2,1)S(1)}, bf16[768,384]{1,0:T(8,128)(2,1)S(1)}, u32[]{:S(2)}, u32[]{:S(2)}) collective-permute-start(bf16[768,384]{1,0:T(8,128)(2,1)S(1)} %fusion.refs_0_), channel_id=1, source_target_pairs={{0,8},{4,12},{8,0},{12,4},{1,9},{5,13},{9,1},{13,5},{2,10},{6,14},... | collective-permute-start | bytes 1769480 | tf_op jit(solution)/shard_map/ppermute | solution.py:441
  118.7 3.7 %collective-permute-start.22 = (bf16[168,384]{1,0:T(8,128)(2,1)S(1)}, bf16[168,384]{1,0:T(8,128)(2,1)S(1)}, u32[]{:S(2)}, u32[]{:S(2)}) collective-permute-start(bf16[168,384]{1,0:T(8,128)(2,1)S(1)} %get-tuple-element.139), channel_id=1, source_target_pairs={{0,0},{2,1},{4,2},{6,3},{1,4},{3,5},{5,6},{7,7},{8,8},{10,9},{12,1... | collective-permute-start | bytes 387080 | tf_op jit(solution)/shard_map/ppermute | solution.py:452
  119.3 9.6 %collective-permute-start.23 = (bf16[168,384]{1,0:T(8,128)(2,1)S(1)}, bf16[168,384]{1,0:T(8,128)(2,1)S(1)}, u32[]{:S(2)}, u32[]{:S(2)}) collective-permute-start(bf16[168,384]{1,0:T(8,128)(2,1)S(1)} %get-tuple-element.140), channel_id=1, source_target_pairs={{2,0},{0,1},{6,2},{4,3},{3,4},{1,5},{7,6},{5,7},{10,8},{8,9},{14,1... | collective-permute-start | bytes 387080 | tf_op jit(solution)/shard_map/ppermute | solution.py:452
  133.0 11.6 %collective-permute-start.31 = (bf16[192,384]{1,0:T(8,128)(2,1)S(1)}, bf16[192,384]{1,0:T(8,128)(2,1)S(1)}, u32[]{:S(2)}, u32[]{:S(2)}) collective-permute-start(bf16[192,384]{1,0:T(8,128)(2,1)S(1)} %pad_maximum_fusion.4), channel_id=1, source_target_pairs={{0,2},{1,3},{2,0},{3,1},{4,6},{5,7},{6,4},{7,5},{8,10},{9,11},{10,... | collective-permute-start | bytes 442376 | tf_op jit(solution)/shard_map/ppermute | solution.py:446
  134.5 11.4 %collective-permute-start.32 = (bf16[192,384]{1,0:T(8,128)(2,1)S(1)}, bf16[192,384]{1,0:T(8,128)(2,1)S(1)}, u32[]{:S(2)}, u32[]{:S(2)}) collective-permute-start(bf16[192,384]{1,0:T(8,128)(2,1)S(1)} %pad_maximum_fusion.5), channel_id=1, source_target_pairs={{0,3},{1,0},{2,1},{3,2},{4,7},{5,4},{6,5},{7,6},{8,11},{9,8},{10,9... | collective-permute-start | bytes 442376 | tf_op jit(solution)/shard_map/ppermute | solution.py:446
  135.0 2.0 %collective-permute-start.25 = (bf16[2,400,384]{2,1,0:T(8,128)(2,1)S(1)}, bf16[2,400,384]{2,1,0:T(8,128)(2,1)S(1)}, u32[]{:S(2)}, u32[]{:S(2)}) collective-permute-start(bf16[2,400,384]{2,1,0:T(8,128)(2,1)S(1)} %get-tuple-element.95), channel_id=1, source_target_pairs={{0,4},{4,0},{8,12},{12,8},{1,5},{5,1},{9,13},{13,9},{2,6},{6,2},{1... | collective-permute-start | bytes 1843208 | tf_op jit(solution)/shard_map/ppermute | solution.py:436
  135.0 10.9 %collective-permute-start.30 = (bf16[192,384]{1,0:T(8,128)(2,1)S(1)}, bf16[192,384]{1,0:T(8,128)(2,1)S(1)}, u32[]{:S(2)}, u32[]{:S(2)}) collective-permute-start(bf16[192,384]{1,0:T(8,128)(2,1)S(1)} %pad_maximum_fusion.3), channel_id=1, source_target_pairs={{0,1},{1,2},{2,3},{3,0},{4,5},{5,6},{6,7},{7,4},{8,9},{9,10},{10,1... | collective-permute-start | bytes 442376 | tf_op jit(solution)/shard_map/ppermute | solution.py:446
  137.1 10.3 %collective-permute-start.26 = (bf16[400,384]{1,0:T(8,128)(2,1)S(1)}, bf16[400,384]{1,0:T(8,128)(2,1)S(1)}, u32[]{:S(2)}, u32[]{:S(2)}) collective-permute-start(bf16[400,384]{1,0:T(8,128)(2,1)S(1)} %fusion.1), channel_id=1, source_target_pairs={{0,8},{4,12},{8,0},{12,4},{1,9},{5,13},{9,1},{13,5},{2,10},{6,14},... | collective-permute-start | bytes 921608 | tf_op jit(solution)/shard_map/ppermute | solution.py:441
  147.7 7.3 %collective-permute-start.27 = (bf16[112,384]{1,0:T(8,128)(2,1)S(1)}, bf16[112,384]{1,0:T(8,128)(2,1)S(1)}, u32[]{:S(2)}, u32[]{:S(2)}) collective-permute-start(bf16[112,384]{1,0:T(8,128)(2,1)S(1)} %get-tuple-element.145), channel_id=1, source_target_pairs={{0,1},{1,2},{2,3},{3,0},{4,5},{5,6},{6,7},{7,4},{8,9},{9,10},{10,1... | collective-permute-start | bytes 258056 | tf_op jit(solution)/shard_map/ppermute | solution.py:446
  150.2 7.7 %collective-permute-start.28 = (bf16[112,384]{1,0:T(8,128)(2,1)S(1)}, bf16[112,384]{1,0:T(8,128)(2,1)S(1)}, u32[]{:S(2)}, u32[]{:S(2)}) collective-permute-start(bf16[112,384]{1,0:T(8,128)(2,1)S(1)} %get-tuple-element.146), channel_id=1, source_target_pairs={{0,2},{1,3},{2,0},{3,1},{4,6},{5,7},{6,4},{7,5},{8,10},{9,11},{10,... | collective-permute-start | bytes 258056 | tf_op jit(solution)/shard_map/ppermute | solution.py:446
  150.2 7.7 %collective-permute-start.29 = (bf16[112,384]{1,0:T(8,128)(2,1)S(1)}, bf16[112,384]{1,0:T(8,128)(2,1)S(1)}, u32[]{:S(2)}, u32[]{:S(2)}) collective-permute-start(bf16[112,384]{1,0:T(8,128)(2,1)S(1)} %get-tuple-element.147), channel_id=1, source_target_pairs={{0,3},{1,0},{2,1},{3,2},{4,7},{5,4},{6,5},{7,6},{8,11},{9,8},{10,9... | collective-permute-start | bytes 258056 | tf_op jit(solution)/shard_map/ppermute | solution.py:446

commit v4 on v3

--- a/solution.py
+++ b/solution.py
@@ -2,6 +2,7 @@
 import math
 import jax
 import jax.numpy as jnp
+import numpy as np
 from jax import lax
 from jax.experimental import pallas as pl
 from jax.experimental.pallas import tpu as pltpu
@@ -91,7 +92,11 @@
     mid_ref[...] = masked[:own] + mul(attended, wa_ref[3]) + row_of(vec_ref, 6)
 
 
-def feed_forward(mid_ref, mask_ref, w1_ref, w2_ref, vec_ref, c_s, acc_s, h_s, y_ref):
+def gelu_slope(hidden, cdf):
+    return cdf + hidden * jnp.exp(-0.5 * hidden * hidden) * (1.0 / math.sqrt(2 * math.pi))
+
+
+def feed_forward(mid_ref, mask_ref, w1_ref, w2_ref, vec_ref, c_s, acc_s, stored, y_ref):
     own, width = mid_ref.shape
     unit, _ = norm_parts(mid_ref[...])
     c_s[...] = (unit * row_of(vec_ref, 1) + row_of(vec_ref, 3)).astype(BF16)
@@ -100,9 +105,11 @@
     @pl.loop(0, w1_ref.shape[0])
     def _(k):
         hidden = mul(c_s[...], w1_ref[k]) + vec_ref[pl.ds(8 + k, 1), :]
-        if h_s is not None:
-            h_s[k] = hidden
-        active = (hidden * gelu_cdf(hidden)).astype(BF16)
+        cdf = gelu_cdf(hidden)
+        active = (hidden * cdf).astype(BF16)
+        if stored is not None:
+            stored[0][k] = active
+            stored[1][k] = gelu_slope(hidden, cdf)
         rows = pl.ds(pl.multiple_of(k * width, 128), width)
         acc_s[...] += mul(active, w2_ref[rows, :])
 
@@ -112,7 +119,7 @@
 
 
 def feed_backward(
-    mid_ref, mask_ref, dy_ref, w1_ref, w2_ref, vec_ref, c_s, acc_s, h_s, gmid_ref, grads
+    mid_ref, mask_ref, dy_ref, w1_ref, w2_ref, vec_ref, c_s, acc_s, stored, gmid_ref, grads
 ):
     own, width = mid_ref.shape
     acc_s[...] = jnp.zeros_like(acc_s)
@@ -120,18 +127,17 @@
 
     @pl.loop(0, w1_ref.shape[0])
     def _(k):
-        if h_s is None:
+        if stored is None:
             hidden = mul(c_s[...], w1_ref[k]) + vec_ref[pl.ds(8 + k, 1), :]
+            slope = gelu_slope(hidden, gelu_cdf(hidden))
         else:
-            hidden = h_s[k]
-        cdf = gelu_cdf(hidden)
-        slope = cdf + hidden * jnp.exp(-0.5 * hidden * hidden) * (1.0 / math.sqrt(2 * math.pi))
+            slope = stored[1][k]
         grad_second = (dy_ref[...].astype(F32) * mask_ref[:own, :1]).astype(BF16)
         rows = pl.ds(pl.multiple_of(k * width, 128), width)
         grad_hidden = (mul(grad_second, w2_ref[rows, :], 1, 1) * slope).astype(BF16)
         acc_s[...] += mul(grad_hidden, w1_ref[k], 1, 1)
         if grads is not None:
-            active = (hidden * cdf).astype(BF16)
+            active = stored[0][k]
             g1_s[k] = mul(c_s[...], grad_hidden, 0, 0).astype(BF16)
             g2_s[rows, :] = mul(active, grad_second, 0, 0).astype(BF16)
             gv_ref[pl.ds(8 + k, 1), :] = total_of(grad_hidden.astype(F32))
@@ -205,7 +211,7 @@
     du_ref[...] = (grad_u * mask).astype(BF16)
 
 
-def pack_kernel(place_ref, qkv_ref, out_ref, fc1_ref, fc2_ref, gains_ref, shifts_ref, bias_ref, a_ref, b_ref):
+def pack_kernel(place_ref, qkv_ref, out_ref, fc1_ref, fc2_ref, gains_ref, shifts_ref, bias_ref, a_ref, b_ref, c_ref):
     rows, width = out_ref.shape
     index = place_ref[3]
 
@@ -229,19 +235,31 @@
         base += used
     blocks = columns(qkv_ref, 3) + [out_ref[...].astype(F32), tail]
     a_ref[...] = jnp.concatenate(blocks, axis=0).astype(BF16)
-    blocks = columns(fc1_ref, 4) + [fc2_ref[...].astype(F32)]
-    b_ref[...] = jnp.concatenate(blocks, axis=0).astype(BF16)
-
-
-def piece_groups(place_ref, mine, theirs):
+    b_ref[...] = jnp.concatenate(columns(fc1_ref, 4), axis=0).astype(BF16)
+    c_ref[...] = fc2_ref[...]
+
+
+def piece_groups(place_ref, mine, theirs, turns):
     outer, core, line = place_ref[0], place_ref[1], place_ref[2]
     count = mine[0].shape[0]
     for side, members in enumerate((mine, theirs)):
-        for turn, ref in enumerate(members):
-            index = lax.rem(outer + (len(mine) - turn), len(mine)) * 2 + (core if side == 0 else 1 - core)
-            blocks = [
-                ref[lax.rem(line - z + count, count)].astype(F32) for z in range(count)
+        for turn in range(turns):
+            index = lax.rem(outer + (turns - turn), turns) * 2 + (core if side == 0 else 1 - core)
+            yield index, [
+                members[turn][turned_bits(line ^ z, count)].astype(F32) for z in range(count)
             ]
+
+
+def halved_groups(place_ref, mine, theirs, turns):
+    outer, core, line = place_ref[0], place_ref[1], place_ref[2]
+    count = mine[0].shape[0] // turns * 2
+    for side, (even, odd) in enumerate((mine, theirs)):
+        for turn in range(turns):
+            index = lax.rem(outer + (turns - turn), turns) * 2 + (core if side == 0 else 1 - core)
+            blocks = []
+            for z in range(count):
+                entry = turned_bits((line ^ z) // 2, count // 2) * turns + turn
+                blocks.append(jnp.where((line ^ z) % 2 == 0, even[entry], odd[entry]).astype(F32))
             yield index, blocks
 
 
@@ -252,7 +270,7 @@
         mid_ref, wa_out, vec_out = outs
         wa_ref, vec_ref = wa_out, vec_out
         vector = None
-        for index, blocks in piece_groups(place_ref, mine, theirs):
+        for index, blocks in piece_groups(place_ref, mine, theirs, loose):
             span = rows * len(blocks)
             start = pl.multiple_of(index * span, 16)
             for s in range(4):
@@ -269,45 +287,48 @@
 
 
 def second_kernel(loose, rows, ins, outs, scratch):
-    place_ref, mid_ref = ins[:2]
+    place_ref, mid_ref, mask_ref, vec_ref = ins[:4]
     c_s, acc_s = scratch
     if loose:
-        mine, theirs = ins[4 : 4 + loose], ins[4 + loose :]
-        y_ref, w1_out, w2_out = outs
-        w1_ref, w2_ref = w1_out, w2_out
-        for index, blocks in piece_groups(place_ref, mine, theirs):
+        sets = [ins[4 : 4 + loose], ins[4 + loose : 4 + 2 * loose], ins[-4:-2], ins[-2:]]
+        y_ref, w1_ref, w2_ref = outs
+        for index, blocks in piece_groups(place_ref, sets[0], sets[1], loose):
             span = rows * len(blocks)
             start = pl.multiple_of(index * span, 16)
             for s in range(4):
                 group = jnp.concatenate([b[s * rows : (s + 1) * rows] for b in blocks], axis=0)
                 w1_ref[s, pl.ds(start, span), :] = group.astype(BF16)
-            group = jnp.concatenate([b[4 * rows : 8 * rows] for b in blocks], axis=0)
-            w2_ref[pl.ds(pl.multiple_of(4 * start, 16), 4 * span), :] = group.astype(BF16)
+        for index, blocks in halved_groups(place_ref, sets[2], sets[3], loose):
+            span = 4 * rows * len(blocks)
+            group = jnp.concatenate(blocks, axis=0)
+            w2_ref[pl.ds(pl.multiple_of(index * span, 16), span), :] = group.astype(BF16)
     else:
-        w1_ref, w2_ref = (member for member in ins[4:])
+        w1_ref, w2_ref = ins[4:]
         (y_ref,) = outs
-    mask_ref, vec_ref = ins[2], ins[3]
     feed_forward(mid_ref, mask_ref, w1_ref, w2_ref, vec_ref, c_s, acc_s, None, y_ref)
 
 
 def middle_kernel(ins, outs, scratch):
-    x_ref, mask_in, vec_in, wa_in, w1_in, w2_in, dy_in = ins
-    du_ref, y_out, mid_out, *kept = outs
-    vt_s, c_s, acc_s, h_s, gmid_s, do_s, dq_s, dk_s, dv_s = scratch
-    q_s, k_s, v_s, ot_s, kt_s, p_s = [member for member in kept]
-    mid_ref, y_ref = mid_out, y_out
-    mask_ref, vec_ref, wa_ref = mask_in, vec_in, wa_in
+    x_ref, mask_ref, vec_ref, wa_ref, w1_ref, w2_ref, dy_ref = ins
+    du_ref, mid_ref, c_s, *kept = outs
+    vt_s, acc_s, gmid_s, *grad_scratch = scratch
+    q_s, k_s, v_s, ot_s, kt_s, p_s = kept
     attend_forward(
         x_ref, mask_ref, wa_ref, vec_ref, (q_s, k_s, v_s, vt_s, ot_s, kt_s, p_s), mid_ref
     )
-    w1_ref, w2_ref = w1_in, w2_in
-    feed_forward(mid_ref, mask_ref, w1_ref, w2_ref, vec_ref, c_s, acc_s, h_s, y_ref)
+    unit, _ = norm_parts(mid_ref[...])
+    c_s[...] = (unit * row_of(vec_ref, 1) + row_of(vec_ref, 3)).astype(BF16)
     feed_backward(
-        mid_ref, mask_ref, dy_in, w1_ref, w2_ref, vec_ref, c_s, acc_s, h_s, gmid_s, None
-    )
-    attend_backward(
-        x_ref, mask_ref, wa_ref, vec_ref, (q_s, k_s, v_s, ot_s, kt_s, p_s),
-        (do_s, dq_s, dk_s, dv_s), gmid_s, du_ref, None,
+        mid_ref, mask_ref, dy_ref, w1_ref, w2_ref, vec_ref, c_s, acc_s, None, gmid_s, None
+    )
+    attend_backward(x_ref, mask_ref, wa_ref, vec_ref, kept, grad_scratch, gmid_s, du_ref, None)
+
+
+def output_kernel(ins, outs, scratch):
+    mid_ref, mask_ref, vec_ref, w1_ref, w2_ref = ins
+    y_ref, active_ref, slope_ref = outs
+    feed_forward(
+        mid_ref, mask_ref, w1_ref, w2_ref, vec_ref, *scratch, (active_ref, slope_ref), y_ref
     )
 
 
@@ -319,20 +340,15 @@
 
 
 def feed_grad_kernel(ins, outs, scratch):
-    place_ref, dy_ref, mid_in, vec_in, mask_in, w1_in, w2_in = ins
-    kept_ref, sent_ref, gmid_out, gv_out = outs
-    c_s, acc_s, g1_s, g2_s = scratch
-    gmid_ref, gv_ref = gmid_out, gv_out
-    mid_ref, vec_ref = mid_in, vec_in
-    unit, _ = norm_parts(mid_ref[...])
-    c_s[...] = (unit * row_of(vec_ref, 1) + row_of(vec_ref, 3)).astype(BF16)
+    place_ref, dy_ref, mid_ref, vec_ref, mask_ref, w1_ref, w2_ref, c_ref, active_ref, slope_ref = ins
+    kept_ref, sent_ref, gmid_ref, gv_ref = outs
+    acc_s, g1_s, g2_s = scratch
     gv_ref[...] = jnp.zeros_like(gv_ref)
-    mask_ref, w1_ref, w2_ref = mask_in, w1_in, w2_in
     outer_count = kept_ref.shape[0]
     span = w1_ref.shape[1] // (2 * outer_count)
     feed_backward(
-        mid_ref, mask_ref, dy_ref, w1_ref, w2_ref, vec_ref, c_s, acc_s, None, gmid_ref,
-        (g1_s, g2_s, gv_ref),
+        mid_ref, mask_ref, dy_ref, w1_ref, w2_ref, vec_ref, c_ref, acc_s,
+        (active_ref, slope_ref), gmid_ref, (g1_s, g2_s, gv_ref),
     )
     core = place_ref[1]
     for s in range(4):
@@ -425,13 +441,25 @@
         "first": lax.axis_index("section") == 0,
         "operand": jnp.stack([o, d % 2, z, index]).astype(jnp.int32),
         "outer": [unsigned((o + k) % outer_count) for k in range(outer_count)],
-        "line": [unsigned((z + k) % seq_count) for k in range(seq_count)],
+                "bits": [
+            (unsigned(z // step % 2), unsigned(1 - z // step % 2)) for step in reversed(line_steps())
+        ],
         "even": z % 2 == 0,
         "micro": z // block // 2 == 0,
         "slots": [unsigned(index * length) for length in lengths],
     }
 
 
+def pick(value, index, axis, rows=None):
+    starts = [np.uint32(0)] * value.ndim
+    starts[axis] = index
+    sizes = list(value.shape)
+    sizes[axis] = 1
+    if rows is not None:
+        starts[axis + 1], sizes[axis + 1] = np.uint32(rows[0]), rows[1] - rows[0]
+    return lax.dynamic_slice(value, starts, sizes).reshape(sizes[:axis] + sizes[axis + 1 :])
+
+
 def swap_core(value):
     return lax.ppermute(value, "dp", [(d, d ^ 1) for d in range(lax.axis_size("dp"))])
 
@@ -452,8 +480,35 @@
     return lax.ppermute(value, ("dp", "seq"), pairs)
 
 
-def gather_line(piece):
-    return [piece] + [turn_line(piece, k) for k in range(1, lax.axis_size("seq"))]
+def line_steps():
+    count, steps = lax.axis_size("seq"), []
+    while count > 1:
+        count //= 2
+        steps.append(count)
+    return steps
+
+
+def cross_line(value, distance):
+    count = lax.axis_size("seq")
+    return lax.ppermute(value, "seq", [(z, z ^ distance) for z in range(count)])
+
+
+def gather_step(pieces, step):
+    return jnp.concatenate([pieces, cross_line(pieces, line_steps()[step])])
+
+
+def gather_from(pieces, step, stop=None):
+    for later in range(step, len(line_steps()) if stop is None else stop):
+        pieces = gather_step(pieces, later)
+    return pieces
+
+
+def turned_bits(value, count):
+    result, low, high = value * 0, 1, count // 2
+    while high:
+        result = result + (value // high) % 2 * low
+        low, high = low * 2, high // 2
+    return result
 
 
 def gather_outer(stacked):
@@ -467,18 +522,17 @@
     turned = jnp.stack([jnp.stack(mine), jnp.stack(theirs)])
     sides = (jnp.arange(2) + c) % 2
     outers = (o - jnp.arange(outer_count)) % outer_count
-    lines = (z - jnp.arange(seq_count)) % seq_count
+    lines = turned_bits(z ^ jnp.arange(seq_count), seq_count)
     ordered = turned[sides][:, outers][:, :, lines]
     return ordered.transpose(1, 0, 2, 3, 4).reshape((-1,) + mine[0].shape[1:])
 
 
-def scatter_core(kept, sent, at):
-    came = swap_core(sent)
-
+def scatter_core(kept, came, at, rows):
     def both(index):
-        return lax.dynamic_index_in_dim(kept, index, 0, keepdims=False).astype(
-            F32
-        ) + lax.dynamic_index_in_dim(came, index, 0, keepdims=False).astype(F32)
+        mine, theirs = (
+            pick(member, index, 0, rows).astype(F32) for member in (kept, came)
+        )
+        return mine + theirs
 
     return both(at["outer"][0]), [both(index).astype(BF16) for index in at["outer"][1:]]
 
@@ -489,12 +543,38 @@
     return total
 
 
-def scatter_line(total, take, at):
-    low = total.astype(BF16)
-    result = take(total, at["line"][0])
-    for k in range(1, len(at["line"])):
-        result = result + turn_line(take(low, at["line"][k]), k).astype(F32)
-    return result
+def line_blocks(total, lead, tail=0):
+    body, rest = total[: total.shape[0] - tail], total[total.shape[0] - tail :]
+    return body.reshape(lead, lax.axis_size("seq"), -1, total.shape[1]), rest
+
+
+def halve_parts(state, at, step):
+    body, rest = state
+    mine, other = at["bits"][step]
+    lead, count, _, width = body.shape
+    halves = body.reshape(lead, count // 2, 2, -1, width)
+    body, sent = pick(halves, mine, 2), pick(halves, other, 2).reshape(-1, width)
+    if rest.shape[0]:
+        sent = jnp.concatenate([sent, rest])
+    return (body, rest), sent.astype(BF16)
+
+
+def halve_sum(state, sent, step):
+    body, rest = state
+    came = cross_line(sent, line_steps()[-1 - step]).astype(F32)
+    tail = rest.shape[0]
+    body = body + came[: came.shape[0] - tail].reshape(body.shape)
+    return body, rest + came[came.shape[0] - tail :]
+
+
+def halve_line(state, at, step):
+    return halve_sum(*halve_parts(state, at, step), step)
+
+
+def halve_rest(state, at, step):
+    for later in range(step, len(at["bits"])):
+        state = halve_line(state, at, later)
+    return state
 
 
 def image_moves(step):
@@ -520,14 +600,15 @@
     return jnp.concatenate([low, high], axis=0)
 
 
-def from_images(rows_own, at):
+def from_images(rows_own, at, after):
     half = rows_own.shape[0] // 2
     low, high = rows_own[:half], rows_own[half:]
     arrived = []
     for step in range(2):
         sent = jnp.where(at["micro"], *((low, high) if step == 0 else (high, low)))
         arrived.append(joint_permute(sent, [(b, a) for a, b in image_moves(step)]))
-    return jnp.stack([jnp.where(at["even"], arrived[m], arrived[1 - m]) for m in range(2)])
+    after, *arrived = lax.optimization_barrier((after, *arrived))
+    return jnp.stack([jnp.where(at["even"], arrived[m], arrived[1 - m]) for m in range(2)]), after
 
 
 def group_members():
@@ -626,24 +707,35 @@
     pairs = width // 128
     span = width // dp_count
     loose = outer_count if rows % 8 == 0 else 0
-    own_start = to_images(boundary[0, :, 0], at)
     if loose:
-        piece_a, piece_b = call_whole(
+        piece_a, piece_b, piece_c = call_whole(
             pack_kernel,
             [place, w_qkv[0], w_out[0], w_fc1[0], w_fc2[0], gains, shifts, fc1_bias],
-            [((4 * rows + 16, width), BF16), ((8 * rows, width), BF16)],
+            [((4 * rows + 16, width), BF16)] + [((4 * rows, width), BF16)] * 2,
         )
     else:
         tail = vector_slots((gains[0], shifts[0], fc1_bias[0]), width)
         piece_a = jnp.concatenate([by_column(w_qkv[0], width), w_out[0], tail])
-        piece_b = jnp.concatenate([by_column(w_fc1[0], width), w_fc2[0]])
+        piece_b, piece_c = by_column(w_fc1[0], width), w_fc2[0]
     piece_a, at = lax.optimization_barrier((piece_a, at))
-    line_a = jnp.stack(gather_line(piece_a))
-    line_a, piece_b, own_start = lax.optimization_barrier((line_a, piece_b, own_start))
-    line_b = jnp.stack(gather_line(piece_b))
+    half_a = gather_step(piece_a[None], 0)
+    near_c = jnp.stack(gather_outer(piece_c))
+    half_a, piece_b, near_c = lax.optimization_barrier((half_a, piece_b, near_c))
+    line_a = gather_from(half_a, 1)
+    half_b = gather_step(piece_b[None], 0)
+    line_a, half_b, near_c, blocks = lax.optimization_barrier(
+        (line_a, half_b, near_c, boundary[0, :, 0])
+    )
     mine_a = gather_outer(line_a)
-    line_b, *mine_a = lax.optimization_barrier((line_b, *mine_a))
+    line_b = gather_from(half_b, 1)
+    half_c = gather_step(near_c, 0)
+    own_start = to_images(blocks, at)
+    line_b, half_c, own_start, *mine_a = lax.optimization_barrier(
+        (line_b, half_c, own_start, *mine_a)
+    )
     mine_b = gather_outer(line_b)
+    half_c = gather_from(half_c, 1, len(line_steps()) - 1)
+    mine_c = [half_c, cross_line(half_c, line_steps()[-1])]
     mask = slot_mask(lengths, slot_count)
     all_start = gather_group(own_start)
     theirs_a = [swap_core(member) for member in mine_a]
@@ -660,6 +752,7 @@
     kt_shape = ((pairs, 128, total), BF16)
     p_shape = ((HEADS, total, own), BF16)
     h_shape = ((4, own, width), F32)
+    active_shape = ((4, own, width), BF16)
     shared_b = ((outer_count, 8 * span, width), BF16)
     shared_a = ((outer_count, 4 * span + 16, width), BF16)
 
@@ -672,25 +765,35 @@
             [mid_shape, w_shape, vec_shape],
             head_scratch, 10**9, [line_b],
         )
-        middle, *mine_b = lax.optimization_barrier((middle, *mine_b))
+        middle, mine_c[1], *mine_b[1:] = lax.optimization_barrier(
+            (middle, mine_c[1], *mine_b[1:])
+        )
         theirs_b = [swap_core(member) for member in mine_b]
+        theirs_c = [swap_core(member) for member in mine_c]
         first_out, w_1, w_2 = call(
             functools.partial(second_kernel, loose, rows),
             [("s", place), ("v", middle), ("v", mask), ("v", vectors)]
-            + [("v", member) for member in (*mine_b, *theirs_b)],
+            + [("v", member) for member in (*mine_b, *theirs_b, *mine_c, *theirs_c)],
             [low_shape, w_shape, tall_shape],
             [low_shape, mid_shape], 10**9,
         )
     else:
         theirs_b = [swap_core(member) for member in mine_b]
+        theirs_c = [swap_core(member) for member in mine_c]
         ordered = assemble(mine_a, theirs_a)
         w_a = ordered[:, : 4 * rows].reshape(-1, 4, rows, width).transpose(1, 0, 2, 3)
         w_a = w_a.reshape(4, width, width)
         vectors = jnp.sum(ordered[:, 4 * rows :].astype(F32), axis=0)
-        ordered = assemble(mine_b, theirs_b)
-        w_1 = ordered[:, : 4 * rows].reshape(-1, 4, rows, width).transpose(1, 0, 2, 3)
+        w_1 = assemble(mine_b, theirs_b).reshape(-1, 4, rows, width).transpose(1, 0, 2, 3)
         w_1 = w_1.reshape(4, width, width)
-        w_2 = ordered[:, 4 * rows :].reshape(hidden, width)
+        apart = [
+            [
+                jnp.concatenate(member).reshape(seq_count, outer_count, -1, width)[:, k]
+                for k in range(outer_count)
+            ]
+            for member in (mine_c, theirs_c)
+        ]
+        w_2 = assemble(*apart).reshape(hidden, width)
         (middle,) = call(
             functools.partial(first_kernel, loose, rows),
             [("s", place), ("v", all_start), ("v", mask), ("v", w_a), ("v", vectors)],
@@ -704,24 +807,36 @@
     arrived = gather_group(to_section(first_out, 1))
     layer_in = jnp.where(at["first"], all_start, arrived)
     grad_scratch = [q_shape, qt_shape, k_shape, k_shape]
-    saved = [mid_shape, q_shape, k_shape, k_shape, qt_shape, kt_shape, p_shape]
-    partial, layer_out, middle, q, k, v, ot, kt, p = call(
+    saved = [mid_shape, low_shape, q_shape, k_shape, k_shape, qt_shape, kt_shape, p_shape]
+    partial, middle, normed, q, k, v, ot, kt, p = call(
         middle_kernel,
         [("v", layer_in)]
         + [("v", member) for member in (mask, vectors, w_a, w_1, w_2, own_start)],
-        [all_shape, low_shape, *saved],
-        [kt_shape, low_shape, mid_shape, h_shape, mid_shape, *grad_scratch], 4 * 10**9,
-    )
-    returned = to_section(scatter_group(partial, own), -1)
+        [all_shape, *saved],
+        [kt_shape, mid_shape, mid_shape, *grad_scratch], 4 * 10**9,
+    )
+    sent_back = scatter_group(partial, own)
+    returned = to_section(sent_back, -1)
+    layer_out, active, slope = call(
+        output_kernel,
+        [("v", member) for member in (middle, mask, vectors, w_1, w_2)],
+        [low_shape, active_shape, h_shape], [low_shape, mid_shape], 2 * 10**9, [sent_back],
+    )
     grad_out = jnp.where(at["first"], returned, own_start)
     kept_b, sent_b, grad_mid, grad_vectors = call(
         feed_grad_kernel,
         [("s", place), ("v", grad_out)]
-        + [("v", member) for member in (middle, vectors, mask, w_1, w_2)],
+        + [
+            ("v", member)
+            for member in (middle, vectors, mask, w_1, w_2, normed, active, slope)
+        ],
         [shared_b, shared_b, mid_shape, vec_shape],
-        [low_shape, mid_shape, w_shape, tall_shape], 2 * 10**9,
-    )
-    kept_b, sent_b = scatter_core(kept_b, sent_b, at)
+        [mid_shape, w_shape, tall_shape], 2 * 10**9,
+    )
+    came_b = swap_core(sent_b)
+    both_c = kept_b[:, 4 * span :].astype(F32) + came_b[:, 4 * span :].astype(F32)
+    state_c, sent_c = halve_parts(line_blocks(both_c.reshape(-1, width), outer_count), at, 0)
+    kept_b, sent_b = scatter_core(kept_b, came_b, at, (0, 4 * span))
     partial, kept_a, sent_a = call(
         attend_grad_kernel,
         [("s", place)]
@@ -732,35 +847,40 @@
             )
         ],
         [all_shape, shared_a, shared_a],
-        [*grad_scratch, w_shape, vec_shape], 10**10, sent_b,
-    )
-
-    def line_block(wide, index):
-        split = wide.reshape(4, seq_count, rows, width)
-        return lax.dynamic_index_in_dim(split, index, 1, keepdims=False).reshape(-1, width)
-
-    def take_b(value, index):
-        tall = value[4 * span :].reshape(seq_count, 4 * rows, width)
-        tall = lax.dynamic_index_in_dim(tall, index, 0, keepdims=False)
-        return jnp.concatenate([line_block(value[: 4 * span], index), tall])
-
-    def take_a(value, index):
-        return jnp.concatenate([line_block(value[: 4 * span], index), value[4 * span :]])
+        [*grad_scratch, w_shape, vec_shape], 10**10, [*sent_b, sent_c],
+    )
 
     total_b = scatter_outer(kept_b, sent_b)
+    state_c = halve_sum(state_c, sent_c, 0)
+    total_b, state_c, sent_a, partial = lax.optimization_barrier(
+        (total_b, state_c, sent_a, partial)
+    )
+    kept_a, sent_a = scatter_core(kept_a, swap_core(sent_a), at, None)
     grad_in = scatter_group(partial, own)
-    rows_out = from_images(jnp.where(at["first"], grad_in, layer_out), at)
-    total_b, sent_a = lax.optimization_barrier((total_b, sent_a))
-    kept_a, sent_a = scatter_core(kept_a, sent_a, at)
+    total_b, state_c, *sent_a = lax.optimization_barrier((total_b, state_c, *sent_a))
     total_a = scatter_outer(kept_a, sent_a)
-    summed_b = scatter_line(total_b, take_b, at)
-    summed_a = scatter_line(total_a, take_a, at)
+    state_b = halve_line(line_blocks(total_b, 4), at, 0)
+    body_c = halve_rest(state_c, at, 1)[0].reshape(outer_count, -1, width)
+    rows_last = jnp.where(at["first"], grad_in, layer_out)
+    total_a, state_b, body_c, rows_last = lax.optimization_barrier(
+        (total_a, state_b, body_c, rows_last)
+    )
+    state_a = halve_line(line_blocks(total_a, 4, 16), at, 0)
+    summed_b = halve_rest(state_b, at, 1)[0].reshape(-1, width)
+    summed_c = scatter_outer(
+        pick(body_c, at["outer"][0], 0),
+        [pick(body_c, index, 0).astype(BF16) for index in at["outer"][1:]],
+    )
+    state_a, summed_b, summed_c = lax.optimization_barrier((state_a, summed_b, summed_c))
+    summed_a, summed_v = halve_rest(state_a, at, 1)
+    rows_out, summed_v = from_images(rows_last, at, summed_v)
+    summed_a = summed_a.reshape(-1, width)
     grads = (
         from_columns(summed_a[: 3 * rows], rows),
-        summed_a[3 * rows : 4 * rows],
-        from_columns(summed_b[: 4 * rows], rows),
-        summed_b[4 * rows :],
-        *own_slots(summed_a[4 * rows :], lens, at),
+        summed_a[3 * rows :],
+        from_columns(summed_b, rows),
+        summed_c,
+        *own_slots(summed_v, lens, at),
     )
     return (rows_out[None, :, None], *[member[None] for member in grads])
 

time: 161 us -> 153 us (0.950)
  waiting for transfers between devices: 62.7 us -> 55 us
  starting transfers between devices: 42.6 us -> 39.7 us
    ppermute x12, waiting for transfers between devices: 22.5 us -> 29.9 us  [cross_line(): return lax.ppermute(value, 'seq', [(z, z ^ distance) for z in range(count)])]
    ppermute x8, waiting for transfers between devices: 12.2 us -> 5.9 us  [joint_permute(): return lax.ppermute(value, ('dp', 'seq'), pairs)]
    ppermute x4 -> x6, waiting for transfers between devices: 7.12 us -> 2.35 us  [turn_outer(): lax.ppermute(value, 'dp', [(d, (d + 2 * steps) % count) for d in range(co...]
    ppermute x2, waiting for transfers between devices: 14.5 us -> 11.1 us  [to_section(): return lax.ppermute(value, 'section', [(0, 1)] if steps == 1 else [(1, 0)])]
    ppermute x8, starting transfers between devices: 9.08 us -> 6.25 us  [joint_permute(): return lax.ppermute(value, ('dp', 'seq'), pairs)]
    ppermute x12, starting transfers between devices: 21.3 us -> 19.1 us  [cross_line(): return lax.ppermute(value, 'seq', [(z, z ^ distance) for z in range(count)])]
    concatenate x4 -> x7, other arithmetic: 0.08 us -> 1.96 us  [the longest x5 1.93 us: gather_step(): return jnp.concatenate([pieces, cross_line(pieces, line_steps()[step])])]
    ppermute x4 -> x6, starting transfers between devices: 6.23 us -> 7.61 us  [turn_outer(): lax.ppermute(value, 'dp', [(d, (d + 2 * steps) % count) for d in range(co...]
  transfers between devices with their start and end apart: 33 -> 37, of which waited for: 22 -> 23; matrix products, arithmetic and copies ran while one was open for 4% -> 5% of each run, Pallas kernels for 4% -> 11%
where the time goes in v4:
time: 153 us; the launch traced here: 152 us
  waiting for transfers between devices  55 us (36%)
  Pallas kernels  44.1 us (29%)
  starting transfers between devices  39.7 us (26%)
  other arithmetic  6.97 us (5%)
  local copies, waits for them, and re-layouts  4.73 us (3%)
    pallas_call x6, Pallas kernels, call(): pl.pallas_call(body, out_shape=[jax.ShapeDtypeStruct(*result) for result...  42.3 us
    ppermute x12, waiting for transfers between devices, cross_line(): return lax.ppermute(value, 'seq', [(z, z ^ distance) for z in range(count)])  29.9 us
    ppermute x12, starting transfers between devices, cross_line(): return lax.ppermute(value, 'seq', [(z, z ^ distance) for z in range(count)])  19.1 us
    ppermute x2, waiting for transfers between devices, to_section(): return lax.ppermute(value, 'section', [(0, 1)] if steps == 1 else [(1, 0)])  11.1 us
    ppermute x6, starting transfers between devices, turn_outer(): lax.ppermute(value, 'dp', [(d, (d + 2 * steps) % count) for d in range(co...  7.61 us
    ppermute x8, starting transfers between devices, joint_permute(): return lax.ppermute(value, ('dp', 'seq'), pairs)  6.25 us
    ppermute x8, waiting for transfers between devices, joint_permute(): return lax.ppermute(value, ('dp', 'seq'), pairs)  5.9 us
    ppermute x9, waiting for transfers between devices, swap_core(): lax.ppermute(value, 'dp', [(d, d ^ 1) for d in range(lax.axis_size('dp'))])  5.77 us
  transfers between devices with their start and end apart: 37, of which 23 were waited for; matrix products, arithmetic and copies ran while one was open for 5% of the time, Pallas kernels for 11%

profile of v4, /device:TPU:0, one launch (start us, length us, event | category | flops | bytes accessed | tf_op | source)
XLA Modules:
  0.0 151.6 jit_solution(2281988428945934641)
XLA Ops:
  0.7 0.6 pad_add_fusion.place_ref.refs_1_.refs_0_.refs_2_
  1.3 1.7 %shard_map.152 = (bf16[112,384]{1,0:T(8,128)(2,1)}, bf16[96,384]{1,0:T(8,128)(2,1)}, bf16[96,384]{1,0:T(8,128)(2,1)}) custom-call(s32[4]{0:T(128)} %pad_add_fusion.place_ref.refs_1_.refs_0_.refs_2_, bf16[24,1152]{1,0:T(8,128)(2,1)} %bitcast.123, bf16[24,384]{1,0:T(8,128)(2,1)} %bitcast.124, bf16[24,1536]{1,0:T(8,128)(2,1)} %bitcast.115, ...), custom_call_target="tpu_custom_call" | custom-call | tf_op jit(solution)/shard_map/pallas_call | solution.py:413
  3.0 3.0 %collective-permute-start.1 = (bf16[96,384]{1,0:T(8,128)(2,1)}, bf16[96,384]{1,0:T(8,128)(2,1)S(1)}, u32[]{:S(2)}, u32[]{:S(2)}) collective-permute-start(bf16[96,384]{1,0:T(8,128)(2,1)} %get-tuple-element.87), channel_id=1, source_target_pairs={{0,8},{4,12},{8,0},{12,4},{1,9},{5,13},{9,1},{13,5},{2,10},{6,14},... | collective-permute-start | bytes 221192 | tf_op jit(solution)/shard_map/ppermute | solution.py:469
  6.0 2.6 %collective-permute-start = (bf16[1,112,384]{2,1,0:T(8,128)(2,1)}, bf16[1,112,384]{2,1,0:T(8,128)(2,1)S(1)}, u32[]{:S(2)}, u32[]{:S(2)}) collective-permute-start(bf16[1,112,384]{2,1,0:T(8,128)(2,1)} %bitcast.113), channel_id=1, source_target_pairs={{0,2},{1,3},{2,0},{3,1},{4,6},{5,7},{6,4},{7,5},{8,10},{9,11},{10,... | collective-permute-start | bytes 258056 | tf_op jit(solution)/shard_map/ppermute | solution.py:493
  8.6 0.9 pad_maximum_fusion.6
  9.5 4.4 %collective-permute-done = bf16[1,112,384]{2,1,0:T(8,128)(2,1)S(1)} collective-permute-done((bf16[1,112,384]{2,1,0:T(8,128)(2,1)}, bf16[1,112,384]{2,1,0:T(8,128)(2,1)S(1)}, u32[]{:S(2)}, u32[]{:S(2)}) %collective-permute-start) | collective-permute-done | bytes 86048 | tf_op jit(solution)/shard_map/ppermute | solution.py:493
  13.9 0.9 pad_maximum_fusion.4
  14.8 0.9 collective-permute-start.3
  15.7 3.2 %collective-permute-start.2 = (bf16[2,112,384]{2,1,0:T(8,128)(2,1)S(1)}, bf16[2,112,384]{2,1,0:T(8,128)(2,1)S(1)}, u32[]{:S(2)}, u32[]{:S(2)}) collective-permute-start(bf16[2,112,384]{2,1,0:T(8,128)(2,1)S(1)} %pad_maximum_fusion.4), channel_id=1, source_target_pairs={{0,1},{1,0},{2,3},{3,2},{4,5},{5,4},{6,7},{7,6},{8,9},{9,8},{10,11... | collective-permute-start | bytes 516104 | tf_op jit(solution)/shard_map/ppermute | solution.py:493
  18.9 0.7 broadcast_select_fusion.5
  19.6 2.4 %collective-permute-done.3 = bf16[1,96,384]{2,1,0:T(8,128)(2,1)S(1)} collective-permute-done((bf16[1,96,384]{2,1,0:T(8,128)(2,1)}, bf16[1,96,384]{2,1,0:T(8,128)(2,1)S(1)}, u32[]{:S(2)}, u32[]{:S(2)}) %collective-permute-start.3) | collective-permute-done | bytes 73760 | tf_op jit(solution)/shard_map/ppermute | solution.py:493
  21.9 0.9 pad_maximum_fusion.7
  22.8 1.2 collective-permute-done.2
  24.1 0.7 collective-permute-start.6
  24.8 3.1 %collective-permute-start.7 = (bf16[168,384]{1,0:T(8,128)(2,1)S(1)}, bf16[168,384]{1,0:T(8,128)(2,1)S(1)}, u32[]{:S(2)}, u32[]{:S(2)}) collective-permute-start(bf16[168,384]{1,0:T(8,128)(2,1)S(1)} %get-tuple-element.187), channel_id=1, source_target_pairs={{0,2},{1,0},{2,6},{3,4},{4,3},{5,1},{6,7},{7,5},{8,10},{9,8},{10,1... | collective-permute-start | bytes 387080 | tf_op jit(solution)/shard_map/ppermute | solution.py:480
  28.0 3.2 %collective-permute-start.5 = (bf16[2,96,384]{2,1,0:T(8,128)(2,1)S(1)}, bf16[2,96,384]{2,1,0:T(8,128)(2,1)S(1)}, u32[]{:S(2)}, u32[]{:S(2)}) collective-permute-start(bf16[2,96,384]{2,1,0:T(8,128)(2,1)S(1)} %pad_maximum_fusion.6), channel_id=1, source_target_pairs={{0,2},{1,3},{2,0},{3,1},{4,6},{5,7},{6,4},{7,5},{8,10},{9,11},{10,... | collective-permute-start | bytes 442376 | tf_op jit(solution)/shard_map/ppermute | solution.py:493
  31.7 2.3 %collective-permute-done.7 = bf16[168,384]{1,0:T(8,128)(2,1)S(1)} collective-permute-done((bf16[168,384]{1,0:T(8,128)(2,1)S(1)}, bf16[168,384]{1,0:T(8,128)(2,1)S(1)}, u32[]{:S(2)}, u32[]{:S(2)}) %collective-permute-start.7) | collective-permute-done | bytes 129056 | tf_op jit(solution)/shard_map/ppermute | solution.py:480
  34.1 5.8 %collective-permute-done.4 = bf16[2,96,384]{2,1,0:T(8,128)(2,1)S(1)} collective-permute-done((bf16[2,96,384]{2,1,0:T(8,128)(2,1)S(1)}, bf16[2,96,384]{2,1,0:T(8,128)(2,1)S(1)}, u32[]{:S(2)}, u32[]{:S(2)}) %collective-permute-start.4) | collective-permute-done | bytes 147488 | tf_op jit(solution)/shard_map/ppermute | solution.py:493
  39.9 1.3 collective-permute-done.8.refs_5_
  42.1 0.7 collective-permute-start.13
  43.5 0.6 collective-permute-start.15
  44.2 6.0 %shard_map.153 = (f32[336,384]{1,0:T(8,128)S(1)}, bf16[4,384,384]{2,1,0:T(8,128)(2,1)S(1)}, f32[16,384]{1,0:T(8,128)S(1)}) custom-call(bf16[4,96,384]{2,1,0:T(8,128)(2,1)S(1)} %pad_maximum_fusion.1.refs_0_.refs_4_, s32[4]{0:T(128)S(1)} %copy-done, bf16[672,384]{1,0:T(8,128)(2,1)S(1)} %constant_dynamic-update-slice_fusion.refs_2_, ...), custom_call_target="tpu_custom_call" | custom-call | flops 1000000000 | bytes 4000000 | tf_op jit(solution)/shard_map/pallas_call | solution.py:397
  50.3 1.3 collective-permute-done.13.refs_9_
  52.4 1.1 collective-permute-done.16.refs_7_
  53.9 3.7 %shard_map.154 = (bf16[336,384]{1,0:T(8,128)(2,1)S(1)}, bf16[4,384,384]{2,1,0:T(8,128)(2,1)S(1)}, bf16[1536,384]{1,0:T(8,128)(2,1)S(1)}) custom-call(s32[4]{0:T(128)S(1)} %copy-done, f32[336,384]{1,0:T(8,128)S(1)} %get-tuple-element.102.refs_1_, f32[672,128]{1,0:T(8,128)S(1)} %broadcast_in_dim.42.refs_3_.refs_2_.refs_1_.refs_4_.refs_12_, ...), custom_call_target="tpu_custom_call" | custom-call | flops 1000000000 | bytes 4000000 | tf_op jit(solution)/shard_map/pallas_call | solution.py:397
  57.6 3.6 %collective-permute-start.19 = (bf16[336,384]{1,0:T(8,128)(2,1)S(1)}, bf16[336,384]{1,0:T(8,128)(2,1)S(1)}, u32[]{:S(2)}, u32[]{:S(2)}) collective-permute-start(bf16[336,384]{1,0:T(8,128)(2,1)S(1)} %get-tuple-element.106), channel_id=1, source_target_pairs={{0,16},{1,17},{2,18},{3,19},{4,20},{5,21},{6,22},{7,23},{8,24},{9,... | collective-permute-start | bytes 774152 | tf_op jit(solution)/shard_map/ppermute | solution.py:661
  61.2 5.6 %collective-permute-done.19 = bf16[336,384]{1,0:T(8,128)(2,1)S(1)} collective-permute-done((bf16[336,384]{1,0:T(8,128)(2,1)S(1)}, bf16[336,384]{1,0:T(8,128)(2,1)S(1)}, u32[]{:S(2)}, u32[]{:S(2)}) %collective-permute-start.19) | collective-permute-done | bytes 258080 | tf_op jit(solution)/shard_map/ppermute | solution.py:661
  66.7 1.5 %collective-permute-done.20 = bf16[336,384]{1,0:T(8,128)(2,1)S(1)} collective-permute-done((bf16[336,384]{1,0:T(8,128)(2,1)S(1)}, bf16[336,384]{1,0:T(8,128)(2,1)S(1)}, u32[]{:S(2)}, u32[]{:S(2)}) %collective-permute-start.20) | collective-permute-done | bytes 258080 | tf_op jit(solution)/shard_map/ppermute | solution.py:480
  68.4 16.0 %shard_map.155 = (bf16[672,384]{1,0:T(8,128)(2,1)S(1)}, f32[336,384]{1,0:T(8,128)S(1)}, bf16[336,384]{1,0:T(8,128)(2,1)S(1)}, bf16[3,336,128]{2,1,0:T(8,128)(2,1...) custom-call(bf16[672,384]{1,0:T(8,128)(2,1)S(1)} %maximum_select_fus, ...), custom_call_target="tpu_custom_call" | custom-call | flops 4000000000 | bytes 4000000 | tf_op jit(solution)/shard_map/pallas_call | solution.py:397
  84.6 1.4 collective-permute-done.21
  86.1 1.3 collective-permute-start.22
  87.4 3.4 %shard_map.156 = (bf16[336,384]{1,0:T(8,128)(2,1)S(1)}, bf16[4,336,384]{2,1,0:T(8,128)(2,1)S(1)}, f32[4,336,384]{2,1,0:T(8,128)S(1)}) custom-call(bf16[336,384]{1,0:T(8,128)(2,1)S(1)} %add_convert_fusion.3.refs_0_, f32[336,384]{1,0:T(8,128)S(1)} %get-tuple-element.111.refs_1_.refs_2_, ...), custom_call_target="tpu_custom_call" | custom-call | flops 2000000000 | bytes 4000000 | tf_op jit(solution)/shard_map/pallas_call | solution.py:397
  90.8 5.5 %collective-permute-done.22 = bf16[336,384]{1,0:T(8,128)(2,1)S(1)} collective-permute-done((bf16[336,384]{1,0:T(8,128)(2,1)S(1)}, bf16[336,384]{1,0:T(8,128)(2,1)S(1)}, u32[]{:S(2)}, u32[]{:S(2)}) %collective-permute-start.22) | collective-permute-done | bytes 258080 | tf_op jit(solution)/shard_map/ppermute | solution.py:661
  96.4 5.5 %shard_map.157 = (bf16[2,768,384]{2,1,0:T(8,128)(2,1)S(1)}, bf16[2,768,384]{2,1,0:T(8,128)(2,1)S(1)}, f32[336,384]{1,0:T(8,128)S(1)}, f32[16,384]{1,0:T(8,128)S(1)}) custom-call(s32[4]{0:T(128)S(1)} %copy-done, bf16[336,384]{1,0:T(8,128)(2,1)S(1)} %broadcast_select_fusion.refs_1_, f32[336,384]{1,0:T(8,128)S(1)} %get-tuple-element.111.refs_1_.refs_2_, ...), custom_call_target="tpu_custom_call" | custom-call | flops 2000000000 | bytes 4000000 | tf_op jit(solution)/shard_map/pallas_call | solution.py:397
  102.0 2.8 %collective-permute-done.23 = bf16[2,768,384]{2,1,0:T(8,128)(2,1)S(1)} collective-permute-done((bf16[2,768,384]{2,1,0:T(8,128)(2,1)S(1)}, bf16[2,768,384]{2,1,0:T(8,128)(2,1)S(1)}, u32[]{:S(2)}, u32[]{:S(2)}) %collective-permute-start.23) | collective-permute-done | bytes 1179680 | tf_op jit(solution)/shard_map/ppermute | solution.py:464
  104.9 0.6 collective-permute-start.24
  105.6 1.5 collective-permute-start.25
  107.1 7.8 %shard_map.158 = (bf16[672,384]{1,0:T(8,128)(2,1)S(1)}, bf16[2,400,384]{2,1,0:T(8,128)(2,1)S(1)}, bf16[2,400,384]{2,1,0:T(8,128)(2,1)S(1)}) custom-call(bf16[384,384]{1,0:T(8,128)(2,1)S(1)} %fusion.1.refs_0_, bf16[384,384]{1,0:T(8,128)(2,1)S(1)} %bitcast.94, s32[4]{0:T(128)S(1)} %copy-done, f32[336,384]{1,0:T(8,128)S(1)} %get-tuple-element.119.refs_3_, ...), custom_call_target="tpu_custom_call" | custom-call | flops 10000000000 | bytes 4000000 | tf_op jit(solution)/shard_map/pallas_call | solution.py:397
  115.2 0.6 collective-permute-start.30
  115.8 1.4 collective-permute-done.26
  117.3 1.0 collective-permute-start.28
  118.5 1.8 %collective-permute-start.29 = (bf16[192,384]{1,0:T(8,128)(2,1)S(1)}, bf16[192,384]{1,0:T(8,128)(2,1)S(1)}, u32[]{:S(2)}, u32[]{:S(2)}) collective-permute-start(bf16[192,384]{1,0:T(8,128)(2,1)S(1)} %bitcast.112), channel_id=1, source_target_pairs={{0,2},{1,3},{2,0},{3,1},{4,6},{5,7},{6,4},{7,5},{8,10},{9,11},{10,... | collective-permute-start | bytes 442376 | tf_op jit(solution)/shard_map/ppermute | solution.py:493
  120.3 1.5 %collective-permute-start.27 = (bf16[400,384]{1,0:T(8,128)(2,1)S(1)}, bf16[400,384]{1,0:T(8,128)(2,1)S(1)}, u32[]{:S(2)}, u32[]{:S(2)}) collective-permute-start(bf16[400,384]{1,0:T(8,128)(2,1)S(1)} %fusion), channel_id=1, source_target_pairs={{0,8},{4,12},{8,0},{12,4},{1,9},{5,13},{9,1},{13,5},{2,10},{6,14},... | collective-permute-start | bytes 921608 | tf_op jit(solution)/shard_map/ppermute | solution.py:469
  121.8 4.0 %collective-permute-done.28 = bf16[192,384]{1,0:T(8,128)(2,1)S(1)} collective-permute-done((bf16[192,384]{1,0:T(8,128)(2,1)S(1)}, bf16[192,384]{1,0:T(8,128)(2,1)S(1)}, u32[]{:S(2)}, u32[]{:S(2)}) %collective-permute-start.28) | collective-permute-done | bytes 147488 | tf_op jit(solution)/shard_map/ppermute | solution.py:493
  125.8 2.5 %collective-permute-done.29 = bf16[192,384]{1,0:T(8,128)(2,1)S(1)} collective-permute-done((bf16[192,384]{1,0:T(8,128)(2,1)S(1)}, bf16[192,384]{1,0:T(8,128)(2,1)S(1)}, u32[]{:S(2)}, u32[]{:S(2)}) %collective-permute-start.29) | collective-permute-done | bytes 147488 | tf_op jit(solution)/shard_map/ppermute | solution.py:493
  128.3 0.7 collective-permute-done.27
  129.3 1.3 collective-permute-start.32
  130.5 1.5 %collective-permute-start.33 = (bf16[96,384]{1,0:T(8,128)(2,1)S(1)}, bf16[96,384]{1,0:T(8,128)(2,1)S(1)}, u32[]{:S(2)}, u32[]{:S(2)}) collective-permute-start(bf16[96,384]{1,0:T(8,128)(2,1)S(1)} %fusion.4), channel_id=1, source_target_pairs={{0,8},{4,12},{8,0},{12,4},{1,9},{5,13},{9,1},{13,5},{2,10},{6,14},... | collective-permute-start | bytes 221192 | tf_op jit(solution)/shard_map/ppermute | solution.py:469
  132.1 1.1 collective-permute-start.31
  133.2 1.7 %collective-permute-done.32 = bf16[96,384]{1,0:T(8,128)(2,1)S(1)} collective-permute-done((bf16[96,384]{1,0:T(8,128)(2,1)S(1)}, bf16[96,384]{1,0:T(8,128)(2,1)S(1)}, u32[]{:S(2)}, u32[]{:S(2)}) %collective-permute-start.32) | collective-permute-done | bytes 73760 | tf_op jit(solution)/shard_map/ppermute | solution.py:493
  135.0 0.7 bitcast_add_fusion.5
  135.7 1.8 %collective-permute-done.31 = bf16[208,384]{1,0:T(8,128)(2,1)S(1)} collective-permute-done((bf16[208,384]{1,0:T(8,128)(2,1)S(1)}, bf16[208,384]{1,0:T(8,128)(2,1)S(1)}, u32[]{:S(2)}, u32[]{:S(2)}) %collective-permute-start.31) | collective-permute-done | bytes 159776 | tf_op jit(solution)/shard_map/ppermute | solution.py:493
  137.6 1.8 %collective-permute-start.34 = (bf16[112,384]{1,0:T(8,128)(2,1)S(1)}, bf16[112,384]{1,0:T(8,128)(2,1)S(1)}, u32[]{:S(2)}, u32[]{:S(2)}) collective-permute-start(bf16[112,384]{1,0:T(8,128)(2,1)S(1)} %pad_maximum_fusion.8), channel_id=1, source_target_pairs={{0,2},{1,3},{2,0},{3,1},{4,6},{5,7},{6,4},{7,5},{8,10},{9,11},{10,... | collective-permute-start | bytes 258056 | tf_op jit(solution)/shard_map/ppermute | solution.py:493
  139.5 1.0 collective-permute-start.36
  140.5 0.7 collective-permute-start.35
  141.2 0.7 broadcast_in_dim_reshape.7
  141.9 5.0 %collective-permute-done.34 = bf16[112,384]{1,0:T(8,128)(2,1)S(1)} collective-permute-done((bf16[112,384]{1,0:T(8,128)(2,1)S(1)}, bf16[112,384]{1,0:T(8,128)(2,1)S(1)}, u32[]{:S(2)}, u32[]{:S(2)}) %collective-permute-start.34) | collective-permute-done | bytes 86048 | tf_op jit(solution)/shard_map/ppermute | solution.py:493
  146.9 0.6 slice_bitcast_fusion.1
  147.6 0.7 collective-permute-done.36
  148.3 0.7 broadcast_in_dim_reshape.6
  149.1 0.7 maximum_bitcast_fusion
  149.8 0.6 dynamic-slice_bitcast_fusion.1
  150.4 0.6 dynamic_slice.94
  151.0 0.6 dynamic-slice_bitcast_fusion
  (95 shorter events, 5.7 us)
Async XLA Ops:
  0.6 23.4 %copy-start.1 = (bf16[1,2,1,168,384]{4,3,2,1,0:T(8,128)(2,1)S(1)}, bf16[1,2,1,168,384]{4,3,2,1,0:T(8,128)(2,1)}, u32[]{:S(2)}) copy-start(bf16[1,2,1,168,384]{4,3,2,1,0:T(8,128)(2,1)} %param.9) | copy-start | bytes 774148
  3.0 5.6 %collective-permute-start.1 = (bf16[96,384]{1,0:T(8,128)(2,1)}, bf16[96,384]{1,0:T(8,128)(2,1)S(1)}, u32[]{:S(2)}, u32[]{:S(2)}) collective-permute-start(bf16[96,384]{1,0:T(8,128)(2,1)} %get-tuple-element.87), channel_id=1, source_target_pairs={{0,8},{4,12},{8,0},{12,4},{1,9},{5,13},{9,1},{13,5},{2,10},{6,14},... | collective-permute-start | bytes 221192 | tf_op jit(solution)/shard_map/ppermute | solution.py:469
  6.0 12.9 %collective-permute-start.10 = (s32[2,4]{1,0:T(2,128)}, s32[2,4]{1,0:T(2,128)S(1)}, u32[]{:S(2)}, u32[]{:S(2)}) collective-permute-start(s32[2,4]{1,0:T(2,128)} %bitcast.125), channel_id=1, source_target_pairs={{0,4},{4,0},{8,12},{12,8},{1,5},{5,1},{9,13},{13,9},{2,6},{6,2},{1... | collective-permute-start | bytes 104 | tf_op jit(solution)/shard_map/ppermute | solution.py:464
  6.0 7.9 %collective-permute-start = (bf16[1,112,384]{2,1,0:T(8,128)(2,1)}, bf16[1,112,384]{2,1,0:T(8,128)(2,1)S(1)}, u32[]{:S(2)}, u32[]{:S(2)}) collective-permute-start(bf16[1,112,384]{2,1,0:T(8,128)(2,1)} %bitcast.113), channel_id=1, source_target_pairs={{0,2},{1,3},{2,0},{3,1},{4,6},{5,7},{6,4},{7,5},{8,10},{9,11},{10,... | collective-permute-start | bytes 258056 | tf_op jit(solution)/shard_map/ppermute | solution.py:493
  14.8 7.2 %collective-permute-start.3 = (bf16[1,96,384]{2,1,0:T(8,128)(2,1)}, bf16[1,96,384]{2,1,0:T(8,128)(2,1)S(1)}, u32[]{:S(2)}, u32[]{:S(2)}) collective-permute-start(bf16[1,96,384]{2,1,0:T(8,128)(2,1)} %bitcast.118), channel_id=1, source_target_pairs={{0,2},{1,3},{2,0},{3,1},{4,6},{5,7},{6,4},{7,5},{8,10},{9,11},{10,... | collective-permute-start | bytes 221192 | tf_op jit(solution)/shard_map/ppermute | solution.py:493
  15.7 8.3 %collective-permute-start.2 = (bf16[2,112,384]{2,1,0:T(8,128)(2,1)S(1)}, bf16[2,112,384]{2,1,0:T(8,128)(2,1)S(1)}, u32[]{:S(2)}, u32[]{:S(2)}) collective-permute-start(bf16[2,112,384]{2,1,0:T(8,128)(2,1)S(1)} %pad_maximum_fusion.4), channel_id=1, source_target_pairs={{0,1},{1,0},{2,3},{3,2},{4,5},{5,4},{6,7},{7,6},{8,9},{9,8},{10,11... | collective-permute-start | bytes 516104 | tf_op jit(solution)/shard_map/ppermute | solution.py:493
  24.1 7.6 %collective-permute-start.6 = (bf16[168,384]{1,0:T(8,128)(2,1)S(1)}, bf16[168,384]{1,0:T(8,128)(2,1)S(1)}, u32[]{:S(2)}, u32[]{:S(2)}) collective-permute-start(bf16[168,384]{1,0:T(8,128)(2,1)S(1)} %get-tuple-element.186), channel_id=1, source_target_pairs={{0,0},{1,2},{2,4},{3,6},{4,1},{5,3},{6,5},{7,7},{8,8},{9,10},{10,1... | collective-permute-start | bytes 387080 | tf_op jit(solution)/shard_map/ppermute | solution.py:480
  24.8 9.2 %collective-permute-start.7 = (bf16[168,384]{1,0:T(8,128)(2,1)S(1)}, bf16[168,384]{1,0:T(8,128)(2,1)S(1)}, u32[]{:S(2)}, u32[]{:S(2)}) collective-permute-start(bf16[168,384]{1,0:T(8,128)(2,1)S(1)} %get-tuple-element.187), channel_id=1, source_target_pairs={{0,2},{1,0},{2,6},{3,4},{4,3},{5,1},{6,7},{7,5},{8,10},{9,8},{10,1... | collective-permute-start | bytes 387080 | tf_op jit(solution)/shard_map/ppermute | solution.py:480
  28.0 11.8 %collective-permute-start.4 = (bf16[2,96,384]{2,1,0:T(8,128)(2,1)S(1)}, bf16[2,96,384]{2,1,0:T(8,128)(2,1)S(1)}, u32[]{:S(2)}, u32[]{:S(2)}) collective-permute-start(bf16[2,96,384]{2,1,0:T(8,128)(2,1)S(1)} %pad_maximum_fusion.7), channel_id=1, source_target_pairs={{0,1},{1,0},{2,3},{3,2},{4,5},{5,4},{6,7},{7,6},{8,9},{9,8},{10,11... | collective-permute-start | bytes 442376 | tf_op jit(solution)/shard_map/ppermute | solution.py:493
  28.0 11.9 %collective-permute-start.5 = (bf16[2,96,384]{2,1,0:T(8,128)(2,1)S(1)}, bf16[2,96,384]{2,1,0:T(8,128)(2,1)S(1)}, u32[]{:S(2)}, u32[]{:S(2)}) collective-permute-start(bf16[2,96,384]{2,1,0:T(8,128)(2,1)S(1)} %pad_maximum_fusion.6), channel_id=1, source_target_pairs={{0,2},{1,3},{2,0},{3,1},{4,6},{5,7},{6,4},{7,5},{8,10},{9,11},{10,... | collective-permute-start | bytes 442376 | tf_op jit(solution)/shard_map/ppermute | solution.py:493
  31.2 10.0 %collective-permute-start.8 = (bf16[4,112,384]{2,1,0:T(8,128)(2,1)S(1)}, bf16[4,112,384]{2,1,0:T(8,128)(2,1)S(1)}, u32[]{:S(2)}, u32[]{:S(2)}) collective-permute-start(bf16[4,112,384]{2,1,0:T(8,128)(2,1)S(1)} %pad_maximum_fusion.refs_4_), channel_id=1, source_target_pairs={{0,8},{4,12},{8,0},{12,4},{1,9},{5,13},{9,1},{13,5},{2,10},{6,14},... | collective-permute-start | bytes 1032200 | tf_op jit(solution)/shard_map/ppermute | solution.py:469
  34.1 10.1 %copy-start = (s32[4]{0:T(128)S(1)}, s32[4]{0:T(128)}, u32[]{:S(2)}) copy-start(s32[4]{0:T(128)} %pad_add_fusion.place_ref.refs_1_.refs_0_.refs_2_) | copy-start | bytes 52
  41.2 2.1 %collective-permute-start.9 = (bf16[336,384]{1,0:T(8,128)(2,1)S(1)}, bf16[336,384]{1,0:T(8,128)(2,1)S(1)}, u32[]{:S(2)}, u32[]{:S(2)}) collective-permute-start(bf16[336,384]{1,0:T(8,128)(2,1)S(1)} %pad_maximum_fusion.3.refs_6_), channel_id=1, source_target_pairs={{4,0},{5,1},{6,2},{7,3},{0,4},{1,5},{2,6},{3,7},{12,8},{13,9},{14,... | collective-permute-start | bytes 774152 | tf_op jit(solution)/shard_map/ppermute | solution.py:480
  41.2 2.3 %collective-permute-start.11 = (bf16[4,112,384]{2,1,0:T(8,128)(2,1)S(1)}, bf16[4,112,384]{2,1,0:T(8,128)(2,1)S(1)}, u32[]{:S(2)}, u32[]{:S(2)}) collective-permute-start(bf16[4,112,384]{2,1,0:T(8,128)(2,1)S(1)} %pad_maximum_fusion.refs_4_), channel_id=1, source_target_pairs={{0,4},{4,0},{8,12},{12,8},{1,5},{5,1},{9,13},{13,9},{2,6},{6,2},{1... | collective-permute-start | bytes 1032200 | tf_op jit(solution)/shard_map/ppermute | solution.py:464
  41.7 2.3 %collective-permute-start.12 = (bf16[4,112,384]{2,1,0:T(8,128)(2,1)S(1)}, bf16[4,112,384]{2,1,0:T(8,128)(2,1)S(1)}, u32[]{:S(2)}, u32[]{:S(2)}) collective-permute-start(bf16[4,112,384]{2,1,0:T(8,128)(2,1)S(1)} %collective-permute-done.8.refs_5_), channel_id=1, source_target_pairs={{0,4},{4,0},{8,12},{12,8},{1,5},{5,1},{9,13},{13,9},{2,6},{6,2},{1... | collective-permute-start | bytes 1032200 | tf_op jit(solution)/shard_map/ppermute | solution.py:464
  42.1 9.5 %collective-permute-start.13 = (bf16[4,96,384]{2,1,0:T(8,128)(2,1)S(1)}, bf16[4,96,384]{2,1,0:T(8,128)(2,1)S(1)}, u32[]{:S(2)}, u32[]{:S(2)}) collective-permute-start(bf16[4,96,384]{2,1,0:T(8,128)(2,1)S(1)} %pad_maximum_fusion.2.refs_8_), channel_id=1, source_target_pairs={{0,1},{1,0},{2,3},{3,2},{4,5},{5,4},{6,7},{7,6},{8,9},{9,8},{10,11... | collective-permute-start | bytes 884744 | tf_op jit(solution)/shard_map/ppermute | solution.py:493
  42.8 9.1 %collective-permute-start.14 = (bf16[4,96,384]{2,1,0:T(8,128)(2,1)S(1)}, bf16[4,96,384]{2,1,0:T(8,128)(2,1)S(1)}, u32[]{:S(2)}, u32[]{:S(2)}) collective-permute-start(bf16[4,96,384]{2,1,0:T(8,128)(2,1)S(1)} %pad_maximum_fusion.1.refs_0_.refs_4_), channel_id=1, source_target_pairs={{0,8},{4,12},{8,0},{12,4},{1,9},{5,13},{9,1},{13,5},{2,10},{6,14},... | collective-permute-start | bytes 884744 | tf_op jit(solution)/shard_map/ppermute | solution.py:469
  43.4 9.0 %collective-permute-start.17 = (bf16[4,96,384]{2,1,0:T(8,128)(2,1)S(1)}, bf16[4,96,384]{2,1,0:T(8,128)(2,1)S(1)}, u32[]{:S(2)}, u32[]{:S(2)}) collective-permute-start(bf16[4,96,384]{2,1,0:T(8,128)(2,1)S(1)} %pad_maximum_fusion.2.refs_8_), channel_id=1, source_target_pairs={{0,4},{4,0},{8,12},{12,8},{1,5},{5,1},{9,13},{13,9},{2,6},{6,2},{1... | collective-permute-start | bytes 884744 | tf_op jit(solution)/shard_map/ppermute | solution.py:464
  43.5 8.9 %collective-permute-start.15 = (bf16[4,96,384]{2,1,0:T(8,128)(2,1)S(1)}, bf16[4,96,384]{2,1,0:T(8,128)(2,1)S(1)}, u32[]{:S(2)}, u32[]{:S(2)}) collective-permute-start(bf16[4,96,384]{2,1,0:T(8,128)(2,1)S(1)} %pad_maximum_fusion.1.refs_0_.refs_4_), channel_id=1, source_target_pairs={{0,4},{4,0},{8,12},{12,8},{1,5},{5,1},{9,13},{13,9},{2,6},{6,2},{1... | collective-permute-start | bytes 884744 | tf_op jit(solution)/shard_map/ppermute | solution.py:464
  51.9 1.6 %collective-permute-start.16 = (bf16[4,96,384]{2,1,0:T(8,128)(2,1)S(1)}, bf16[4,96,384]{2,1,0:T(8,128)(2,1)S(1)}, u32[]{:S(2)}, u32[]{:S(2)}) collective-permute-start(bf16[4,96,384]{2,1,0:T(8,128)(2,1)S(1)} %collective-permute-done.14.refs_5_), channel_id=1, source_target_pairs={{0,4},{4,0},{8,12},{12,8},{1,5},{5,1},{9,13},{13,9},{2,6},{6,2},{1... | collective-permute-start | bytes 884744 | tf_op jit(solution)/shard_map/ppermute | solution.py:464
  51.9 2.0 %collective-permute-start.18 = (bf16[4,96,384]{2,1,0:T(8,128)(2,1)S(1)}, bf16[4,96,384]{2,1,0:T(8,128)(2,1)S(1)}, u32[]{:S(2)}, u32[]{:S(2)}) collective-permute-start(bf16[4,96,384]{2,1,0:T(8,128)(2,1)S(1)} %collective-permute-done.13.refs_9_), channel_id=1, source_target_pairs={{0,4},{4,0},{8,12},{12,8},{1,5},{5,1},{9,13},{13,9},{2,6},{6,2},{1... | collective-permute-start | bytes 884744 | tf_op jit(solution)/shard_map/ppermute | solution.py:464
  57.6 9.2 %collective-permute-start.19 = (bf16[336,384]{1,0:T(8,128)(2,1)S(1)}, bf16[336,384]{1,0:T(8,128)(2,1)S(1)}, u32[]{:S(2)}, u32[]{:S(2)}) collective-permute-start(bf16[336,384]{1,0:T(8,128)(2,1)S(1)} %get-tuple-element.106), channel_id=1, source_target_pairs={{0,16},{1,17},{2,18},{3,19},{4,20},{5,21},{6,22},{7,23},{8,24},{9,... | collective-permute-start | bytes 774152 | tf_op jit(solution)/shard_map/ppermute | solution.py:661
  66.7 1.5 %collective-permute-start.20 = (bf16[336,384]{1,0:T(8,128)(2,1)S(1)}, bf16[336,384]{1,0:T(8,128)(2,1)S(1)}, u32[]{:S(2)}, u32[]{:S(2)}) collective-permute-start(bf16[336,384]{1,0:T(8,128)(2,1)S(1)} %collective-permute-done.19), channel_id=1, source_target_pairs={{4,0},{5,1},{6,2},{7,3},{0,4},{1,5},{2,6},{3,7},{12,8},{13,9},{14,... | collective-permute-start | bytes 774152 | tf_op jit(solution)/shard_map/ppermute | solution.py:480
  84.4 1.6 %collective-permute-start.21 = (bf16[336,384]{1,0:T(8,128)(2,1)S(1)}, bf16[336,384]{1,0:T(8,128)(2,1)S(1)}, u32[]{:S(2)}, u32[]{:S(2)}) collective-permute-start(bf16[336,384]{1,0:T(8,128)(2,1)S(1)} %slice.78), channel_id=1, source_target_pairs={{0,4},{1,5},{2,6},{3,7},{4,0},{5,1},{6,2},{7,3},{8,12},{9,13},{10,... | collective-permute-start | bytes 774152 | tf_op jit(solution)/shard_map/ppermute | solution.py:480
  86.1 10.3 %collective-permute-start.22 = (bf16[336,384]{1,0:T(8,128)(2,1)S(1)}, bf16[336,384]{1,0:T(8,128)(2,1)S(1)}, u32[]{:S(2)}, u32[]{:S(2)}) collective-permute-start(bf16[336,384]{1,0:T(8,128)(2,1)S(1)} %add_convert_fusion.3.refs_0_), channel_id=1, source_target_pairs={{16,0},{17,1},{18,2},{19,3},{20,4},{21,5},{22,6},{23,7},{24,8},{25... | collective-permute-start | bytes 774152 | tf_op jit(solution)/shard_map/ppermute | solution.py:661
  101.9 2.9 %collective-permute-start.23 = (bf16[2,768,384]{2,1,0:T(8,128)(2,1)S(1)}, bf16[2,768,384]{2,1,0:T(8,128)(2,1)S(1)}, u32[]{:S(2)}, u32[]{:S(2)}) collective-permute-start(bf16[2,768,384]{2,1,0:T(8,128)(2,1)S(1)} %get-tuple-element.117), channel_id=1, source_target_pairs={{0,4},{4,0},{8,12},{12,8},{1,5},{5,1},{9,13},{13,9},{2,6},{6,2},{1... | collective-permute-start | bytes 3538952 | tf_op jit(solution)/shard_map/ppermute | solution.py:464
  104.9 10.1 %collective-permute-start.24 = (bf16[384,384]{1,0:T(8,128)(2,1)S(1)}, bf16[384,384]{1,0:T(8,128)(2,1)S(1)}, u32[]{:S(2)}, u32[]{:S(2)}) collective-permute-start(bf16[384,384]{1,0:T(8,128)(2,1)S(1)} %fusion.1.refs_0_), channel_id=1, source_target_pairs={{0,8},{4,12},{8,0},{12,4},{1,9},{5,13},{9,1},{13,5},{2,10},{6,14},... | collective-permute-start | bytes 884744 | tf_op jit(solution)/shard_map/ppermute | solution.py:469
  105.6 9.3 %collective-permute-start.25 = (bf16[384,384]{1,0:T(8,128)(2,1)S(1)}, bf16[384,384]{1,0:T(8,128)(2,1)S(1)}, u32[]{:S(2)}, u32[]{:S(2)}) collective-permute-start(bf16[384,384]{1,0:T(8,128)(2,1)S(1)} %bitcast.93), channel_id=1, source_target_pairs={{0,1},{1,0},{2,3},{3,2},{4,5},{5,4},{6,7},{7,6},{8,9},{9,8},{10,11... | collective-permute-start | bytes 884744 | tf_op jit(solution)/shard_map/ppermute | solution.py:493
  115.1 2.1 %collective-permute-start.26 = (bf16[2,400,384]{2,1,0:T(8,128)(2,1)S(1)}, bf16[2,400,384]{2,1,0:T(8,128)(2,1)S(1)}, u32[]{:S(2)}, u32[]{:S(2)}) collective-permute-start(bf16[2,400,384]{2,1,0:T(8,128)(2,1)S(1)} %get-tuple-element.132), channel_id=1, source_target_pairs={{0,4},{4,0},{8,12},{12,8},{1,5},{5,1},{9,13},{13,9},{2,6},{6,2},{1... | collective-permute-start | bytes 1843208 | tf_op jit(solution)/shard_map/ppermute | solution.py:464
  115.2 3.1 %collective-permute-start.30 = (bf16[336,384]{1,0:T(8,128)(2,1)S(1)}, bf16[336,384]{1,0:T(8,128)(2,1)S(1)}, u32[]{:S(2)}, u32[]{:S(2)}) collective-permute-start(bf16[336,384]{1,0:T(8,128)(2,1)S(1)} %slice.82), channel_id=1, source_target_pairs={{0,4},{1,5},{2,6},{3,7},{4,0},{5,1},{6,2},{7,3},{8,12},{9,13},{10,... | collective-permute-start | bytes 774152 | tf_op jit(solution)/shard_map/ppermute | solution.py:480
  117.3 8.4 %collective-permute-start.28 = (bf16[192,384]{1,0:T(8,128)(2,1)S(1)}, bf16[192,384]{1,0:T(8,128)(2,1)S(1)}, u32[]{:S(2)}, u32[]{:S(2)}) collective-permute-start(bf16[192,384]{1,0:T(8,128)(2,1)S(1)} %bitcast.111), channel_id=1, source_target_pairs={{0,1},{1,0},{2,3},{3,2},{4,5},{5,4},{6,7},{7,6},{8,9},{9,8},{10,11... | collective-permute-start | bytes 442376 | tf_op jit(solution)/shard_map/ppermute | solution.py:493
  118.5 9.8 %collective-permute-start.29 = (bf16[192,384]{1,0:T(8,128)(2,1)S(1)}, bf16[192,384]{1,0:T(8,128)(2,1)S(1)}, u32[]{:S(2)}, u32[]{:S(2)}) collective-permute-start(bf16[192,384]{1,0:T(8,128)(2,1)S(1)} %bitcast.112), channel_id=1, source_target_pairs={{0,2},{1,3},{2,0},{3,1},{4,6},{5,7},{6,4},{7,5},{8,10},{9,11},{10,... | collective-permute-start | bytes 442376 | tf_op jit(solution)/shard_map/ppermute | solution.py:493
  120.3 8.8 %collective-permute-start.27 = (bf16[400,384]{1,0:T(8,128)(2,1)S(1)}, bf16[400,384]{1,0:T(8,128)(2,1)S(1)}, u32[]{:S(2)}, u32[]{:S(2)}) collective-permute-start(bf16[400,384]{1,0:T(8,128)(2,1)S(1)} %fusion), channel_id=1, source_target_pairs={{0,8},{4,12},{8,0},{12,4},{1,9},{5,13},{9,1},{13,5},{2,10},{6,14},... | collective-permute-start | bytes 921608 | tf_op jit(solution)/shard_map/ppermute | solution.py:469
  129.3 5.7 %collective-permute-start.32 = (bf16[96,384]{1,0:T(8,128)(2,1)S(1)}, bf16[96,384]{1,0:T(8,128)(2,1)S(1)}, u32[]{:S(2)}, u32[]{:S(2)}) collective-permute-start(bf16[96,384]{1,0:T(8,128)(2,1)S(1)} %bitcast.117), channel_id=1, source_target_pairs={{0,2},{1,3},{2,0},{3,1},{4,6},{5,7},{6,4},{7,5},{8,10},{9,11},{10,... | collective-permute-start | bytes 221192 | tf_op jit(solution)/shard_map/ppermute | solution.py:493
  130.5 4.5 %collective-permute-start.33 = (bf16[96,384]{1,0:T(8,128)(2,1)S(1)}, bf16[96,384]{1,0:T(8,128)(2,1)S(1)}, u32[]{:S(2)}, u32[]{:S(2)}) collective-permute-start(bf16[96,384]{1,0:T(8,128)(2,1)S(1)} %fusion.4), channel_id=1, source_target_pairs={{0,8},{4,12},{8,0},{12,4},{1,9},{5,13},{9,1},{13,5},{2,10},{6,14},... | collective-permute-start | bytes 221192 | tf_op jit(solution)/shard_map/ppermute | solution.py:469
  132.1 5.3 %collective-permute-start.31 = (bf16[208,384]{1,0:T(8,128)(2,1)S(1)}, bf16[208,384]{1,0:T(8,128)(2,1)S(1)}, u32[]{:S(2)}, u32[]{:S(2)}) collective-permute-start(bf16[208,384]{1,0:T(8,128)(2,1)S(1)} %pad_maximum_fusion.5), channel_id=1, source_target_pairs={{0,1},{1,0},{2,3},{3,2},{4,5},{5,4},{6,7},{7,6},{8,9},{9,8},{10,11... | collective-permute-start | bytes 479240 | tf_op jit(solution)/shard_map/ppermute | solution.py:493
  137.6 9.2 %collective-permute-start.34 = (bf16[112,384]{1,0:T(8,128)(2,1)S(1)}, bf16[112,384]{1,0:T(8,128)(2,1)S(1)}, u32[]{:S(2)}, u32[]{:S(2)}) collective-permute-start(bf16[112,384]{1,0:T(8,128)(2,1)S(1)} %pad_maximum_fusion.8), channel_id=1, source_target_pairs={{0,2},{1,3},{2,0},{3,1},{4,6},{5,7},{6,4},{7,5},{8,10},{9,11},{10,... | collective-permute-start | bytes 258056 | tf_op jit(solution)/shard_map/ppermute | solution.py:493
  139.5 8.8 %collective-permute-start.36 = (bf16[168,384]{1,0:T(8,128)(2,1)S(1)}, bf16[168,384]{1,0:T(8,128)(2,1)S(1)}, u32[]{:S(2)}, u32[]{:S(2)}) collective-permute-start(bf16[168,384]{1,0:T(8,128)(2,1)S(1)} %get-tuple-element.182), channel_id=1, source_target_pairs={{2,0},{0,1},{6,2},{4,3},{3,4},{1,5},{7,6},{5,7},{10,8},{8,9},{14,1... | collective-permute-start | bytes 387080 | tf_op jit(solution)/shard_map/ppermute | solution.py:480
  140.5 7.8 %collective-permute-start.35 = (bf16[168,384]{1,0:T(8,128)(2,1)S(1)}, bf16[168,384]{1,0:T(8,128)(2,1)S(1)}, u32[]{:S(2)}, u32[]{:S(2)}) collective-permute-start(bf16[168,384]{1,0:T(8,128)(2,1)S(1)} %get-tuple-element.183), channel_id=1, source_target_pairs={{0,0},{2,1},{4,2},{6,3},{1,4},{3,5},{5,6},{7,7},{8,8},{10,9},{12,1... | collective-permute-start | bytes 387080 | tf_op jit(solution)/shard_map/ppermute | solution.py:480

commit v5 on v4

--- a/solution.py
+++ b/solution.py
@@ -239,6 +239,32 @@
     c_ref[...] = fc2_ref[...]
 
 
+def finish_kernel(place_ref, body_ref, rest_ref, came_ref, qkv_ref, out_ref, *vector_refs):
+    rows, width = out_ref.shape[1:]
+    index = place_ref[3]
+    count = 4 * rows
+    summed = body_ref[...] + came_ref[:count, :].astype(F32)
+    vectors = rest_ref[...] + came_ref[count:, :].astype(F32)
+    for s in range(3):
+        qkv_ref[0, :, s * width : (s + 1) * width] = summed[s * rows : (s + 1) * rows]
+    out_ref[0] = summed[3 * rows :]
+    lane = lax.broadcasted_iota(jnp.int32, (8, width), 1)
+    row = lax.broadcasted_iota(jnp.int32, (16, width), 0)
+    base = 0
+    for ref, used in zip(vector_refs, (2, 6, 4)):
+        length = ref.shape[1]
+        first, offset = index * length // width, lax.rem(index * length, width)
+
+        def turned(which):
+            picked = total_of(jnp.where(row == which, vectors, 0.0))
+            picked = jnp.broadcast_to(picked, (8, width))
+            return pltpu.roll(picked, lax.rem(width - offset, width), 1)
+
+        whole = jnp.where(lane < width - offset, turned(base + first), turned(base + first + 1))
+        ref[...] = whole[:1, :length]
+        base += used
+
+
 def piece_groups(place_ref, mine, theirs, turns):
     outer, core, line = place_ref[0], place_ref[1], place_ref[2]
     count = mine[0].shape[0]
@@ -406,7 +432,7 @@
     )(*after, *[array for _, array in operands])
 
 
-def call_whole(kernel, operands, shapes):
+def call_whole(kernel, operands, shapes, flops):
     def block(shape):
         return pl.BlockSpec(shape, lambda i: (0,) * len(shape))
 
@@ -417,6 +443,7 @@
         in_specs=[pl.BlockSpec(memory_space=pltpu.SMEM)]
         + [block(operand.shape) for operand in operands[1:]],
         out_specs=[block(shape[0]) for shape in shapes],
+        cost_estimate=pl.CostEstimate(flops=flops, bytes_accessed=10**6, transcendentals=0),
     )(*operands)
 
 
@@ -712,27 +739,26 @@
             pack_kernel,
             [place, w_qkv[0], w_out[0], w_fc1[0], w_fc2[0], gains, shifts, fc1_bias],
             [((4 * rows + 16, width), BF16)] + [((4 * rows, width), BF16)] * 2,
+            10**9,
         )
     else:
         tail = vector_slots((gains[0], shifts[0], fc1_bias[0]), width)
         piece_a = jnp.concatenate([by_column(w_qkv[0], width), w_out[0], tail])
         piece_b, piece_c = by_column(w_fc1[0], width), w_fc2[0]
+    own_start = to_images(boundary[0, :, 0], at)
     piece_a, at = lax.optimization_barrier((piece_a, at))
     half_a = gather_step(piece_a[None], 0)
     near_c = jnp.stack(gather_outer(piece_c))
-    half_a, piece_b, near_c = lax.optimization_barrier((half_a, piece_b, near_c))
+    half_a, piece_b, near_c, own_start = lax.optimization_barrier(
+        (half_a, piece_b, near_c, own_start)
+    )
     line_a = gather_from(half_a, 1)
     half_b = gather_step(piece_b[None], 0)
-    line_a, half_b, near_c, blocks = lax.optimization_barrier(
-        (line_a, half_b, near_c, boundary[0, :, 0])
-    )
+    line_a, half_b, near_c = lax.optimization_barrier((line_a, half_b, near_c))
     mine_a = gather_outer(line_a)
     line_b = gather_from(half_b, 1)
     half_c = gather_step(near_c, 0)
-    own_start = to_images(blocks, at)
-    line_b, half_c, own_start, *mine_a = lax.optimization_barrier(
-        (line_b, half_c, own_start, *mine_a)
-    )
+    line_b, half_c, *mine_a = lax.optimization_barrier((line_b, half_c, *mine_a))
     mine_b = gather_outer(line_b)
     half_c = gather_from(half_c, 1, len(line_steps()) - 1)
     mine_c = [half_c, cross_line(half_c, line_steps()[-1])]
@@ -862,9 +888,7 @@
     state_b = halve_line(line_blocks(total_b, 4), at, 0)
     body_c = halve_rest(state_c, at, 1)[0].reshape(outer_count, -1, width)
     rows_last = jnp.where(at["first"], grad_in, layer_out)
-    total_a, state_b, body_c, rows_last = lax.optimization_barrier(
-        (total_a, state_b, body_c, rows_last)
-    )
+    total_a, state_b, body_c = lax.optimization_barrier((total_a, state_b, body_c))
     state_a = halve_line(line_blocks(total_a, 4, 16), at, 0)
     summed_b = halve_rest(state_b, at, 1)[0].reshape(-1, width)
     summed_c = scatter_outer(
@@ -872,17 +896,35 @@
         [pick(body_c, index, 0).astype(BF16) for index in at["outer"][1:]],
     )
     state_a, summed_b, summed_c = lax.optimization_barrier((state_a, summed_b, summed_c))
-    summed_a, summed_v = halve_rest(state_a, at, 1)
-    rows_out, summed_v = from_images(rows_last, at, summed_v)
-    summed_a = summed_a.reshape(-1, width)
-    grads = (
-        from_columns(summed_a[: 3 * rows], rows),
-        summed_a[3 * rows :],
-        from_columns(summed_b, rows),
-        summed_c,
-        *own_slots(summed_v, lens, at),
-    )
-    return (rows_out[None, :, None], *[member[None] for member in grads])
+    last = len(at["bits"]) - 1
+    for step in range(1, last):
+        state_a = halve_line(state_a, at, step)
+    (body, rest), sent_a = halve_parts(state_a, at, last)
+    sent_a, body, rows_last = lax.optimization_barrier((sent_a, body, rows_last))
+    if loose:
+        came = cross_line(sent_a, line_steps()[-1 - last])
+        finished = call_whole(
+            finish_kernel,
+            [place, body.reshape(-1, width), rest, came],
+            [((1, rows, 3 * width), F32), ((1, rows, width), F32)]
+            + [((1, length), F32) for length in lens],
+            10**10,
+        )
+        rows_out, _ = from_images(rows_last, at, came)
+    else:
+        summed_a, summed_v = halve_sum((body, rest), sent_a, last)
+        rows_out, summed_v = from_images(rows_last, at, summed_v)
+        summed_a = summed_a.reshape(-1, width)
+        finished = [
+            member[None]
+            for member in (
+                from_columns(summed_a[: 3 * rows], rows),
+                summed_a[3 * rows :],
+                *own_slots(summed_v, lens, at),
+            )
+        ]
+    grads = (*finished[:2], from_columns(summed_b, rows)[None], summed_c[None], *finished[2:])
+    return (rows_out[None, :, None], *grads)
 
 
 def solution(mesh):

time: 153 us -> 149 us (0.974)
  waiting for transfers between devices: 55 us -> 52.7 us
  local copies, waits for them, and re-layouts: 4.73 us -> 2.84 us
  Pallas kernels: 44.1 us -> 45.8 us
    broadcast_in_dim x3 -> x0, local copies, waits for them, and re-layouts: 1.79 us -> none  [on_device(): return (rows_out[None, :, None], *[member[None] for member in grads])]
    pallas_call x1 -> x2, Pallas kernels: 1.74 us -> 3.48 us  [call_whole(): pl.pallas_call(kernel, grid=(1,), out_shape=[jax.ShapeDtypeStruct(*shape)...]
  transfers between devices with their start and end apart: 37 -> 37, of which waited for: 23 -> 22; matrix products, arithmetic and copies ran while one was open for 5% -> 4% of each run, Pallas kernels for 11% -> 14%
where the time goes in v5:
time: 149 us; the launch traced here: 148 us
  waiting for transfers between devices  52.7 us (35%)
  Pallas kernels  45.8 us (31%)
  starting transfers between devices  40.3 us (27%)
  other arithmetic  5.44 us (4%)
  local copies, waits for them, and re-layouts  2.84 us (2%)
    pallas_call x6, Pallas kernels, call(): pl.pallas_call(body, out_shape=[jax.ShapeDtypeStruct(*result) for result...  42.3 us
    ppermute x12, waiting for transfers between devices, cross_line(): return lax.ppermute(value, 'seq', [(z, z ^ distance) for z in range(count)])  28.6 us
    ppermute x12, starting transfers between devices, cross_line(): return lax.ppermute(value, 'seq', [(z, z ^ distance) for z in range(count)])  19.3 us
    ppermute x2, waiting for transfers between devices, to_section(): return lax.ppermute(value, 'section', [(0, 1)] if steps == 1 else [(1, 0)])  11.1 us
    ppermute x6, starting transfers between devices, turn_outer(): lax.ppermute(value, 'dp', [(d, (d + 2 * steps) % count) for d in range(co...  7.26 us
    ppermute x8, starting transfers between devices, joint_permute(): return lax.ppermute(value, ('dp', 'seq'), pairs)  6.58 us
    ppermute x9, waiting for transfers between devices, swap_core(): lax.ppermute(value, 'dp', [(d, d ^ 1) for d in range(lax.axis_size('dp'))])  5.77 us
    ppermute x2, starting transfers between devices, to_section(): return lax.ppermute(value, 'section', [(0, 1)] if steps == 1 else [(1, 0)])  4.88 us
  transfers between devices with their start and end apart: 37, of which 22 were waited for; matrix products, arithmetic and copies ran while one was open for 4% of the time, Pallas kernels for 14%

profile of v5, /device:TPU:0, one launch (start us, length us, event | category | flops | bytes accessed | tf_op | source)
XLA Modules:
  0.0 148.2 jit_solution(17710362435918485496)
XLA Ops:
  0.6 0.5 collective-permute-start.10
  1.1 0.7 pad_add_fusion.place_ref.refs_1_.refs_0_.refs_2_
  1.8 1.8 %shard_map.152 = (bf16[112,384]{1,0:T(8,128)(2,1)}, bf16[96,384]{1,0:T(8,128)(2,1)}, bf16[96,384]{1,0:T(8,128)(2,1)}) custom-call(s32[4]{0:T(128)} %pad_add_fusion.place_ref.refs_1_.refs_0_.refs_2_, bf16[24,1152]{1,0:T(8,128)(2,1)} %bitcast.108, bf16[24,384]{1,0:T(8,128)(2,1)} %bitcast.109, bf16[24,1536]{1,0:T(8,128)(2,1)} %bitcast.106, ...), custom_call_target="tpu_custom_call" | custom-call | flops 1000000000 | bytes 1000000 | tf_op jit(solution)/shard_map/pallas_call | solution.py:439
  3.6 2.6 %collective-permute-start.1 = (bf16[96,384]{1,0:T(8,128)(2,1)}, bf16[96,384]{1,0:T(8,128)(2,1)S(1)}, u32[]{:S(2)}, u32[]{:S(2)}) collective-permute-start(bf16[96,384]{1,0:T(8,128)(2,1)} %get-tuple-element.89), channel_id=1, source_target_pairs={{0,8},{4,12},{8,0},{12,4},{1,9},{5,13},{9,1},{13,5},{2,10},{6,14},... | collective-permute-start | bytes 221192 | tf_op jit(solution)/shard_map/ppermute | solution.py:496
  6.2 2.6 %collective-permute-start = (bf16[1,112,384]{2,1,0:T(8,128)(2,1)}, bf16[1,112,384]{2,1,0:T(8,128)(2,1)S(1)}, u32[]{:S(2)}, u32[]{:S(2)}) collective-permute-start(bf16[1,112,384]{2,1,0:T(8,128)(2,1)} %bitcast.96), channel_id=1, source_target_pairs={{0,2},{1,3},{2,0},{3,1},{4,6},{5,7},{6,4},{7,5},{8,10},{9,11},{10,... | collective-permute-start | bytes 258056 | tf_op jit(solution)/shard_map/ppermute | solution.py:520
  8.9 0.7 collective-permute-start.2
  9.5 3.7 %collective-permute-start.3 = (bf16[168,384]{1,0:T(8,128)(2,1)S(1)}, bf16[168,384]{1,0:T(8,128)(2,1)S(1)}, u32[]{:S(2)}, u32[]{:S(2)}) collective-permute-start(bf16[168,384]{1,0:T(8,128)(2,1)S(1)} %get-tuple-element.191), channel_id=1, source_target_pairs={{0,2},{1,0},{2,6},{3,4},{4,3},{5,1},{6,7},{7,5},{8,10},{9,8},{10,1... | collective-permute-start | bytes 387080 | tf_op jit(solution)/shard_map/ppermute | solution.py:507
  13.3 0.9 pad_maximum_fusion.6
  14.2 0.9 pad_maximum_fusion.4
  15.1 1.9 %collective-permute-done.3 = bf16[168,384]{1,0:T(8,128)(2,1)S(1)} collective-permute-done((bf16[168,384]{1,0:T(8,128)(2,1)S(1)}, bf16[168,384]{1,0:T(8,128)(2,1)S(1)}, u32[]{:S(2)}, u32[]{:S(2)}) %collective-permute-start.3) | collective-permute-done | bytes 129056 | tf_op jit(solution)/shard_map/ppermute | solution.py:507
  17.1 5.0 %collective-permute-start.6 = (bf16[1,96,384]{2,1,0:T(8,128)(2,1)S(1)}, bf16[1,96,384]{2,1,0:T(8,128)(2,1)S(1)}, u32[]{:S(2)}, u32[]{:S(2)}) collective-permute-start(bf16[1,96,384]{2,1,0:T(8,128)(2,1)S(1)} %bitcast.99), channel_id=1, source_target_pairs={{0,2},{1,3},{2,0},{3,1},{4,6},{5,7},{6,4},{7,5},{8,10},{9,11},{10,... | collective-permute-start | bytes 221192 | tf_op jit(solution)/shard_map/ppermute | solution.py:520
  22.1 1.4 collective-permute-start.5
  23.5 2.8 %collective-permute-done.6 = bf16[1,96,384]{2,1,0:T(8,128)(2,1)S(1)} collective-permute-done((bf16[1,96,384]{2,1,0:T(8,128)(2,1)S(1)}, bf16[1,96,384]{2,1,0:T(8,128)(2,1)S(1)}, u32[]{:S(2)}, u32[]{:S(2)}) %collective-permute-start.6) | collective-permute-done | bytes 73760 | tf_op jit(solution)/shard_map/ppermute | solution.py:520
  26.3 1.6 %collective-permute-done.5 = bf16[2,112,384]{2,1,0:T(8,128)(2,1)S(1)} collective-permute-done((bf16[2,112,384]{2,1,0:T(8,128)(2,1)S(1)}, bf16[2,112,384]{2,1,0:T(8,128)(2,1)S(1)}, u32[]{:S(2)}, u32[]{:S(2)}) %collective-permute-start.5) | collective-permute-done | bytes 172064 | tf_op jit(solution)/shard_map/ppermute | solution.py:520
  28.0 1.0 collective-permute-start.7
  29.0 1.4 collective-permute-start.8
  30.4 0.5 collective-permute-start.9
  31.0 3.3 %collective-permute-done.7 = bf16[2,96,384]{2,1,0:T(8,128)(2,1)S(1)} collective-permute-done((bf16[2,96,384]{2,1,0:T(8,128)(2,1)S(1)}, bf16[2,96,384]{2,1,0:T(8,128)(2,1)S(1)}, u32[]{:S(2)}, u32[]{:S(2)}) %collective-permute-start.7) | collective-permute-done | bytes 147488 | tf_op jit(solution)/shard_map/ppermute | solution.py:520
  34.3 3.3 %collective-permute-done.8 = bf16[2,96,384]{2,1,0:T(8,128)(2,1)S(1)} collective-permute-done((bf16[2,96,384]{2,1,0:T(8,128)(2,1)S(1)}, bf16[2,96,384]{2,1,0:T(8,128)(2,1)S(1)}, u32[]{:S(2)}, u32[]{:S(2)}) %collective-permute-start.8) | collective-permute-done | bytes 147488 | tf_op jit(solution)/shard_map/ppermute | solution.py:520
  37.7 1.0 collective-permute-done.9.refs_5_
  38.7 0.5 collective-permute-start.12
  39.5 1.7 %collective-permute-start.13 = (bf16[4,96,384]{2,1,0:T(8,128)(2,1)S(1)}, bf16[4,96,384]{2,1,0:T(8,128)(2,1)S(1)}, u32[]{:S(2)}, u32[]{:S(2)}) collective-permute-start(bf16[4,96,384]{2,1,0:T(8,128)(2,1)S(1)} %pad_maximum_fusion.2.refs_8_), channel_id=1, source_target_pairs={{0,1},{1,0},{2,3},{3,2},{4,5},{5,4},{6,7},{7,6},{8,9},{9,8},{10,11... | collective-permute-start | bytes 884744 | tf_op jit(solution)/shard_map/ppermute | solution.py:520
  41.2 0.5 collective-permute-start.14
  41.9 0.5 collective-permute-start.15
  42.6 6.0 %shard_map.153 = (f32[336,384]{1,0:T(8,128)S(1)}, bf16[4,384,384]{2,1,0:T(8,128)(2,1)S(1)}, f32[16,384]{1,0:T(8,128)S(1)}) custom-call(bf16[4,96,384]{2,1,0:T(8,128)(2,1)S(1)} %pad_maximum_fusion.1.refs_0_.refs_4_, s32[4]{0:T(128)S(1)} %copy-done, bf16[672,384]{1,0:T(8,128)(2,1)S(1)} %constant_dynamic-update-slice_fusion.refs_2_, ...), custom_call_target="tpu_custom_call" | custom-call | flops 1000000000 | bytes 4000000 | tf_op jit(solution)/shard_map/pallas_call | solution.py:423
  48.6 1.2 collective-permute-done.14.refs_5_
  49.9 0.5 collective-permute-start.18
  50.4 1.1 collective-permute-done.16.refs_7_
  51.9 3.7 %shard_map.154 = (bf16[336,384]{1,0:T(8,128)(2,1)S(1)}, bf16[4,384,384]{2,1,0:T(8,128)(2,1)S(1)}, bf16[1536,384]{1,0:T(8,128)(2,1)S(1)}) custom-call(s32[4]{0:T(128)S(1)} %copy-done, f32[336,384]{1,0:T(8,128)S(1)} %get-tuple-element.102.refs_1_, f32[672,128]{1,0:T(8,128)S(1)} %broadcast_in_dim.30.refs_3_.refs_2_.refs_1_.refs_4_.refs_12_, ...), custom_call_target="tpu_custom_call" | custom-call | flops 1000000000 | bytes 4000000 | tf_op jit(solution)/shard_map/pallas_call | solution.py:423
  55.6 3.6 %collective-permute-start.19 = (bf16[336,384]{1,0:T(8,128)(2,1)S(1)}, bf16[336,384]{1,0:T(8,128)(2,1)S(1)}, u32[]{:S(2)}, u32[]{:S(2)}) collective-permute-start(bf16[336,384]{1,0:T(8,128)(2,1)S(1)} %get-tuple-element.106), channel_id=1, source_target_pairs={{0,16},{1,17},{2,18},{3,19},{4,20},{5,21},{6,22},{7,23},{8,24},{9,... | collective-permute-start | bytes 774152 | tf_op jit(solution)/shard_map/ppermute | solution.py:688
  59.2 5.6 %collective-permute-done.19 = bf16[336,384]{1,0:T(8,128)(2,1)S(1)} collective-permute-done((bf16[336,384]{1,0:T(8,128)(2,1)S(1)}, bf16[336,384]{1,0:T(8,128)(2,1)S(1)}, u32[]{:S(2)}, u32[]{:S(2)}) %collective-permute-start.19) | collective-permute-done | bytes 258080 | tf_op jit(solution)/shard_map/ppermute | solution.py:688
  64.7 1.5 %collective-permute-done.20 = bf16[336,384]{1,0:T(8,128)(2,1)S(1)} collective-permute-done((bf16[336,384]{1,0:T(8,128)(2,1)S(1)}, bf16[336,384]{1,0:T(8,128)(2,1)S(1)}, u32[]{:S(2)}, u32[]{:S(2)}) %collective-permute-start.20) | collective-permute-done | bytes 258080 | tf_op jit(solution)/shard_map/ppermute | solution.py:507
  66.4 16.0 %shard_map.155 = (bf16[672,384]{1,0:T(8,128)(2,1)S(1)}, f32[336,384]{1,0:T(8,128)S(1)}, bf16[336,384]{1,0:T(8,128)(2,1)S(1)}, bf16[3,336,128]{2,1,0:T(8,128)(2,1...) custom-call(bf16[672,384]{1,0:T(8,128)(2,1)S(1)} %maximum_select_fus, ...), custom_call_target="tpu_custom_call" | custom-call | flops 4000000000 | bytes 4000000 | tf_op jit(solution)/shard_map/pallas_call | solution.py:423
  82.6 1.4 collective-permute-done.21
  84.1 1.3 collective-permute-start.22
  85.4 3.4 %shard_map.156 = (bf16[336,384]{1,0:T(8,128)(2,1)S(1)}, bf16[4,336,384]{2,1,0:T(8,128)(2,1)S(1)}, f32[4,336,384]{2,1,0:T(8,128)S(1)}) custom-call(bf16[336,384]{1,0:T(8,128)(2,1)S(1)} %add_convert_fusion.3.refs_0_, f32[336,384]{1,0:T(8,128)S(1)} %get-tuple-element.111.refs_1_.refs_2_, ...), custom_call_target="tpu_custom_call" | custom-call | flops 2000000000 | bytes 4000000 | tf_op jit(solution)/shard_map/pallas_call | solution.py:423
  88.8 5.5 %collective-permute-done.22 = bf16[336,384]{1,0:T(8,128)(2,1)S(1)} collective-permute-done((bf16[336,384]{1,0:T(8,128)(2,1)S(1)}, bf16[336,384]{1,0:T(8,128)(2,1)S(1)}, u32[]{:S(2)}, u32[]{:S(2)}) %collective-permute-start.22) | collective-permute-done | bytes 258080 | tf_op jit(solution)/shard_map/ppermute | solution.py:688
  94.4 5.5 %shard_map.157 = (bf16[2,768,384]{2,1,0:T(8,128)(2,1)S(1)}, bf16[2,768,384]{2,1,0:T(8,128)(2,1)S(1)}, f32[336,384]{1,0:T(8,128)S(1)}, f32[16,384]{1,0:T(8,128)S(1)}) custom-call(s32[4]{0:T(128)S(1)} %copy-done, bf16[336,384]{1,0:T(8,128)(2,1)S(1)} %broadcast_select_fusion.refs_1_, f32[336,384]{1,0:T(8,128)S(1)} %get-tuple-element.111.refs_1_.refs_2_, ...), custom_call_target="tpu_custom_call" | custom-call | flops 2000000000 | bytes 4000000 | tf_op jit(solution)/shard_map/pallas_call | solution.py:423
  99.9 2.8 %collective-permute-done.23 = bf16[2,768,384]{2,1,0:T(8,128)(2,1)S(1)} collective-permute-done((bf16[2,768,384]{2,1,0:T(8,128)(2,1)S(1)}, bf16[2,768,384]{2,1,0:T(8,128)(2,1)S(1)}, u32[]{:S(2)}, u32[]{:S(2)}) %collective-permute-start.23) | collective-permute-done | bytes 1179680 | tf_op jit(solution)/shard_map/ppermute | solution.py:491
  102.9 0.6 collective-permute-start.24
  104.1 7.8 %shard_map.158 = (bf16[672,384]{1,0:T(8,128)(2,1)S(1)}, bf16[2,400,384]{2,1,0:T(8,128)(2,1)S(1)}, bf16[2,400,384]{2,1,0:T(8,128)(2,1)S(1)}) custom-call(bf16[384,384]{1,0:T(8,128)(2,1)S(1)} %fusion.1.refs_0_, bf16[384,384]{1,0:T(8,128)(2,1)S(1)} %bitcast.78, s32[4]{0:T(128)S(1)} %copy-done, f32[336,384]{1,0:T(8,128)S(1)} %get-tuple-element.119.refs_3_, ...), custom_call_target="tpu_custom_call" | custom-call | flops 10000000000 | bytes 4000000 | tf_op jit(solution)/shard_map/pallas_call | solution.py:423
  111.9 0.6 collective-permute-done.25
  112.8 0.6 collective-permute-start.33
  113.3 1.4 collective-permute-done.26
  114.9 1.1 collective-permute-start.28
  116.1 0.6 collective-permute-start.29
  116.8 1.5 %collective-permute-start.27 = (bf16[400,384]{1,0:T(8,128)(2,1)S(1)}, bf16[400,384]{1,0:T(8,128)(2,1)S(1)}, u32[]{:S(2)}, u32[]{:S(2)}) collective-permute-start(bf16[400,384]{1,0:T(8,128)(2,1)S(1)} %fusion), channel_id=1, source_target_pairs={{0,8},{4,12},{8,0},{12,4},{1,9},{5,13},{9,1},{13,5},{2,10},{6,14},... | collective-permute-start | bytes 921608 | tf_op jit(solution)/shard_map/ppermute | solution.py:496
  118.3 3.9 %collective-permute-done.28 = bf16[192,384]{1,0:T(8,128)(2,1)S(1)} collective-permute-done((bf16[192,384]{1,0:T(8,128)(2,1)S(1)}, bf16[192,384]{1,0:T(8,128)(2,1)S(1)}, u32[]{:S(2)}, u32[]{:S(2)}) %collective-permute-start.28) | collective-permute-done | bytes 147488 | tf_op jit(solution)/shard_map/ppermute | solution.py:520
  122.2 3.6 %collective-permute-done.29 = bf16[192,384]{1,0:T(8,128)(2,1)S(1)} collective-permute-done((bf16[192,384]{1,0:T(8,128)(2,1)S(1)}, bf16[192,384]{1,0:T(8,128)(2,1)S(1)}, u32[]{:S(2)}, u32[]{:S(2)}) %collective-permute-start.29) | collective-permute-done | bytes 147488 | tf_op jit(solution)/shard_map/ppermute | solution.py:520
  126.2 2.0 %collective-permute-start.31 = (bf16[96,384]{1,0:T(8,128)(2,1)S(1)}, bf16[96,384]{1,0:T(8,128)(2,1)S(1)}, u32[]{:S(2)}, u32[]{:S(2)}) collective-permute-start(bf16[96,384]{1,0:T(8,128)(2,1)S(1)} %bitcast.98), channel_id=1, source_target_pairs={{0,2},{1,3},{2,0},{3,1},{4,6},{5,7},{6,4},{7,5},{8,10},{9,11},{10,... | collective-permute-start | bytes 221192 | tf_op jit(solution)/shard_map/ppermute | solution.py:520
  128.2 1.5 %collective-permute-start.32 = (bf16[96,384]{1,0:T(8,128)(2,1)S(1)}, bf16[96,384]{1,0:T(8,128)(2,1)S(1)}, u32[]{:S(2)}, u32[]{:S(2)}) collective-permute-start(bf16[96,384]{1,0:T(8,128)(2,1)S(1)} %fusion.4), channel_id=1, source_target_pairs={{0,8},{4,12},{8,0},{12,4},{1,9},{5,13},{9,1},{13,5},{2,10},{6,14},... | collective-permute-start | bytes 221192 | tf_op jit(solution)/shard_map/ppermute | solution.py:496
  129.8 1.0 collective-permute-start.30
  130.8 1.6 %collective-permute-done.31 = bf16[96,384]{1,0:T(8,128)(2,1)S(1)} collective-permute-done((bf16[96,384]{1,0:T(8,128)(2,1)S(1)}, bf16[96,384]{1,0:T(8,128)(2,1)S(1)}, u32[]{:S(2)}, u32[]{:S(2)}) %collective-permute-start.31) | collective-permute-done | bytes 73760 | tf_op jit(solution)/shard_map/ppermute | solution.py:520
  132.5 0.7 bitcast_add_fusion.5
  133.2 1.9 %collective-permute-done.30 = bf16[208,384]{1,0:T(8,128)(2,1)S(1)} collective-permute-done((bf16[208,384]{1,0:T(8,128)(2,1)S(1)}, bf16[208,384]{1,0:T(8,128)(2,1)S(1)}, u32[]{:S(2)}, u32[]{:S(2)}) %collective-permute-start.30) | collective-permute-done | bytes 159776 | tf_op jit(solution)/shard_map/ppermute | solution.py:520
  135.2 0.7 constant_dynamic-slice_fusion
  135.9 1.0 collective-permute-start.34
  137.1 0.7 broadcast_in_dim_reshape.3
  137.8 0.8 collective-permute-start.36
  138.5 0.7 collective-permute-start.35
  139.2 5.9 %collective-permute-done.34.came_ref = bf16[112,384]{1,0:T(8,128)(2,1)S(1)} collective-permute-done((bf16[112,384]{1,0:T(8,128)(2,1)S(1)}, bf16[112,384]{1,0:T(8,128)(2,1)S(1)}, u32[]{:S(2)}, u32[]{:S(2)}) %collective-permute-start.34) | collective-permute-done | bytes 86048 | tf_op jit(solution)/shard_map/ppermute | solution.py:520
  145.1 0.6 copy-done.5
  145.7 1.7 %shard_map.159 = (f32[1,24,1152]{2,1,0:T(8,128)}, f32[1,24,384]{2,1,0:T(8,128)}, f32[1,48]{1,0:T(1,128)}, f32[1,144]{1,0:T(1,128)}, f32[1,96]{1,0:T(1,128)}) custom-call(s32[4]{0:T(128)} %pad_add_fusion.place_ref.refs_1_.refs_0_.refs_2_, f32[96,384]{1,0:T(8,128)} %bitcast.93, f32[16,384]{1,0:T(8,128)} %copy-done.2, bf16[112,384]{1,0:T(8,128)(2,1)} %copy-done.5), custom_call_target="tpu_custom_call" | custom-call | flops 10000000000 | bytes 1000000 | tf_op jit(solution)/shard_map/pallas_call | solution.py:439
  147.5 0.7 maximum_bitcast_fusion
  (88 shorter events, 3.8 us)
Async XLA Ops:
  0.6 22.8 %collective-permute-start.10 = (s32[2,4]{1,0:T(2,128)}, s32[2,4]{1,0:T(2,128)S(1)}, u32[]{:S(2)}, u32[]{:S(2)}) collective-permute-start(s32[2,4]{1,0:T(2,128)} %bitcast.104), channel_id=1, source_target_pairs={{0,4},{4,0},{8,12},{12,8},{1,5},{5,1},{9,13},{13,9},{2,6},{6,2},{1... | collective-permute-start | bytes 104 | tf_op jit(solution)/shard_map/ppermute | solution.py:491
  1.8 7.0 %copy-start.1 = (bf16[1,2,1,168,384]{4,3,2,1,0:T(8,128)(2,1)S(1)}, bf16[1,2,1,168,384]{4,3,2,1,0:T(8,128)(2,1)}, u32[]{:S(2)}) copy-start(bf16[1,2,1,168,384]{4,3,2,1,0:T(8,128)(2,1)} %param.9) | copy-start | bytes 774148
  3.6 13.5 %copy-start.3 = (bf16[96,384]{1,0:T(8,128)(2,1)S(1)}, bf16[96,384]{1,0:T(8,128)(2,1)}, u32[]{:S(2)}) copy-start(bf16[96,384]{1,0:T(8,128)(2,1)} %get-tuple-element.92) | copy-start | bytes 221188
  3.6 19.9 %copy-start.4 = (s32[2,1,4]{2,1,0:T(1,128)S(1)}, s32[2,1,4]{2,1,0:T(1,128)}, u32[]{:S(2)}) copy-start(s32[2,1,4]{2,1,0:T(1,128)} %param.10) | copy-start | bytes 100
  3.6 9.7 %collective-permute-start.1 = (bf16[96,384]{1,0:T(8,128)(2,1)}, bf16[96,384]{1,0:T(8,128)(2,1)S(1)}, u32[]{:S(2)}, u32[]{:S(2)}) collective-permute-start(bf16[96,384]{1,0:T(8,128)(2,1)} %get-tuple-element.89), channel_id=1, source_target_pairs={{0,8},{4,12},{8,0},{12,4},{1,9},{5,13},{9,1},{13,5},{2,10},{6,14},... | collective-permute-start | bytes 221192 | tf_op jit(solution)/shard_map/ppermute | solution.py:496
  6.2 7.9 %collective-permute-start = (bf16[1,112,384]{2,1,0:T(8,128)(2,1)}, bf16[1,112,384]{2,1,0:T(8,128)(2,1)S(1)}, u32[]{:S(2)}, u32[]{:S(2)}) collective-permute-start(bf16[1,112,384]{2,1,0:T(8,128)(2,1)} %bitcast.96), channel_id=1, source_target_pairs={{0,2},{1,3},{2,0},{3,1},{4,6},{5,7},{6,4},{7,5},{8,10},{9,11},{10,... | collective-permute-start | bytes 258056 | tf_op jit(solution)/shard_map/ppermute | solution.py:520
  8.9 6.2 %collective-permute-start.2 = (bf16[168,384]{1,0:T(8,128)(2,1)S(1)}, bf16[168,384]{1,0:T(8,128)(2,1)S(1)}, u32[]{:S(2)}, u32[]{:S(2)}) collective-permute-start(bf16[168,384]{1,0:T(8,128)(2,1)S(1)} %get-tuple-element.190), channel_id=1, source_target_pairs={{0,0},{1,2},{2,4},{3,6},{4,1},{5,3},{6,5},{7,7},{8,8},{9,10},{10,1... | collective-permute-start | bytes 387080 | tf_op jit(solution)/shard_map/ppermute | solution.py:507
  9.5 7.5 %collective-permute-start.3 = (bf16[168,384]{1,0:T(8,128)(2,1)S(1)}, bf16[168,384]{1,0:T(8,128)(2,1)S(1)}, u32[]{:S(2)}, u32[]{:S(2)}) collective-permute-start(bf16[168,384]{1,0:T(8,128)(2,1)S(1)} %get-tuple-element.191), channel_id=1, source_target_pairs={{0,2},{1,0},{2,6},{3,4},{4,3},{5,1},{6,7},{7,5},{8,10},{9,8},{10,1... | collective-permute-start | bytes 387080 | tf_op jit(solution)/shard_map/ppermute | solution.py:507
  17.1 9.2 %collective-permute-start.6 = (bf16[1,96,384]{2,1,0:T(8,128)(2,1)S(1)}, bf16[1,96,384]{2,1,0:T(8,128)(2,1)S(1)}, u32[]{:S(2)}, u32[]{:S(2)}) collective-permute-start(bf16[1,96,384]{2,1,0:T(8,128)(2,1)S(1)} %bitcast.99), channel_id=1, source_target_pairs={{0,2},{1,3},{2,0},{3,1},{4,6},{5,7},{6,4},{7,5},{8,10},{9,11},{10,... | collective-permute-start | bytes 221192 | tf_op jit(solution)/shard_map/ppermute | solution.py:520
  22.1 5.9 %collective-permute-start.5 = (bf16[2,112,384]{2,1,0:T(8,128)(2,1)S(1)}, bf16[2,112,384]{2,1,0:T(8,128)(2,1)S(1)}, u32[]{:S(2)}, u32[]{:S(2)}) collective-permute-start(bf16[2,112,384]{2,1,0:T(8,128)(2,1)S(1)} %pad_maximum_fusion.4), channel_id=1, source_target_pairs={{0,1},{1,0},{2,3},{3,2},{4,5},{5,4},{6,7},{7,6},{8,9},{9,8},{10,11... | collective-permute-start | bytes 516104 | tf_op jit(solution)/shard_map/ppermute | solution.py:520
  28.0 6.3 %collective-permute-start.7 = (bf16[2,96,384]{2,1,0:T(8,128)(2,1)S(1)}, bf16[2,96,384]{2,1,0:T(8,128)(2,1)S(1)}, u32[]{:S(2)}, u32[]{:S(2)}) collective-permute-start(bf16[2,96,384]{2,1,0:T(8,128)(2,1)S(1)} %pad_maximum_fusion.7), channel_id=1, source_target_pairs={{0,1},{1,0},{2,3},{3,2},{4,5},{5,4},{6,7},{7,6},{8,9},{9,8},{10,11... | collective-permute-start | bytes 442376 | tf_op jit(solution)/shard_map/ppermute | solution.py:520
  29.0 8.7 %collective-permute-start.8 = (bf16[2,96,384]{2,1,0:T(8,128)(2,1)S(1)}, bf16[2,96,384]{2,1,0:T(8,128)(2,1)S(1)}, u32[]{:S(2)}, u32[]{:S(2)}) collective-permute-start(bf16[2,96,384]{2,1,0:T(8,128)(2,1)S(1)} %pad_maximum_fusion.6), channel_id=1, source_target_pairs={{0,2},{1,3},{2,0},{3,1},{4,6},{5,7},{6,4},{7,5},{8,10},{9,11},{10,... | collective-permute-start | bytes 442376 | tf_op jit(solution)/shard_map/ppermute | solution.py:520
  30.4 8.3 %collective-permute-start.9 = (bf16[4,112,384]{2,1,0:T(8,128)(2,1)S(1)}, bf16[4,112,384]{2,1,0:T(8,128)(2,1)S(1)}, u32[]{:S(2)}, u32[]{:S(2)}) collective-permute-start(bf16[4,112,384]{2,1,0:T(8,128)(2,1)S(1)} %pad_maximum_fusion.refs_4_), channel_id=1, source_target_pairs={{0,8},{4,12},{8,0},{12,4},{1,9},{5,13},{9,1},{13,5},{2,10},{6,14},... | collective-permute-start | bytes 1032200 | tf_op jit(solution)/shard_map/ppermute | solution.py:496
  30.9 11.6 %copy-start = (s32[4]{0:T(128)S(1)}, s32[4]{0:T(128)}, u32[]{:S(2)}) copy-start(s32[4]{0:T(128)} %pad_add_fusion.place_ref.refs_1_.refs_0_.refs_2_) | copy-start | bytes 52
  30.9 10.9 %collective-permute-start.4 = (bf16[336,384]{1,0:T(8,128)(2,1)S(1)}, bf16[336,384]{1,0:T(8,128)(2,1)S(1)}, u32[]{:S(2)}, u32[]{:S(2)}) collective-permute-start(bf16[336,384]{1,0:T(8,128)(2,1)S(1)} %pad_maximum_fusion.3.refs_6_), channel_id=1, source_target_pairs={{4,0},{5,1},{6,2},{7,3},{0,4},{1,5},{2,6},{3,7},{12,8},{13,9},{14,... | collective-permute-start | bytes 774152 | tf_op jit(solution)/shard_map/ppermute | solution.py:507
  38.7 3.3 %collective-permute-start.11 = (bf16[4,112,384]{2,1,0:T(8,128)(2,1)S(1)}, bf16[4,112,384]{2,1,0:T(8,128)(2,1)S(1)}, u32[]{:S(2)}, u32[]{:S(2)}) collective-permute-start(bf16[4,112,384]{2,1,0:T(8,128)(2,1)S(1)} %pad_maximum_fusion.refs_4_), channel_id=1, source_target_pairs={{0,4},{4,0},{8,12},{12,8},{1,5},{5,1},{9,13},{13,9},{2,6},{6,2},{1... | collective-permute-start | bytes 1032200 | tf_op jit(solution)/shard_map/ppermute | solution.py:491
  38.7 3.8 %collective-permute-start.12 = (bf16[4,112,384]{2,1,0:T(8,128)(2,1)S(1)}, bf16[4,112,384]{2,1,0:T(8,128)(2,1)S(1)}, u32[]{:S(2)}, u32[]{:S(2)}) collective-permute-start(bf16[4,112,384]{2,1,0:T(8,128)(2,1)S(1)} %collective-permute-done.9.refs_5_), channel_id=1, source_target_pairs={{0,4},{4,0},{8,12},{12,8},{1,5},{5,1},{9,13},{13,9},{2,6},{6,2},{1... | collective-permute-start | bytes 1032200 | tf_op jit(solution)/shard_map/ppermute | solution.py:491
  39.5 9.1 %collective-permute-start.13 = (bf16[4,96,384]{2,1,0:T(8,128)(2,1)S(1)}, bf16[4,96,384]{2,1,0:T(8,128)(2,1)S(1)}, u32[]{:S(2)}, u32[]{:S(2)}) collective-permute-start(bf16[4,96,384]{2,1,0:T(8,128)(2,1)S(1)} %pad_maximum_fusion.2.refs_8_), channel_id=1, source_target_pairs={{0,1},{1,0},{2,3},{3,2},{4,5},{5,4},{6,7},{7,6},{8,9},{9,8},{10,11... | collective-permute-start | bytes 884744 | tf_op jit(solution)/shard_map/ppermute | solution.py:520
  41.2 8.6 %collective-permute-start.14 = (bf16[4,96,384]{2,1,0:T(8,128)(2,1)S(1)}, bf16[4,96,384]{2,1,0:T(8,128)(2,1)S(1)}, u32[]{:S(2)}, u32[]{:S(2)}) collective-permute-start(bf16[4,96,384]{2,1,0:T(8,128)(2,1)S(1)} %pad_maximum_fusion.1.refs_0_.refs_4_), channel_id=1, source_target_pairs={{0,8},{4,12},{8,0},{12,4},{1,9},{5,13},{9,1},{13,5},{2,10},{6,14},... | collective-permute-start | bytes 884744 | tf_op jit(solution)/shard_map/ppermute | solution.py:496
  41.8 8.6 %collective-permute-start.17 = (bf16[4,96,384]{2,1,0:T(8,128)(2,1)S(1)}, bf16[4,96,384]{2,1,0:T(8,128)(2,1)S(1)}, u32[]{:S(2)}, u32[]{:S(2)}) collective-permute-start(bf16[4,96,384]{2,1,0:T(8,128)(2,1)S(1)} %pad_maximum_fusion.2.refs_8_), channel_id=1, source_target_pairs={{0,4},{4,0},{8,12},{12,8},{1,5},{5,1},{9,13},{13,9},{2,6},{6,2},{1... | collective-permute-start | bytes 884744 | tf_op jit(solution)/shard_map/ppermute | solution.py:491
  41.9 8.5 %collective-permute-start.15 = (bf16[4,96,384]{2,1,0:T(8,128)(2,1)S(1)}, bf16[4,96,384]{2,1,0:T(8,128)(2,1)S(1)}, u32[]{:S(2)}, u32[]{:S(2)}) collective-permute-start(bf16[4,96,384]{2,1,0:T(8,128)(2,1)S(1)} %pad_maximum_fusion.1.refs_0_.refs_4_), channel_id=1, source_target_pairs={{0,4},{4,0},{8,12},{12,8},{1,5},{5,1},{9,13},{13,9},{2,6},{6,2},{1... | collective-permute-start | bytes 884744 | tf_op jit(solution)/shard_map/ppermute | solution.py:491
  49.9 1.6 %collective-permute-start.16 = (bf16[4,96,384]{2,1,0:T(8,128)(2,1)S(1)}, bf16[4,96,384]{2,1,0:T(8,128)(2,1)S(1)}, u32[]{:S(2)}, u32[]{:S(2)}) collective-permute-start(bf16[4,96,384]{2,1,0:T(8,128)(2,1)S(1)} %collective-permute-done.14.refs_5_), channel_id=1, source_target_pairs={{0,4},{4,0},{8,12},{12,8},{1,5},{5,1},{9,13},{13,9},{2,6},{6,2},{1... | collective-permute-start | bytes 884744 | tf_op jit(solution)/shard_map/ppermute | solution.py:491
  49.9 2.0 %collective-permute-start.18 = (bf16[4,96,384]{2,1,0:T(8,128)(2,1)S(1)}, bf16[4,96,384]{2,1,0:T(8,128)(2,1)S(1)}, u32[]{:S(2)}, u32[]{:S(2)}) collective-permute-start(bf16[4,96,384]{2,1,0:T(8,128)(2,1)S(1)} %collective-permute-done.13.refs_9_), channel_id=1, source_target_pairs={{0,4},{4,0},{8,12},{12,8},{1,5},{5,1},{9,13},{13,9},{2,6},{6,2},{1... | collective-permute-start | bytes 884744 | tf_op jit(solution)/shard_map/ppermute | solution.py:491
  55.6 9.2 %collective-permute-start.19 = (bf16[336,384]{1,0:T(8,128)(2,1)S(1)}, bf16[336,384]{1,0:T(8,128)(2,1)S(1)}, u32[]{:S(2)}, u32[]{:S(2)}) collective-permute-start(bf16[336,384]{1,0:T(8,128)(2,1)S(1)} %get-tuple-element.106), channel_id=1, source_target_pairs={{0,16},{1,17},{2,18},{3,19},{4,20},{5,21},{6,22},{7,23},{8,24},{9,... | collective-permute-start | bytes 774152 | tf_op jit(solution)/shard_map/ppermute | solution.py:688
  64.7 1.5 %collective-permute-start.20 = (bf16[336,384]{1,0:T(8,128)(2,1)S(1)}, bf16[336,384]{1,0:T(8,128)(2,1)S(1)}, u32[]{:S(2)}, u32[]{:S(2)}) collective-permute-start(bf16[336,384]{1,0:T(8,128)(2,1)S(1)} %collective-permute-done.19), channel_id=1, source_target_pairs={{4,0},{5,1},{6,2},{7,3},{0,4},{1,5},{2,6},{3,7},{12,8},{13,9},{14,... | collective-permute-start | bytes 774152 | tf_op jit(solution)/shard_map/ppermute | solution.py:507
  82.4 1.6 %collective-permute-start.21 = (bf16[336,384]{1,0:T(8,128)(2,1)S(1)}, bf16[336,384]{1,0:T(8,128)(2,1)S(1)}, u32[]{:S(2)}, u32[]{:S(2)}) collective-permute-start(bf16[336,384]{1,0:T(8,128)(2,1)S(1)} %slice.57), channel_id=1, source_target_pairs={{0,4},{1,5},{2,6},{3,7},{4,0},{5,1},{6,2},{7,3},{8,12},{9,13},{10,... | collective-permute-start | bytes 774152 | tf_op jit(solution)/shard_map/ppermute | solution.py:507
  84.1 10.3 %collective-permute-start.22 = (bf16[336,384]{1,0:T(8,128)(2,1)S(1)}, bf16[336,384]{1,0:T(8,128)(2,1)S(1)}, u32[]{:S(2)}, u32[]{:S(2)}) collective-permute-start(bf16[336,384]{1,0:T(8,128)(2,1)S(1)} %add_convert_fusion.3.refs_0_), channel_id=1, source_target_pairs={{16,0},{17,1},{18,2},{19,3},{20,4},{21,5},{22,6},{23,7},{24,8},{25... | collective-permute-start | bytes 774152 | tf_op jit(solution)/shard_map/ppermute | solution.py:688
  99.9 2.9 %collective-permute-start.23 = (bf16[2,768,384]{2,1,0:T(8,128)(2,1)S(1)}, bf16[2,768,384]{2,1,0:T(8,128)(2,1)S(1)}, u32[]{:S(2)}, u32[]{:S(2)}) collective-permute-start(bf16[2,768,384]{2,1,0:T(8,128)(2,1)S(1)} %get-tuple-element.117), channel_id=1, source_target_pairs={{0,4},{4,0},{8,12},{12,8},{1,5},{5,1},{9,13},{13,9},{2,6},{6,2},{1... | collective-permute-start | bytes 3538952 | tf_op jit(solution)/shard_map/ppermute | solution.py:491
  102.9 9.7 %collective-permute-start.24 = (bf16[384,384]{1,0:T(8,128)(2,1)S(1)}, bf16[384,384]{1,0:T(8,128)(2,1)S(1)}, u32[]{:S(2)}, u32[]{:S(2)}) collective-permute-start(bf16[384,384]{1,0:T(8,128)(2,1)S(1)} %fusion.1.refs_0_), channel_id=1, source_target_pairs={{0,8},{4,12},{8,0},{12,4},{1,9},{5,13},{9,1},{13,5},{2,10},{6,14},... | collective-permute-start | bytes 884744 | tf_op jit(solution)/shard_map/ppermute | solution.py:496
  103.6 8.8 %collective-permute-start.25 = (bf16[384,384]{1,0:T(8,128)(2,1)S(1)}, bf16[384,384]{1,0:T(8,128)(2,1)S(1)}, u32[]{:S(2)}, u32[]{:S(2)}) collective-permute-start(bf16[384,384]{1,0:T(8,128)(2,1)S(1)} %bitcast.77), channel_id=1, source_target_pairs={{0,1},{1,0},{2,3},{3,2},{4,5},{5,4},{6,7},{7,6},{8,9},{9,8},{10,11... | collective-permute-start | bytes 884744 | tf_op jit(solution)/shard_map/ppermute | solution.py:520
  112.7 2.1 %collective-permute-start.26 = (bf16[2,400,384]{2,1,0:T(8,128)(2,1)S(1)}, bf16[2,400,384]{2,1,0:T(8,128)(2,1)S(1)}, u32[]{:S(2)}, u32[]{:S(2)}) collective-permute-start(bf16[2,400,384]{2,1,0:T(8,128)(2,1)S(1)} %get-tuple-element.132), channel_id=1, source_target_pairs={{0,4},{4,0},{8,12},{12,8},{1,5},{5,1},{9,13},{13,9},{2,6},{6,2},{1... | collective-permute-start | bytes 1843208 | tf_op jit(solution)/shard_map/ppermute | solution.py:491
  112.8 3.2 %collective-permute-start.33 = (bf16[336,384]{1,0:T(8,128)(2,1)S(1)}, bf16[336,384]{1,0:T(8,128)(2,1)S(1)}, u32[]{:S(2)}, u32[]{:S(2)}) collective-permute-start(bf16[336,384]{1,0:T(8,128)(2,1)S(1)} %slice.65), channel_id=1, source_target_pairs={{0,4},{1,5},{2,6},{3,7},{4,0},{5,1},{6,2},{7,3},{8,12},{9,13},{10,... | collective-permute-start | bytes 774152 | tf_op jit(solution)/shard_map/ppermute | solution.py:507
  114.9 7.3 %collective-permute-start.28 = (bf16[192,384]{1,0:T(8,128)(2,1)S(1)}, bf16[192,384]{1,0:T(8,128)(2,1)S(1)}, u32[]{:S(2)}, u32[]{:S(2)}) collective-permute-start(bf16[192,384]{1,0:T(8,128)(2,1)S(1)} %bitcast.94), channel_id=1, source_target_pairs={{0,1},{1,0},{2,3},{3,2},{4,5},{5,4},{6,7},{7,6},{8,9},{9,8},{10,11... | collective-permute-start | bytes 442376 | tf_op jit(solution)/shard_map/ppermute | solution.py:520
  116.1 9.7 %collective-permute-start.29 = (bf16[192,384]{1,0:T(8,128)(2,1)S(1)}, bf16[192,384]{1,0:T(8,128)(2,1)S(1)}, u32[]{:S(2)}, u32[]{:S(2)}) collective-permute-start(bf16[192,384]{1,0:T(8,128)(2,1)S(1)} %bitcast.95), channel_id=1, source_target_pairs={{0,2},{1,3},{2,0},{3,1},{4,6},{5,7},{6,4},{7,5},{8,10},{9,11},{10,... | collective-permute-start | bytes 442376 | tf_op jit(solution)/shard_map/ppermute | solution.py:520
  116.8 9.2 %collective-permute-start.27 = (bf16[400,384]{1,0:T(8,128)(2,1)S(1)}, bf16[400,384]{1,0:T(8,128)(2,1)S(1)}, u32[]{:S(2)}, u32[]{:S(2)}) collective-permute-start(bf16[400,384]{1,0:T(8,128)(2,1)S(1)} %fusion), channel_id=1, source_target_pairs={{0,8},{4,12},{8,0},{12,4},{1,9},{5,13},{9,1},{13,5},{2,10},{6,14},... | collective-permute-start | bytes 921608 | tf_op jit(solution)/shard_map/ppermute | solution.py:496
  126.2 6.2 %collective-permute-start.31 = (bf16[96,384]{1,0:T(8,128)(2,1)S(1)}, bf16[96,384]{1,0:T(8,128)(2,1)S(1)}, u32[]{:S(2)}, u32[]{:S(2)}) collective-permute-start(bf16[96,384]{1,0:T(8,128)(2,1)S(1)} %bitcast.98), channel_id=1, source_target_pairs={{0,2},{1,3},{2,0},{3,1},{4,6},{5,7},{6,4},{7,5},{8,10},{9,11},{10,... | collective-permute-start | bytes 221192 | tf_op jit(solution)/shard_map/ppermute | solution.py:520
  128.2 4.4 %collective-permute-start.32 = (bf16[96,384]{1,0:T(8,128)(2,1)S(1)}, bf16[96,384]{1,0:T(8,128)(2,1)S(1)}, u32[]{:S(2)}, u32[]{:S(2)}) collective-permute-start(bf16[96,384]{1,0:T(8,128)(2,1)S(1)} %fusion.4), channel_id=1, source_target_pairs={{0,8},{4,12},{8,0},{12,4},{1,9},{5,13},{9,1},{13,5},{2,10},{6,14},... | collective-permute-start | bytes 221192 | tf_op jit(solution)/shard_map/ppermute | solution.py:496
  129.8 5.3 %collective-permute-start.30 = (bf16[208,384]{1,0:T(8,128)(2,1)S(1)}, bf16[208,384]{1,0:T(8,128)(2,1)S(1)}, u32[]{:S(2)}, u32[]{:S(2)}) collective-permute-start(bf16[208,384]{1,0:T(8,128)(2,1)S(1)} %pad_maximum_fusion.5), channel_id=1, source_target_pairs={{0,1},{1,0},{2,3},{3,2},{4,5},{5,4},{6,7},{7,6},{8,9},{9,8},{10,11... | collective-permute-start | bytes 479240 | tf_op jit(solution)/shard_map/ppermute | solution.py:520
  135.2 9.9 %copy-start.2 = (f32[16,384]{1,0:T(8,128)}, f32[16,384]{1,0:T(8,128)S(1)}, u32[]{:S(2)}) copy-start(f32[16,384]{1,0:T(8,128)S(1)} %slice_add_fusion.rest_ref) | copy-start | bytes 73732
  135.9 9.1 %collective-permute-start.34 = (bf16[112,384]{1,0:T(8,128)(2,1)S(1)}, bf16[112,384]{1,0:T(8,128)(2,1)S(1)}, u32[]{:S(2)}, u32[]{:S(2)}) collective-permute-start(bf16[112,384]{1,0:T(8,128)(2,1)S(1)} %pad_maximum_fusion.8), channel_id=1, source_target_pairs={{0,2},{1,3},{2,0},{3,1},{4,6},{5,7},{6,4},{7,5},{8,10},{9,11},{10,... | collective-permute-start | bytes 258056 | tf_op jit(solution)/shard_map/ppermute | solution.py:520
  137.8 9.7 %collective-permute-start.36 = (bf16[168,384]{1,0:T(8,128)(2,1)S(1)}, bf16[168,384]{1,0:T(8,128)(2,1)S(1)}, u32[]{:S(2)}, u32[]{:S(2)}) collective-permute-start(bf16[168,384]{1,0:T(8,128)(2,1)S(1)} %get-tuple-element.186), channel_id=1, source_target_pairs={{2,0},{0,1},{6,2},{4,3},{3,4},{1,5},{7,6},{5,7},{10,8},{8,9},{14,1... | collective-permute-start | bytes 387080 | tf_op jit(solution)/shard_map/ppermute | solution.py:507
  138.5 8.9 %collective-permute-start.35 = (bf16[168,384]{1,0:T(8,128)(2,1)S(1)}, bf16[168,384]{1,0:T(8,128)(2,1)S(1)}, u32[]{:S(2)}, u32[]{:S(2)}) collective-permute-start(bf16[168,384]{1,0:T(8,128)(2,1)S(1)} %get-tuple-element.187), channel_id=1, source_target_pairs={{0,0},{2,1},{4,2},{6,3},{1,4},{3,5},{5,6},{7,7},{8,8},{10,9},{12,1... | collective-permute-start | bytes 387080 | tf_op jit(solution)/shard_map/ppermute | solution.py:507
  145.1 0.6 copy-start.5

commit v6 on v5

--- a/solution.py
+++ b/solution.py
@@ -749,12 +749,12 @@
     piece_a, at = lax.optimization_barrier((piece_a, at))
     half_a = gather_step(piece_a[None], 0)
     near_c = jnp.stack(gather_outer(piece_c))
-    half_a, piece_b, near_c, own_start = lax.optimization_barrier(
-        (half_a, piece_b, near_c, own_start)
-    )
+    half_a, piece_b, near_c = lax.optimization_barrier((half_a, piece_b, near_c))
     line_a = gather_from(half_a, 1)
     half_b = gather_step(piece_b[None], 0)
-    line_a, half_b, near_c = lax.optimization_barrier((line_a, half_b, near_c))
+    line_a, half_b, near_c, own_start = lax.optimization_barrier(
+        (line_a, half_b, near_c, own_start)
+    )
     mine_a = gather_outer(line_a)
     line_b = gather_from(half_b, 1)
     half_c = gather_step(near_c, 0)

time: 149 us -> 145 us (0.973)
  waiting for transfers between devices: 52.7 us -> 50.6 us
    ppermute x8, waiting for transfers between devices: 4.85 us -> 2.94 us  [joint_permute(): return lax.ppermute(value, ('dp', 'seq'), pairs)]
  transfers between devices with their start and end apart: 37 -> 37, of which waited for: 22 -> 21; matrix products, arithmetic and copies ran while one was open for 4% -> 4% of each run, Pallas kernels for 14% -> 14%
where the time goes in v6:
time: 145 us
  waiting for transfers between devices  50.6 us (35%)
  Pallas kernels  45.8 us (32%)
  starting transfers between devices  39.2 us (27%)
  other arithmetic  5.45 us (4%)
  local copies, waits for them, and re-layouts  2.84 us (2%)
    pallas_call x6, Pallas kernels, call(): pl.pallas_call(body, out_shape=[jax.ShapeDtypeStruct(*result) for result...  42.3 us
    ppermute x12, waiting for transfers between devices, cross_line(): return lax.ppermute(value, 'seq', [(z, z ^ distance) for z in range(count)])  28.3 us
    ppermute x12, starting transfers between devices, cross_line(): return lax.ppermute(value, 'seq', [(z, z ^ distance) for z in range(count)])  18.1 us
    ppermute x2, waiting for transfers between devices, to_section(): return lax.ppermute(value, 'section', [(0, 1)] if steps == 1 else [(1, 0)])  11.1 us
    ppermute x6, starting transfers between devices, turn_outer(): lax.ppermute(value, 'dp', [(d, (d + 2 * steps) % count) for d in range(co...  7.2 us
    ppermute x8, starting transfers between devices, joint_permute(): return lax.ppermute(value, ('dp', 'seq'), pairs)  6.79 us
    ppermute x9, waiting for transfers between devices, swap_core(): lax.ppermute(value, 'dp', [(d, d ^ 1) for d in range(lax.axis_size('dp'))])  5.77 us
    ppermute x2, starting transfers between devices, to_section(): return lax.ppermute(value, 'section', [(0, 1)] if steps == 1 else [(1, 0)])  4.88 us
  transfers between devices with their start and end apart: 37, of which 21 were waited for; matrix products, arithmetic and copies ran while one was open for 4% of the time, Pallas kernels for 14%

profile of v6, /device:TPU:0, one launch (start us, length us, event | category | flops | bytes accessed | tf_op | source)
XLA Modules:
  0.0 145.0 jit_solution(11544128027922469129)
XLA Ops:
  0.6 0.5 collective-permute-start.10
  1.1 0.7 pad_add_fusion.place_ref.refs_1_.refs_0_.refs_2_
  1.8 1.8 %shard_map.152 = (bf16[112,384]{1,0:T(8,128)(2,1)}, bf16[96,384]{1,0:T(8,128)(2,1)}, bf16[96,384]{1,0:T(8,128)(2,1)}) custom-call(s32[4]{0:T(128)} %pad_add_fusion.place_ref.refs_1_.refs_0_.refs_2_, bf16[24,1152]{1,0:T(8,128)(2,1)} %bitcast.108, bf16[24,384]{1,0:T(8,128)(2,1)} %bitcast.109, bf16[24,1536]{1,0:T(8,128)(2,1)} %bitcast.106, ...), custom_call_target="tpu_custom_call" | custom-call | flops 1000000000 | bytes 1000000 | tf_op jit(solution)/shard_map/pallas_call | solution.py:439
  3.6 2.6 %collective-permute-start.1 = (bf16[96,384]{1,0:T(8,128)(2,1)}, bf16[96,384]{1,0:T(8,128)(2,1)S(1)}, u32[]{:S(2)}, u32[]{:S(2)}) collective-permute-start(bf16[96,384]{1,0:T(8,128)(2,1)} %get-tuple-element.89), channel_id=1, source_target_pairs={{0,8},{4,12},{8,0},{12,4},{1,9},{5,13},{9,1},{13,5},{2,10},{6,14},... | collective-permute-start | bytes 221192 | tf_op jit(solution)/shard_map/ppermute | solution.py:496
  6.2 2.6 %collective-permute-start = (bf16[1,112,384]{2,1,0:T(8,128)(2,1)}, bf16[1,112,384]{2,1,0:T(8,128)(2,1)S(1)}, u32[]{:S(2)}, u32[]{:S(2)}) collective-permute-start(bf16[1,112,384]{2,1,0:T(8,128)(2,1)} %bitcast.96), channel_id=1, source_target_pairs={{0,2},{1,3},{2,0},{3,1},{4,6},{5,7},{6,4},{7,5},{8,10},{9,11},{10,... | collective-permute-start | bytes 258056 | tf_op jit(solution)/shard_map/ppermute | solution.py:520
  8.8 0.7 collective-permute-start.4
  9.5 3.7 %collective-permute-start.5 = (bf16[168,384]{1,0:T(8,128)(2,1)S(1)}, bf16[168,384]{1,0:T(8,128)(2,1)S(1)}, u32[]{:S(2)}, u32[]{:S(2)}) collective-permute-start(bf16[168,384]{1,0:T(8,128)(2,1)S(1)} %get-tuple-element.191), channel_id=1, source_target_pairs={{0,2},{1,0},{2,6},{3,4},{4,3},{5,1},{6,7},{7,5},{8,10},{9,8},{10,1... | collective-permute-start | bytes 387080 | tf_op jit(solution)/shard_map/ppermute | solution.py:507
  13.2 0.9 pad_maximum_fusion.6
  14.1 0.9 pad_maximum_fusion.4
  15.1 0.5 collective-permute-start.3
  15.6 3.4 %collective-permute-start.2 = (bf16[2,112,384]{2,1,0:T(8,128)(2,1)S(1)}, bf16[2,112,384]{2,1,0:T(8,128)(2,1)S(1)}, u32[]{:S(2)}, u32[]{:S(2)}) collective-permute-start(bf16[2,112,384]{2,1,0:T(8,128)(2,1)S(1)} %pad_maximum_fusion.4), channel_id=1, source_target_pairs={{0,1},{1,0},{2,3},{3,2},{4,5},{5,4},{6,7},{7,6},{8,9},{9,8},{10,11... | collective-permute-start | bytes 516104 | tf_op jit(solution)/shard_map/ppermute | solution.py:520
  19.0 4.0 %collective-permute-done.3 = bf16[1,96,384]{2,1,0:T(8,128)(2,1)S(1)} collective-permute-done((bf16[1,96,384]{2,1,0:T(8,128)(2,1)S(1)}, bf16[1,96,384]{2,1,0:T(8,128)(2,1)S(1)}, u32[]{:S(2)}, u32[]{:S(2)}) %collective-permute-start.3) | collective-permute-done | bytes 73760 | tf_op jit(solution)/shard_map/ppermute | solution.py:520
  23.0 2.1 %collective-permute-done.2 = bf16[2,112,384]{2,1,0:T(8,128)(2,1)S(1)} collective-permute-done((bf16[2,112,384]{2,1,0:T(8,128)(2,1)S(1)}, bf16[2,112,384]{2,1,0:T(8,128)(2,1)S(1)}, u32[]{:S(2)}, u32[]{:S(2)}) %collective-permute-start.2) | collective-permute-done | bytes 172064 | tf_op jit(solution)/shard_map/ppermute | solution.py:520
  25.3 2.4 %collective-permute-start.8 = (bf16[2,96,384]{2,1,0:T(8,128)(2,1)S(1)}, bf16[2,96,384]{2,1,0:T(8,128)(2,1)S(1)}, u32[]{:S(2)}, u32[]{:S(2)}) collective-permute-start(bf16[2,96,384]{2,1,0:T(8,128)(2,1)S(1)} %pad_maximum_fusion.6), channel_id=1, source_target_pairs={{0,2},{1,3},{2,0},{3,1},{4,6},{5,7},{6,4},{7,5},{8,10},{9,11},{10,... | collective-permute-start | bytes 442376 | tf_op jit(solution)/shard_map/ppermute | solution.py:520
  27.7 0.5 collective-permute-start.9
  28.3 4.1 %collective-permute-done.7 = bf16[2,96,384]{2,1,0:T(8,128)(2,1)S(1)} collective-permute-done((bf16[2,96,384]{2,1,0:T(8,128)(2,1)S(1)}, bf16[2,96,384]{2,1,0:T(8,128)(2,1)S(1)}, u32[]{:S(2)}, u32[]{:S(2)}) %collective-permute-start.7) | collective-permute-done | bytes 147488 | tf_op jit(solution)/shard_map/ppermute | solution.py:520
  32.4 2.0 %collective-permute-done.8 = bf16[2,96,384]{2,1,0:T(8,128)(2,1)S(1)} collective-permute-done((bf16[2,96,384]{2,1,0:T(8,128)(2,1)S(1)}, bf16[2,96,384]{2,1,0:T(8,128)(2,1)S(1)}, u32[]{:S(2)}, u32[]{:S(2)}) %collective-permute-start.8) | collective-permute-done | bytes 147488 | tf_op jit(solution)/shard_map/ppermute | solution.py:520
  34.4 1.7 %collective-permute-done.9.refs_5_ = bf16[4,112,384]{2,1,0:T(8,128)(2,1)S(1)} collective-permute-done((bf16[4,112,384]{2,1,0:T(8,128)(2,1)S(1)}, bf16[4,112,384]{2,1,0:T(8,128)(2,1)S(1)}, u32[]{:S(2)}, u32[]{:S(2)}) %collective-permute-start.9) | collective-permute-done | bytes 344096 | tf_op jit(solution)/shard_map/ppermute | solution.py:496
  36.1 0.5 collective-permute-start.12
  37.0 0.4 collective-permute-start.13
  37.4 0.5 collective-permute-start.14
  38.1 0.5 collective-permute-start.15
  38.8 6.0 %shard_map.153 = (f32[336,384]{1,0:T(8,128)S(1)}, bf16[4,384,384]{2,1,0:T(8,128)(2,1)S(1)}, f32[16,384]{1,0:T(8,128)S(1)}) custom-call(bf16[4,96,384]{2,1,0:T(8,128)(2,1)S(1)} %pad_maximum_fusion.1.refs_0_.refs_4_, s32[4]{0:T(128)S(1)} %copy-done, bf16[672,384]{1,0:T(8,128)(2,1)S(1)} %constant_dynamic-update-slice_fusion.refs_2_, ...), custom_call_target="tpu_custom_call" | custom-call | flops 1000000000 | bytes 4000000 | tf_op jit(solution)/shard_map/pallas_call | solution.py:423
  44.8 1.2 collective-permute-done.13.refs_9_
  46.1 0.5 collective-permute-start.18
  46.6 1.1 collective-permute-done.16.refs_7_
  47.6 0.4 collective-permute-done.18.refs_11_
  48.1 3.7 %shard_map.154 = (bf16[336,384]{1,0:T(8,128)(2,1)S(1)}, bf16[4,384,384]{2,1,0:T(8,128)(2,1)S(1)}, bf16[1536,384]{1,0:T(8,128)(2,1)S(1)}) custom-call(s32[4]{0:T(128)S(1)} %copy-done, f32[336,384]{1,0:T(8,128)S(1)} %get-tuple-element.102.refs_1_, f32[672,128]{1,0:T(8,128)S(1)} %broadcast_in_dim.30.refs_3_.refs_2_.refs_1_.refs_4_.refs_12_, ...), custom_call_target="tpu_custom_call" | custom-call | flops 1000000000 | bytes 4000000 | tf_op jit(solution)/shard_map/pallas_call | solution.py:423
  51.7 3.6 %collective-permute-start.19 = (bf16[336,384]{1,0:T(8,128)(2,1)S(1)}, bf16[336,384]{1,0:T(8,128)(2,1)S(1)}, u32[]{:S(2)}, u32[]{:S(2)}) collective-permute-start(bf16[336,384]{1,0:T(8,128)(2,1)S(1)} %get-tuple-element.106), channel_id=1, source_target_pairs={{0,16},{1,17},{2,18},{3,19},{4,20},{5,21},{6,22},{7,23},{8,24},{9,... | collective-permute-start | bytes 774152 | tf_op jit(solution)/shard_map/ppermute | solution.py:688
  55.3 5.6 %collective-permute-done.19 = bf16[336,384]{1,0:T(8,128)(2,1)S(1)} collective-permute-done((bf16[336,384]{1,0:T(8,128)(2,1)S(1)}, bf16[336,384]{1,0:T(8,128)(2,1)S(1)}, u32[]{:S(2)}, u32[]{:S(2)}) %collective-permute-start.19) | collective-permute-done | bytes 258080 | tf_op jit(solution)/shard_map/ppermute | solution.py:688
  60.9 1.5 %collective-permute-done.20 = bf16[336,384]{1,0:T(8,128)(2,1)S(1)} collective-permute-done((bf16[336,384]{1,0:T(8,128)(2,1)S(1)}, bf16[336,384]{1,0:T(8,128)(2,1)S(1)}, u32[]{:S(2)}, u32[]{:S(2)}) %collective-permute-start.20) | collective-permute-done | bytes 258080 | tf_op jit(solution)/shard_map/ppermute | solution.py:507
  62.6 16.0 %shard_map.155 = (bf16[672,384]{1,0:T(8,128)(2,1)S(1)}, f32[336,384]{1,0:T(8,128)S(1)}, bf16[336,384]{1,0:T(8,128)(2,1)S(1)}, bf16[3,336,128]{2,1,0:T(8,128)(2,1...) custom-call(bf16[672,384]{1,0:T(8,128)(2,1)S(1)} %maximum_select_fus, ...), custom_call_target="tpu_custom_call" | custom-call | flops 4000000000 | bytes 4000000 | tf_op jit(solution)/shard_map/pallas_call | solution.py:423
  78.8 1.4 collective-permute-done.21
  80.2 1.3 collective-permute-start.22
  81.5 3.4 %shard_map.156 = (bf16[336,384]{1,0:T(8,128)(2,1)S(1)}, bf16[4,336,384]{2,1,0:T(8,128)(2,1)S(1)}, f32[4,336,384]{2,1,0:T(8,128)S(1)}) custom-call(bf16[336,384]{1,0:T(8,128)(2,1)S(1)} %add_convert_fusion.3.refs_0_, f32[336,384]{1,0:T(8,128)S(1)} %get-tuple-element.111.refs_1_.refs_2_, ...), custom_call_target="tpu_custom_call" | custom-call | flops 2000000000 | bytes 4000000 | tf_op jit(solution)/shard_map/pallas_call | solution.py:423
  84.9 5.5 %collective-permute-done.22 = bf16[336,384]{1,0:T(8,128)(2,1)S(1)} collective-permute-done((bf16[336,384]{1,0:T(8,128)(2,1)S(1)}, bf16[336,384]{1,0:T(8,128)(2,1)S(1)}, u32[]{:S(2)}, u32[]{:S(2)}) %collective-permute-start.22) | collective-permute-done | bytes 258080 | tf_op jit(solution)/shard_map/ppermute | solution.py:688
  90.5 5.5 %shard_map.157 = (bf16[2,768,384]{2,1,0:T(8,128)(2,1)S(1)}, bf16[2,768,384]{2,1,0:T(8,128)(2,1)S(1)}, f32[336,384]{1,0:T(8,128)S(1)}, f32[16,384]{1,0:T(8,128)S(1)}) custom-call(s32[4]{0:T(128)S(1)} %copy-done, bf16[336,384]{1,0:T(8,128)(2,1)S(1)} %broadcast_select_fusion.refs_1_, f32[336,384]{1,0:T(8,128)S(1)} %get-tuple-element.111.refs_1_.refs_2_, ...), custom_call_target="tpu_custom_call" | custom-call | flops 2000000000 | bytes 4000000 | tf_op jit(solution)/shard_map/pallas_call | solution.py:423
  96.1 2.8 %collective-permute-done.23 = bf16[2,768,384]{2,1,0:T(8,128)(2,1)S(1)} collective-permute-done((bf16[2,768,384]{2,1,0:T(8,128)(2,1)S(1)}, bf16[2,768,384]{2,1,0:T(8,128)(2,1)S(1)}, u32[]{:S(2)}, u32[]{:S(2)}) %collective-permute-start.23) | collective-permute-done | bytes 1179680 | tf_op jit(solution)/shard_map/ppermute | solution.py:491
  99.0 0.6 collective-permute-start.24
  99.8 1.7 %collective-permute-start.25 = (bf16[384,384]{1,0:T(8,128)(2,1)S(1)}, bf16[384,384]{1,0:T(8,128)(2,1)S(1)}, u32[]{:S(2)}, u32[]{:S(2)}) collective-permute-start(bf16[384,384]{1,0:T(8,128)(2,1)S(1)} %bitcast.77), channel_id=1, source_target_pairs={{0,1},{1,0},{2,3},{3,2},{4,5},{5,4},{6,7},{7,6},{8,9},{9,8},{10,11... | collective-permute-start | bytes 884744 | tf_op jit(solution)/shard_map/ppermute | solution.py:520
  101.5 7.8 %shard_map.158 = (bf16[672,384]{1,0:T(8,128)(2,1)S(1)}, bf16[2,400,384]{2,1,0:T(8,128)(2,1)S(1)}, bf16[2,400,384]{2,1,0:T(8,128)(2,1)S(1)}) custom-call(bf16[384,384]{1,0:T(8,128)(2,1)S(1)} %fusion.1.refs_0_, bf16[384,384]{1,0:T(8,128)(2,1)S(1)} %bitcast.78, s32[4]{0:T(128)S(1)} %copy-done, f32[336,384]{1,0:T(8,128)S(1)} %get-tuple-element.119.refs_3_, ...), custom_call_target="tpu_custom_call" | custom-call | flops 10000000000 | bytes 4000000 | tf_op jit(solution)/shard_map/pallas_call | solution.py:423
  109.6 0.6 collective-permute-start.33
  110.2 1.4 collective-permute-done.26
  111.7 1.0 collective-permute-start.28
  112.9 1.8 %collective-permute-start.29 = (bf16[192,384]{1,0:T(8,128)(2,1)S(1)}, bf16[192,384]{1,0:T(8,128)(2,1)S(1)}, u32[]{:S(2)}, u32[]{:S(2)}) collective-permute-start(bf16[192,384]{1,0:T(8,128)(2,1)S(1)} %bitcast.95), channel_id=1, source_target_pairs={{0,2},{1,3},{2,0},{3,1},{4,6},{5,7},{6,4},{7,5},{8,10},{9,11},{10,... | collective-permute-start | bytes 442376 | tf_op jit(solution)/shard_map/ppermute | solution.py:520
  114.7 1.5 %collective-permute-start.27 = (bf16[400,384]{1,0:T(8,128)(2,1)S(1)}, bf16[400,384]{1,0:T(8,128)(2,1)S(1)}, u32[]{:S(2)}, u32[]{:S(2)}) collective-permute-start(bf16[400,384]{1,0:T(8,128)(2,1)S(1)} %fusion), channel_id=1, source_target_pairs={{0,8},{4,12},{8,0},{12,4},{1,9},{5,13},{9,1},{13,5},{2,10},{6,14},... | collective-permute-start | bytes 921608 | tf_op jit(solution)/shard_map/ppermute | solution.py:496
  116.2 4.0 %collective-permute-done.28 = bf16[192,384]{1,0:T(8,128)(2,1)S(1)} collective-permute-done((bf16[192,384]{1,0:T(8,128)(2,1)S(1)}, bf16[192,384]{1,0:T(8,128)(2,1)S(1)}, u32[]{:S(2)}, u32[]{:S(2)}) %collective-permute-start.28) | collective-permute-done | bytes 147488 | tf_op jit(solution)/shard_map/ppermute | solution.py:520
  120.2 2.5 %collective-permute-done.29 = bf16[192,384]{1,0:T(8,128)(2,1)S(1)} collective-permute-done((bf16[192,384]{1,0:T(8,128)(2,1)S(1)}, bf16[192,384]{1,0:T(8,128)(2,1)S(1)}, u32[]{:S(2)}, u32[]{:S(2)}) %collective-permute-start.29) | collective-permute-done | bytes 147488 | tf_op jit(solution)/shard_map/ppermute | solution.py:520
  122.7 0.7 collective-permute-done.27
  123.7 1.3 collective-permute-start.31
  124.9 1.5 %collective-permute-start.32 = (bf16[96,384]{1,0:T(8,128)(2,1)S(1)}, bf16[96,384]{1,0:T(8,128)(2,1)S(1)}, u32[]{:S(2)}, u32[]{:S(2)}) collective-permute-start(bf16[96,384]{1,0:T(8,128)(2,1)S(1)} %fusion.4), channel_id=1, source_target_pairs={{0,8},{4,12},{8,0},{12,4},{1,9},{5,13},{9,1},{13,5},{2,10},{6,14},... | collective-permute-start | bytes 221192 | tf_op jit(solution)/shard_map/ppermute | solution.py:496
  126.5 1.1 collective-permute-start.30
  127.7 1.7 %collective-permute-done.31 = bf16[96,384]{1,0:T(8,128)(2,1)S(1)} collective-permute-done((bf16[96,384]{1,0:T(8,128)(2,1)S(1)}, bf16[96,384]{1,0:T(8,128)(2,1)S(1)}, u32[]{:S(2)}, u32[]{:S(2)}) %collective-permute-start.31) | collective-permute-done | bytes 73760 | tf_op jit(solution)/shard_map/ppermute | solution.py:520
  129.4 0.7 bitcast_add_fusion.5
  130.1 1.8 %collective-permute-done.30 = bf16[208,384]{1,0:T(8,128)(2,1)S(1)} collective-permute-done((bf16[208,384]{1,0:T(8,128)(2,1)S(1)}, bf16[208,384]{1,0:T(8,128)(2,1)S(1)}, u32[]{:S(2)}, u32[]{:S(2)}) %collective-permute-start.30) | collective-permute-done | bytes 159776 | tf_op jit(solution)/shard_map/ppermute | solution.py:520
  132.0 0.7 constant_dynamic-slice_fusion
  132.7 1.8 %collective-permute-start.34 = (bf16[112,384]{1,0:T(8,128)(2,1)S(1)}, bf16[112,384]{1,0:T(8,128)(2,1)S(1)}, u32[]{:S(2)}, u32[]{:S(2)}) collective-permute-start(bf16[112,384]{1,0:T(8,128)(2,1)S(1)} %pad_maximum_fusion.8), channel_id=1, source_target_pairs={{0,2},{1,3},{2,0},{3,1},{4,6},{5,7},{6,4},{7,5},{8,10},{9,11},{10,... | collective-permute-start | bytes 258056 | tf_op jit(solution)/shard_map/ppermute | solution.py:520
  134.6 0.7 broadcast_in_dim_reshape.3
  135.3 1.0 collective-permute-start.36
  136.3 0.7 collective-permute-start.35
  136.9 4.9 %collective-permute-done.34.came_ref = bf16[112,384]{1,0:T(8,128)(2,1)S(1)} collective-permute-done((bf16[112,384]{1,0:T(8,128)(2,1)S(1)}, bf16[112,384]{1,0:T(8,128)(2,1)S(1)}, u32[]{:S(2)}, u32[]{:S(2)}) %collective-permute-start.34) | collective-permute-done | bytes 86048 | tf_op jit(solution)/shard_map/ppermute | solution.py:520
  141.9 0.6 copy-done.5
  142.5 1.7 %shard_map.159 = (f32[1,24,1152]{2,1,0:T(8,128)}, f32[1,24,384]{2,1,0:T(8,128)}, f32[1,48]{1,0:T(1,128)}, f32[1,144]{1,0:T(1,128)}, f32[1,96]{1,0:T(1,128)}) custom-call(s32[4]{0:T(128)} %pad_add_fusion.place_ref.refs_1_.refs_0_.refs_2_, f32[96,384]{1,0:T(8,128)} %bitcast.93, f32[16,384]{1,0:T(8,128)} %copy-done.2, bf16[112,384]{1,0:T(8,128)(2,1)} %copy-done.5), custom_call_target="tpu_custom_call" | custom-call | flops 10000000000 | bytes 1000000 | tf_op jit(solution)/shard_map/pallas_call | solution.py:439
  144.2 0.7 maximum_bitcast_fusion
  (88 shorter events, 3.0 us)
Async XLA Ops:
  0.6 12.6 %collective-permute-start.10 = (s32[2,4]{1,0:T(2,128)}, s32[2,4]{1,0:T(2,128)S(1)}, u32[]{:S(2)}, u32[]{:S(2)}) collective-permute-start(s32[2,4]{1,0:T(2,128)} %bitcast.104), channel_id=1, source_target_pairs={{0,4},{4,0},{8,12},{12,8},{1,5},{5,1},{9,13},{13,9},{2,6},{6,2},{1... | collective-permute-start | bytes 104 | tf_op jit(solution)/shard_map/ppermute | solution.py:491
  1.8 6.9 %copy-start.1 = (bf16[1,2,1,168,384]{4,3,2,1,0:T(8,128)(2,1)S(1)}, bf16[1,2,1,168,384]{4,3,2,1,0:T(8,128)(2,1)}, u32[]{:S(2)}) copy-start(bf16[1,2,1,168,384]{4,3,2,1,0:T(8,128)(2,1)} %param.9) | copy-start | bytes 774148
  1.8 11.4 %copy-start.4 = (s32[2,1,4]{2,1,0:T(1,128)S(1)}, s32[2,1,4]{2,1,0:T(1,128)}, u32[]{:S(2)}) copy-start(s32[2,1,4]{2,1,0:T(1,128)} %param.10) | copy-start | bytes 100
  3.6 11.5 %copy-start.3 = (bf16[96,384]{1,0:T(8,128)(2,1)S(1)}, bf16[96,384]{1,0:T(8,128)(2,1)}, u32[]{:S(2)}) copy-start(bf16[96,384]{1,0:T(8,128)(2,1)} %get-tuple-element.91) | copy-start | bytes 221188
  3.6 9.6 %collective-permute-start.1 = (bf16[96,384]{1,0:T(8,128)(2,1)}, bf16[96,384]{1,0:T(8,128)(2,1)S(1)}, u32[]{:S(2)}, u32[]{:S(2)}) collective-permute-start(bf16[96,384]{1,0:T(8,128)(2,1)} %get-tuple-element.89), channel_id=1, source_target_pairs={{0,8},{4,12},{8,0},{12,4},{1,9},{5,13},{9,1},{13,5},{2,10},{6,14},... | collective-permute-start | bytes 221192 | tf_op jit(solution)/shard_map/ppermute | solution.py:496
  6.2 8.0 %collective-permute-start = (bf16[1,112,384]{2,1,0:T(8,128)(2,1)}, bf16[1,112,384]{2,1,0:T(8,128)(2,1)S(1)}, u32[]{:S(2)}, u32[]{:S(2)}) collective-permute-start(bf16[1,112,384]{2,1,0:T(8,128)(2,1)} %bitcast.96), channel_id=1, source_target_pairs={{0,2},{1,3},{2,0},{3,1},{4,6},{5,7},{6,4},{7,5},{8,10},{9,11},{10,... | collective-permute-start | bytes 258056 | tf_op jit(solution)/shard_map/ppermute | solution.py:520
  8.8 10.2 %collective-permute-start.4 = (bf16[168,384]{1,0:T(8,128)(2,1)S(1)}, bf16[168,384]{1,0:T(8,128)(2,1)S(1)}, u32[]{:S(2)}, u32[]{:S(2)}) collective-permute-start(bf16[168,384]{1,0:T(8,128)(2,1)S(1)} %get-tuple-element.190), channel_id=1, source_target_pairs={{0,0},{1,2},{2,4},{3,6},{4,1},{5,3},{6,5},{7,7},{8,8},{9,10},{10,1... | collective-permute-start | bytes 387080 | tf_op jit(solution)/shard_map/ppermute | solution.py:507
  9.5 9.5 %collective-permute-start.5 = (bf16[168,384]{1,0:T(8,128)(2,1)S(1)}, bf16[168,384]{1,0:T(8,128)(2,1)S(1)}, u32[]{:S(2)}, u32[]{:S(2)}) collective-permute-start(bf16[168,384]{1,0:T(8,128)(2,1)S(1)} %get-tuple-element.191), channel_id=1, source_target_pairs={{0,2},{1,0},{2,6},{3,4},{4,3},{5,1},{6,7},{7,5},{8,10},{9,8},{10,1... | collective-permute-start | bytes 387080 | tf_op jit(solution)/shard_map/ppermute | solution.py:507
  15.1 7.9 %collective-permute-start.3 = (bf16[1,96,384]{2,1,0:T(8,128)(2,1)S(1)}, bf16[1,96,384]{2,1,0:T(8,128)(2,1)S(1)}, u32[]{:S(2)}, u32[]{:S(2)}) collective-permute-start(bf16[1,96,384]{2,1,0:T(8,128)(2,1)S(1)} %bitcast.99), channel_id=1, source_target_pairs={{0,2},{1,3},{2,0},{3,1},{4,6},{5,7},{6,4},{7,5},{8,10},{9,11},{10,... | collective-permute-start | bytes 221192 | tf_op jit(solution)/shard_map/ppermute | solution.py:520
  15.6 9.6 %collective-permute-start.2 = (bf16[2,112,384]{2,1,0:T(8,128)(2,1)S(1)}, bf16[2,112,384]{2,1,0:T(8,128)(2,1)S(1)}, u32[]{:S(2)}, u32[]{:S(2)}) collective-permute-start(bf16[2,112,384]{2,1,0:T(8,128)(2,1)S(1)} %pad_maximum_fusion.4), channel_id=1, source_target_pairs={{0,1},{1,0},{2,3},{3,2},{4,5},{5,4},{6,7},{7,6},{8,9},{9,8},{10,11... | collective-permute-start | bytes 516104 | tf_op jit(solution)/shard_map/ppermute | solution.py:520
  25.2 7.1 %collective-permute-start.7 = (bf16[2,96,384]{2,1,0:T(8,128)(2,1)S(1)}, bf16[2,96,384]{2,1,0:T(8,128)(2,1)S(1)}, u32[]{:S(2)}, u32[]{:S(2)}) collective-permute-start(bf16[2,96,384]{2,1,0:T(8,128)(2,1)S(1)} %pad_maximum_fusion.7), channel_id=1, source_target_pairs={{0,1},{1,0},{2,3},{3,2},{4,5},{5,4},{6,7},{7,6},{8,9},{9,8},{10,11... | collective-permute-start | bytes 442376 | tf_op jit(solution)/shard_map/ppermute | solution.py:520
  25.3 9.1 %collective-permute-start.8 = (bf16[2,96,384]{2,1,0:T(8,128)(2,1)S(1)}, bf16[2,96,384]{2,1,0:T(8,128)(2,1)S(1)}, u32[]{:S(2)}, u32[]{:S(2)}) collective-permute-start(bf16[2,96,384]{2,1,0:T(8,128)(2,1)S(1)} %pad_maximum_fusion.6), channel_id=1, source_target_pairs={{0,2},{1,3},{2,0},{3,1},{4,6},{5,7},{6,4},{7,5},{8,10},{9,11},{10,... | collective-permute-start | bytes 442376 | tf_op jit(solution)/shard_map/ppermute | solution.py:520
  27.7 8.5 %collective-permute-start.9 = (bf16[4,112,384]{2,1,0:T(8,128)(2,1)S(1)}, bf16[4,112,384]{2,1,0:T(8,128)(2,1)S(1)}, u32[]{:S(2)}, u32[]{:S(2)}) collective-permute-start(bf16[4,112,384]{2,1,0:T(8,128)(2,1)S(1)} %pad_maximum_fusion.refs_4_), channel_id=1, source_target_pairs={{0,8},{4,12},{8,0},{12,4},{1,9},{5,13},{9,1},{13,5},{2,10},{6,14},... | collective-permute-start | bytes 1032200 | tf_op jit(solution)/shard_map/ppermute | solution.py:496
  28.2 10.5 %copy-start = (s32[4]{0:T(128)S(1)}, s32[4]{0:T(128)}, u32[]{:S(2)}) copy-start(s32[4]{0:T(128)} %pad_add_fusion.place_ref.refs_1_.refs_0_.refs_2_) | copy-start | bytes 52
  28.2 9.7 %collective-permute-start.6 = (bf16[336,384]{1,0:T(8,128)(2,1)S(1)}, bf16[336,384]{1,0:T(8,128)(2,1)S(1)}, u32[]{:S(2)}, u32[]{:S(2)}) collective-permute-start(bf16[336,384]{1,0:T(8,128)(2,1)S(1)} %pad_maximum_fusion.3.refs_6_), channel_id=1, source_target_pairs={{4,0},{5,1},{6,2},{7,3},{0,4},{1,5},{2,6},{3,7},{12,8},{13,9},{14,... | collective-permute-start | bytes 774152 | tf_op jit(solution)/shard_map/ppermute | solution.py:507
  36.1 2.0 %collective-permute-start.11 = (bf16[4,112,384]{2,1,0:T(8,128)(2,1)S(1)}, bf16[4,112,384]{2,1,0:T(8,128)(2,1)S(1)}, u32[]{:S(2)}, u32[]{:S(2)}) collective-permute-start(bf16[4,112,384]{2,1,0:T(8,128)(2,1)S(1)} %pad_maximum_fusion.refs_4_), channel_id=1, source_target_pairs={{0,4},{4,0},{8,12},{12,8},{1,5},{5,1},{9,13},{13,9},{2,6},{6,2},{1... | collective-permute-start | bytes 1032200 | tf_op jit(solution)/shard_map/ppermute | solution.py:491
  36.1 2.5 %collective-permute-start.12 = (bf16[4,112,384]{2,1,0:T(8,128)(2,1)S(1)}, bf16[4,112,384]{2,1,0:T(8,128)(2,1)S(1)}, u32[]{:S(2)}, u32[]{:S(2)}) collective-permute-start(bf16[4,112,384]{2,1,0:T(8,128)(2,1)S(1)} %collective-permute-done.9.refs_5_), channel_id=1, source_target_pairs={{0,4},{4,0},{8,12},{12,8},{1,5},{5,1},{9,13},{13,9},{2,6},{6,2},{1... | collective-permute-start | bytes 1032200 | tf_op jit(solution)/shard_map/ppermute | solution.py:491
  37.0 9.0 %collective-permute-start.13 = (bf16[4,96,384]{2,1,0:T(8,128)(2,1)S(1)}, bf16[4,96,384]{2,1,0:T(8,128)(2,1)S(1)}, u32[]{:S(2)}, u32[]{:S(2)}) collective-permute-start(bf16[4,96,384]{2,1,0:T(8,128)(2,1)S(1)} %pad_maximum_fusion.2.refs_8_), channel_id=1, source_target_pairs={{0,1},{1,0},{2,3},{3,2},{4,5},{5,4},{6,7},{7,6},{8,9},{9,8},{10,11... | collective-permute-start | bytes 884744 | tf_op jit(solution)/shard_map/ppermute | solution.py:520
  37.4 8.6 %collective-permute-start.14 = (bf16[4,96,384]{2,1,0:T(8,128)(2,1)S(1)}, bf16[4,96,384]{2,1,0:T(8,128)(2,1)S(1)}, u32[]{:S(2)}, u32[]{:S(2)}) collective-permute-start(bf16[4,96,384]{2,1,0:T(8,128)(2,1)S(1)} %pad_maximum_fusion.1.refs_0_.refs_4_), channel_id=1, source_target_pairs={{0,8},{4,12},{8,0},{12,4},{1,9},{5,13},{9,1},{13,5},{2,10},{6,14},... | collective-permute-start | bytes 884744 | tf_op jit(solution)/shard_map/ppermute | solution.py:496
  38.0 8.6 %collective-permute-start.17 = (bf16[4,96,384]{2,1,0:T(8,128)(2,1)S(1)}, bf16[4,96,384]{2,1,0:T(8,128)(2,1)S(1)}, u32[]{:S(2)}, u32[]{:S(2)}) collective-permute-start(bf16[4,96,384]{2,1,0:T(8,128)(2,1)S(1)} %pad_maximum_fusion.2.refs_8_), channel_id=1, source_target_pairs={{0,4},{4,0},{8,12},{12,8},{1,5},{5,1},{9,13},{13,9},{2,6},{6,2},{1... | collective-permute-start | bytes 884744 | tf_op jit(solution)/shard_map/ppermute | solution.py:491
  38.1 8.5 %collective-permute-start.15 = (bf16[4,96,384]{2,1,0:T(8,128)(2,1)S(1)}, bf16[4,96,384]{2,1,0:T(8,128)(2,1)S(1)}, u32[]{:S(2)}, u32[]{:S(2)}) collective-permute-start(bf16[4,96,384]{2,1,0:T(8,128)(2,1)S(1)} %pad_maximum_fusion.1.refs_0_.refs_4_), channel_id=1, source_target_pairs={{0,4},{4,0},{8,12},{12,8},{1,5},{5,1},{9,13},{13,9},{2,6},{6,2},{1... | collective-permute-start | bytes 884744 | tf_op jit(solution)/shard_map/ppermute | solution.py:491
  46.1 1.6 %collective-permute-start.16 = (bf16[4,96,384]{2,1,0:T(8,128)(2,1)S(1)}, bf16[4,96,384]{2,1,0:T(8,128)(2,1)S(1)}, u32[]{:S(2)}, u32[]{:S(2)}) collective-permute-start(bf16[4,96,384]{2,1,0:T(8,128)(2,1)S(1)} %collective-permute-done.14.refs_5_), channel_id=1, source_target_pairs={{0,4},{4,0},{8,12},{12,8},{1,5},{5,1},{9,13},{13,9},{2,6},{6,2},{1... | collective-permute-start | bytes 884744 | tf_op jit(solution)/shard_map/ppermute | solution.py:491
  46.1 2.0 %collective-permute-start.18 = (bf16[4,96,384]{2,1,0:T(8,128)(2,1)S(1)}, bf16[4,96,384]{2,1,0:T(8,128)(2,1)S(1)}, u32[]{:S(2)}, u32[]{:S(2)}) collective-permute-start(bf16[4,96,384]{2,1,0:T(8,128)(2,1)S(1)} %collective-permute-done.13.refs_9_), channel_id=1, source_target_pairs={{0,4},{4,0},{8,12},{12,8},{1,5},{5,1},{9,13},{13,9},{2,6},{6,2},{1... | collective-permute-start | bytes 884744 | tf_op jit(solution)/shard_map/ppermute | solution.py:491
  51.7 9.2 %collective-permute-start.19 = (bf16[336,384]{1,0:T(8,128)(2,1)S(1)}, bf16[336,384]{1,0:T(8,128)(2,1)S(1)}, u32[]{:S(2)}, u32[]{:S(2)}) collective-permute-start(bf16[336,384]{1,0:T(8,128)(2,1)S(1)} %get-tuple-element.106), channel_id=1, source_target_pairs={{0,16},{1,17},{2,18},{3,19},{4,20},{5,21},{6,22},{7,23},{8,24},{9,... | collective-permute-start | bytes 774152 | tf_op jit(solution)/shard_map/ppermute | solution.py:688
  60.9 1.5 %collective-permute-start.20 = (bf16[336,384]{1,0:T(8,128)(2,1)S(1)}, bf16[336,384]{1,0:T(8,128)(2,1)S(1)}, u32[]{:S(2)}, u32[]{:S(2)}) collective-permute-start(bf16[336,384]{1,0:T(8,128)(2,1)S(1)} %collective-permute-done.19), channel_id=1, source_target_pairs={{4,0},{5,1},{6,2},{7,3},{0,4},{1,5},{2,6},{3,7},{12,8},{13,9},{14,... | collective-permute-start | bytes 774152 | tf_op jit(solution)/shard_map/ppermute | solution.py:507
  78.6 1.6 %collective-permute-start.21 = (bf16[336,384]{1,0:T(8,128)(2,1)S(1)}, bf16[336,384]{1,0:T(8,128)(2,1)S(1)}, u32[]{:S(2)}, u32[]{:S(2)}) collective-permute-start(bf16[336,384]{1,0:T(8,128)(2,1)S(1)} %slice.57), channel_id=1, source_target_pairs={{0,4},{1,5},{2,6},{3,7},{4,0},{5,1},{6,2},{7,3},{8,12},{9,13},{10,... | collective-permute-start | bytes 774152 | tf_op jit(solution)/shard_map/ppermute | solution.py:507
  80.2 10.3 %collective-permute-start.22 = (bf16[336,384]{1,0:T(8,128)(2,1)S(1)}, bf16[336,384]{1,0:T(8,128)(2,1)S(1)}, u32[]{:S(2)}, u32[]{:S(2)}) collective-permute-start(bf16[336,384]{1,0:T(8,128)(2,1)S(1)} %add_convert_fusion.3.refs_0_), channel_id=1, source_target_pairs={{16,0},{17,1},{18,2},{19,3},{20,4},{21,5},{22,6},{23,7},{24,8},{25... | collective-permute-start | bytes 774152 | tf_op jit(solution)/shard_map/ppermute | solution.py:688
  96.0 2.9 %collective-permute-start.23 = (bf16[2,768,384]{2,1,0:T(8,128)(2,1)S(1)}, bf16[2,768,384]{2,1,0:T(8,128)(2,1)S(1)}, u32[]{:S(2)}, u32[]{:S(2)}) collective-permute-start(bf16[2,768,384]{2,1,0:T(8,128)(2,1)S(1)} %get-tuple-element.117), channel_id=1, source_target_pairs={{0,4},{4,0},{8,12},{12,8},{1,5},{5,1},{9,13},{13,9},{2,6},{6,2},{1... | collective-permute-start | bytes 3538952 | tf_op jit(solution)/shard_map/ppermute | solution.py:491
  99.0 10.4 %collective-permute-start.24 = (bf16[384,384]{1,0:T(8,128)(2,1)S(1)}, bf16[384,384]{1,0:T(8,128)(2,1)S(1)}, u32[]{:S(2)}, u32[]{:S(2)}) collective-permute-start(bf16[384,384]{1,0:T(8,128)(2,1)S(1)} %fusion.1.refs_0_), channel_id=1, source_target_pairs={{0,8},{4,12},{8,0},{12,4},{1,9},{5,13},{9,1},{13,5},{2,10},{6,14},... | collective-permute-start | bytes 884744 | tf_op jit(solution)/shard_map/ppermute | solution.py:496
  99.8 9.5 %collective-permute-start.25 = (bf16[384,384]{1,0:T(8,128)(2,1)S(1)}, bf16[384,384]{1,0:T(8,128)(2,1)S(1)}, u32[]{:S(2)}, u32[]{:S(2)}) collective-permute-start(bf16[384,384]{1,0:T(8,128)(2,1)S(1)} %bitcast.77), channel_id=1, source_target_pairs={{0,1},{1,0},{2,3},{3,2},{4,5},{5,4},{6,7},{7,6},{8,9},{9,8},{10,11... | collective-permute-start | bytes 884744 | tf_op jit(solution)/shard_map/ppermute | solution.py:520
  109.5 2.1 %collective-permute-start.26 = (bf16[2,400,384]{2,1,0:T(8,128)(2,1)S(1)}, bf16[2,400,384]{2,1,0:T(8,128)(2,1)S(1)}, u32[]{:S(2)}, u32[]{:S(2)}) collective-permute-start(bf16[2,400,384]{2,1,0:T(8,128)(2,1)S(1)} %get-tuple-element.132), channel_id=1, source_target_pairs={{0,4},{4,0},{8,12},{12,8},{1,5},{5,1},{9,13},{13,9},{2,6},{6,2},{1... | collective-permute-start | bytes 1843208 | tf_op jit(solution)/shard_map/ppermute | solution.py:491
  109.6 3.1 %collective-permute-start.33 = (bf16[336,384]{1,0:T(8,128)(2,1)S(1)}, bf16[336,384]{1,0:T(8,128)(2,1)S(1)}, u32[]{:S(2)}, u32[]{:S(2)}) collective-permute-start(bf16[336,384]{1,0:T(8,128)(2,1)S(1)} %slice.65), channel_id=1, source_target_pairs={{0,4},{1,5},{2,6},{3,7},{4,0},{5,1},{6,2},{7,3},{8,12},{9,13},{10,... | collective-permute-start | bytes 774152 | tf_op jit(solution)/shard_map/ppermute | solution.py:507
  111.7 8.4 %collective-permute-start.28 = (bf16[192,384]{1,0:T(8,128)(2,1)S(1)}, bf16[192,384]{1,0:T(8,128)(2,1)S(1)}, u32[]{:S(2)}, u32[]{:S(2)}) collective-permute-start(bf16[192,384]{1,0:T(8,128)(2,1)S(1)} %bitcast.94), channel_id=1, source_target_pairs={{0,1},{1,0},{2,3},{3,2},{4,5},{5,4},{6,7},{7,6},{8,9},{9,8},{10,11... | collective-permute-start | bytes 442376 | tf_op jit(solution)/shard_map/ppermute | solution.py:520
  112.9 9.8 %collective-permute-start.29 = (bf16[192,384]{1,0:T(8,128)(2,1)S(1)}, bf16[192,384]{1,0:T(8,128)(2,1)S(1)}, u32[]{:S(2)}, u32[]{:S(2)}) collective-permute-start(bf16[192,384]{1,0:T(8,128)(2,1)S(1)} %bitcast.95), channel_id=1, source_target_pairs={{0,2},{1,3},{2,0},{3,1},{4,6},{5,7},{6,4},{7,5},{8,10},{9,11},{10,... | collective-permute-start | bytes 442376 | tf_op jit(solution)/shard_map/ppermute | solution.py:520
  114.7 8.8 %collective-permute-start.27 = (bf16[400,384]{1,0:T(8,128)(2,1)S(1)}, bf16[400,384]{1,0:T(8,128)(2,1)S(1)}, u32[]{:S(2)}, u32[]{:S(2)}) collective-permute-start(bf16[400,384]{1,0:T(8,128)(2,1)S(1)} %fusion), channel_id=1, source_target_pairs={{0,8},{4,12},{8,0},{12,4},{1,9},{5,13},{9,1},{13,5},{2,10},{6,14},... | collective-permute-start | bytes 921608 | tf_op jit(solution)/shard_map/ppermute | solution.py:496
  123.7 5.7 %collective-permute-start.31 = (bf16[96,384]{1,0:T(8,128)(2,1)S(1)}, bf16[96,384]{1,0:T(8,128)(2,1)S(1)}, u32[]{:S(2)}, u32[]{:S(2)}) collective-permute-start(bf16[96,384]{1,0:T(8,128)(2,1)S(1)} %bitcast.98), channel_id=1, source_target_pairs={{0,2},{1,3},{2,0},{3,1},{4,6},{5,7},{6,4},{7,5},{8,10},{9,11},{10,... | collective-permute-start | bytes 221192 | tf_op jit(solution)/shard_map/ppermute | solution.py:520
  124.9 4.4 %collective-permute-start.32 = (bf16[96,384]{1,0:T(8,128)(2,1)S(1)}, bf16[96,384]{1,0:T(8,128)(2,1)S(1)}, u32[]{:S(2)}, u32[]{:S(2)}) collective-permute-start(bf16[96,384]{1,0:T(8,128)(2,1)S(1)} %fusion.4), channel_id=1, source_target_pairs={{0,8},{4,12},{8,0},{12,4},{1,9},{5,13},{9,1},{13,5},{2,10},{6,14},... | collective-permute-start | bytes 221192 | tf_op jit(solution)/shard_map/ppermute | solution.py:496
  126.5 5.3 %collective-permute-start.30 = (bf16[208,384]{1,0:T(8,128)(2,1)S(1)}, bf16[208,384]{1,0:T(8,128)(2,1)S(1)}, u32[]{:S(2)}, u32[]{:S(2)}) collective-permute-start(bf16[208,384]{1,0:T(8,128)(2,1)S(1)} %pad_maximum_fusion.5), channel_id=1, source_target_pairs={{0,1},{1,0},{2,3},{3,2},{4,5},{5,4},{6,7},{7,6},{8,9},{9,8},{10,11... | collective-permute-start | bytes 479240 | tf_op jit(solution)/shard_map/ppermute | solution.py:520
  132.0 9.9 %copy-start.2 = (f32[16,384]{1,0:T(8,128)}, f32[16,384]{1,0:T(8,128)S(1)}, u32[]{:S(2)}) copy-start(f32[16,384]{1,0:T(8,128)S(1)} %slice_add_fusion.rest_ref) | copy-start | bytes 73732
  132.7 9.1 %collective-permute-start.34 = (bf16[112,384]{1,0:T(8,128)(2,1)S(1)}, bf16[112,384]{1,0:T(8,128)(2,1)S(1)}, u32[]{:S(2)}, u32[]{:S(2)}) collective-permute-start(bf16[112,384]{1,0:T(8,128)(2,1)S(1)} %pad_maximum_fusion.8), channel_id=1, source_target_pairs={{0,2},{1,3},{2,0},{3,1},{4,6},{5,7},{6,4},{7,5},{8,10},{9,11},{10,... | collective-permute-start | bytes 258056 | tf_op jit(solution)/shard_map/ppermute | solution.py:520
  135.3 8.9 %collective-permute-start.36 = (bf16[168,384]{1,0:T(8,128)(2,1)S(1)}, bf16[168,384]{1,0:T(8,128)(2,1)S(1)}, u32[]{:S(2)}, u32[]{:S(2)}) collective-permute-start(bf16[168,384]{1,0:T(8,128)(2,1)S(1)} %get-tuple-element.186), channel_id=1, source_target_pairs={{2,0},{0,1},{6,2},{4,3},{3,4},{1,5},{7,6},{5,7},{10,8},{8,9},{14,1... | collective-permute-start | bytes 387080 | tf_op jit(solution)/shard_map/ppermute | solution.py:507
  136.3 7.9 %collective-permute-start.35 = (bf16[168,384]{1,0:T(8,128)(2,1)S(1)}, bf16[168,384]{1,0:T(8,128)(2,1)S(1)}, u32[]{:S(2)}, u32[]{:S(2)}) collective-permute-start(bf16[168,384]{1,0:T(8,128)(2,1)S(1)} %get-tuple-element.187), channel_id=1, source_target_pairs={{0,0},{2,1},{4,2},{6,3},{1,4},{3,5},{5,6},{7,7},{8,8},{10,9},{12,1... | collective-permute-start | bytes 387080 | tf_op jit(solution)/shard_map/ppermute | solution.py:507
  141.9 0.6 copy-start.5
